TPU v7x, 256 devices: a whole 4x4x8 slice. The times are simulated.
256 devices in a mesh: leaf: 256 (over y, z, x, core).
Axes of the slice: x: 4, y: 4, z: 8, core: 2. Of those that a mesh axis runs over, the one named last changes fastest.
Arguments:
- rhs: float32 [16, 524288], P(None, 'leaf'), may hold values from -180 to 180
- box_rows: int32 [1024], P('leaf'), may hold values from 384 to 512, as said below
- dense: float32 [1024, 512, 256], P('leaf'), may hold values from -0.375 to 0.375
- row_basis: float32 [1024, 512, 128], P('leaf'), may hold values from -0.5 to 0.5
- col_basis: float32 [1024, 256, 128], P('leaf'), may hold values from -0.375 to 0.375
- local_col_transfer: float32 [768, 256, 128], P('leaf'), may hold values from -0.4375 to 0.4375
- local_row_transfer: float32 [768, 256, 128], P('leaf'), may hold values from -0.4375 to 0.4375
- local_coupling: float32 [768, 2, 128, 128], P('leaf'), may hold values from -0.5 to 0.5
- upper_col_transfer: float32 [7, 256, 128], replicated, may hold values from -0.4375 to 0.4375
- upper_row_transfer: float32 [7, 256, 128], replicated, may hold values from -0.4375 to 0.4375
- upper_coupling: float32 [8, 2, 128, 128], replicated, may hold values from -0.5 to 0.5
Outputs:
- solution: float32 [16, 262144], P(None, 'leaf')
Inputs may be any that keep to these rules, and one draw needn't show every extreme that they name: `box_rows`: 512 in some leaf and 384 in another, in every draw.
All inputs are finite; a program needn't handle non-finite values.
Results may differ from a plain program's by a relative error of at most 0.00017.
Values sent between devices are 32-bit elements; how exact they have to be, the bound alone decides.
No kernel may reach another device: no remote copies, remote signals or barrier semaphores. Data moves between devices by JAX's collectives and lax.ppermute only.
A program may use at most 128 MiB of HBM per device.

v0:
```python
import jax
import jax.numpy as jnp
from jax import lax
from jax.sharding import PartitionSpec as P

ITERS = 2


precise = lax.Precision.HIGHEST


def climb(children, transfer):
    node_count = transfer.shape[0]
    paired = children.reshape(node_count, 2, children.shape[1], children.shape[2])
    blocks = transfer.reshape(node_count, 2, children.shape[2], transfer.shape[2])
    return jnp.einsum("minj,mijk->mnk", paired, blocks, precision=precise)


def descend(parent, transfer):
    node_count = transfer.shape[0]
    blocks = transfer.reshape(node_count, 2, transfer.shape[2], transfer.shape[2])
    spread = jnp.einsum("mnk,mijk->minj", parent, blocks, precision=precise)
    return spread.reshape(node_count * 2, parent.shape[1], parent.shape[2])


def couple_forward(children, coupling):
    node_count = coupling.shape[0]
    paired = children.reshape(node_count, 2, children.shape[1], children.shape[2])
    sibling = jnp.flip(paired, 1)
    gained = jnp.einsum("minj,mijk->mink", sibling, coupling, precision=precise)
    return gained.reshape(children.shape)


def couple_adjoint(children, coupling):
    node_count = coupling.shape[0]
    paired = children.reshape(node_count, 2, children.shape[1], children.shape[2])
    gained = jnp.einsum("mink,mijk->minj", paired, coupling, precision=precise)
    return jnp.flip(gained, 1).reshape(children.shape)


def shared_climb(children, transfer):
    node_count = children.shape[0] // 2
    rank_size = children.shape[2]
    paired = children.reshape(node_count, 2, children.shape[1], rank_size)
    blocks = transfer.reshape(2, rank_size, transfer.shape[1])
    return jnp.einsum("minj,ijk->mnk", paired, blocks, precision=precise)


def shared_descend(parent, transfer):
    rank_size = parent.shape[2]
    blocks = transfer.reshape(2, rank_size, transfer.shape[1])
    spread = jnp.einsum("mnk,ijk->minj", parent, blocks, precision=precise)
    return spread.reshape(parent.shape[0] * 2, parent.shape[1], rank_size)


def shared_couple(children, coupling, adjoint_mode):
    node_count = children.shape[0] // 2
    paired = children.reshape(node_count, 2, children.shape[1], children.shape[2])
    if adjoint_mode:
        gained = jnp.flip(jnp.einsum("mink,ijk->minj", paired, coupling, precision=precise), 1)
    else:
        gained = jnp.einsum("minj,ijk->mink", jnp.flip(paired, 1), coupling, precision=precise)
    return gained.reshape(children.shape)


def column_norm(vector):
    partial_sum = jnp.sum(vector * vector, axis=1)
    return jnp.sqrt(lax.psum(partial_sum, "leaf"))


def upper_by_gather(root_summary, climbers, descenders, couplers, adjoint_mode):
    all_roots = lax.all_gather(root_summary[None], "leaf", axis=0, tiled=True)
    height_total = couplers.shape[0]
    summaries = [all_roots]
    coupled = []
    for height in range(height_total):
        coupled.append(shared_couple(summaries[height], couplers[height], adjoint_mode))
        if height + 1 < height_total:
            summaries.append(shared_climb(summaries[height], climbers[height]))
    potential = coupled[height_total - 1]
    for height in reversed(range(height_total - 1)):
        potential = coupled[height] + shared_descend(potential, descenders[height])
    return lax.dynamic_index_in_dim(potential, lax.axis_index("leaf"), 0, keepdims=False)


def upper_tree(root_summary, climbers, descenders, couplers, adjoint_mode):
    potential = upper_by_gather(root_summary, climbers, descenders, couplers, adjoint_mode)
    return potential


def local_tree(
    leaf_summary,
    climbers,
    descenders,
    couplers,
    adjoint_mode,
    upper_climb,
    upper_descend,
    upper_couple,
):
    cross_fn = couple_adjoint if adjoint_mode else couple_forward
    leaf_count = leaf_summary.shape[0]
    local_levels = leaf_count.bit_length() - 1
    summaries = [leaf_summary]
    coupled = []
    offsets = []
    offset = 0
    for height in range(local_levels):
        node_width = leaf_count >> height + 1
        coupled.append(cross_fn(summaries[height], couplers[offset : offset + node_width]))
        summaries.append(climb(summaries[height], climbers[offset : offset + node_width]))
        offsets.append(offset)
        offset += node_width
    potential = upper_tree(
        summaries[local_levels][0], upper_climb, upper_descend, upper_couple, adjoint_mode
    )[None]
    for height in reversed(range(local_levels)):
        node_width = leaf_count >> height + 1
        start_row = offsets[height]
        potential = coupled[height] + descend(
            potential, descenders[start_row : start_row + node_width]
        )
    return potential


def local(
    rhs,
    box_rows,
    dense,
    row_basis,
    col_basis,
    local_col_transfer,
    local_row_transfer,
    local_coupling,
    upper_col_transfer,
    upper_row_transfer,
    upper_coupling,
):
    rhs_count = rhs.shape[0]
    leaf_count = dense.shape[0]
    leaf_rows = dense.shape[1]
    leaf_cols = dense.shape[2]
    slots = lax.broadcasted_iota(jnp.int32, (leaf_count, leaf_rows), 1)
    live_rows = (slots < box_rows[:, None]).astype(jnp.float32)

    def forward(vector):
        blocks = vector.reshape(rhs_count, leaf_count, leaf_cols)
        summary = jnp.einsum("nqc,qck->qnk", blocks, col_basis, precision=precise)
        potential = local_tree(
            summary,
            local_col_transfer,
            local_row_transfer,
            local_coupling,
            False,
            upper_col_transfer,
            upper_row_transfer,
            upper_coupling,
        )
        result = jnp.einsum("qrc,nqc->nqr", dense, blocks, precision=precise)
        result = result + jnp.einsum("qrk,qnk->nqr", row_basis, potential, precision=precise)
        return (result * live_rows[None]).reshape(rhs_count, leaf_count * leaf_rows)

    def adjoint(vector):
        blocks = vector.reshape(rhs_count, leaf_count, leaf_rows) * live_rows[None]
        summary = jnp.einsum("nqr,qrk->qnk", blocks, row_basis, precision=precise)
        potential = local_tree(
            summary,
            local_row_transfer,
            local_col_transfer,
            local_coupling,
            True,
            upper_row_transfer,
            upper_col_transfer,
            upper_coupling,
        )
        result = jnp.einsum("qrc,nqr->nqc", dense, blocks, precision=precise)
        result = result + jnp.einsum("qck,qnk->nqc", col_basis, potential, precision=precise)
        return result.reshape(rhs_count, leaf_count * leaf_cols)

    def advance(apply_fn, unscaled, previous):
        scale_value = column_norm(unscaled)
        normalized = unscaled / scale_value[:, None]
        following = apply_fn(normalized)
        if previous is not None:
            following = following - scale_value[:, None] * previous
        return (scale_value, normalized, following)

    masked_rhs = rhs * live_rows.reshape(1, leaf_count * leaf_rows)
    beta_norm, left_vector, unscaled = advance(adjoint, masked_rhs, None)
    alpha_norm, right_vector, unscaled = advance(forward, unscaled, left_vector)
    search = right_vector
    solution = jnp.zeros((rhs_count, leaf_count * leaf_cols), jnp.float32)
    phi_bar = beta_norm
    rho_bar = alpha_norm
    for iteration in range(ITERS):
        beta_norm, left_vector, unscaled = advance(adjoint, unscaled, right_vector)
        if iteration + 1 < ITERS:
            alpha_norm, right_vector, unscaled = advance(forward, unscaled, left_vector)
        else:
            alpha_norm = column_norm(unscaled)
            right_vector = unscaled / alpha_norm[:, None]
        rho_value = jnp.sqrt(rho_bar * rho_bar + beta_norm * beta_norm)
        cosine = rho_bar / rho_value
        sine_value = beta_norm / rho_value
        theta_value = sine_value * alpha_norm
        rho_bar = -cosine * alpha_norm
        phi_value = cosine * phi_bar
        phi_bar = sine_value * phi_bar
        solution = solution + (phi_value / rho_value)[:, None] * search
        search = right_vector - (theta_value / rho_value)[:, None] * search
    return solution


def solution(mesh):
    return jax.shard_map(
        local,
        mesh=mesh,
        in_specs=(
            P(None, "leaf"),
            P("leaf"),
            P("leaf", None, None),
            P("leaf", None, None),
            P("leaf", None, None),
            P("leaf", None, None),
            P("leaf", None, None),
            P("leaf", None, None, None),
            P(),
            P(),
            P(),
        ),
        out_specs=P(None, "leaf"),
        check_vma=False,
    )
```

profile of v0, /device:TPU:2, one launch (start us, length us, event | category | flops | bytes accessed | tf_op | source)
XLA Modules:
  0.0 1041.4 jit_solution(17155005844562723856)
XLA Ops:
  10.4 78.7 %psum.35 = f32[16]{0:T(128)S(1)} all-reduce(f32[16]{0:T(128)S(1)} %multiply_reduce_fusion.2), channel_id=1, replica_groups=mesh['leaf'=256] {'leaf'}, use_global_device_ids=true, to_apply=%region_1.0 | all-reduce | flops 16 | bytes 128 | tf_op jit(solution)/shard_map/psum | solution.py:68
  101.5 92.5 %all-gather.9.cloned.1.call-done = f32[4096,128]{1,0:T(8,128)} async-done(((f32[16,128]{1,0:T(8,128)}), f32[4096,128]{1,0:T(8,128)}) %all-gather.9.cloned.1.call-update) | async-done | bytes 2097168 | tf_op jit(solution)/shard_map/all_gather | solution.py:72
  194.0 3.4 fusion.199
  228.2 2.3 rev.118
  230.4 2.6 fusion.13
  233.2 3.3 fusion.4
  242.1 75.6 %psum.36 = f32[16]{0:T(128)} all-reduce(f32[16]{0:T(128)} %get-tuple-element.29), channel_id=1, replica_groups=mesh['leaf'=256] {'leaf'}, use_global_device_ids=true, to_apply=%region_3.4 | all-reduce | flops 16 | bytes 128 | tf_op jit(solution)/shard_map/psum | solution.py:68
  330.4 3.3 fusion.196
  333.7 90.9 %all-gather.11.cloned.1.call-done = f32[4096,128]{1,0:T(8,128)} async-done(((f32[16,128]{1,0:T(8,128)}), f32[4096,128]{1,0:T(8,128)}) %all-gather.11.cloned.1.call-update) | async-done | bytes 2097168 | tf_op jit(solution)/shard_map/all_gather | solution.py:72
  424.7 3.4 fusion.204
  461.7 2.3 rev.127
  463.9 2.3 convolution_bitcast_fusion.5
  468.4 2.9 copy.93
  471.3 3.2 rev.126
  474.5 3.6 fusion.105
  484.2 75.6 %psum.37 = f32[16]{0:T(128)} all-reduce(f32[16]{0:T(128)} %multiply_reduce_fusion.1), channel_id=1, replica_groups=mesh['leaf'=256] {'leaf'}, use_global_device_ids=true, to_apply=%region_5.6 | all-reduce | flops 16 | bytes 128 | tf_op jit(solution)/shard_map/psum | solution.py:68
  574.6 2.6 fusion.127
  577.3 91.4 %all-gather.13.cloned.1.call-done = f32[4096,128]{1,0:T(8,128)} async-done(((f32[16,128]{1,0:T(8,128)}), f32[4096,128]{1,0:T(8,128)}) %all-gather.13.cloned.1.call-update) | async-done | bytes 2097168 | tf_op jit(solution)/shard_map/all_gather | solution.py:72
  668.6 3.4 fusion.209
  702.8 2.3 rev.135
  705.0 2.6 fusion.11
  707.8 3.3 fusion.7
  716.2 76.0 %psum.38 = f32[16]{0:T(128)} all-reduce(f32[16]{0:T(128)S(1)} %get-tuple-element.10), channel_id=1, replica_groups=mesh['leaf'=256] {'leaf'}, use_global_device_ids=true, to_apply=%region_7.8 | all-reduce | flops 16 | bytes 128 | tf_op jit(solution)/shard_map/psum | solution.py:68
  806.2 3.3 fusion.180
  809.5 89.7 %all-gather.15.cloned.1.call-done = f32[4096,128]{1,0:T(8,128)} async-done(((f32[16,128]{1,0:T(8,128)}), f32[4096,128]{1,0:T(8,128)}) %all-gather.15.cloned.1.call-update) | async-done | bytes 2097168 | tf_op jit(solution)/shard_map/all_gather | solution.py:72
  899.2 3.4 fusion.214
  935.1 2.3 rev.144
  937.4 2.3 convolution_bitcast_fusion.1
  942.1 2.5 copy.140
  944.6 3.2 rev.143
  947.8 3.6 fusion.102
  956.3 75.6 %psum.39 = f32[16]{0:T(128)S(1)} all-reduce(f32[16]{0:T(128)S(1)} %multiply_reduce_fusion), channel_id=1, replica_groups=mesh['leaf'=256] {'leaf'}, use_global_device_ids=true, to_apply=%region_9.10 | all-reduce | flops 16 | bytes 128 | tf_op jit(solution)/shard_map/psum | solution.py:68
  (393 shorter events, 213.1 us)
Async XLA Ops:
  6.5 93.2 %copy-start = (f32[4,512,256]{2,1,0:T(8,128)S(1)}, f32[4,512,256]{2,1,0:T(8,128)}, u32[]{:S(2)}) copy-start(f32[4,512,256]{2,1,0:T(8,128)} %param.13) | copy-start | bytes 6291460
  6.5 86.6 %copy-start.68 = (f32[3,256,128]{2,1,0:T(8,128)S(1)}, f32[3,256,128]{2,1,0:T(8,128)}, u32[]{:S(2)}) copy-start(f32[3,256,128]{2,1,0:T(8,128)} %param.16) | copy-start | bytes 1179652
  6.5 88.0 %copy-start.14 = (f32[3,2,128,128]{3,2,1,0:T(8,128)S(1)}, f32[3,2,128,128]{3,2,1,0:T(8,128)}, u32[]{:S(2)}) copy-start(f32[3,2,128,128]{3,2,1,0:T(8,128)} %param.18) | copy-start | bytes 1179652
  6.5 187.5 %all-gather.9.cloned.1.call-start = ((), (), s32[]{:S(2)}) async-start(), calls=%async_computation | async-start | bytes 2105344 | tf_op jit(solution)/shard_map/all_gather | solution.py:72
  10.4 88.4 %copy-start.28 = (f32[1,256,128]{2,1,0:T(8,128)}, f32[1,256,128]{2,1,0:T(8,128)S(1)}, u32[]{:S(2)}) copy-start(f32[1,256,128]{2,1,0:T(8,128)S(1)} %slice.59) | copy-start | bytes 393220
  93.0 331.6 %all-gather.11.cloned.1.call-start = ((), (), s32[]{:S(2)}) async-start(), calls=%async_computation.1 | async-start | bytes 2105344 | tf_op jit(solution)/shard_map/all_gather | solution.py:72
  101.5 95.9 %copy-start.1 = (f32[8,2,128,128]{3,2,1,0:T(8,128)S(1)}, f32[8,2,128,128]{3,2,1,0:T(8,128)}, u32[]{:S(2)}) copy-start(f32[8,2,128,128]{3,2,1,0:T(8,128)} %param.21) | copy-start | bytes 3145732
  194.0 5.5 copy-start.42
  197.5 4.4 copy-start.31
  199.5 4.1 copy-start.34
  200.5 5.8 copy-start.23
  200.5 6.9 copy-start.26
  323.8 344.8 %all-gather.13.cloned.1.call-start = ((), (), s32[]{:S(2)}) async-start(), calls=%async_computation.2 | async-start | bytes 2105344 | tf_op jit(solution)/shard_map/all_gather | solution.py:72
  424.7 4.4 copy-start.46
  424.7 6.2 copy-start.40
  428.1 3.8 copy-start.21
  428.1 4.7 copy-start.19
  474.5 3.6 copy-start.18
  474.5 3.6 copy-start.48
  567.8 331.4 %all-gather.15.cloned.1.call-start = ((), (), s32[]{:S(2)}) async-start(), calls=%async_computation.3 | async-start | bytes 2105344 | tf_op jit(solution)/shard_map/all_gather | solution.py:72
  668.6 3.5 copy-start.44
  668.6 4.5 copy-start.32
  899.2 4.4 copy-start.47
  899.2 6.2 copy-start.41
  902.6 3.8 copy-start.22
  902.7 4.0 copy-start.20
  902.7 5.3 copy-start.25
  925.4 7.3 copy-start.33
  935.1 4.6 copy-start.45
  947.8 3.6 copy-start.17
  947.8 3.6 copy-start.49
  954.5 78.8 %copy-start.74 = (f32[4,2,8,256]{3,2,0,1:T(8,128)S(1)}, f32[4,2,8,256]{3,2,0,1:T(8,128)}, u32[]{:S(2)}) copy-start(f32[4,2,8,256]{3,2,0,1:T(8,128)} %copy.264) | copy-start | bytes 196612
  (68 other events, 107.0 us)
Sparse Core Ops, SparseCore 0:
  93.2 100.8 all-gather.8
  324.0 100.6 all-gather.10
  567.9 100.6 all-gather.12
  798.5 100.6 all-gather.14
where the time goes:
time: 1060 us; the launch traced here: 1040 us
  blocking collectives  381 us (36%)
  waiting for transfers between devices  365 us (34%)
  matrix products  163 us (15%)
  local copies, waits for them, and re-layouts  108 us (10%)
  between operations  15 us (1%)
    psum x5, blocking collectives, column_norm(): return jnp.sqrt(lax.psum(partial_sum, 'leaf'))  381 us
    all_gather x4, waiting for transfers between devices, upper_by_gather(): all_roots = lax.all_gather(root_summary[None], 'leaf', axis=0, tiled=True)  364 us
    dot_general x28, matrix products, shared_descend(): spread = jnp.einsum('mnk,ijk->minj', parent, blocks, precision=precise)  41.7 us
    dot_general x28, matrix products, shared_climb(): return jnp.einsum('minj,ijk->mnk', paired, blocks, precision=precise)  26.9 us
    rev x14, local copies, waits for them, and re-layouts, shared_couple(): jnp.flip(paired, 1)  26.9 us
    dot_general x16, matrix products, shared_couple(): jnp.einsum('minj,ijk->mink', jnp.flip(paired, 1), coupling, precision=pre...  26 us
    dot_general x16, matrix products, shared_couple(): jnp.einsum('mink,ijk->minj', paired, coupling, precision=precise)  23.3 us
    rev x14, local copies, waits for them, and re-layouts, shared_couple(): jnp.flip(jnp.einsum('mink,ijk->minj', paired, coupling, precision=precise...  23 us
  transfers between devices with their start and end apart: 4, of which 4 were waited for; matrix products, arithmetic and copies ran while one was open for 4% of the time, Pallas kernels for 0%

commit v1 on v0

v1 whole, which is shorter than its diff:
```python
import functools

import jax
import jax.numpy as jnp
from jax import lax
from jax.experimental import pallas as pl
from jax.experimental.pallas import tpu as pltpu
from jax.sharding import PartitionSpec as P

RHS = 16
RANK = 128
LEAF_DEV = 4
LEAF_ROWS = 512
LEAF_COLS = 256
MSG = 24
GROUP = 16
VMEM_LIMIT = 40 * 1024 * 1024

f32 = jnp.float32
bf16 = jnp.bfloat16


def split(v):
    head = v.astype(bf16)
    return head, (v - head.astype(f32)).astype(bf16)


def mm(x, w, transposed=False):
    xh, xl = split(x)
    wh, wl = split(w)
    dims = (((1,), (1 if transposed else 0,)), ((), ()))
    n = x.shape[0]
    both = lax.dot_general(jnp.concatenate([xh, xl], 0), wh, dims, preferred_element_type=f32)
    rest = lax.dot_general(xh, wl, dims, preferred_element_type=f32)
    return both[:n] + (both[n:] + rest)


def eye():
    return (
        lax.broadcasted_iota(jnp.int32, (RHS, RANK), 0)
        == lax.broadcasted_iota(jnp.int32, (RHS, RANK), 1)
    ).astype(f32)


def stat_row(column):
    row = jnp.sum(column * eye(), axis=0, keepdims=True)
    first = (lax.broadcasted_iota(jnp.int32, (8, RANK), 0) == 0).astype(f32)
    return row * first


def stat_column(block):
    row = jnp.sum(block, axis=0, keepdims=True)
    return jnp.sum(row * eye(), axis=1, keepdims=True)


def sum_squares(v):
    return jnp.sum(v * v, axis=1, keepdims=True)


def send(out_ref, value):
    for peer in range(GROUP):
        out_ref[peer] = value


def local_up(parts, basis_ref, climb_ref):
    leaf = [mm(parts[q], basis_ref[q]) for q in range(LEAF_DEV)]
    node = [
        mm(jnp.concatenate([leaf[2 * m], leaf[2 * m + 1]], 1), climb_ref[m]) for m in range(2)
    ]
    root = mm(jnp.concatenate(node, 1), climb_ref[2])
    return leaf, node, root


def couple(sibling, coupling_ref, node, child, adjoint):
    if adjoint:
        return mm(sibling, coupling_ref[node, 1 - child], transposed=True)
    return mm(sibling, coupling_ref[node, child])


def local_down(root, leaf, node, coupling_ref, descend_ref, adjoint):
    spread = mm(root, descend_ref[2], transposed=True)
    out = []
    for m in range(2):
        here = couple(node[1 - m], coupling_ref, 2, m, adjoint)
        here = here + spread[:, m * RANK : (m + 1) * RANK]
        below = mm(here, descend_ref[m], transposed=True)
        for i in range(2):
            gained = couple(leaf[2 * m + 1 - i], coupling_ref, m, i, adjoint)
            out.append(gained + below[:, i * RANK : (i + 1) * RANK])
    return out


def live_mask(rows_ref, q):
    slots = lax.broadcasted_iota(jnp.int32, (RHS, LEAF_ROWS), 1)
    return (slots < rows_ref[q]).astype(f32)


def row_part(v, q):
    return v[:, q * LEAF_ROWS : (q + 1) * LEAF_ROWS]


def col_part(v, q):
    return v[:, q * LEAF_COLS : (q + 1) * LEAF_COLS]


def finish_up(parts, basis_ref, climb_ref, msg_ref, keep_ref, squares):
    leaf, node, root = local_up(parts, basis_ref, climb_ref)
    for k, value in enumerate(leaf + node):
        keep_ref[k] = value
    send(msg_ref, jnp.concatenate([root, stat_row(squares)], 0))


def start_kernel(rows_ref, rhs_ref, row_basis_ref, local_row_ref, z_ref, msg_ref, keep_ref):
    parts = []
    squares = jnp.zeros((RHS, 1), f32)
    for q in range(LEAF_DEV):
        part = rhs_ref[:, q * LEAF_ROWS : (q + 1) * LEAF_ROWS] * live_mask(rows_ref, q)
        z_ref[:, q * LEAF_ROWS : (q + 1) * LEAF_ROWS] = part
        squares = squares + sum_squares(part)
        parts.append(part)
    finish_up(parts, row_basis_ref, local_row_ref, msg_ref, keep_ref, squares)


def lower_kernel(me_ref, recv_ref, climb_ref, msg_ref, sib_ref, scratch_ref):
    place = me_ref[0] % GROUP
    level = [recv_ref[d, :RHS] for d in range(GROUP)]
    sib_ref[0] = recv_ref[place ^ 1, :RHS]
    base = 0
    for height in range(4):
        count = len(level) // 2
        paired = jnp.concatenate(
            [jnp.concatenate([level[2 * m], level[2 * m + 1]], 1) for m in range(count)], 0
        )
        parents = mm(paired, climb_ref[height])
        level = [parents[m * RHS : (m + 1) * RHS] for m in range(count)]
        if height < 3:
            for m in range(count):
                scratch_ref[base + m] = level[m]
            sib_ref[height + 1] = scratch_ref[base + ((place >> (height + 1)) ^ 1)]
            base += count
    stats = recv_ref[0, RHS:]
    for d in range(1, GROUP):
        stats = stats + recv_ref[d, RHS:]
    send(msg_ref, jnp.concatenate([level[0], stats], 0))


def upper_potential(me_ref, recv_ref, sib_ref, climb_ref, descend_ref, coupling_ref, scratch_ref, adjoint):
    me = me_ref[0]
    place = me // GROUP
    level = [recv_ref[d, :RHS] for d in range(GROUP)]
    siblings = [sib_ref[j] for j in range(4)]
    siblings.append(recv_ref[place ^ 1, :RHS])
    base = 0
    for height in range(3):
        count = len(level) // 2
        paired = jnp.concatenate(
            [jnp.concatenate([level[2 * m], level[2 * m + 1]], 1) for m in range(count)], 0
        )
        parents = mm(paired, climb_ref[4 + height])
        level = [parents[m * RHS : (m + 1) * RHS] for m in range(count)]
        for m in range(count):
            scratch_ref[base + m] = level[m]
        siblings.append(scratch_ref[base + ((place >> (height + 1)) ^ 1)])
        base += count
    gained = []
    for j in range(8):
        child = (me >> j) & 1
        if adjoint:
            gained.append(mm(siblings[j], coupling_ref[j, 1 - child], transposed=True))
        else:
            gained.append(mm(siblings[j], coupling_ref[j, child]))
    potential = gained[7]
    for j in reversed(range(7)):
        child = (me >> j) & 1
        half = descend_ref[j, pl.ds(pl.multiple_of(child * RANK, RANK), RANK), :]
        potential = gained[j] + mm(potential, half, transposed=True)
    stats = recv_ref[0, RHS:]
    for d in range(1, GROUP):
        stats = stats + recv_ref[d, RHS:]
    return potential, jnp.sqrt(stat_column(stats))


def adjoint_kernel(
    first,
    me_ref,
    recv_ref,
    sib_ref,
    up_row_ref,
    up_col_ref,
    up_couple_ref,
    keep_ref,
    dense_ref,
    col_basis_ref,
    local_row_ref,
    local_col_ref,
    local_couple_ref,
    z_ref,
    *rest,
):
    if first:
        u_ref, v_ref, norm_ref, msg_ref, next_ref, scratch_ref = rest
    else:
        prev_ref, u_ref, v_ref, norm_ref, msg_ref, next_ref, scratch_ref = rest
    potential, norm = upper_potential(
        me_ref, recv_ref, sib_ref, up_row_ref, up_col_ref, up_couple_ref, scratch_ref, True
    )
    inverse = 1.0 / norm
    norm_ref[...] = jnp.broadcast_to(norm, (RHS, RANK))
    leaf = [keep_ref[q] for q in range(LEAF_DEV)]
    node = [keep_ref[LEAF_DEV + m] for m in range(2)]
    down = local_down(potential, leaf, node, local_couple_ref, local_col_ref, True)
    parts = []
    squares = jnp.zeros((RHS, 1), f32)
    for q in range(LEAF_DEV):
        rows = slice(q * LEAF_ROWS, (q + 1) * LEAF_ROWS)
        cols = slice(q * LEAF_COLS, (q + 1) * LEAF_COLS)
        z = z_ref[:, rows]
        u_ref[:, rows] = z * inverse
        v = mm(z, dense_ref[q]) + mm(down[q], col_basis_ref[q], transposed=True)
        v = v * inverse
        if not first:
            v = v - norm * prev_ref[:, cols]
        v_ref[:, cols] = v
        squares = squares + sum_squares(v)
        parts.append(v)
    finish_up(parts, col_basis_ref, local_col_ref, msg_ref, next_ref, squares)


def forward_kernel(
    last,
    me_ref,
    recv_ref,
    sib_ref,
    up_row_ref,
    up_col_ref,
    up_couple_ref,
    keep_ref,
    dense_ref,
    row_basis_ref,
    local_row_ref,
    local_col_ref,
    local_couple_ref,
    rows_ref,
    x_ref,
    u_ref,
    *rest,
):
    if last:
        v_ref, norm_ref, msg_ref, scratch_ref = rest
    else:
        v_ref, z_ref, norm_ref, msg_ref, next_ref, scratch_ref = rest
    potential, norm = upper_potential(
        me_ref, recv_ref, sib_ref, up_col_ref, up_row_ref, up_couple_ref, scratch_ref, False
    )
    inverse = 1.0 / norm
    norm_ref[...] = jnp.broadcast_to(norm, (RHS, RANK))
    leaf = [keep_ref[q] for q in range(LEAF_DEV)]
    node = [keep_ref[LEAF_DEV + m] for m in range(2)]
    down = local_down(potential, leaf, node, local_couple_ref, local_row_ref, False)
    parts = []
    squares = jnp.zeros((RHS, 1), f32)
    for q in range(LEAF_DEV):
        rows = slice(q * LEAF_ROWS, (q + 1) * LEAF_ROWS)
        cols = slice(q * LEAF_COLS, (q + 1) * LEAF_COLS)
        x = x_ref[:, cols]
        v_ref[:, cols] = x * inverse
        z = mm(x, dense_ref[q], transposed=True) + mm(down[q], row_basis_ref[q], transposed=True)
        z = z * live_mask(rows_ref, q) * inverse - norm * u_ref[:, rows]
        squares = squares + sum_squares(z)
        if not last:
            z_ref[:, rows] = z
            parts.append(z)
    if last:
        send(msg_ref, stat_row(squares))
    else:
        finish_up(parts, row_basis_ref, local_row_ref, msg_ref, next_ref, squares)


def relay_kernel(recv_ref, msg_ref):
    stats = recv_ref[0]
    for d in range(1, GROUP):
        stats = stats + recv_ref[d]
    send(msg_ref, stats)


def final_kernel(recv_ref, beta1_ref, alpha1_ref, beta2_ref, alpha2_ref, v1_ref, v2_ref, out_ref):
    stats = recv_ref[0]
    for d in range(1, GROUP):
        stats = stats + recv_ref[d]
    beta3 = jnp.sqrt(stat_column(stats))
    phi_bar = beta1_ref[:, :1]
    alpha1 = alpha1_ref[:, :1]
    beta2 = beta2_ref[:, :1]
    alpha2 = alpha2_ref[:, :1]
    rho1 = jnp.sqrt(alpha1 * alpha1 + beta2 * beta2)
    cosine = alpha1 / rho1
    sine = beta2 / rho1
    theta = sine * alpha2
    rho_bar = -cosine * alpha2
    phi1 = cosine * phi_bar
    phi_bar = sine * phi_bar
    rho2 = jnp.sqrt(rho_bar * rho_bar + beta3 * beta3)
    phi2 = rho_bar / rho2 * phi_bar
    v1 = v1_ref[...]
    search = v2_ref[...] - (theta / rho1) * v1
    out_ref[...] = (phi1 / rho1) * v1 + (phi2 / rho2) * search


def call(kernel, outs, operands, scalars=0, scratch=()):
    smem = pl.BlockSpec(memory_space=pltpu.SMEM)
    vmem = pl.BlockSpec(memory_space=pltpu.VMEM)
    return pl.pallas_call(
        kernel,
        out_shape=[jax.ShapeDtypeStruct(shape, f32) for shape in outs],
        in_specs=[smem if isinstance(k, Scalar) else vmem for k in operands],
        out_specs=[vmem] * len(outs),
        scratch_shapes=list(scratch),
        compiler_params=pltpu.CompilerParams(vmem_limit_bytes=VMEM_LIMIT),
    )(*[k.value if isinstance(k, Scalar) else k for k in operands])


class Scalar:
    def __init__(self, value):
        self.value = value


def device_groups(devices, stride):
    out = []
    for base in range(devices):
        if (base // stride) % GROUP == 0:
            out.append([base + k * stride for k in range(GROUP)])
    return out


def local(
    devices,
    rhs,
    box_rows,
    dense,
    row_basis,
    col_basis,
    local_col,
    local_row,
    local_couple,
    up_col,
    up_row,
    up_couple,
):
    me = Scalar(lax.axis_index("leaf").astype(jnp.int32).reshape(1))
    rows = Scalar(box_rows)
    near = device_groups(devices, 1)
    far = device_groups(devices, GROUP)

    def swap(message, groups):
        return lax.all_to_all(message, "leaf", 0, 0, axis_index_groups=groups)

    message_shape = (GROUP, MSG, RANK)
    keep_shape = (6, RHS, RANK)
    row_shape = (RHS, LEAF_DEV * LEAF_ROWS)
    col_shape = (RHS, LEAF_DEV * LEAF_COLS)
    norm_shape = (RHS, RANK)
    nodes = pltpu.VMEM((14, RHS, RANK), f32)

    def climb_group(message, climbers):
        received = swap(message, near)
        message, siblings = call(
            lower_kernel,
            [message_shape, (4, RHS, RANK)],
            [me, received, climbers],
            scratch=[nodes],
        )
        return swap(message, far), siblings

    z, message, keep = call(
        start_kernel, [row_shape, message_shape, keep_shape], [rows, rhs, row_basis, local_row]
    )
    prev = None
    norms = []
    vectors = []
    u = None
    for step in range(2):
        received, siblings = climb_group(message, up_row)
        outs = call(
            functools.partial(adjoint_kernel, prev is None),
            [row_shape, col_shape, norm_shape, message_shape, keep_shape],
            [me, received, siblings, up_row, up_col, up_couple, keep]
            + [dense, col_basis, local_row, local_col, local_couple, z]
            + ([] if prev is None else [prev]),
            scratch=[nodes],
        )
        u, x, norm, message, keep = outs
        norms.append(norm)
        received, siblings = climb_group(message, up_col)
        operands = [me, received, siblings, up_row, up_col, up_couple, keep]
        operands += [dense, row_basis, local_row, local_col, local_couple, rows, x, u]
        if step == 0:
            prev, z, norm, message, keep = call(
                functools.partial(forward_kernel, False),
                [col_shape, row_shape, norm_shape, message_shape, keep_shape],
                operands,
                scratch=[nodes],
            )
            vectors.append(prev)
        else:
            v, norm, message = call(
                functools.partial(forward_kernel, True),
                [col_shape, norm_shape, (GROUP, 8, RANK)],
                operands,
                scratch=[nodes],
            )
            vectors.append(v)
        norms.append(norm)
    received = swap(message, near)
    (message,) = call(relay_kernel, [(GROUP, 8, RANK)], [received])
    received = swap(message, far)
    (out,) = call(final_kernel, [col_shape], [received] + norms + vectors)
    return out


def solution(mesh):
    devices = mesh.shape["leaf"]
    return jax.shard_map(
        functools.partial(local, devices),
        mesh=mesh,
        in_specs=(
            P(None, "leaf"),
            P("leaf"),
            P("leaf", None, None),
            P("leaf", None, None),
            P("leaf", None, None),
            P("leaf", None, None),
            P("leaf", None, None),
            P("leaf", None, None, None),
            P(),
            P(),
            P(),
        ),
        out_specs=P(None, "leaf"),
        check_vma=False,
    )
```

time: 1060 us -> 163 us (0.15); the launches traced: 1040 us -> 161 us
  waiting for transfers between devices: 365 us -> 5.17 us
  blocking collectives: 381 us -> 120 us
  matrix products: 163 us -> 0 us
  local copies, waits for them, and re-layouts: 108 us -> 11.5 us
  Pallas kernels: 0 us -> 18.5 us
  between operations: 15 us -> 0.13 us
    psum x5 -> x0, blocking collectives: 381 us -> none  [column_norm(): return jnp.sqrt(lax.psum(partial_sum, 'leaf'))]
    all_gather x4 -> x0, waiting for transfers between devices: 364 us -> none  [upper_by_gather(): all_roots = lax.all_gather(root_summary[None], 'leaf', axis=0, tiled=True)]
    dot_general x124 -> x0, matrix products: 163 us -> none  [the longest x28 41.7 us: shared_descend(): spread = jnp.einsum('mnk,ijk->minj', parent, blocks, precision=precise)]
    all_to_all x0 -> x9, blocking collectives: none -> 120 us  [swap(): return lax.all_to_all(message, 'leaf', 0, 0, axis_index_groups=groups)]
    rev x32 -> x0, local copies, waits for them, and re-layouts: 54.6 us -> none  [the longest x14 26.9 us: shared_couple(): jnp.flip(paired, 1)]
    add x28 -> x0, local copies, waits for them, and re-layouts: 20.8 us -> none  [upper_by_gather(): potential = coupled[height] + shared_descend(potential, descenders[height])]
    pallas_call x0 -> x11, Pallas kernels: none -> 18.5 us  [call(): pl.pallas_call(kernel, out_shape=[jax.ShapeDtypeStruct(shape, f32) for sh...]
  transfers between devices with their start and end apart: 4 -> 1, of which waited for: 4 -> 1; matrix products, arithmetic and copies ran while one was open for 4% -> 0% of each run, Pallas kernels for 0% -> 0%
where the time goes in v1:
time: 163 us; the launch traced here: 161 us
  blocking collectives  120 us (74%)
  Pallas kernels  18.5 us (11%)
  local copies, waits for them, and re-layouts  11.5 us (7%)
  starting transfers between devices  6.2 us (4%)
  waiting for transfers between devices  5.17 us (3%)
    all_to_all x9, blocking collectives, swap(): return lax.all_to_all(message, 'leaf', 0, 0, axis_index_groups=groups)  120 us
    pallas_call x11, Pallas kernels, call(): pl.pallas_call(kernel, out_shape=[jax.ShapeDtypeStruct(shape, f32) for sh...  18.5 us
    unnamed x40, local copies, waits for them, and re-layouts  11.5 us
    all_to_all x1, starting transfers between devices, swap(): return lax.all_to_all(message, 'leaf', 0, 0, axis_index_groups=groups)  6.2 us
    all_to_all x1, waiting for transfers between devices, swap(): return lax.all_to_all(message, 'leaf', 0, 0, axis_index_groups=groups)  5.17 us
  transfers between devices with their start and end apart: 1, of which 1 were waited for; matrix products, arithmetic and copies ran while one was open for 0% of the time, Pallas kernels for 0%

profile of v1, /device:TPU:2, one launch (start us, length us, event | category | flops | bytes accessed | tf_op | source)
XLA Modules:
  0.0 161.4 jit_solution(14983602426815249163)
XLA Ops:
  0.0 1.1 copy-done.5
  1.2 1.2 copy-done.7
  2.4 0.9 copy-done.15
  3.3 0.7 copy-done.18
  3.9 1.1 shard_map.109
  5.0 0.7 copy-done.14
  6.3 6.2 %all-to-all-start = ((f32[16,24,128]{2,1,0:T(8,128)}), f32[16,24,128]{2,1,0:T(8,128)}, u32[]{:S(2)}, u32[]{:S(2)}) async-start(f32[16,24,128]{2,1,0:T(8,128)} %copy-done.14), calls=%async_computation | async-start | bytes 393216 | tf_op jit(solution)/shard_map/all_to_all | solution.py:355
  12.5 5.2 %all-to-all-done.recv_ref = f32[16,24,128]{2,1,0:T(8,128)} async-done(((f32[16,24,128]{2,1,0:T(8,128)}), f32[16,24,128]{2,1,0:T(8,128)}, u32[]{:S(2)}, u32[]{:S(2)}) %all-to-all-start) | async-done | bytes 196640 | tf_op jit(solution)/shard_map/all_to_all | solution.py:355
  17.7 1.6 shard_map.110
  19.3 22.7 %all_to_all.50.recv_ref = f32[16,24,128]{2,1,0:T(8,128)S(1)} all-to-all(f32[16,24,128]{2,1,0:T(8,128)S(1)} %get-tuple-element.35), channel_id=1, replica_groups={{0,16,32,48,64,80,96,112,128,144,160,176,192,208,224,240},{1,17,33,49,6..., dimensions={0} | all-to-all | bytes 393216 | tf_op jit(solution)/shard_map/all_to_all | solution.py:355
  42.0 1.2 copy-done.2
  43.2 1.2 copy-done.4
  44.4 1.0 copy-done.9
  45.4 1.0 copy-done.11
  46.4 1.0 copy-done.13
  47.4 0.8 copy-done.17
  48.2 3.0 %shard_map.111 = (f32[16,2048]{1,0:T(8,128)S(1)}, f32[16,1024]{1,0:T(8,128)S(1)}, f32[16,128]{1,0:T(8,128)S(1)}, f32[16,24,128]{2,1,0:T(8,128)S(1)}, f32[6,16,128]{2,1,0:T(8,128)S(1)}) custom-call(s32[1]{0:T(128)} %bitcast.me_ref, f32[16,24,128]{2,1,0:T(8,128)S(1)} %all_to_all.50.recv_ref, f32[4,16,128]{2,1,0:T(8,128)S(1)} %get-tuple-element.36.sib_ref, ...), custom_call_target="tpu_custom_call" | custom-call | tf_op jit(solution)/shard_map/pallas_call | solution.py:312
  51.3 9.2 %all_to_all.51.recv_ref = f32[16,24,128]{2,1,0:T(8,128)S(1)} all-to-all(f32[16,24,128]{2,1,0:T(8,128)S(1)} %get-tuple-element.39), channel_id=1, replica_groups={{0,1,2,3,4,5,6,7,8,9,10,11,12,13,14,15},{16,17,18,19,20,21,22,23,24,25,..., dimensions={0} | all-to-all | bytes 393216 | tf_op jit(solution)/shard_map/all_to_all | solution.py:355
  60.5 0.6 shard_map.112
  61.2 15.8 %all_to_all.52.recv_ref = f32[16,24,128]{2,1,0:T(8,128)S(1)} all-to-all(f32[16,24,128]{2,1,0:T(8,128)S(1)} %get-tuple-element.40), channel_id=1, replica_groups={{0,16,32,48,64,80,96,112,128,144,160,176,192,208,224,240},{1,17,33,49,6..., dimensions={0} | all-to-all | bytes 393216 | tf_op jit(solution)/shard_map/all_to_all | solution.py:355
  77.0 3.7 %shard_map.113 = (f32[16,1024]{1,0:T(8,128)S(1)}, f32[16,2048]{1,0:T(8,128)S(1)}, f32[16,128]{1,0:T(8,128)S(1)}, f32[16,24,128]{2,1,0:T(8,128)S(1)}, f32[6,16,128]{2,1,0:T(8,128)S(1)}) custom-call(s32[1]{0:T(128)} %bitcast.me_ref, f32[16,24,128]{2,1,0:T(8,128)S(1)} %all_to_all.52.recv_ref, f32[4,16,128]{2,1,0:T(8,128)S(1)} %get-tuple-element.41.sib_ref, ...), custom_call_target="tpu_custom_call" | custom-call | tf_op jit(solution)/shard_map/pallas_call | solution.py:312
  80.7 9.3 %all_to_all.53.recv_ref = f32[16,24,128]{2,1,0:T(8,128)S(1)} all-to-all(f32[16,24,128]{2,1,0:T(8,128)S(1)} %get-tuple-element.45), channel_id=1, replica_groups={{0,1,2,3,4,5,6,7,8,9,10,11,12,13,14,15},{16,17,18,19,20,21,22,23,24,25,..., dimensions={0} | all-to-all | bytes 393216 | tf_op jit(solution)/shard_map/all_to_all | solution.py:355
  90.0 0.6 shard_map.114
  90.6 15.8 %all_to_all.54.recv_ref = f32[16,24,128]{2,1,0:T(8,128)S(1)} all-to-all(f32[16,24,128]{2,1,0:T(8,128)S(1)} %get-tuple-element.46), channel_id=1, replica_groups={{0,16,32,48,64,80,96,112,128,144,160,176,192,208,224,240},{1,17,33,49,6..., dimensions={0} | all-to-all | bytes 393216 | tf_op jit(solution)/shard_map/all_to_all | solution.py:355
  106.4 3.0 %shard_map.115 = (f32[16,2048]{1,0:T(8,128)S(1)}, f32[16,1024]{1,0:T(8,128)S(1)}, f32[16,128]{1,0:T(8,128)S(1)}, f32[16,24,128]{2,1,0:T(8,128)S(1)}, f32[6,16,128]{2,1,0:T(8,128)S(1)}) custom-call(s32[1]{0:T(128)} %bitcast.me_ref, f32[16,24,128]{2,1,0:T(8,128)S(1)} %all_to_all.54.recv_ref, f32[4,16,128]{2,1,0:T(8,128)S(1)} %get-tuple-element.47.sib_ref, ...), custom_call_target="tpu_custom_call" | custom-call | tf_op jit(solution)/shard_map/pallas_call | solution.py:312
  109.4 9.1 %all_to_all.55.recv_ref = f32[16,24,128]{2,1,0:T(8,128)S(1)} all-to-all(f32[16,24,128]{2,1,0:T(8,128)S(1)} %get-tuple-element.51), channel_id=1, replica_groups={{0,1,2,3,4,5,6,7,8,9,10,11,12,13,14,15},{16,17,18,19,20,21,22,23,24,25,..., dimensions={0} | all-to-all | bytes 393216 | tf_op jit(solution)/shard_map/all_to_all | solution.py:355
  118.5 0.6 shard_map.116
  119.2 15.8 %all_to_all.56.recv_ref = f32[16,24,128]{2,1,0:T(8,128)S(1)} all-to-all(f32[16,24,128]{2,1,0:T(8,128)S(1)} %get-tuple-element.52), channel_id=1, replica_groups={{0,16,32,48,64,80,96,112,128,144,160,176,192,208,224,240},{1,17,33,49,6..., dimensions={0} | all-to-all | bytes 393216 | tf_op jit(solution)/shard_map/all_to_all | solution.py:355
  135.0 3.4 %shard_map.117 = (f32[16,1024]{1,0:T(8,128)S(1)}, f32[16,128]{1,0:T(8,128)S(1)}, f32[16,8,128]{2,1,0:T(8,128)S(1)}) custom-call(s32[1]{0:T(128)} %bitcast.me_ref, f32[16,24,128]{2,1,0:T(8,128)S(1)} %all_to_all.56.recv_ref, f32[4,16,128]{2,1,0:T(8,128)S(1)} %get-tuple-element.53.sib_ref, f32[7,256,128]{2,1,0:T(8,128)S(1)} %copy-done.1, ...), custom_call_target="tpu_custom_call" | custom-call | tf_op jit(solution)/shard_map/pallas_call | solution.py:312
  138.4 8.9 %all_to_all.57.recv_ref = f32[16,8,128]{2,1,0:T(8,128)S(1)} all-to-all(f32[16,8,128]{2,1,0:T(8,128)S(1)} %get-tuple-element.57), channel_id=1, replica_groups={{0,1,2,3,4,5,6,7,8,9,10,11,12,13,14,15},{16,17,18,19,20,21,22,23,24,25,..., dimensions={0} | all-to-all | bytes 131072 | tf_op jit(solution)/shard_map/all_to_all | solution.py:355
  147.3 13.3 %all_to_all.58.recv_ref = f32[16,8,128]{2,1,0:T(8,128)S(1)} all-to-all(f32[16,8,128]{2,1,0:T(8,128)S(1)} %shard_map.118), channel_id=1, replica_groups={{0,16,32,48,64,80,96,112,128,144,160,176,192,208,224,240},{1,17,33,49,6..., dimensions={0} | all-to-all | bytes 131072 | tf_op jit(solution)/shard_map/all_to_all | solution.py:355
  160.5 0.8 shard_map.119
  (30 shorter events, 0.7 us)
Async XLA Ops:
  0.0 17.7 %copy-start.1 = (f32[7,256,128]{2,1,0:T(8,128)S(1)}, f32[7,256,128]{2,1,0:T(8,128)}, u32[]{:S(2)}) copy-start(f32[7,256,128]{2,1,0:T(8,128)} %up_row_ref.7) | copy-start | bytes 2752516
  0.0 42.0 %copy-start = (f32[4,512,256]{2,1,0:T(8,128)S(1)}, f32[4,512,256]{2,1,0:T(8,128)}, u32[]{:S(2)}) copy-start(f32[4,512,256]{2,1,0:T(8,128)} %dense_ref.7) | copy-start | bytes 6291460
  0.0 1.1 copy-start.5
  1.2 1.2 copy-start.7
  2.4 0.9 copy-start.15
  3.3 0.7 copy-start.18
  3.9 38.1 %copy-start.6 = (f32[3,256,128]{2,1,0:T(8,128)S(1)}, f32[3,256,128]{2,1,0:T(8,128)}, u32[]{:S(2)}) copy-start(f32[3,256,128]{2,1,0:T(8,128)} %local_row_ref.9) | copy-start | bytes 1179652
  5.0 0.7 copy-start.14
  5.7 0.6 copy-start.16
  6.3 11.4 %all-to-all-start = ((f32[16,24,128]{2,1,0:T(8,128)}), f32[16,24,128]{2,1,0:T(8,128)}, u32[]{:S(2)}, u32[]{:S(2)}) async-start(f32[16,24,128]{2,1,0:T(8,128)} %copy-done.14), calls=%async_computation | async-start | bytes 393216 | tf_op jit(solution)/shard_map/all_to_all | solution.py:355
  42.0 1.2 copy-start.2
  43.2 1.2 copy-start.4
  44.4 1.0 copy-start.9
  45.4 1.0 copy-start.11
  46.4 1.0 copy-start.13
  47.4 0.8 copy-start.17
  48.2 12.3 %copy-start.3 = (f32[7,256,128]{2,1,0:T(8,128)S(1)}, f32[7,256,128]{2,1,0:T(8,128)}, u32[]{:S(2)}) copy-start(f32[7,256,128]{2,1,0:T(8,128)} %up_col_ref.7) | copy-start | bytes 2752516
  48.2 28.7 %copy-start.19 = (s32[4]{0:T(128)S(1)}, s32[4]{0:T(128)}, u32[]{:S(2)}) copy-start(s32[4]{0:T(128)} %rows_ref.5) | copy-start | bytes 52
  51.2 25.7 %copy-start.8 = (f32[4,512,128]{2,1,0:T(8,128)S(1)}, f32[4,512,128]{2,1,0:T(8,128)}, u32[]{:S(2)}) copy-start(f32[4,512,128]{2,1,0:T(8,128)} %row_basis_ref.5) | copy-start | bytes 3145732
  51.3 25.7 %copy-start.10 = (f32[3,256,128]{2,1,0:T(8,128)S(1)}, f32[3,256,128]{2,1,0:T(8,128)}, u32[]{:S(2)}) copy-start(f32[3,256,128]{2,1,0:T(8,128)} %local_col_ref.7) | copy-start | bytes 1179652
  80.7 25.7 %copy-start.12 = (f32[3,2,128,128]{3,2,1,0:T(8,128)S(1)}, f32[3,2,128,128]{3,2,1,0:T(8,128)}, u32[]{:S(2)}) copy-start(f32[3,2,128,128]{3,2,1,0:T(8,128)} %local_couple_ref.7) | copy-start | bytes 1179652

commit v2 on v1

v2 whole, which is shorter than its diff:
```python
import functools

import jax
import jax.numpy as jnp
from jax import lax
from jax.experimental import pallas as pl
from jax.experimental.pallas import tpu as pltpu
from jax.sharding import PartitionSpec as P

RHS = 16
RANK = 128
LEAF_DEV = 4
LEAF_ROWS = 512
LEAF_COLS = 256
TINY = 1.2e-38
GROUP = 16
VMEM_LIMIT = 40 * 1024 * 1024

f32 = jnp.float32
bf16 = jnp.bfloat16


def split(v):
    head = v.astype(bf16)
    return head, (v - head.astype(f32)).astype(bf16)


def mm_inner(a, b):
    ah, al = split(a)
    bh, bl = split(b)
    dims = (((0,), (0,)), ((), ()))
    m = a.shape[1]
    both = lax.dot_general(jnp.concatenate([ah, al], 1), bh, dims, preferred_element_type=f32)
    rest = lax.dot_general(ah, bl, dims, preferred_element_type=f32)
    return both[:m] + (both[m:] + rest)


def mm(x, w, transposed=False):
    xh, xl = split(x)
    wh, wl = split(w)
    dims = (((1,), (1 if transposed else 0,)), ((), ()))
    n = x.shape[0]
    both = lax.dot_general(jnp.concatenate([xh, xl], 0), wh, dims, preferred_element_type=f32)
    rest = lax.dot_general(xh, wl, dims, preferred_element_type=f32)
    return both[:n] + (both[n:] + rest)


def eye():
    return (
        lax.broadcasted_iota(jnp.int32, (RHS, RANK), 0)
        == lax.broadcasted_iota(jnp.int32, (RHS, RANK), 1)
    ).astype(f32)


def stat_block(first, second):
    rows = lax.broadcasted_iota(jnp.int32, (8, RANK), 0)
    return first * (rows == 0).astype(f32) + second * (rows == 1).astype(f32)


def column_of(row):
    return jnp.sum(row * eye(), axis=1, keepdims=True)


def row_of(column):
    return jnp.sum(column * eye(), axis=0, keepdims=True)


def inverse_norm(squares):
    return jnp.where(squares >= TINY, 1.0 / jnp.sqrt(squares), 1.0)


def sum_squares(v):
    return jnp.sum(v * v, axis=1, keepdims=True)


def send(out_ref, value):
    for peer in range(GROUP):
        out_ref[peer] = value


def stack(blocks):
    return jnp.concatenate(blocks, 0)


def unstack(value, count):
    size = value.shape[0] // count
    return [value[k * size : (k + 1) * size] for k in range(count)]


def climb(blocks, transfer):
    count = len(blocks) // 2
    paired = [jnp.concatenate([blocks[2 * m], blocks[2 * m + 1]], 1) for m in range(count)]
    return unstack(mm(stack(paired), transfer), count)


def descend(blocks, transfer):
    spread = unstack(mm(stack(blocks), transfer, transposed=True), len(blocks))
    out = []
    for block in spread:
        out += [block[:, :RANK], block[:, RANK:]]
    return out


def couple_all(blocks, coupling):
    count = len(blocks) // 2
    even = unstack(mm(stack(blocks[1::2]), coupling[0]), count)
    odd = unstack(mm(stack(blocks[0::2]), coupling[1]), count)
    out = []
    for m in range(count):
        out += [even[m], odd[m]]
    return out


def local_up(parts, basis_ref, climb_ref):
    leaf = [mm(parts[q], basis_ref[q]) for q in range(LEAF_DEV)]
    node = [
        mm(jnp.concatenate([leaf[2 * m], leaf[2 * m + 1]], 1), climb_ref[m]) for m in range(2)
    ]
    return leaf, node


def local_root(node, climb_ref):
    return mm(jnp.concatenate(node, 1), climb_ref[2])


def couple(sibling, coupling_ref, node, child, adjoint):
    if adjoint:
        return mm(sibling, coupling_ref[node, 1 - child], transposed=True)
    return mm(sibling, coupling_ref[node, child])


def local_down(root, leaf, node, coupling_ref, descend_ref, adjoint):
    spread = None if root is None else mm(root, descend_ref[2], transposed=True)
    out = []
    for m in range(2):
        here = None if spread is None else spread[:, m * RANK : (m + 1) * RANK]
        if node is not None:
            gained = couple(node[1 - m], coupling_ref, 2, m, adjoint)
            here = gained if here is None else here + gained
        below = mm(here, descend_ref[m], transposed=True)
        for i in range(2):
            value = below[:, i * RANK : (i + 1) * RANK]
            if leaf is not None:
                value = value + couple(leaf[2 * m + 1 - i], coupling_ref, m, i, adjoint)
            out.append(value)
    return out


def live_mask(rows_ref, q):
    slots = lax.broadcasted_iota(jnp.int32, (RHS, LEAF_ROWS), 1)
    return (slots < rows_ref[q]).astype(f32)


def row_part(q):
    return slice(q * LEAF_ROWS, (q + 1) * LEAF_ROWS)


def col_part(q):
    return slice(q * LEAF_COLS, (q + 1) * LEAF_COLS)


def pair_up(parts, local, rows_ref, msg_ref, own_ref, inner_ref):
    dense_ref, row_basis_ref, col_basis_ref, local_row_ref, local_col_ref, couple_ref = local
    squares = sum_squares(parts[0])
    for part in parts[1:]:
        squares = squares + sum_squares(part)
    scale = inverse_norm(squares)
    parts = [part * scale for part in parts]
    leaf, node = local_up(parts, col_basis_ref, local_col_ref)
    root = local_root(node, local_col_ref)
    down = local_down(None, leaf, node, couple_ref, local_row_ref, False)
    result = []
    energy = jnp.zeros((RHS, 1), f32)
    for q in range(LEAF_DEV):
        y = mm(parts[q], dense_ref[q], transposed=True)
        y = y + mm(down[q], row_basis_ref[q], transposed=True)
        y = y * live_mask(rows_ref, q)
        if inner_ref is not None:
            inner_ref[:, row_part(q)] = y
        energy = energy + sum_squares(y)
        result.append(y)
    _, row_node = local_up(result, row_basis_ref, local_row_ref)
    row_root = local_root(row_node, local_row_ref)
    stats = stat_block(row_of(squares), row_of(energy))
    own_ref[...] = stats
    send(msg_ref, stack([root, row_root, stats]))


def start_kernel(rows_ref, rhs_ref, row_basis_ref, local_row_ref, z_ref, msg_ref, keep_ref):
    parts = []
    squares = jnp.zeros((RHS, 1), f32)
    for q in range(LEAF_DEV):
        part = rhs_ref[:, row_part(q)] * live_mask(rows_ref, q)
        z_ref[:, row_part(q)] = part
        squares = squares + sum_squares(part)
        parts.append(part)
    leaf, node = local_up(parts, row_basis_ref, local_row_ref)
    for k, value in enumerate(leaf + node):
        keep_ref[k] = value
    root = local_root(node, local_row_ref)
    row = row_of(squares)
    send(msg_ref, stack([root, stat_block(row, row)]))


def both_sides(grams, half):
    left = mm(jnp.transpose(half), jnp.concatenate(grams, 1))
    columns = [left[:, k * RANK : (k + 1) * RANK] for k in range(len(grams))]
    return unstack(mm(stack(columns), half), len(grams))


def gram_climb(grams, transfer):
    even = both_sides(grams[0::2], transfer[:RANK])
    odd = both_sides(grams[1::2], transfer[RANK:])
    return [a + b for a, b in zip(even, odd)]


def gram_kernel(rows_ref, row_basis_ref, local_row_ref, out_ref):
    grams = []
    for q in range(LEAF_DEV):
        slots = lax.broadcasted_iota(jnp.int32, (LEAF_ROWS, RANK), 0)
        basis = jnp.where(slots < rows_ref[q], row_basis_ref[q], 0.0)
        grams.append(mm_inner(basis, basis))
    nodes = [gram_climb(grams[2 * m : 2 * m + 2], local_row_ref[m])[0] for m in range(2)]
    out_ref[...] = gram_climb(nodes, local_row_ref[2])[0]


def group_gram_kernel(gram_ref, up_row_ref, nodes_ref, out_ref):
    grams = [gram_ref[d] for d in range(GROUP)]
    base = 0
    for height in range(4):
        grams = gram_climb(grams, up_row_ref[height])
        if height < 3:
            for k, value in enumerate(grams):
                nodes_ref[base + k] = value
            base += len(grams)
    out_ref[...] = grams[0]


def lower_kernel(me_ref, recv_ref, climb_ref, msg_ref, sib_ref, scratch_ref):
    place = me_ref[0] % GROUP
    level = [recv_ref[d, :RHS] for d in range(GROUP)]
    sib_ref[0] = recv_ref[place ^ 1, :RHS]
    base = 0
    for height in range(4):
        level = climb(level, climb_ref[height])
        if height < 3:
            for m, value in enumerate(level):
                scratch_ref[base + m] = value
            sib_ref[height + 1] = scratch_ref[base + ((place >> (height + 1)) ^ 1)]
            base += len(level)
    stats = recv_ref[0, RHS:]
    for d in range(1, GROUP):
        stats = stats + recv_ref[d, RHS:]
    send(msg_ref, stack([level[0], stats]))


def first_kernel(
    me_ref,
    rows_ref,
    recv_ref,
    sib_ref,
    up_row_ref,
    up_col_ref,
    up_couple_ref,
    keep_ref,
    dense_ref,
    row_basis_ref,
    col_basis_ref,
    local_row_ref,
    local_col_ref,
    local_couple_ref,
    z_ref,
    x_ref,
    beta_ref,
    msg_ref,
    own_ref,
    inner_ref,
    scratch_ref,
):
    me = me_ref[0]
    place = me // GROUP
    level = [recv_ref[d, :RHS] for d in range(GROUP)]
    siblings = [sib_ref[j] for j in range(4)]
    siblings.append(recv_ref[place ^ 1, :RHS])
    base = 0
    for height in range(3):
        level = climb(level, up_row_ref[4 + height])
        for m, value in enumerate(level):
            scratch_ref[base + m] = value
        siblings.append(scratch_ref[base + ((place >> (height + 1)) ^ 1)])
        base += len(level)
    potential = None
    for j in reversed(range(8)):
        child = (me >> j) & 1
        gained = mm(siblings[j], up_couple_ref[j, 1 - child], transposed=True)
        if potential is not None:
            gained = gained + mm(potential, half_of(up_col_ref, j, child), transposed=True)
        potential = gained
    stats = recv_ref[0, RHS:]
    for d in range(1, GROUP):
        stats = stats + recv_ref[d, RHS:]
    beta = jnp.sqrt(column_of(stats[:1]))
    inverse = 1.0 / beta
    beta_ref[...] = jnp.broadcast_to(beta, (RHS, RANK))
    leaf = [keep_ref[q] for q in range(LEAF_DEV)]
    node = [keep_ref[LEAF_DEV + m] for m in range(2)]
    down = local_down(potential, leaf, node, local_couple_ref, local_col_ref, True)
    parts = []
    for q in range(LEAF_DEV):
        x = mm(z_ref[:, row_part(q)], dense_ref[q])
        x = (x + mm(down[q], col_basis_ref[q], transposed=True)) * inverse
        x_ref[:, col_part(q)] = x
        parts.append(x)
    local = (dense_ref, row_basis_ref, col_basis_ref, local_row_ref, local_col_ref, local_couple_ref)
    pair_up(parts, local, rows_ref, msg_ref, own_ref, inner_ref)


def half_of(table_ref, j, child):
    return table_ref[j, pl.ds(pl.multiple_of(child * RANK, RANK), RANK), :]


def rescale(recv_ref):
    base = 2 * RHS
    squares = stack([recv_ref[d, base : base + 1] for d in range(GROUP)])
    energy = stack([recv_ref[d, base + 1 : base + 2] for d in range(GROUP)])
    total = jnp.sum(squares, axis=0, keepdims=True)
    factor = inverse_norm(total) / inverse_norm(squares)
    energy = jnp.sum(energy * factor * factor, axis=0, keepdims=True)
    first = []
    second = []
    for d in range(GROUP):
        column = column_of(factor[d : d + 1])
        first.append(recv_ref[d, :RHS] * column)
        second.append(recv_ref[d, RHS : 2 * RHS] * column)
    return first, second, factor, total, energy


def lower_pair_kernel(
    me_ref,
    recv_ref,
    up_row_ref,
    up_col_ref,
    up_couple_ref,
    gram_ref,
    nodes_ref,
    msg_ref,
    path_ref,
    gain_ref,
    below_ref,
):
    place = me_ref[0] % GROUP
    first, second, _, total, energy = rescale(recv_ref)
    cross = jnp.zeros((RHS, RANK), f32)
    base = 0
    for j in range(4):
        gained = couple_all(first, (up_couple_ref[j, 0], up_couple_ref[j, 1]))
        summed = []
        for k in range(len(first)):
            gram = gram_ref[k] if j == 0 else nodes_ref[base - GROUP + k]
            moved = mm(gained[k], gram)
            cross = cross + gained[k] * (2.0 * second[k] + moved)
            summed.append(second[k] + moved)
            gain_ref[base + k] = gained[k]
            below_ref[base + k] = second[k]
        own = place >> j
        path_ref[3 * j] = gain_ref[base + own]
        path_ref[3 * j + 1] = gain_ref[base + (own ^ 1)]
        path_ref[3 * j + 2] = below_ref[base + (own ^ 1)]
        base += len(first)
        first = climb(first, up_col_ref[j])
        second = climb(summed, up_row_ref[j])
    energy = energy + row_of(jnp.sum(cross, axis=1, keepdims=True))
    send(msg_ref, stack([first[0], second[0], stat_block(total, energy)]))


def top_levels(recv_ref, up_row_ref, up_col_ref, up_couple_ref, gram_ref):
    first, second, factor, total, energy = rescale(recv_ref)
    gained = []
    for j in range(4, 8):
        gained.append(couple_all(first, (up_couple_ref[j, 0], up_couple_ref[j, 1])))
        if j < 7:
            first = climb(first, up_col_ref[j])
    potential = gained[3]
    for j in (6, 5, 4):
        below = descend(potential, up_row_ref[j])
        potential = [a + b for a, b in zip(gained[j - 4], below)]
    cross = jnp.zeros((RHS, RANK), f32)
    summed = []
    for d in range(GROUP):
        moved = mm(potential[d], gram_ref[d])
        cross = cross + potential[d] * (2.0 * second[d] + moved)
        summed.append(second[d] + moved)
    energy = column_of(energy) + jnp.sum(cross, axis=1, keepdims=True)
    return potential, summed, factor, column_of(total), energy


def middle_kernel(
    me_ref,
    rows_ref,
    recv_ref,
    path_ref,
    up_row_ref,
    up_col_ref,
    up_couple_ref,
    top_gram_ref,
    gram_ref,
    nodes_ref,
    dense_ref,
    row_basis_ref,
    col_basis_ref,
    local_row_ref,
    local_col_ref,
    local_couple_ref,
    x_ref,
    stats_ref,
    inner_ref,
    v_ref,
    next_ref,
    alpha_ref,
    rho_ref,
    msg_ref,
    own_ref,
    a_ref,
    b_ref,
    c_ref,
):
    me = me_ref[0]
    place = me // GROUP
    inside = me % GROUP
    potential, summed, factor, squares, energy = top_levels(
        recv_ref, up_row_ref, up_col_ref, up_couple_ref, top_gram_ref
    )
    alpha = jnp.sqrt(squares)
    rho = jnp.sqrt(energy)
    alpha_ref[...] = jnp.broadcast_to(alpha, (RHS, RANK))
    rho_ref[...] = jnp.broadcast_to(rho, (RHS, RANK))
    scale = inverse_norm(squares)
    for d in range(GROUP):
        a_ref[d] = potential[d]
    c_ref[...] = factor
    forward = a_ref[place]
    group_factor = column_of(c_ref[pl.ds(place, 1), :])
    siblings = {}
    for j in range(4, 8):
        for k, value in enumerate(summed):
            b_ref[k] = value
        siblings[j] = b_ref[(place >> (j - 4)) ^ 1]
        if j < 7:
            summed = climb(summed, up_row_ref[j])
    for j in reversed(range(4)):
        child = (me >> j) & 1
        spread = mm(forward, up_row_ref[j], transposed=True)
        low = spread[:, :RANK]
        high = spread[:, RANK:]
        own = jnp.where(child == 0, low, high)
        other = jnp.where(child == 0, high, low)
        forward = path_ref[3 * j] * group_factor + own
        other = path_ref[3 * j + 1] * group_factor + other
        sibling = (inside >> j) ^ 1
        gram = gram_ref[sibling] if j == 0 else nodes_ref[(0, 0, 8, 12)[j] + sibling]
        siblings[j] = path_ref[3 * j + 2] * group_factor + mm(other, gram)
    backward = None
    for j in reversed(range(8)):
        child = (me >> j) & 1
        gained = mm(siblings[j], up_couple_ref[j, 1 - child], transposed=True)
        if backward is not None:
            gained = gained + mm(backward, half_of(up_col_ref, j, child), transposed=True)
        backward = gained
    own_factor = scale / inverse_norm(column_of(stats_ref[:1]))
    outer = local_down(forward, None, None, local_couple_ref, local_row_ref, False)
    images = []
    for q in range(LEAF_DEV):
        y = mm(outer[q], row_basis_ref[q], transposed=True) * live_mask(rows_ref, q)
        images.append(y + inner_ref[:, row_part(q)] * own_factor)
    leaf, node = local_up(images, row_basis_ref, local_row_ref)
    down = local_down(backward, leaf, node, local_couple_ref, local_col_ref, True)
    inverse = 1.0 / rho
    parts = []
    for q in range(LEAF_DEV):
        v = x_ref[:, col_part(q)] * scale
        v_ref[:, col_part(q)] = v
        x = mm(images[q], dense_ref[q]) + mm(down[q], col_basis_ref[q], transposed=True)
        x = x * inverse - rho * v
        next_ref[:, col_part(q)] = x
        parts.append(x)
    local = (dense_ref, row_basis_ref, col_basis_ref, local_row_ref, local_col_ref, local_couple_ref)
    pair_up(parts, local, rows_ref, msg_ref, own_ref, None)


def final_kernel(
    recv_ref,
    up_row_ref,
    up_col_ref,
    up_couple_ref,
    top_gram_ref,
    beta_ref,
    alpha_ref,
    rho_ref,
    v_ref,
    x_ref,
    out_ref,
):
    _, _, _, squares, energy = top_levels(
        recv_ref, up_row_ref, up_col_ref, up_couple_ref, top_gram_ref
    )
    theta = jnp.sqrt(squares)
    rho2 = jnp.sqrt(energy - squares)
    rho = rho_ref[:, :1]
    phi = alpha_ref[:, :1] / rho * beta_ref[:, :1]
    v = v_ref[...]
    search = x_ref[...] * inverse_norm(squares) - (theta / rho) * v
    out_ref[...] = (phi / rho) * v - (phi * (theta / rho2) / rho2) * search


def call(kernel, outs, operands, scratch=()):
    smem = pl.BlockSpec(memory_space=pltpu.SMEM)
    vmem = pl.BlockSpec(memory_space=pltpu.VMEM)
    return pl.pallas_call(
        kernel,
        out_shape=[jax.ShapeDtypeStruct(shape, f32) for shape in outs],
        in_specs=[smem if k.dtype == jnp.int32 else vmem for k in operands],
        out_specs=[vmem] * len(outs),
        scratch_shapes=[pltpu.VMEM(shape, f32) for shape in scratch],
        compiler_params=pltpu.CompilerParams(vmem_limit_bytes=VMEM_LIMIT),
    )(*operands)


def device_groups(devices, stride, size):
    out = []
    for base in range(devices):
        if (base // stride) % size == 0:
            out.append([base + k * stride for k in range(size)])
    return out


def local_program(
    devices,
    rhs,
    box_rows,
    dense,
    row_basis,
    col_basis,
    local_col,
    local_row,
    local_couple,
    up_col,
    up_row,
    up_couple,
):
    me = lax.axis_index("leaf").astype(jnp.int32).reshape(1)
    near = device_groups(devices, 1, GROUP)
    far = device_groups(devices, GROUP, GROUP)

    def swap(message, groups):
        return lax.all_to_all(message, "leaf", 0, 0, axis_index_groups=groups)

    def collect(value, stride, size):
        groups = device_groups(devices, stride, size)
        return lax.all_gather(value, "leaf", axis_index_groups=groups)

    tile = (RHS, RANK)
    row_shape = (RHS, LEAF_DEV * LEAF_ROWS)
    col_shape = (RHS, LEAF_DEV * LEAF_COLS)
    first_message = (GROUP, RHS + 8, RANK)
    pair_message = (GROUP, 2 * RHS + 8, RANK)
    gram_shape = (RANK, RANK)
    tables = [up_row, up_col, up_couple]
    blocks = [dense, row_basis, col_basis, local_row, local_col, local_couple]

    (gram,) = call(gram_kernel, [gram_shape], [box_rows, row_basis, local_row])
    grams = collect(gram, 1, GROUP)
    z, message, keep = call(
        start_kernel, [row_shape, first_message, (6,) + tile], [box_rows, rhs, row_basis, local_row]
    )
    received = swap(message, near)
    message, siblings = call(
        lower_kernel, [first_message, (4,) + tile], [me, received, up_row], [(14,) + tile]
    )
    received = swap(message, far)
    grams, received = lax.optimization_barrier((grams, received))
    nodes, group_gram = call(group_gram_kernel, [(14,) + gram_shape, gram_shape], [grams, up_row])
    group_gram, received = lax.optimization_barrier((group_gram, received))
    top_grams = collect(group_gram, GROUP, 4)
    x, beta, message, own, inner = call(
        first_kernel,
        [col_shape, tile, pair_message, (8, RANK), row_shape],
        [me, box_rows, received, siblings] + tables + [keep] + blocks + [z],
        [(14,) + tile],
    )

    def lower_pair(message):
        received = swap(message, near)
        return call(
            lower_pair_kernel,
            [pair_message, (12,) + tile],
            [me, received] + tables + [grams, nodes],
            [(30,) + tile, (30,) + tile],
        )

    message, path = lower_pair(message)
    top_grams, message = lax.optimization_barrier((top_grams, message))
    top_grams = collect(top_grams, 4 * GROUP, 4).reshape((GROUP,) + gram_shape)
    received = swap(message, far)
    v, x, alpha, rho, message, _ = call(
        middle_kernel,
        [col_shape, col_shape, tile, tile, pair_message, (8, RANK)],
        [me, box_rows, received, path] + tables + [top_grams, grams, nodes] + blocks + [x, own, inner],
        [(GROUP,) + tile, (GROUP,) + tile, tile],
    )
    message, _ = lower_pair(message)
    received = swap(message, far)
    (out,) = call(
        final_kernel, [col_shape], [received] + tables + [top_grams, beta, alpha, rho, v, x]
    )
    return out


def solution(mesh):
    devices = mesh.shape["leaf"]
    return jax.shard_map(
        functools.partial(local_program, devices),
        mesh=mesh,
        in_specs=(
            P(None, "leaf"),
            P("leaf"),
            P("leaf", None, None),
            P("leaf", None, None),
            P("leaf", None, None),
            P("leaf", None, None),
            P("leaf", None, None),
            P("leaf", None, None, None),
            P(),
            P(),
            P(),
        ),
        out_specs=P(None, "leaf"),
        check_vma=False,
    )
```

time: 163 us -> 193 us (1.18)
  blocking collectives: 120 us -> 90 us
  local copies, waits for them, and re-layouts: 11.5 us -> 34 us
  between operations: 0.13 us -> 13.6 us
  Pallas kernels: 18.5 us -> 29.2 us
  starting transfers between devices: 6.2 us -> 12.8 us
  waiting for transfers between devices: 5.17 us -> 11.7 us
    all_to_all x9 -> x4, blocking collectives: 120 us -> 74.9 us  [swap(): return lax.all_to_all(message, 'leaf', 0, 0, axis_index_groups=groups)]
    unnamed x40 -> x86, local copies, waits for them, and re-layouts: 11.5 us -> 34 us
    all_gather x0 -> x1, blocking collectives: none -> 15.2 us  [collect(): return lax.all_gather(value, 'leaf', axis_index_groups=groups)]
    pallas_call x11 -> x9, Pallas kernels: 18.5 us -> 29.2 us  [call(): pl.pallas_call(kernel, out_shape=[jax.ShapeDtypeStruct(shape, f32) for sh...]
    all_gather x0 -> x2, waiting for transfers between devices: none -> 6.62 us  [collect(): return lax.all_gather(value, 'leaf', axis_index_groups=groups)]
    all_to_all x1 -> x2, starting transfers between devices: 6.2 us -> 12.8 us  [swap(): return lax.all_to_all(message, 'leaf', 0, 0, axis_index_groups=groups)]
    all_to_all x1 -> x2, waiting for transfers between devices: 5.17 us -> 5.05 us  [swap(): return lax.all_to_all(message, 'leaf', 0, 0, axis_index_groups=groups)]
  transfers between devices with their start and end apart: 1 -> 4, of which waited for: 1 -> 2; matrix products, arithmetic and copies ran while one was open for 0% -> 0% of each run, Pallas kernels for 0% -> 1%
where the time goes in v2:
time: 193 us; the launch traced here: 191 us
  blocking collectives  90 us (47%)
  local copies, waits for them, and re-layouts  34 us (18%)
  Pallas kernels  29.2 us (15%)
  between operations  13.6 us (7%)
  starting transfers between devices  12.8 us (7%)
  waiting for transfers between devices  11.7 us (6%)
    all_to_all x4, blocking collectives, swap(): return lax.all_to_all(message, 'leaf', 0, 0, axis_index_groups=groups)  74.9 us
    unnamed x86, local copies, waits for them, and re-layouts  34 us
    pallas_call x9, Pallas kernels, call(): pl.pallas_call(kernel, out_shape=[jax.ShapeDtypeStruct(shape, f32) for sh...  29.2 us
    all_gather x1, blocking collectives, collect(): return lax.all_gather(value, 'leaf', axis_index_groups=groups)  15.2 us
    all_to_all x2, starting transfers between devices, swap(): return lax.all_to_all(message, 'leaf', 0, 0, axis_index_groups=groups)  12.8 us
    all_gather x2, waiting for transfers between devices, collect(): return lax.all_gather(value, 'leaf', axis_index_groups=groups)  6.62 us
    all_to_all x2, waiting for transfers between devices, swap(): return lax.all_to_all(message, 'leaf', 0, 0, axis_index_groups=groups)  5.05 us
  transfers between devices with their start and end apart: 4, of which 2 were waited for; matrix products, arithmetic and copies ran while one was open for 0% of the time, Pallas kernels for 1%

profile of v2, /device:TPU:2, one launch (start us, length us, event | category | flops | bytes accessed | tf_op | source)
XLA Modules:
  0.0 191.2 jit_solution(16631098976285791243)
XLA Ops:
  6.5 1.3 copy-done.3
  7.8 1.0 copy-done.15
  9.5 2.5 %shard_map.109 = f32[128,128]{1,0:T(8,128)} custom-call(s32[4]{0:T(128)S(1)} %copy-done.40, f32[4,512,128]{2,1,0:T(8,128)S(1)} %copy-done.3, f32[3,256,128]{2,1,0:T(8,128)S(1)} %copy-done.15), custom_call_target="tpu_custom_call" | custom-call | tf_op jit(solution)/shard_map/pallas_call | solution.py:518
  12.0 1.2 copy-done.4
  13.2 1.0 copy-done.16
  15.8 1.1 shard_map.110
  18.8 6.3 %all-to-all-start = ((f32[16,24,128]{2,1,0:T(8,128)}), f32[16,24,128]{2,1,0:T(8,128)S(1)}, u32[]{:S(2)}, u32[]{:S(2)}) async-start(f32[16,24,128]{2,1,0:T(8,128)} %copy-done.28), calls=%async_computation | async-start | bytes 393216 | tf_op jit(solution)/shard_map/all_to_all | solution.py:555
  25.2 5.0 %all-to-all-done.recv_ref = f32[16,24,128]{2,1,0:T(8,128)S(1)} async-done(((f32[16,24,128]{2,1,0:T(8,128)}), f32[16,24,128]{2,1,0:T(8,128)S(1)}, u32[]{:S(2)}, u32[]{:S(2)}) %all-to-all-start) | async-done | bytes 196640 | tf_op jit(solution)/shard_map/all_to_all | solution.py:555
  31.4 22.8 %all_to_all.30.recv_ref = f32[16,24,128]{2,1,0:T(8,128)S(1)} all-to-all(f32[16,24,128]{2,1,0:T(8,128)S(1)} %get-tuple-element.32), channel_id=1, replica_groups={{0,16,32,48,64,80,96,112,128,144,160,176,192,208,224,240},{1,17,33,49,6..., dimensions={0} | all-to-all | bytes 393216 | tf_op jit(solution)/shard_map/all_to_all | solution.py:555
  54.3 1.3 copy-done.7
  55.6 3.4 %shard_map.112 = (f32[14,128,128]{2,1,0:T(8,128)S(1)}, f32[128,128]{1,0:T(8,128)S(1)}) custom-call(f32[16,128,128]{2,1,0:T(8,128)S(1)} %bitcast.3, f32[7,256,128]{2,1,0:T(8,128)S(1)} %copy-done), custom_call_target="tpu_custom_call" | custom-call | tf_op jit(solution)/shard_map/pallas_call | solution.py:518
  59.9 1.6 copy-done.10
  61.5 1.0 copy-done.21
  66.0 5.0 %shard_map.113 = (f32[16,1024]{1,0:T(8,128)S(1)}, f32[16,128]{1,0:T(8,128)S(1)}, f32[16,40,128]{2,1,0:T(8,128)S(1)}, f32[8,128]{1,0:T(8,128)S(1)}, f32[16,2048]{1,0:T(8,128)S(1)}) custom-call(s32[1]{0:T(128)} %bitcast.me_ref, s32[4]{0:T(128)S(1)} %copy-done.42, f32[16,24,128]{2,1,0:T(8,128)S(1)} %all_to_all.30.recv_ref, f32[4,16,128]{2,1,0:T(8,128)S(1)} %copy-done.39, ...), custom_call_target="tpu_custom_call" | custom-call | tf_op jit(solution)/shard_map/pallas_call | solution.py:518
  73.1 6.4 %all-to-all-start.2 = ((f32[16,40,128]{2,1,0:T(8,128)}), f32[16,40,128]{2,1,0:T(8,128)}, u32[]{:S(2)}, u32[]{:S(2)}) async-start(f32[16,40,128]{2,1,0:T(8,128)} %copy-done.26), calls=%async_computation.2 | async-start | bytes 655360 | tf_op jit(solution)/shard_map/all_to_all | solution.py:555
  79.5 15.2 %all-gather.1 = f32[512,128]{1,0:T(8,128)} all-gather(f32[128,128]{1,0:T(8,128)S(1)} %get-tuple-element.36), channel_id=3, replica_groups={{0,16,32,48},{1,17,33,49},{2,18,34,50},{3,19,35,51},{4,20,36,52},{5,21,..., dimensions={0}, use_global_device_ids=true | all-gather | bytes 327680 | tf_op jit(solution)/shard_map/all_gather | solution.py:559
  94.7 1.2 copy-done.8
  95.9 1.2 copy-done.13
  97.1 2.9 %shard_map.114 = (f32[16,40,128]{2,1,0:T(8,128)S(1)}, f32[12,16,128]{2,1,0:T(8,128)S(1)}) custom-call(s32[1]{0:T(128)} %bitcast.me_ref, f32[16,40,128]{2,1,0:T(8,128)} %all-to-all-done.2.recv_ref, f32[7,256,128]{2,1,0:T(8,128)S(1)} %copy-done, f32[7,256,128]{2,1,0:T(8,128)S(1)} %copy-done.2, f32[8,2,128,128]{3,2,1,0:T(8,128)S(1)} %copy-done.1, ...), custom_call_target="tpu_custom_call" | custom-call | tf_op jit(solution)/shard_map/pallas_call | solution.py:518
  100.8 18.3 %all_to_all.31.recv_ref = f32[16,40,128]{2,1,0:T(8,128)} all-to-all(f32[16,40,128]{2,1,0:T(8,128)} %copy-done.27), channel_id=1, replica_groups={{0,16,32,48,64,80,96,112,128,144,160,176,192,208,224,240},{1,17,33,49,6..., dimensions={0} | all-to-all | bytes 655360 | tf_op jit(solution)/shard_map/all_to_all | solution.py:555
  119.0 6.6 %all-gather.8.cloned.1.call-done.top_gram_ref = f32[16,128,128]{2,1,0:T(8,128)} async-done(((f32[4,128,128]{2,1,0:T(8,128)}), f32[16,128,128]{2,1,0:T(8,128)}) %all-gather.8.cloned.1.call-update) | async-done | bytes 1048592 | tf_op jit(solution)/shard_map/all_gather | solution.py:559
  125.7 1.2 copy-done.6
  126.9 1.2 copy-done.9
  128.1 1.6 copy-done.11
  129.7 1.2 copy-done.14
  130.9 1.2 copy-done.18
  132.1 1.0 copy-done.20
  137.0 8.8 %shard_map.115 = (f32[16,1024]{1,0:T(8,128)S(1)}, f32[16,1024]{1,0:T(8,128)S(1)}, f32[16,128]{1,0:T(8,128)S(1)}, f32[16,128]{1,0:T(8,128)S(1)}, f32[16,40,128]{2,1,0:T(8,128)S(1)}, /*index=5*/f32[8,128]{1,0:T(8,128)}) custom-call(s32[1]{0:T(128)} %bitcast.me_ref, s32[4]{0:T(128)S(1)} %copy-done.42, f32[16,40,128]{2,1,0:T(8,128)S(1)} %copy-done.25, ...), custom_call_target="tpu_custom_call" | custom-call | tf_op jit(solution)/shard_map/pallas_call | solution.py:518
  145.7 11.8 %all_to_all.32.recv_ref = f32[16,40,128]{2,1,0:T(8,128)S(1)} all-to-all(f32[16,40,128]{2,1,0:T(8,128)S(1)} %get-tuple-element.50), channel_id=1, replica_groups={{0,1,2,3,4,5,6,7,8,9,10,11,12,13,14,15},{16,17,18,19,20,21,22,23,24,25,..., dimensions={0} | all-to-all | bytes 655360 | tf_op jit(solution)/shard_map/all_to_all | solution.py:555
  157.5 2.3 %shard_map.116 = (f32[16,40,128]{2,1,0:T(8,128)S(1)}, f32[12,16,128]{2,1,0:T(8,128)}) custom-call(s32[1]{0:T(128)} %bitcast.me_ref, f32[16,40,128]{2,1,0:T(8,128)S(1)} %all_to_all.32.recv_ref, f32[7,256,128]{2,1,0:T(8,128)S(1)} %copy-done, f32[7,256,128]{2,1,0:T(8,128)S(1)} %copy-done.2, f32[8,2,128,128]{3,2,1,0:T(8,128)S(1)} %copy-done.1, ...), custom_call_target="tpu_custom_call" | custom-call | tf_op jit(solution)/shard_map/pallas_call | solution.py:518
  159.8 22.0 %all_to_all.33.recv_ref = f32[16,40,128]{2,1,0:T(8,128)S(1)} all-to-all(f32[16,40,128]{2,1,0:T(8,128)S(1)} %get-tuple-element.51), channel_id=1, replica_groups={{0,16,32,48,64,80,96,112,128,144,160,176,192,208,224,240},{1,17,33,49,6..., dimensions={0} | all-to-all | bytes 655360 | tf_op jit(solution)/shard_map/all_to_all | solution.py:555
  181.8 2.6 %shard_map.117 = f32[16,1024]{1,0:T(8,128)} custom-call(f32[16,40,128]{2,1,0:T(8,128)S(1)} %all_to_all.33.recv_ref, f32[7,256,128]{2,1,0:T(8,128)S(1)} %copy-done, f32[7,256,128]{2,1,0:T(8,128)S(1)} %copy-done.2, f32[8,2,128,128]{3,2,1,0:T(8,128)S(1)} %copy-done.1, f32[16,128,128]{2,1,0:T(8,128)S(1)} %copy-done.18, ...), custom_call_target="tpu_custom_call" | custom-call | tf_op jit(solution)/shard_map/pallas_call | solution.py:518
  (78 shorter events, 16.4 us)
Async XLA Ops:
  6.5 23.7 %copy-start = (f32[7,256,128]{2,1,0:T(8,128)S(1)}, f32[7,256,128]{2,1,0:T(8,128)}, u32[]{:S(2)}) copy-start(f32[7,256,128]{2,1,0:T(8,128)} %up_row_ref.11) | copy-start | bytes 2752516
  6.5 47.7 %all-gather.6.cloned.1.call-start = ((), (), s32[]{:S(2)}) async-start(), calls=%async_computation.6 | async-start | bytes 1114112 | tf_op jit(solution)/shard_map/all_gather | solution.py:559
  6.5 1.3 copy-start.3
  7.8 1.0 copy-start.15
  12.0 1.2 copy-start.4
  13.2 1.0 copy-start.16
  15.8 44.1 %copy-start.17 = (f32[3,256,128]{2,1,0:T(8,128)S(1)}, f32[3,256,128]{2,1,0:T(8,128)}, u32[]{:S(2)}) copy-start(f32[3,256,128]{2,1,0:T(8,128)} %local_row_ref.7) | copy-start | bytes 1179652
  15.8 44.1 %copy-start.42 = (s32[4]{0:T(128)S(1)}, s32[4]{0:T(128)}, u32[]{:S(2)}) copy-start(s32[4]{0:T(128)} %rows_ref.7) | copy-start | bytes 52
  18.8 41.1 %copy-start.1 = (f32[8,2,128,128]{3,2,1,0:T(8,128)S(1)}, f32[8,2,128,128]{3,2,1,0:T(8,128)}, u32[]{:S(2)}) copy-start(f32[8,2,128,128]{3,2,1,0:T(8,128)} %up_couple_ref.9) | copy-start | bytes 3145732
  18.8 41.1 %copy-start.2 = (f32[7,256,128]{2,1,0:T(8,128)S(1)}, f32[7,256,128]{2,1,0:T(8,128)}, u32[]{:S(2)}) copy-start(f32[7,256,128]{2,1,0:T(8,128)} %up_col_ref.9) | copy-start | bytes 2752516
  18.8 11.4 %all-to-all-start = ((f32[16,24,128]{2,1,0:T(8,128)}), f32[16,24,128]{2,1,0:T(8,128)S(1)}, u32[]{:S(2)}, u32[]{:S(2)}) async-start(f32[16,24,128]{2,1,0:T(8,128)} %copy-done.28), calls=%async_computation | async-start | bytes 393216 | tf_op jit(solution)/shard_map/all_to_all | solution.py:555
  54.3 5.6 %copy-start.5 = (f32[4,512,128]{2,1,0:T(8,128)S(1)}, f32[4,512,128]{2,1,0:T(8,128)}, u32[]{:S(2)}) copy-start(f32[4,512,128]{2,1,0:T(8,128)} %row_basis_ref.7) | copy-start | bytes 3145732
  54.3 1.3 copy-start.7
  55.6 4.3 %copy-start.19 = (f32[4,256,128]{2,1,0:T(8,128)S(1)}, f32[4,256,128]{2,1,0:T(8,128)}, u32[]{:S(2)}) copy-start(f32[4,256,128]{2,1,0:T(8,128)} %col_basis_ref.3) | copy-start | bytes 1572868
  59.0 0.9 copy-start.12
  59.9 1.6 copy-start.10
  61.5 1.0 copy-start.21
  62.5 1.0 copy-start.23
  73.1 21.6 %all-to-all-start.2 = ((f32[16,40,128]{2,1,0:T(8,128)}), f32[16,40,128]{2,1,0:T(8,128)}, u32[]{:S(2)}, u32[]{:S(2)}) async-start(f32[16,40,128]{2,1,0:T(8,128)} %copy-done.26), calls=%async_computation.2 | async-start | bytes 655360 | tf_op jit(solution)/shard_map/all_to_all | solution.py:555
  79.5 46.2 %all-gather.8.cloned.1.call-start = ((), (), s32[]{:S(2)}) async-start(), calls=%async_computation.7 | async-start | bytes 1310720 | tf_op jit(solution)/shard_map/all_gather | solution.py:559
  94.7 1.2 copy-start.8
  95.9 1.2 copy-start.13
  97.1 28.6 %copy-start.30 = (f32[16,2048]{1,0:T(8,128)S(1)}, f32[16,2048]{1,0:T(8,128)}, u32[]{:S(2)}) copy-start(f32[16,2048]{1,0:T(8,128)} %copy-done.29) | copy-start | bytes 393220
  125.7 1.2 copy-start.6
  126.9 1.2 copy-start.9
  128.1 1.6 copy-start.11
  129.7 1.2 copy-start.14
  130.9 1.2 copy-start.18
  132.1 1.0 copy-start.20
  133.2 1.0 copy-start.22
  134.2 1.0 copy-start.24
  135.1 1.0 copy-start.25
  (15 other events, 10.8 us)
Sparse Core Ops, SparseCore 0:
  12.1 38.3 all-gather.5
  100.9 24.7 all-gather.7

commit v3 on v2

v3 whole, which is shorter than its diff:
```python
import functools

import jax
import jax.numpy as jnp
from jax import lax
from jax.experimental import pallas as pl
from jax.experimental.pallas import tpu as pltpu
from jax.sharding import PartitionSpec as P

RHS = 16
RANK = 128
LEAF_DEV = 4
LEAF_ROWS = 512
LEAF_COLS = 256
PATH = 3
LEVEL_BASE = (0, 8, 12)
PACKED = 72
TINY = 1.2e-38
NEAR = 8
MID = 8
FAR = 4
VMEM_MIB = 24
VMEM_LIMIT = VMEM_MIB * 1024 * 1024

f32 = jnp.float32
bf16 = jnp.bfloat16


def split(v):
    head = v.astype(bf16)
    return head, (v - head.astype(f32)).astype(bf16)


def mm(x, pair, transposed=False):
    xh, xl = split(x)
    wh, wl = pair
    dims = (((1,), (1 if transposed else 0,)), ((), ()))
    n = x.shape[0]
    both = lax.dot_general(jnp.concatenate([xh, xl], 0), wh, dims, preferred_element_type=f32)
    rest = lax.dot_general(xh, wl, dims, preferred_element_type=f32)
    return both[:n] + (both[n:] + rest)


def mm_inner(a, b):
    ah, al = split(a)
    bh, bl = split(b)
    dims = (((0,), (0,)), ((), ()))
    m = a.shape[1]
    both = lax.dot_general(jnp.concatenate([ah, al], 1), bh, dims, preferred_element_type=f32)
    rest = lax.dot_general(ah, bl, dims, preferred_element_type=f32)
    return both[:m] + (both[m:] + rest)


def pair_at(ref, *index):
    if ref.dtype == bf16:
        return ref[(0,) + index], ref[(1,) + index]
    return split(ref[index])


def pairs_of(ref):
    return functools.partial(pair_at, ref)


def half_of(ref, j, child):
    return pair_at(ref, j, pl.ds(pl.multiple_of(child * RANK, RANK), RANK))


def eye():
    return (
        lax.broadcasted_iota(jnp.int32, (RHS, RANK), 0)
        == lax.broadcasted_iota(jnp.int32, (RHS, RANK), 1)
    ).astype(f32)


def stat_block(first, second):
    rows = lax.broadcasted_iota(jnp.int32, (8, RANK), 0)
    return first * (rows == 0).astype(f32) + second * (rows == 1).astype(f32)


def column_of(row):
    return jnp.sum(row * eye(), axis=1, keepdims=True)


def row_of(column):
    return jnp.sum(column * eye(), axis=0, keepdims=True)


def inverse_norm(squares):
    return jnp.where(squares >= TINY, 1.0 / jnp.sqrt(squares), 1.0)


def sum_squares(v):
    return jnp.sum(v * v, axis=1, keepdims=True)


def send(out_ref, value):
    for peer in range(out_ref.shape[0]):
        out_ref[peer] = value


def stack(blocks):
    return jnp.concatenate(blocks, 0)


def unstack(value, count):
    size = value.shape[0] // count
    return [value[k * size : (k + 1) * size] for k in range(count)]


def climb(blocks, transfer):
    count = len(blocks) // 2
    paired = [jnp.concatenate([blocks[2 * m], blocks[2 * m + 1]], 1) for m in range(count)]
    return unstack(mm(stack(paired), transfer), count)


def descend(blocks, transfer):
    spread = unstack(mm(stack(blocks), transfer, transposed=True), len(blocks))
    out = []
    for block in spread:
        out += [block[:, :RANK], block[:, RANK:]]
    return out


def couple_all(blocks, coupling):
    count = len(blocks) // 2
    even = unstack(mm(stack(blocks[1::2]), coupling[0]), count)
    odd = unstack(mm(stack(blocks[0::2]), coupling[1]), count)
    out = []
    for m in range(count):
        out += [even[m], odd[m]]
    return out


def local_up(parts, basis, transfer):
    leaf = [mm(parts[q], basis(q)) for q in range(LEAF_DEV)]
    node = [
        mm(jnp.concatenate([leaf[2 * m], leaf[2 * m + 1]], 1), transfer(m)) for m in range(2)
    ]
    return leaf, node


def local_root(node, transfer):
    return mm(jnp.concatenate(node, 1), transfer(2))


def couple(sibling, coupling, node, child, adjoint):
    if adjoint:
        return mm(sibling, coupling(node, 1 - child), transposed=True)
    return mm(sibling, coupling(node, child))


def local_down(root, leaf, node, coupling, transfer, adjoint):
    spread = None if root is None else mm(root, transfer(2), transposed=True)
    out = []
    for m in range(2):
        here = None if spread is None else spread[:, m * RANK : (m + 1) * RANK]
        if node is not None:
            gained = couple(node[1 - m], coupling, 2, m, adjoint)
            here = gained if here is None else here + gained
        below = mm(here, transfer(m), transposed=True)
        for i in range(2):
            value = below[:, i * RANK : (i + 1) * RANK]
            if leaf is not None:
                value = value + couple(leaf[2 * m + 1 - i], coupling, m, i, adjoint)
            out.append(value)
    return out


def live_mask(rows_ref, q):
    slots = lax.broadcasted_iota(jnp.int32, (RHS, LEAF_ROWS), 1)
    return (slots < rows_ref[q]).astype(f32)


def row_part(q):
    return slice(q * LEAF_ROWS, (q + 1) * LEAF_ROWS)


def col_part(q):
    return slice(q * LEAF_COLS, (q + 1) * LEAF_COLS)


def pair_up(parts, local, rows_ref, msg_ref, own_ref, inner_ref):
    dense, row_basis, col_basis, local_row, local_col, coupling = local
    squares = sum_squares(parts[0])
    for part in parts[1:]:
        squares = squares + sum_squares(part)
    scale = inverse_norm(squares)
    parts = [part * scale for part in parts]
    leaf, node = local_up(parts, col_basis, local_col)
    root = local_root(node, local_col)
    down = local_down(None, leaf, node, coupling, local_row, False)
    result = []
    energy = jnp.zeros((RHS, 1), f32)
    for q in range(LEAF_DEV):
        y = mm(parts[q], dense(q), transposed=True)
        y = y + mm(down[q], row_basis(q), transposed=True)
        y = y * live_mask(rows_ref, q)
        if inner_ref is not None:
            inner_ref[:, row_part(q)] = y
        energy = energy + sum_squares(y)
        result.append(y)
    _, row_node = local_up(result, row_basis, local_row)
    row_root = local_root(row_node, local_row)
    stats = stat_block(row_of(squares), row_of(energy))
    own_ref[...] = stats
    send(msg_ref, stack([root, row_root, stats]))


def both_sides(grams, half):
    full = half[0].astype(f32) + half[1].astype(f32)
    left = mm(jnp.transpose(full), split(jnp.concatenate(grams, 1)))
    columns = [left[:, k * RANK : (k + 1) * RANK] for k in range(len(grams))]
    return unstack(mm(stack(columns), half), len(grams))


def gram_climb(grams, transfer):
    even = both_sides(grams[0::2], (transfer[0][:RANK], transfer[1][:RANK]))
    odd = both_sides(grams[1::2], (transfer[0][RANK:], transfer[1][RANK:]))
    return [a + b for a, b in zip(even, odd)]


def pack(gram):
    half = RANK // 2
    row = lax.broadcasted_iota(jnp.int32, (half, RANK), 0)
    col = lax.broadcasted_iota(jnp.int32, (half, RANK), 1)
    last = gram[half:]
    top = jnp.where((col < half) & (col > row), pltpu.roll(last, half, 1), gram[:half])
    diagonal = jnp.sum(jnp.where(col - half == row, last, 0.0), axis=0, keepdims=True)
    first = (lax.broadcasted_iota(jnp.int32, (8, RANK), 0) == 0).astype(f32)
    return stack([top, diagonal * first])


def unpack(packed):
    half = RANK // 2
    row = lax.broadcasted_iota(jnp.int32, (half, RANK), 0)
    col = lax.broadcasted_iota(jnp.int32, (half, RANK), 1)
    top = packed[:half]
    diagonal = packed[half : half + 1]
    upper = jnp.where((col >= half) | (col < row), top, jnp.where(col == row, 0.5 * top, 0.0))
    lower = jnp.where(
        col - half > row,
        pltpu.roll(top, half, 1),
        jnp.where(col - half == row, 0.5 * diagonal, 0.0),
    )
    part = stack([upper, lower])
    return part + jnp.transpose(part)


def start_kernel(
    me_ref, rows_ref, rhs_ref, row_basis_ref, local_row_ref, z_ref, msg_ref, keep_ref
):
    row_basis = [split(row_basis_ref[q]) for q in range(LEAF_DEV)]
    local_row = [split(local_row_ref[m]) for m in range(3)]
    parts = []
    squares = jnp.zeros((RHS, 1), f32)
    for q in range(LEAF_DEV):
        part = rhs_ref[:, row_part(q)] * live_mask(rows_ref, q)
        z_ref[:, row_part(q)] = part
        squares = squares + sum_squares(part)
        parts.append(part)
    leaf, node = local_up(parts, row_basis.__getitem__, local_row.__getitem__)
    for k, value in enumerate(leaf + node):
        keep_ref[k] = value
    root = local_root(node, local_row.__getitem__)
    row = row_of(squares)
    grams = []
    for q in range(LEAF_DEV):
        slots = lax.broadcasted_iota(jnp.int32, (LEAF_ROWS, RANK), 0)
        basis = jnp.where(slots < rows_ref[q], row_basis_ref[q], 0.0)
        grams.append(mm_inner(basis, basis))
    nodes = [gram_climb(grams[2 * m : 2 * m + 2], local_row[m])[0] for m in range(2)]
    gram = gram_climb(nodes, local_row[2])[0]
    send(msg_ref, stack([root, stat_block(row, row), pack(gram)]))


def sum_stats(recv_ref):
    stats = recv_ref[0, RHS : RHS + 8]
    for d in range(1, recv_ref.shape[0]):
        stats = stats + recv_ref[d, RHS : RHS + 8]
    return stats


def lower_kernel(level, me_ref, recv_ref, climb_ref, msg_ref, sib_ref, nodes_ref, scratch_ref):
    place = (me_ref[0] >> level) % NEAR
    peers = range(recv_ref.shape[0])
    summaries = [recv_ref[d, :RHS] for d in peers]
    grams = [unpack(recv_ref[d, RHS + 8 :]) for d in peers]
    for height in range(PATH):
        base = LEVEL_BASE[height]
        for m, value in enumerate(summaries):
            scratch_ref[base + m] = value
        sib_ref[height] = scratch_ref[base + ((place >> height) ^ 1)]
        for k, value in enumerate(grams):
            high, low = split(value)
            nodes_ref[0, base + k] = high
            nodes_ref[1, base + k] = low
        transfer = pair_at(climb_ref, level + height)
        summaries = climb(summaries, transfer)
        grams = gram_climb(grams, transfer)
    send(msg_ref, stack([summaries[0], sum_stats(recv_ref), pack(grams[0])]))


def readers(local):
    return [pairs_of(ref) for ref in local]


def first_kernel(
    me_ref,
    rows_ref,
    recv_ref,
    near_ref,
    mid_ref,
    up_row_ref,
    up_col_ref,
    up_couple_ref,
    keep_ref,
    dense_ref,
    row_basis_ref,
    col_basis_ref,
    local_row_ref,
    local_col_ref,
    local_couple_ref,
    z_ref,
    x_ref,
    beta_ref,
    msg_ref,
    own_ref,
    inner_ref,
    nodes_ref,
    scratch_ref,
):
    me = me_ref[0]
    place = me >> (2 * PATH)
    summaries = [recv_ref[d, :RHS] for d in range(FAR)]
    siblings = [near_ref[j] for j in range(PATH)] + [mid_ref[j] for j in range(PATH)]
    siblings.append(recv_ref[place ^ 1, :RHS])
    summaries = climb(summaries, pair_at(up_row_ref, 6))
    for m, value in enumerate(summaries):
        scratch_ref[m] = value
    siblings.append(scratch_ref[(place >> 1) ^ 1])
    potential = None
    for j in reversed(range(8)):
        child = (me >> j) & 1
        gained = mm(siblings[j], pair_at(up_couple_ref, j, 1 - child), transposed=True)
        if potential is not None:
            gained = gained + mm(potential, half_of(up_col_ref, j, child), transposed=True)
        potential = gained
    beta = jnp.sqrt(column_of(sum_stats(recv_ref)[:1]))
    for d in range(FAR):
        high, low = split(unpack(recv_ref[d, RHS + 8 :]))
        nodes_ref[0, d] = high
        nodes_ref[1, d] = low
    inverse = 1.0 / beta
    beta_ref[...] = jnp.broadcast_to(beta, (RHS, RANK))
    local = readers(
        (dense_ref, row_basis_ref, col_basis_ref, local_row_ref, local_col_ref, local_couple_ref)
    )
    dense, _, col_basis, _, local_col, coupling = local
    leaf = [keep_ref[q] for q in range(LEAF_DEV)]
    node = [keep_ref[LEAF_DEV + m] for m in range(2)]
    down = local_down(potential, leaf, node, coupling, local_col, True)
    parts = []
    for q in range(LEAF_DEV):
        x = mm(z_ref[:, row_part(q)], dense(q))
        x = (x + mm(down[q], col_basis(q), transposed=True)) * inverse
        x_ref[:, col_part(q)] = x
        parts.append(x)
    pair_up(parts, local, rows_ref, msg_ref, own_ref, inner_ref)


def rescale(recv_ref):
    base = 2 * RHS
    squares = stack([recv_ref[d, base : base + 1] for d in range(recv_ref.shape[0])])
    energy = stack([recv_ref[d, base + 1 : base + 2] for d in range(recv_ref.shape[0])])
    total = jnp.sum(squares, axis=0, keepdims=True)
    factor = inverse_norm(total) / inverse_norm(squares)
    energy = jnp.sum(energy * factor * factor, axis=0, keepdims=True)
    first = []
    second = []
    for d in range(recv_ref.shape[0]):
        column = column_of(factor[d : d + 1])
        first.append(recv_ref[d, :RHS] * column)
        second.append(recv_ref[d, RHS : 2 * RHS] * column)
    return first, second, factor, total, energy


def lower_pair_kernel(
    level,
    me_ref,
    recv_ref,
    up_row_ref,
    up_col_ref,
    up_couple_ref,
    nodes_ref,
    msg_ref,
    path_ref,
    own_ref,
    gain_ref,
    below_ref,
):
    place = (me_ref[0] >> level) % NEAR
    first, second, _, total, energy = rescale(recv_ref)
    cross = jnp.zeros((RHS, RANK), f32)
    for height in range(PATH):
        j = level + height
        base = LEVEL_BASE[height]
        gained = couple_all(first, (pair_at(up_couple_ref, j, 0), pair_at(up_couple_ref, j, 1)))
        summed = []
        for k in range(len(first)):
            moved = mm(gained[k], pair_at(nodes_ref, base + k))
            cross = cross + gained[k] * (2.0 * second[k] + moved)
            summed.append(second[k] + moved)
            gain_ref[base + k] = gained[k]
            below_ref[base + k] = second[k]
        own = base + (place >> height)
        other = base + ((place >> height) ^ 1)
        path_ref[3 * height] = gain_ref[own]
        path_ref[3 * height + 1] = gain_ref[other]
        path_ref[3 * height + 2] = below_ref[other]
        first = climb(first, pair_at(up_col_ref, j))
        second = climb(summed, pair_at(up_row_ref, j))
    energy = energy + row_of(jnp.sum(cross, axis=1, keepdims=True))
    stats = stat_block(total, energy)
    own_ref[...] = stats
    send(msg_ref, stack([first[0], second[0], stats]))


def top_levels(recv_ref, up_row_ref, up_col_ref, up_couple_ref, gram_ref):
    first, second, _, total, energy = rescale(recv_ref)
    gained = couple_all(first, (pair_at(up_couple_ref, 6, 0), pair_at(up_couple_ref, 6, 1)))
    first = climb(first, pair_at(up_col_ref, 6))
    potential = couple_all(first, (pair_at(up_couple_ref, 7, 0), pair_at(up_couple_ref, 7, 1)))
    below = descend(potential, pair_at(up_row_ref, 6))
    potential = [a + b for a, b in zip(gained, below)]
    cross = jnp.zeros((RHS, RANK), f32)
    summed = []
    for d in range(FAR):
        moved = mm(potential[d], pair_at(gram_ref, d))
        cross = cross + potential[d] * (2.0 * second[d] + moved)
        summed.append(second[d] + moved)
    energy = column_of(energy) + jnp.sum(cross, axis=1, keepdims=True)
    return potential, summed, column_of(total), energy


def middle_kernel(
    me_ref,
    rows_ref,
    recv_ref,
    near_path_ref,
    near_own_ref,
    mid_path_ref,
    mid_own_ref,
    up_row_ref,
    up_col_ref,
    up_couple_ref,
    top_gram_ref,
    near_nodes_ref,
    mid_nodes_ref,
    dense_ref,
    row_basis_ref,
    col_basis_ref,
    local_row_ref,
    local_col_ref,
    local_couple_ref,
    x_ref,
    own_in_ref,
    inner_ref,
    v_ref,
    next_ref,
    alpha_ref,
    rho_ref,
    msg_ref,
    own_ref,
    a_ref,
    b_ref,
):
    me = me_ref[0]
    place = me >> (2 * PATH)
    potential, summed, squares, energy = top_levels(
        recv_ref, up_row_ref, up_col_ref, up_couple_ref, top_gram_ref
    )
    alpha = jnp.sqrt(squares)
    rho = jnp.sqrt(energy)
    alpha_ref[...] = jnp.broadcast_to(alpha, (RHS, RANK))
    rho_ref[...] = jnp.broadcast_to(rho, (RHS, RANK))
    scale = inverse_norm(squares)
    for d in range(FAR):
        a_ref[d] = potential[d]
        b_ref[d] = summed[d]
    forward = a_ref[place]
    siblings = {6: b_ref[place ^ 1]}
    for k, value in enumerate(climb(summed, pair_at(up_row_ref, 6))):
        a_ref[FAR + k] = value
    siblings[7] = a_ref[FAR + ((place >> 1) ^ 1)]
    for level, path_ref, part_ref, nodes_ref in (
        (PATH, mid_path_ref, mid_own_ref, mid_nodes_ref),
        (0, near_path_ref, near_own_ref, near_nodes_ref),
    ):
        factor = scale / inverse_norm(column_of(part_ref[:1]))
        inside = (me >> level) % NEAR
        for height in reversed(range(PATH)):
            j = level + height
            child = (me >> j) & 1
            spread = mm(forward, pair_at(up_row_ref, j), transposed=True)
            low = spread[:, :RANK]
            high = spread[:, RANK:]
            forward = path_ref[3 * height] * factor + jnp.where(child == 0, low, high)
            other = path_ref[3 * height + 1] * factor + jnp.where(child == 0, high, low)
            gram = pair_at(nodes_ref, LEVEL_BASE[height] + ((inside >> height) ^ 1))
            siblings[j] = path_ref[3 * height + 2] * factor + mm(other, gram)
    backward = None
    for j in reversed(range(8)):
        child = (me >> j) & 1
        gained = mm(siblings[j], pair_at(up_couple_ref, j, 1 - child), transposed=True)
        if backward is not None:
            gained = gained + mm(backward, half_of(up_col_ref, j, child), transposed=True)
        backward = gained
    local = readers(
        (dense_ref, row_basis_ref, col_basis_ref, local_row_ref, local_col_ref, local_couple_ref)
    )
    dense, row_basis, col_basis, local_row, local_col, coupling = local
    own_factor = scale / inverse_norm(column_of(own_in_ref[:1]))
    outer = local_down(forward, None, None, coupling, local_row, False)
    images = []
    for q in range(LEAF_DEV):
        y = mm(outer[q], row_basis(q), transposed=True) * live_mask(rows_ref, q)
        images.append(y + inner_ref[:, row_part(q)] * own_factor)
    leaf, node = local_up(images, row_basis, local_row)
    down = local_down(backward, leaf, node, coupling, local_col, True)
    inverse = 1.0 / rho
    parts = []
    for q in range(LEAF_DEV):
        v = x_ref[:, col_part(q)] * scale
        v_ref[:, col_part(q)] = v
        x = mm(images[q], dense(q)) + mm(down[q], col_basis(q), transposed=True)
        x = x * inverse - rho * v
        next_ref[:, col_part(q)] = x
        parts.append(x)
    pair_up(parts, local, rows_ref, msg_ref, own_ref, None)


def final_kernel(
    recv_ref,
    up_row_ref,
    up_col_ref,
    up_couple_ref,
    top_gram_ref,
    beta_ref,
    alpha_ref,
    rho_ref,
    v_ref,
    x_ref,
    out_ref,
):
    _, _, squares, energy = top_levels(
        recv_ref, up_row_ref, up_col_ref, up_couple_ref, top_gram_ref
    )
    theta = jnp.sqrt(squares)
    rho2 = jnp.sqrt(energy - squares)
    rho = rho_ref[:, :1]
    phi = alpha_ref[:, :1] / rho * beta_ref[:, :1]
    v = v_ref[...]
    search = x_ref[...] * inverse_norm(squares) - (theta / rho) * v
    out_ref[...] = (phi / rho) * v - (phi * (theta / rho2) / rho2) * search


def call(kernel, outs, operands, scratch=()):
    spaces = [pltpu.SMEM if k.dtype == jnp.int32 else pltpu.VMEM for k in operands]
    outs = [shape if isinstance(shape, jax.ShapeDtypeStruct) else jax.ShapeDtypeStruct(shape, f32) for shape in outs]
    return pl.pallas_call(
        kernel,
        out_shape=outs,
        in_specs=[pl.BlockSpec(memory_space=space) for space in spaces],
        out_specs=[pl.BlockSpec(memory_space=pltpu.VMEM)] * len(outs),
        scratch_shapes=[pltpu.VMEM(shape, f32) for shape in scratch],
        compiler_params=pltpu.CompilerParams(vmem_limit_bytes=VMEM_LIMIT),
    )(*operands)


def device_groups(devices, stride, size):
    out = []
    for base in range(devices):
        if (base // stride) % size == 0:
            out.append([base + k * stride for k in range(size)])
    return out


def local_program(
    devices,
    rhs,
    box_rows,
    dense,
    row_basis,
    col_basis,
    local_col,
    local_row,
    local_couple,
    up_col,
    up_row,
    up_couple,
):
    me = lax.axis_index("leaf").astype(jnp.int32).reshape(1)
    near, mid, far = (1, NEAR), (NEAR, MID), (NEAR * MID, FAR)

    def swap(message, group):
        return lax.all_to_all(message, "leaf", 0, 0, axis_index_groups=device_groups(devices, *group))

    tile = (RHS, RANK)
    row_shape = (RHS, LEAF_DEV * LEAF_ROWS)
    col_shape = (RHS, LEAF_DEV * LEAF_COLS)
    single = (RHS + 8 + PACKED, RANK)
    double = (2 * RHS + 8, RANK)
    stat = (8, RANK)
    gram_shape = (RANK, RANK)
    tables = [up_row, up_col, up_couple]
    blocks = [dense, row_basis, col_basis, local_row, local_col, local_couple]

    def nodes_shape(count):
        return jax.ShapeDtypeStruct((2, count) + gram_shape, bf16)

    def lower(level, message, peers):
        return call(
            functools.partial(lower_kernel, level),
            [(peers,) + single, (PATH,) + tile, nodes_shape(14)],
            [me, message, up_row],
            [(14,) + tile],
        )

    def lower_pair(level, message, peers, nodes):
        return call(
            functools.partial(lower_pair_kernel, level),
            [(peers,) + double, (3 * PATH,) + tile, stat],
            [me, message] + tables + [nodes],
            [(14,) + tile, (14,) + tile],
        )

    z, message, keep = call(
        start_kernel,
        [row_shape, (NEAR,) + single, (6,) + tile],
        [me, box_rows, rhs, row_basis, local_row],
    )
    message, near_sib, near_nodes = lower(0, swap(message, near), MID)
    message, mid_sib, mid_nodes = lower(PATH, swap(message, mid), FAR)
    received = swap(message, far)
    x, beta, message, own, inner, top_nodes = call(
        first_kernel,
        [col_shape, tile, (NEAR,) + double, stat, row_shape, nodes_shape(FAR)],
        [me, box_rows, received, near_sib, mid_sib] + tables + [keep] + blocks + [z],
        [(2,) + tile],
    )
    message, near_path, near_own = lower_pair(0, swap(message, near), MID, near_nodes)
    message, mid_path, mid_own = lower_pair(PATH, swap(message, mid), FAR, mid_nodes)
    received = swap(message, far)
    v, x, alpha, rho, message, _ = call(
        middle_kernel,
        [col_shape, col_shape, tile, tile, (NEAR,) + double, stat],
        [me, box_rows, received, near_path, near_own, mid_path, mid_own]
        + tables
        + [top_nodes, near_nodes, mid_nodes]
        + blocks
        + [x, own, inner],
        [(6,) + tile, (4,) + tile],
    )
    message, _, _ = lower_pair(0, swap(message, near), MID, near_nodes)
    message, _, _ = lower_pair(PATH, swap(message, mid), FAR, mid_nodes)
    received = swap(message, far)
    (out,) = call(
        final_kernel, [col_shape], [received] + tables + [top_nodes, beta, alpha, rho, v, x]
    )
    return out


def solution(mesh):
    devices = mesh.shape["leaf"]
    return jax.shard_map(
        functools.partial(local_program, devices),
        mesh=mesh,
        in_specs=(
            P(None, "leaf"),
            P("leaf"),
            P("leaf", None, None),
            P("leaf", None, None),
            P("leaf", None, None),
            P("leaf", None, None),
            P("leaf", None, None),
            P("leaf", None, None, None),
            P(),
            P(),
            P(),
        ),
        out_specs=P(None, "leaf"),
        check_vma=False,
    )
```

time: 193 us -> 139 us (0.72)
  local copies, waits for them, and re-layouts: 34 us -> 7.91 us
  blocking collectives: 90 us -> 104 us
  between operations: 13.6 us -> 0.1 us
  starting transfers between devices: 12.8 us -> 0 us
  waiting for transfers between devices: 11.7 us -> 0 us
  Pallas kernels: 29.2 us -> 26.8 us
    all_to_all x4 -> x9, blocking collectives: 74.9 us -> 104 us  [swap(): lax.all_to_all(message, 'leaf', 0, 0, axis_index_groups=device_groups(dev...]
    unnamed x86 -> x28, local copies, waits for them, and re-layouts: 34 us -> 7.91 us
    all_gather x1 -> x0, blocking collectives: 15.2 us -> none  [collect(): return lax.all_gather(value, 'leaf', axis_index_groups=groups)]
    all_to_all x2 -> x0, starting transfers between devices: 12.8 us -> none  [swap(): return lax.all_to_all(message, 'leaf', 0, 0, axis_index_groups=groups)]
    all_gather x2 -> x0, waiting for transfers between devices: 6.62 us -> none  [collect(): return lax.all_gather(value, 'leaf', axis_index_groups=groups)]
    all_to_all x2 -> x0, waiting for transfers between devices: 5.05 us -> none  [swap(): return lax.all_to_all(message, 'leaf', 0, 0, axis_index_groups=groups)]
    pallas_call x9 -> x10, Pallas kernels: 29.2 us -> 26.8 us  [call(): pl.pallas_call(kernel, out_shape=outs, in_specs=[pl.BlockSpec(memory_spac...]
  transfers between devices with their start and end apart: 4 -> 0, of which waited for: 2 -> 0; matrix products, arithmetic and copies ran while one was open for 0% -> 0% of each run, Pallas kernels for 1% -> 0%
where the time goes in v3:
time: 139 us
  blocking collectives  104 us (75%)
  Pallas kernels  26.8 us (19%)
  local copies, waits for them, and re-layouts  7.91 us (6%)
    all_to_all x9, blocking collectives, swap(): lax.all_to_all(message, 'leaf', 0, 0, axis_index_groups=device_groups(dev...  104 us
    pallas_call x10, Pallas kernels, call(): pl.pallas_call(kernel, out_shape=outs, in_specs=[pl.BlockSpec(memory_spac...  26.8 us
    unnamed x28, local copies, waits for them, and re-layouts  7.91 us

profile of v3, /device:TPU:2, one launch (start us, length us, event | category | flops | bytes accessed | tf_op | source)
XLA Modules:
  0.0 138.5 jit_solution(8777448104027014297)
XLA Ops:
  0.0 1.3 copy-done.3
  1.3 1.0 copy-done.6
  2.3 0.9 copy-done.11
  3.2 0.7 copy-done.12
  3.9 2.3 %shard_map.109 = (f32[16,2048]{1,0:T(8,128)S(1)}, f32[8,96,128]{2,1,0:T(8,128)S(1)}, f32[6,16,128]{2,1,0:T(8,128)S(1)}) custom-call(s32[1]{0:T(128)} %bitcast.me_ref, s32[4]{0:T(128)S(1)} %copy-done.12, f32[16,2048]{1,0:T(8,128)S(1)} %copy-done.11, f32[4,512,128]{2,1,0:T(8,128)S(1)} %copy-done.3, f32[3,256,128]{2,1,0:T(8,128)S(1)} %copy-done.6), custom_call_target="tpu_custom_call" | custom-call | tf_op jit(solution)/shard_map/pallas_call | solution.py:570
  6.2 12.1 %all_to_all.45.recv_ref = f32[8,96,128]{2,1,0:T(8,128)S(1)} all-to-all(f32[8,96,128]{2,1,0:T(8,128)S(1)} %get-tuple-element.33), channel_id=1, replica_groups={{0,1,2,3,4,5,6,7},{8,9,10,11,12,13,14,15},{16,17,18,19,20,21,22,23},{24..., dimensions={0} | all-to-all | bytes 786432 | tf_op jit(solution)/shard_map/all_to_all | solution.py:606
  18.4 0.0 copy-done
  18.4 0.0 copy-start.13
  18.4 1.9 %shard_map.110 = (f32[8,96,128]{2,1,0:T(8,128)S(1)}, f32[3,16,128]{2,1,0:T(8,128)S(1)}, bf16[2,14,128,128]{3,2,1,0:T(8,128)(2,1)S(1)}) custom-call(s32[1]{0:T(128)} %bitcast.me_ref, f32[8,96,128]{2,1,0:T(8,128)S(1)} %all_to_all.45.recv_ref, f32[7,256,128]{2,1,0:T(8,128)S(1)} %copy-done), custom_call_target="tpu_custom_call" | custom-call | tf_op jit(solution)/shard_map/pallas_call | solution.py:570
  20.4 22.7 %all_to_all.46.recv_ref = f32[8,96,128]{2,1,0:T(8,128)S(1)} all-to-all(f32[8,96,128]{2,1,0:T(8,128)S(1)} %get-tuple-element.34), channel_id=1, replica_groups={{0,8,16,24,32,40,48,56},{1,9,17,25,33,41,49,57},{2,10,18,26,34,42,50,58..., dimensions={0} | all-to-all | bytes 786432 | tf_op jit(solution)/shard_map/all_to_all | solution.py:606
  43.1 1.9 %shard_map.111 = (f32[4,96,128]{2,1,0:T(8,128)S(1)}, f32[3,16,128]{2,1,0:T(8,128)S(1)}, bf16[2,14,128,128]{3,2,1,0:T(8,128)(2,1)S(1)}) custom-call(s32[1]{0:T(128)} %bitcast.me_ref, f32[8,96,128]{2,1,0:T(8,128)S(1)} %all_to_all.46.recv_ref, f32[7,256,128]{2,1,0:T(8,128)S(1)} %copy-done), custom_call_target="tpu_custom_call" | custom-call | tf_op jit(solution)/shard_map/pallas_call | solution.py:570
  45.0 10.6 %all_to_all.47.recv_ref = f32[4,96,128]{2,1,0:T(8,128)S(1)} all-to-all(f32[4,96,128]{2,1,0:T(8,128)S(1)} %get-tuple-element.35), channel_id=1, replica_groups={{0,64,128,192},{1,65,129,193},{2,66,130,194},{3,67,131,195},{4,68,132,1..., dimensions={0} | all-to-all | bytes 393216 | tf_op jit(solution)/shard_map/all_to_all | solution.py:606
  55.6 0.0 copy-done.5
  55.6 0.0 copy-done.1
  55.7 0.0 copy-start.7
  55.7 1.0 copy-done.7
  56.7 1.0 copy-done.8
  57.7 1.0 copy-done.9
  58.7 1.0 copy-done.10
  59.7 4.8 %shard_map.112 = (f32[16,1024]{1,0:T(8,128)S(1)}, f32[16,128]{1,0:T(8,128)S(1)}, f32[8,40,128]{2,1,0:T(8,128)S(1)}, f32[8,128]{1,0:T(8,128)S(1)}, f32[16,2048]{1...) custom-call(s32[1]{0:T(128)} %bitcast.me_ref, s32[4]{0:T(128)S(1)} %copy-done.13, f32[4,96,128]{2,1,0:T(8,128)S(1)} %all_to_all.47.recv_ref, ...), custom_call_target="tpu_custom_call" | custom-call | tf_op jit(solution)/shard_map/pallas_call | solution.py:570
  64.5 8.9 %all_to_all.48.recv_ref = f32[8,40,128]{2,1,0:T(8,128)S(1)} all-to-all(f32[8,40,128]{2,1,0:T(8,128)S(1)} %get-tuple-element.40), channel_id=1, replica_groups={{0,1,2,3,4,5,6,7},{8,9,10,11,12,13,14,15},{16,17,18,19,20,21,22,23},{24..., dimensions={0} | all-to-all | bytes 327680 | tf_op jit(solution)/shard_map/all_to_all | solution.py:606
  73.4 1.3 shard_map.113
  74.6 12.2 %all_to_all.49.recv_ref = f32[8,40,128]{2,1,0:T(8,128)S(1)} all-to-all(f32[8,40,128]{2,1,0:T(8,128)S(1)} %get-tuple-element.42), channel_id=1, replica_groups={{0,8,16,24,32,40,48,56},{1,9,17,25,33,41,49,57},{2,10,18,26,34,42,50,58..., dimensions={0} | all-to-all | bytes 327680 | tf_op jit(solution)/shard_map/all_to_all | solution.py:606
  86.8 1.3 shard_map.114
  88.1 8.1 %all_to_all.50.recv_ref = f32[4,40,128]{2,1,0:T(8,128)S(1)} all-to-all(f32[4,40,128]{2,1,0:T(8,128)S(1)} %get-tuple-element.44), channel_id=1, replica_groups={{0,64,128,192},{1,65,129,193},{2,66,130,194},{3,67,131,195},{4,68,132,1..., dimensions={0} | all-to-all | bytes 163840 | tf_op jit(solution)/shard_map/all_to_all | solution.py:606
  96.2 8.0 %shard_map.115 = (f32[16,1024]{1,0:T(8,128)S(1)}, f32[16,1024]{1,0:T(8,128)S(1)}, f32[16,128]{1,0:T(8,128)S(1)}, f32[16,128]{1,0:T(8,128)S(1)}, f32[8,40,128]{2,1,0:T(8,128)S(1)}, /*index=5*/f32[8,128]{1,0:T(8,128)}) custom-call(s32[1]{0:T(128)} %bitcast.me_ref, s32[4]{0:T(128)S(1)} %copy-done.13, f32[4,40,128]{2,1,0:T(8,128)S(1)} %all_to_all.50.recv_ref, ...), custom_call_target="tpu_custom_call" | custom-call | tf_op jit(solution)/shard_map/pallas_call | solution.py:570
  104.2 8.9 %all_to_all.51.recv_ref = f32[8,40,128]{2,1,0:T(8,128)S(1)} all-to-all(f32[8,40,128]{2,1,0:T(8,128)S(1)} %get-tuple-element.53), channel_id=1, replica_groups={{0,1,2,3,4,5,6,7},{8,9,10,11,12,13,14,15},{16,17,18,19,20,21,22,23},{24..., dimensions={0} | all-to-all | bytes 327680 | tf_op jit(solution)/shard_map/all_to_all | solution.py:606
  113.0 1.8 %shard_map.116 = (f32[8,40,128]{2,1,0:T(8,128)S(1)}, f32[9,16,128]{2,1,0:T(8,128)}, f32[8,128]{1,0:T(8,128)}) custom-call(s32[1]{0:T(128)} %bitcast.me_ref, f32[8,40,128]{2,1,0:T(8,128)S(1)} %all_to_all.51.recv_ref, f32[7,256,128]{2,1,0:T(8,128)S(1)} %copy-done, f32[7,256,128]{2,1,0:T(8,128)S(1)} %copy-done.2, f32[8,2,128,128]{3,2,1,0:T(8,128)S(1)} %copy-done.1, ...), custom_call_target="tpu_custom_call" | custom-call | tf_op jit(solution)/shard_map/pallas_call | solution.py:570
  114.9 12.2 %all_to_all.52.recv_ref = f32[8,40,128]{2,1,0:T(8,128)S(1)} all-to-all(f32[8,40,128]{2,1,0:T(8,128)S(1)} %get-tuple-element.54), channel_id=1, replica_groups={{0,8,16,24,32,40,48,56},{1,9,17,25,33,41,49,57},{2,10,18,26,34,42,50,58..., dimensions={0} | all-to-all | bytes 327680 | tf_op jit(solution)/shard_map/all_to_all | solution.py:606
  127.1 1.8 %shard_map.117 = (f32[4,40,128]{2,1,0:T(8,128)S(1)}, f32[9,16,128]{2,1,0:T(8,128)}, f32[8,128]{1,0:T(8,128)}) custom-call(s32[1]{0:T(128)} %bitcast.me_ref, f32[8,40,128]{2,1,0:T(8,128)S(1)} %all_to_all.52.recv_ref, f32[7,256,128]{2,1,0:T(8,128)S(1)} %copy-done, f32[7,256,128]{2,1,0:T(8,128)S(1)} %copy-done.2, f32[8,2,128,128]{3,2,1,0:T(8,128)S(1)} %copy-done.1, ...), custom_call_target="tpu_custom_call" | custom-call | tf_op jit(solution)/shard_map/pallas_call | solution.py:570
  128.9 8.1 %all_to_all.53.recv_ref = f32[4,40,128]{2,1,0:T(8,128)S(1)} all-to-all(f32[4,40,128]{2,1,0:T(8,128)S(1)} %get-tuple-element.55), channel_id=1, replica_groups={{0,64,128,192},{1,65,129,193},{2,66,130,194},{3,67,131,195},{4,68,132,1..., dimensions={0} | all-to-all | bytes 163840 | tf_op jit(solution)/shard_map/all_to_all | solution.py:606
  137.0 1.6 %shard_map.118 = f32[16,1024]{1,0:T(8,128)} custom-call(f32[4,40,128]{2,1,0:T(8,128)S(1)} %all_to_all.53.recv_ref, f32[7,256,128]{2,1,0:T(8,128)S(1)} %copy-done, f32[7,256,128]{2,1,0:T(8,128)S(1)} %copy-done.2, f32[8,2,128,128]{3,2,1,0:T(8,128)S(1)} %copy-done.1, bf16[2,4,128,128]{3,2,1,0:T(8,128)(2,1)S(1)} %get-tuple-element.49.top_gram_ref, ...), custom_call_target="tpu_custom_call" | custom-call | tf_op jit(solution)/shard_map/pallas_call | solution.py:570
  (15 shorter events, 0.0 us)
Async XLA Ops:
  0.0 18.4 %copy-start = (f32[7,256,128]{2,1,0:T(8,128)S(1)}, f32[7,256,128]{2,1,0:T(8,128)}, u32[]{:S(2)}) copy-start(f32[7,256,128]{2,1,0:T(8,128)} %up_row_ref.13) | copy-start | bytes 2752516
  0.0 1.3 copy-start.3
  1.3 1.0 copy-start.6
  2.3 0.9 copy-start.11
  3.2 0.7 copy-start.12
  3.9 51.8 %copy-start.5 = (f32[4,512,256]{2,1,0:T(8,128)S(1)}, f32[4,512,256]{2,1,0:T(8,128)}, u32[]{:S(2)}) copy-start(f32[4,512,256]{2,1,0:T(8,128)} %dense_ref.3) | copy-start | bytes 6291460
  18.4 37.3 %copy-start.1 = (f32[8,2,128,128]{3,2,1,0:T(8,128)S(1)}, f32[8,2,128,128]{3,2,1,0:T(8,128)}, u32[]{:S(2)}) copy-start(f32[8,2,128,128]{3,2,1,0:T(8,128)} %up_couple_ref.13) | copy-start | bytes 3145732
  18.4 37.3 %copy-start.2 = (f32[7,256,128]{2,1,0:T(8,128)S(1)}, f32[7,256,128]{2,1,0:T(8,128)}, u32[]{:S(2)}) copy-start(f32[7,256,128]{2,1,0:T(8,128)} %up_col_ref.13) | copy-start | bytes 2752516
  18.4 37.3 %copy-start.4 = (f32[4,512,128]{2,1,0:T(8,128)S(1)}, f32[4,512,128]{2,1,0:T(8,128)}, u32[]{:S(2)}) copy-start(f32[4,512,128]{2,1,0:T(8,128)} %row_basis_ref.5) | copy-start | bytes 3145732
  18.4 37.3 %copy-start.13 = (s32[4]{0:T(128)S(1)}, s32[4]{0:T(128)}, u32[]{:S(2)}) copy-start(s32[4]{0:T(128)} %rows_ref.5) | copy-start | bytes 52
  55.7 1.0 copy-start.7
  56.7 1.0 copy-start.8
  57.7 1.0 copy-start.9
  58.7 1.0 copy-start.10

commit v4 on v3

--- a/solution.py
+++ b/solution.py
@@ -14,13 +14,17 @@
 LEAF_COLS = 256
 PATH = 3
 LEVEL_BASE = (0, 8, 12)
-PACKED = 72
+HALF = RANK // 2
+SLICE = 8
+COST_FLOPS = 6000000000
+KEEP = LEAF_DEV * LEAF_ROWS
 TINY = 1.2e-38
 NEAR = 8
 MID = 8
 FAR = 4
 VMEM_MIB = 24
 VMEM_LIMIT = VMEM_MIB * 1024 * 1024
+START_LIMIT = 60 * 1024 * 1024
 
 f32 = jnp.float32
 bf16 = jnp.bfloat16
@@ -72,9 +76,12 @@
     ).astype(f32)
 
 
-def stat_block(first, second):
+def stat_block(*values):
     rows = lax.broadcasted_iota(jnp.int32, (8, RANK), 0)
-    return first * (rows == 0).astype(f32) + second * (rows == 1).astype(f32)
+    block = jnp.where(rows == 0, values[0], 0.0)
+    for k in range(1, len(values)):
+        block = jnp.where(rows == k, values[k], block)
+    return block
 
 
 def column_of(row):
@@ -179,7 +186,7 @@
     return slice(q * LEAF_COLS, (q + 1) * LEAF_COLS)
 
 
-def pair_up(parts, local, rows_ref, msg_ref, own_ref, inner_ref):
+def pair_up(parts, local, rows_ref, msg_ref, own_ref, inner_ref, extra):
     dense, row_basis, col_basis, local_row, local_col, coupling = local
     squares = sum_squares(parts[0])
     for part in parts[1:]:
@@ -202,8 +209,9 @@
     _, row_node = local_up(result, row_basis, local_row)
     row_root = local_root(row_node, local_row)
     stats = stat_block(row_of(squares), row_of(energy))
-    own_ref[...] = stats
-    send(msg_ref, stack([root, row_root, stats]))
+    if own_ref is not None:
+        own_ref[...] = stats
+    send(msg_ref, stack([root, row_root, stats] + extra))
 
 
 def both_sides(grams, half):
@@ -220,57 +228,91 @@
 
 
 def pack(gram):
-    half = RANK // 2
-    row = lax.broadcasted_iota(jnp.int32, (half, RANK), 0)
-    col = lax.broadcasted_iota(jnp.int32, (half, RANK), 1)
-    last = gram[half:]
-    top = jnp.where((col < half) & (col > row), pltpu.roll(last, half, 1), gram[:half])
-    diagonal = jnp.sum(jnp.where(col - half == row, last, 0.0), axis=0, keepdims=True)
-    first = (lax.broadcasted_iota(jnp.int32, (8, RANK), 0) == 0).astype(f32)
-    return stack([top, diagonal * first])
-
-
-def unpack(packed):
-    half = RANK // 2
-    row = lax.broadcasted_iota(jnp.int32, (half, RANK), 0)
-    col = lax.broadcasted_iota(jnp.int32, (half, RANK), 1)
-    top = packed[:half]
-    diagonal = packed[half : half + 1]
-    upper = jnp.where((col >= half) | (col < row), top, jnp.where(col == row, 0.5 * top, 0.0))
+    row = lax.broadcasted_iota(jnp.int32, (HALF, RANK), 0)
+    col = lax.broadcasted_iota(jnp.int32, (HALF, RANK), 1)
+    last = gram[HALF:]
+    top = jnp.where((col < HALF) & (col > row), pltpu.roll(last, HALF, 1), gram[:HALF])
+    diagonal = jnp.sum(jnp.where(col - HALF == row, last, 0.0), axis=0, keepdims=True)
+    return top, diagonal
+
+
+def unpack(top, diagonal):
+    row = lax.broadcasted_iota(jnp.int32, (HALF, RANK), 0)
+    col = lax.broadcasted_iota(jnp.int32, (HALF, RANK), 1)
+    upper = jnp.where((col >= HALF) | (col < row), top, jnp.where(col == row, 0.5 * top, 0.0))
     lower = jnp.where(
-        col - half > row,
-        pltpu.roll(top, half, 1),
-        jnp.where(col - half == row, 0.5 * diagonal, 0.0),
+        col - HALF > row,
+        pltpu.roll(top, HALF, 1),
+        jnp.where(col - HALF == row, 0.5 * diagonal, 0.0),
     )
     part = stack([upper, lower])
     return part + jnp.transpose(part)
 
 
+def store_pair(ref, index, value):
+    high, low = split(value)
+    ref[0, index] = high
+    ref[1, index] = low
+
+
+def group_grams(level, grams, up_row_ref, nodes_ref):
+    for height in range(PATH):
+        for k, value in enumerate(grams):
+            store_pair(nodes_ref, LEVEL_BASE[height] + k, value)
+        grams = gram_climb(grams, pair_at(up_row_ref, level + height))
+    return grams[0]
+
+
+def start_copies(pairs, sems):
+    copies = [
+        pltpu.make_async_copy(source, target, sems.at[k])
+        for k, (source, target) in enumerate(pairs)
+    ]
+    for copy in copies:
+        copy.start()
+    return copies
+
+
 def start_kernel(
-    me_ref, rows_ref, rhs_ref, row_basis_ref, local_row_ref, z_ref, msg_ref, keep_ref
+    me_ref,
+    rows_hbm,
+    rhs_hbm,
+    row_basis_hbm,
+    local_row_hbm,
+    z_ref,
+    msg_ref,
+    rows_ref,
+    rhs_ref,
+    row_basis_ref,
+    local_row_ref,
+    sems,
 ):
-    row_basis = [split(row_basis_ref[q]) for q in range(LEAF_DEV)]
+    pairs = [(rows_hbm, rows_ref), (rhs_hbm, rhs_ref)]
+    pairs += [(row_basis_hbm, row_basis_ref), (local_row_hbm, local_row_ref)]
+    for copy in start_copies(pairs, sems):
+        copy.wait()
+    squares = jnp.zeros((RHS, 1), f32)
     local_row = [split(local_row_ref[m]) for m in range(3)]
-    parts = []
-    squares = jnp.zeros((RHS, 1), f32)
+    leaf = []
+    grams = []
     for q in range(LEAF_DEV):
         part = rhs_ref[:, row_part(q)] * live_mask(rows_ref, q)
         z_ref[:, row_part(q)] = part
         squares = squares + sum_squares(part)
-        parts.append(part)
-    leaf, node = local_up(parts, row_basis.__getitem__, local_row.__getitem__)
-    for k, value in enumerate(leaf + node):
-        keep_ref[k] = value
-    root = local_root(node, local_row.__getitem__)
-    row = row_of(squares)
-    grams = []
+        leaf.append(mm(part, split(row_basis_ref[q])))
     for q in range(LEAF_DEV):
         slots = lax.broadcasted_iota(jnp.int32, (LEAF_ROWS, RANK), 0)
         basis = jnp.where(slots < rows_ref[q], row_basis_ref[q], 0.0)
         grams.append(mm_inner(basis, basis))
+    node = [climb(leaf[2 * m : 2 * m + 2], local_row[m])[0] for m in range(2)]
+    for k, value in enumerate(leaf + node):
+        z_ref[:, KEEP + k * RANK : KEEP + (k + 1) * RANK] = value
+    root = climb(node, local_row[2])[0]
+    row = row_of(squares)
     nodes = [gram_climb(grams[2 * m : 2 * m + 2], local_row[m])[0] for m in range(2)]
     gram = gram_climb(nodes, local_row[2])[0]
-    send(msg_ref, stack([root, stat_block(row, row), pack(gram)]))
+    top, diagonal = pack(gram)
+    send(msg_ref, stack([root, stat_block(row, row, diagonal), top]))
 
 
 def sum_stats(recv_ref):
@@ -280,24 +322,100 @@
     return stats
 
 
-def lower_kernel(level, me_ref, recv_ref, climb_ref, msg_ref, sib_ref, nodes_ref, scratch_ref):
+def climb_group(level, me_ref, recv_ref, climb_ref, sib_ref, scratch_ref):
     place = (me_ref[0] >> level) % NEAR
-    peers = range(recv_ref.shape[0])
-    summaries = [recv_ref[d, :RHS] for d in peers]
-    grams = [unpack(recv_ref[d, RHS + 8 :]) for d in peers]
+    summaries = [recv_ref[d, :RHS] for d in range(recv_ref.shape[0])]
     for height in range(PATH):
         base = LEVEL_BASE[height]
         for m, value in enumerate(summaries):
             scratch_ref[base + m] = value
         sib_ref[height] = scratch_ref[base + ((place >> height) ^ 1)]
-        for k, value in enumerate(grams):
-            high, low = split(value)
-            nodes_ref[0, base + k] = high
-            nodes_ref[1, base + k] = low
-        transfer = pair_at(climb_ref, level + height)
-        summaries = climb(summaries, transfer)
-        grams = gram_climb(grams, transfer)
-    send(msg_ref, stack([summaries[0], sum_stats(recv_ref), pack(grams[0])]))
+        summaries = climb(summaries, pair_at(climb_ref, level + height))
+    return summaries[0]
+
+
+def path_product(me, level, path, up_col_ref):
+    half = half_of(up_col_ref, level, (me >> level) & 1)
+    return mm(path, half)
+
+
+def sibling_gain(me, level, path, up_couple_ref):
+    child = 1 - ((me >> level) & 1)
+    return mm(path, pair_at(up_couple_ref, level, child))
+
+
+def near_kernel(
+    me_ref,
+    recv_ref,
+    up_row_ref,
+    up_col_ref,
+    up_couple_ref,
+    msg_ref,
+    sib_ref,
+    nodes_ref,
+    gain_ref,
+    path_ref,
+    scratch_ref,
+    slice_ref,
+):
+    me = me_ref[0]
+    summary = climb_group(0, me_ref, recv_ref, up_row_ref, sib_ref, scratch_ref)
+    base = RHS + 8
+    grams = [unpack(recv_ref[d, base:], recv_ref[d, RHS + 2 : RHS + 3]) for d in range(NEAR)]
+    gram = group_grams(0, grams, up_row_ref, nodes_ref)
+    child = 1 - (me & 1)
+    first = up_couple_ref[0, child]
+    store_pair(gain_ref, 0, first)
+    path = up_col_ref[0, pl.ds(pl.multiple_of((me & 1) * RANK, RANK), RANK), :]
+    for j in range(1, PATH):
+        store_pair(gain_ref, j, sibling_gain(me, j, path, up_couple_ref))
+        path = path_product(me, j, path, up_col_ref)
+    path_ref[...] = path
+    top, diagonal = pack(gram)
+    slice_ref[...] = top
+    part = slice_ref[pl.ds(pl.multiple_of((me % NEAR) * SLICE, SLICE), SLICE), :]
+    stats = sum_stats(recv_ref)
+    send(msg_ref, stack([summary, stat_block(stats[:1], stats[1:2], diagonal), part]))
+
+
+def mid_kernel(
+    me_ref,
+    recv_ref,
+    up_row_ref,
+    up_col_ref,
+    up_couple_ref,
+    path_ref,
+    msg_ref,
+    sib_ref,
+    gain_ref,
+    part_ref,
+    diagonal_ref,
+    scratch_ref,
+):
+    me = me_ref[0]
+    summary = climb_group(PATH, me_ref, recv_ref, up_row_ref, sib_ref, scratch_ref)
+    path = path_ref[...]
+    for j in range(PATH, 8):
+        store_pair(gain_ref, j - PATH, sibling_gain(me, j, path, up_couple_ref))
+        if j < 7:
+            path = path_product(me, j, path, up_col_ref)
+    for d in range(MID):
+        part_ref[d * SLICE : (d + 1) * SLICE] = recv_ref[d, RHS + 8 :]
+        diagonal_ref[d : d + 1] = recv_ref[d, RHS + 2 : RHS + 3]
+    send(msg_ref, stack([summary, sum_stats(recv_ref)]))
+
+
+def from_siblings(siblings, near_gain_ref, mid_gain_ref):
+    gains = [pair_at(near_gain_ref, j) for j in range(PATH)]
+    gains += [pair_at(mid_gain_ref, j) for j in range(8 - PATH)]
+    gains = tuple(jnp.concatenate([g[k] for g in gains], 1) for k in range(2))
+    return mm(jnp.concatenate(siblings, 1), gains, transposed=True)
+
+
+def gather_far(me, parts, out_ref):
+    place = me >> (2 * PATH)
+    for k, part in enumerate(parts):
+        out_ref[place ^ k] = part[0]
 
 
 def readers(local):
@@ -307,13 +425,16 @@
 def first_kernel(
     me_ref,
     rows_ref,
-    recv_ref,
+    part0_ref,
+    part1_ref,
+    part2_ref,
+    part3_ref,
     near_ref,
     mid_ref,
+    near_gain_ref,
+    mid_gain_ref,
+    part_ref,
     up_row_ref,
-    up_col_ref,
-    up_couple_ref,
-    keep_ref,
     dense_ref,
     row_basis_ref,
     col_basis_ref,
@@ -326,10 +447,11 @@
     msg_ref,
     own_ref,
     inner_ref,
-    nodes_ref,
     scratch_ref,
+    recv_ref,
 ):
     me = me_ref[0]
+    gather_far(me, (part0_ref, part1_ref, part2_ref, part3_ref), recv_ref)
     place = me >> (2 * PATH)
     summaries = [recv_ref[d, :RHS] for d in range(FAR)]
     siblings = [near_ref[j] for j in range(PATH)] + [mid_ref[j] for j in range(PATH)]
@@ -338,26 +460,16 @@
     for m, value in enumerate(summaries):
         scratch_ref[m] = value
     siblings.append(scratch_ref[(place >> 1) ^ 1])
-    potential = None
-    for j in reversed(range(8)):
-        child = (me >> j) & 1
-        gained = mm(siblings[j], pair_at(up_couple_ref, j, 1 - child), transposed=True)
-        if potential is not None:
-            gained = gained + mm(potential, half_of(up_col_ref, j, child), transposed=True)
-        potential = gained
+    potential = from_siblings(siblings, near_gain_ref, mid_gain_ref)
     beta = jnp.sqrt(column_of(sum_stats(recv_ref)[:1]))
-    for d in range(FAR):
-        high, low = split(unpack(recv_ref[d, RHS + 8 :]))
-        nodes_ref[0, d] = high
-        nodes_ref[1, d] = low
     inverse = 1.0 / beta
     beta_ref[...] = jnp.broadcast_to(beta, (RHS, RANK))
     local = readers(
         (dense_ref, row_basis_ref, col_basis_ref, local_row_ref, local_col_ref, local_couple_ref)
     )
     dense, _, col_basis, _, local_col, coupling = local
-    leaf = [keep_ref[q] for q in range(LEAF_DEV)]
-    node = [keep_ref[LEAF_DEV + m] for m in range(2)]
+    keep = [z_ref[:, KEEP + k * RANK : KEEP + (k + 1) * RANK] for k in range(LEAF_DEV + 2)]
+    leaf, node = keep[:LEAF_DEV], keep[LEAF_DEV:]
     down = local_down(potential, leaf, node, coupling, local_col, True)
     parts = []
     for q in range(LEAF_DEV):
@@ -365,7 +477,7 @@
         x = (x + mm(down[q], col_basis(q), transposed=True)) * inverse
         x_ref[:, col_part(q)] = x
         parts.append(x)
-    pair_up(parts, local, rows_ref, msg_ref, own_ref, inner_ref)
+    pair_up(parts, local, rows_ref, msg_ref, own_ref, inner_ref, [part_ref[...]])
 
 
 def rescale(recv_ref):
@@ -384,20 +496,7 @@
     return first, second, factor, total, energy
 
 
-def lower_pair_kernel(
-    level,
-    me_ref,
-    recv_ref,
-    up_row_ref,
-    up_col_ref,
-    up_couple_ref,
-    nodes_ref,
-    msg_ref,
-    path_ref,
-    own_ref,
-    gain_ref,
-    below_ref,
-):
+def pair_group(level, me_ref, recv_ref, up_row_ref, up_col_ref, up_couple_ref, nodes_ref, keep):
     place = (me_ref[0] >> level) % NEAR
     first, second, _, total, energy = rescale(recv_ref)
     cross = jnp.zeros((RHS, RANK), f32)
@@ -410,19 +509,83 @@
             moved = mm(gained[k], pair_at(nodes_ref, base + k))
             cross = cross + gained[k] * (2.0 * second[k] + moved)
             summed.append(second[k] + moved)
-            gain_ref[base + k] = gained[k]
-            below_ref[base + k] = second[k]
-        own = base + (place >> height)
-        other = base + ((place >> height) ^ 1)
-        path_ref[3 * height] = gain_ref[own]
-        path_ref[3 * height + 1] = gain_ref[other]
-        path_ref[3 * height + 2] = below_ref[other]
+        if keep is not None:
+            path_ref, gain_ref, below_ref = keep
+            for k in range(len(first)):
+                gain_ref[base + k] = gained[k]
+                below_ref[base + k] = second[k]
+            own = base + (place >> height)
+            other = base + ((place >> height) ^ 1)
+            path_ref[3 * height] = gain_ref[own]
+            path_ref[3 * height + 1] = gain_ref[other]
+            path_ref[3 * height + 2] = below_ref[other]
         first = climb(first, pair_at(up_col_ref, j))
         second = climb(summed, pair_at(up_row_ref, j))
     energy = energy + row_of(jnp.sum(cross, axis=1, keepdims=True))
-    stats = stat_block(total, energy)
+    return first[0], second[0], stat_block(total, energy)
+
+
+def near_pair_kernel(
+    me_ref,
+    recv_ref,
+    up_row_ref,
+    up_col_ref,
+    up_couple_ref,
+    nodes_ref,
+    diagonal_ref,
+    msg_ref,
+    path_ref,
+    own_ref,
+    mid_nodes_ref,
+    gram_ref,
+    gain_ref,
+    below_ref,
+):
+    keep = (path_ref, gain_ref, below_ref)
+    first, second, stats = pair_group(
+        0, me_ref, recv_ref, up_row_ref, up_col_ref, up_couple_ref, nodes_ref, keep
+    )
     own_ref[...] = stats
-    send(msg_ref, stack([first[0], second[0], stats]))
+    send(msg_ref, stack([first, second, stats]))
+    base = 2 * RHS + 8
+    grams = []
+    for d in range(MID):
+        low = base + d * SLICE
+        top = stack([recv_ref[p, low : low + SLICE] for p in range(NEAR)])
+        grams.append(unpack(top, diagonal_ref[d : d + 1]))
+    top, diagonal = pack(group_grams(PATH, grams, up_row_ref, mid_nodes_ref))
+    gram_ref[...] = stack([top, stat_block(diagonal)])
+
+
+def mid_pair_kernel(
+    me_ref,
+    recv_ref,
+    up_row_ref,
+    up_col_ref,
+    up_couple_ref,
+    nodes_ref,
+    gram_ref,
+    msg_ref,
+    path_ref,
+    own_ref,
+    gain_ref,
+    below_ref,
+):
+    keep = (path_ref, gain_ref, below_ref)
+    first, second, stats = pair_group(
+        PATH, me_ref, recv_ref, up_row_ref, up_col_ref, up_couple_ref, nodes_ref, keep
+    )
+    own_ref[...] = stats
+    send(msg_ref, stack([first, second, stats, gram_ref[...]]))
+
+
+def last_pair_kernel(
+    level, me_ref, recv_ref, up_row_ref, up_col_ref, up_couple_ref, nodes_ref, msg_ref
+):
+    parts = pair_group(
+        level, me_ref, recv_ref, up_row_ref, up_col_ref, up_couple_ref, nodes_ref, None
+    )
+    send(msg_ref, stack(parts))
 
 
 def top_levels(recv_ref, up_row_ref, up_col_ref, up_couple_ref, gram_ref):
@@ -445,15 +608,19 @@
 def middle_kernel(
     me_ref,
     rows_ref,
-    recv_ref,
+    part0_ref,
+    part1_ref,
+    part2_ref,
+    part3_ref,
     near_path_ref,
     near_own_ref,
     mid_path_ref,
     mid_own_ref,
+    near_gain_ref,
+    mid_gain_ref,
     up_row_ref,
     up_col_ref,
     up_couple_ref,
-    top_gram_ref,
     near_nodes_ref,
     mid_nodes_ref,
     dense_ref,
@@ -470,12 +637,18 @@
     alpha_ref,
     rho_ref,
     msg_ref,
-    own_ref,
+    top_gram_ref,
     a_ref,
     b_ref,
+    recv_ref,
 ):
     me = me_ref[0]
+    gather_far(me, (part0_ref, part1_ref, part2_ref, part3_ref), recv_ref)
     place = me >> (2 * PATH)
+    base = 2 * RHS + 8
+    for d in range(FAR):
+        gram = unpack(recv_ref[d, base : base + HALF], recv_ref[d, base + HALF : base + HALF + 1])
+        store_pair(top_gram_ref, d, gram)
     potential, summed, squares, energy = top_levels(
         recv_ref, up_row_ref, up_col_ref, up_couple_ref, top_gram_ref
     )
@@ -508,13 +681,7 @@
             other = path_ref[3 * height + 1] * factor + jnp.where(child == 0, high, low)
             gram = pair_at(nodes_ref, LEVEL_BASE[height] + ((inside >> height) ^ 1))
             siblings[j] = path_ref[3 * height + 2] * factor + mm(other, gram)
-    backward = None
-    for j in reversed(range(8)):
-        child = (me >> j) & 1
-        gained = mm(siblings[j], pair_at(up_couple_ref, j, 1 - child), transposed=True)
-        if backward is not None:
-            gained = gained + mm(backward, half_of(up_col_ref, j, child), transposed=True)
-        backward = gained
+    backward = from_siblings([siblings[j] for j in range(8)], near_gain_ref, mid_gain_ref)
     local = readers(
         (dense_ref, row_basis_ref, col_basis_ref, local_row_ref, local_col_ref, local_couple_ref)
     )
@@ -536,11 +703,15 @@
         x = x * inverse - rho * v
         next_ref[:, col_part(q)] = x
         parts.append(x)
-    pair_up(parts, local, rows_ref, msg_ref, own_ref, None)
+    pair_up(parts, local, rows_ref, msg_ref, None, None, [])
 
 
 def final_kernel(
-    recv_ref,
+    me_ref,
+    part0_ref,
+    part1_ref,
+    part2_ref,
+    part3_ref,
     up_row_ref,
     up_col_ref,
     up_couple_ref,
@@ -551,7 +722,9 @@
     v_ref,
     x_ref,
     out_ref,
+    recv_ref,
 ):
+    gather_far(me_ref[0], (part0_ref, part1_ref, part2_ref, part3_ref), recv_ref)
     _, _, squares, energy = top_levels(
         recv_ref, up_row_ref, up_col_ref, up_couple_ref, top_gram_ref
     )
@@ -564,16 +737,22 @@
     out_ref[...] = (phi / rho) * v - (phi * (theta / rho2) / rho2) * search
 
 
-def call(kernel, outs, operands, scratch=()):
-    spaces = [pltpu.SMEM if k.dtype == jnp.int32 else pltpu.VMEM for k in operands]
+def call(kernel, outs, operands, scratch=(), far=(), limit=VMEM_LIMIT):
+    spaces = []
+    for index, operand in enumerate(operands):
+        space = pltpu.SMEM if operand.dtype == jnp.int32 else pltpu.VMEM
+        spaces.append(pl.ANY if index in far else space)
     outs = [shape if isinstance(shape, jax.ShapeDtypeStruct) else jax.ShapeDtypeStruct(shape, f32) for shape in outs]
     return pl.pallas_call(
         kernel,
         out_shape=outs,
         in_specs=[pl.BlockSpec(memory_space=space) for space in spaces],
         out_specs=[pl.BlockSpec(memory_space=pltpu.VMEM)] * len(outs),
-        scratch_shapes=[pltpu.VMEM(shape, f32) for shape in scratch],
-        compiler_params=pltpu.CompilerParams(vmem_limit_bytes=VMEM_LIMIT),
+        scratch_shapes=[
+            pltpu.VMEM(shape, f32) if isinstance(shape, tuple) else shape for shape in scratch
+        ],
+        compiler_params=pltpu.CompilerParams(vmem_limit_bytes=limit),
+        cost_estimate=pl.CostEstimate(flops=COST_FLOPS, bytes_accessed=0, transcendentals=0),
     )(*operands)
 
 
@@ -600,7 +779,14 @@
     up_couple,
 ):
     me = lax.axis_index("leaf").astype(jnp.int32).reshape(1)
-    near, mid, far = (1, NEAR), (NEAR, MID), (NEAR * MID, FAR)
+    near, mid = (1, NEAR), (NEAR, MID)
+
+    def swap_far(message):
+        parts = [message]
+        for k in range(1, FAR):
+            pairs = [(i, i ^ (k * NEAR * MID)) for i in range(devices)]
+            parts.append(lax.ppermute(message, "leaf", pairs))
+        return parts
 
     def swap(message, group):
         return lax.all_to_all(message, "leaf", 0, 0, axis_index_groups=device_groups(devices, *group))
@@ -608,64 +794,97 @@
     tile = (RHS, RANK)
     row_shape = (RHS, LEAF_DEV * LEAF_ROWS)
     col_shape = (RHS, LEAF_DEV * LEAF_COLS)
-    single = (RHS + 8 + PACKED, RANK)
+    single = (RHS + 8, RANK)
     double = (2 * RHS + 8, RANK)
+
+    def longer(shape, rows):
+        return (shape[0] + rows, shape[1])
+
     stat = (8, RANK)
     gram_shape = (RANK, RANK)
     tables = [up_row, up_col, up_couple]
-    blocks = [dense, row_basis, col_basis, local_row, local_col, local_couple]
 
     def nodes_shape(count):
         return jax.ShapeDtypeStruct((2, count) + gram_shape, bf16)
 
-    def lower(level, message, peers):
+    path_shape = (3 * PATH,) + tile
+    pair_scratch = [(14,) + tile, (14,) + tile]
+
+    def last_pair(level, message, peers, nodes):
         return call(
-            functools.partial(lower_kernel, level),
-            [(peers,) + single, (PATH,) + tile, nodes_shape(14)],
-            [me, message, up_row],
-            [(14,) + tile],
-        )
-
-    def lower_pair(level, message, peers, nodes):
-        return call(
-            functools.partial(lower_pair_kernel, level),
-            [(peers,) + double, (3 * PATH,) + tile, stat],
+            functools.partial(last_pair_kernel, level),
+            [(peers,) + double],
             [me, message] + tables + [nodes],
-            [(14,) + tile, (14,) + tile],
-        )
-
-    z, message, keep = call(
+        )[0]
+
+    z, message = call(
         start_kernel,
-        [row_shape, (NEAR,) + single, (6,) + tile],
+        [(RHS, KEEP + 6 * RANK), (NEAR,) + longer(single, HALF)],
         [me, box_rows, rhs, row_basis, local_row],
-    )
-    message, near_sib, near_nodes = lower(0, swap(message, near), MID)
-    message, mid_sib, mid_nodes = lower(PATH, swap(message, mid), FAR)
-    received = swap(message, far)
-    x, beta, message, own, inner, top_nodes = call(
+        [pltpu.SMEM(box_rows.shape, jnp.int32)]
+        + [k.shape for k in (rhs, row_basis, local_row)]
+        + [pltpu.SemaphoreType.DMA((4,))],
+        range(1, 5),
+        START_LIMIT,
+    )
+    blocks = [dense, row_basis, col_basis, local_row, local_col, local_couple]
+    message, near_sib, near_nodes, near_gain, path = call(
+        near_kernel,
+        [(MID,) + longer(single, SLICE), (PATH,) + tile, nodes_shape(14), nodes_shape(PATH), gram_shape],
+        [me, swap(message, near)] + tables,
+        [(14,) + tile, (HALF, RANK)],
+    )
+    message, mid_sib, mid_gain, part, diagonal = call(
+        mid_kernel,
+        [(1,) + single, (PATH,) + tile, nodes_shape(8 - PATH), (HALF, RANK), stat],
+        [me, swap(message, mid)] + tables + [path],
+        [(14,) + tile],
+    )
+    gains = [near_gain, mid_gain]
+    x, beta, message, own, inner = call(
         first_kernel,
-        [col_shape, tile, (NEAR,) + double, stat, row_shape, nodes_shape(FAR)],
-        [me, box_rows, received, near_sib, mid_sib] + tables + [keep] + blocks + [z],
-        [(2,) + tile],
-    )
-    message, near_path, near_own = lower_pair(0, swap(message, near), MID, near_nodes)
-    message, mid_path, mid_own = lower_pair(PATH, swap(message, mid), FAR, mid_nodes)
-    received = swap(message, far)
-    v, x, alpha, rho, message, _ = call(
+        [col_shape, tile, (NEAR,) + longer(double, HALF), stat, row_shape],
+        [me, box_rows]
+        + swap_far(message)
+        + [near_sib, mid_sib]
+        + gains
+        + [part, up_row]
+        + blocks
+        + [z],
+        [(2,) + tile, (FAR,) + single],
+    )
+    message, near_path, near_own, mid_nodes, gram = call(
+        near_pair_kernel,
+        [(MID,) + double, path_shape, stat, nodes_shape(14), (HALF + 8, RANK)],
+        [me, swap(message, near)] + tables + [near_nodes, diagonal],
+        pair_scratch,
+    )
+    message, mid_path, mid_own = call(
+        mid_pair_kernel,
+        [(1,) + longer(double, HALF + 8), path_shape, stat],
+        [me, swap(message, mid)] + tables + [mid_nodes, gram],
+        pair_scratch,
+    )
+    v, x, alpha, rho, message, top_nodes = call(
         middle_kernel,
-        [col_shape, col_shape, tile, tile, (NEAR,) + double, stat],
-        [me, box_rows, received, near_path, near_own, mid_path, mid_own]
+        [col_shape, col_shape, tile, tile, (NEAR,) + double, nodes_shape(FAR)],
+        [me, box_rows]
+        + swap_far(message)
+        + [near_path, near_own, mid_path, mid_own]
+        + gains
         + tables
-        + [top_nodes, near_nodes, mid_nodes]
+        + [near_nodes, mid_nodes]
         + blocks
         + [x, own, inner],
-        [(6,) + tile, (4,) + tile],
-    )
-    message, _, _ = lower_pair(0, swap(message, near), MID, near_nodes)
-    message, _, _ = lower_pair(PATH, swap(message, mid), FAR, mid_nodes)
-    received = swap(message, far)
+        [(6,) + tile, (4,) + tile, (FAR,) + longer(double, HALF + 8)],
+    )
+    message = last_pair(0, swap(message, near), MID, near_nodes)
+    message = last_pair(PATH, swap(message, mid), 1, mid_nodes)
     (out,) = call(
-        final_kernel, [col_shape], [received] + tables + [top_nodes, beta, alpha, rho, v, x]
+        final_kernel,
+        [col_shape],
+        [me] + swap_far(message) + tables + [top_nodes, beta, alpha, rho, v, x],
+        [(FAR,) + double],
     )
     return out
 

time: 139 us -> 124 us (0.89)
  blocking collectives: 104 us -> 74.3 us
  starting transfers between devices: 0 us -> 12.5 us
  waiting for transfers between devices: 0 us -> 10.1 us
  local copies, waits for them, and re-layouts: 7.91 us -> 0.05 us
    all_to_all x9 -> x6, blocking collectives: 104 us -> 74.3 us  [swap(): lax.all_to_all(message, 'leaf', 0, 0, axis_index_groups=device_groups(dev...]
    ppermute x0 -> x9, starting transfers between devices: none -> 12.5 us  [swap_far(): parts.append(lax.ppermute(message, 'leaf', pairs))]
    ppermute x0 -> x9, waiting for transfers between devices: none -> 10.1 us  [swap_far(): parts.append(lax.ppermute(message, 'leaf', pairs))]
    unnamed x28 -> x22, local copies, waits for them, and re-layouts: 7.91 us -> 0.05 us
  transfers between devices with their start and end apart: 0 -> 9, of which waited for: 0 -> 6; matrix products, arithmetic and copies ran while one was open for 0% -> 0% of each run, Pallas kernels for 0% -> 0%
where the time goes in v4:
time: 124 us
  blocking collectives  74.3 us (60%)
  Pallas kernels  26.6 us (21%)
  starting transfers between devices  12.5 us (10%)
  waiting for transfers between devices  10.1 us (8%)
    all_to_all x6, blocking collectives, swap(): lax.all_to_all(message, 'leaf', 0, 0, axis_index_groups=device_groups(dev...  74.3 us
    pallas_call x10, Pallas kernels, call(): pl.pallas_call(kernel, out_shape=outs, in_specs=[pl.BlockSpec(memory_spac...  26.6 us
    ppermute x9, starting transfers between devices, swap_far(): parts.append(lax.ppermute(message, 'leaf', pairs))  12.5 us
    ppermute x9, waiting for transfers between devices, swap_far(): parts.append(lax.ppermute(message, 'leaf', pairs))  10.1 us
  transfers between devices with their start and end apart: 9, of which 6 were waited for; matrix products, arithmetic and copies ran while one was open for 0% of the time, Pallas kernels for 0%

profile of v4, /device:TPU:2, one launch (start us, length us, event | category | flops | bytes accessed | tf_op | source)
XLA Modules:
  0.0 123.7 jit_solution(5179963967458814165)
XLA Ops:
  0.0 4.1 %shard_map.109 = (f32[16,2816]{1,0:T(8,128)}, f32[8,88,128]{2,1,0:T(8,128)}) custom-call(s32[1]{0:T(128)} %bitcast.me_ref, s32[4]{0:T(128)} %rows_ref.3, f32[16,2048]{1,0:T(8,128)} %rhs_hbm.1, f32[4,512,128]{2,1,0:T(8,128)} %row_basis_ref.3, f32[3,256,128]{2,1,0:T(8,128)} %local_row_ref.3), custom_call_target="tpu_custom_call" | custom-call | flops 6000000000 | tf_op jit(solution)/shard_map/pallas_call | solution.py:746
  4.1 12.8 %all_to_all.30.recv_ref = f32[8,88,128]{2,1,0:T(8,128)S(1)} all-to-all(f32[8,88,128]{2,1,0:T(8,128)} %get-tuple-element.36), channel_id=1, replica_groups={{0,1,2,3,4,5,6,7},{8,9,10,11,12,13,14,15},{16,17,18,19,20,21,22,23},{24..., dimensions={0} | all-to-all | bytes 720896 | tf_op jit(solution)/shard_map/all_to_all | solution.py:792
  16.9 2.2 %shard_map.110 = (f32[8,32,128]{2,1,0:T(8,128)S(1)}, f32[3,16,128]{2,1,0:T(8,128)S(1)}, bf16[2,14,128,128]{3,2,1,0:T(8,128)(2,1)S(1)}, bf16[2,3,128,128]{3,2,1,0:T(8,128)(2,1)S(1)}, f32[128,128]{1,0:T(8,128)S(1)}) custom-call(s32[1]{0:T(128)} %bitcast.me_ref, f32[8,88,128]{2,1,0:T(8,128)S(1)} %all_to_all.30.recv_ref, f32[7,256,128]{2,1,0:T(8,128)S(1)} %copy-done.3, ...), custom_call_target="tpu_custom_call" | custom-call | flops 6000000000 | tf_op jit(solution)/shard_map/pallas_call | solution.py:746
  19.1 16.6 %all_to_all.31.recv_ref = f32[8,32,128]{2,1,0:T(8,128)S(1)} all-to-all(f32[8,32,128]{2,1,0:T(8,128)S(1)} %get-tuple-element.37), channel_id=1, replica_groups={{0,8,16,24,32,40,48,56},{1,9,17,25,33,41,49,57},{2,10,18,26,34,42,50,58..., dimensions={0} | all-to-all | bytes 262144 | tf_op jit(solution)/shard_map/all_to_all | solution.py:792
  35.6 0.0 copy-start.7
  35.7 1.2 shard_map.111
  36.9 3.1 %collective-permute-start.2 = (f32[1,24,128]{2,1,0:T(8,128)S(1)}, f32[1,24,128]{2,1,0:T(8,128)S(1)}, u32[]{:S(2)}, u32[]{:S(2)}) collective-permute-start(f32[1,24,128]{2,1,0:T(8,128)S(1)} %get-tuple-element.39.part0_ref), channel_id=1, source_target_pairs={{0,192},{1,193},{2,194},{3,195},{4,196},{5,197},{6,198},{7,199},{8... | collective-permute-start | bytes 36872 | tf_op jit(solution)/shard_map/ppermute | solution.py:788
  40.0 0.6 collective-permute-start.1
  40.6 0.5 collective-permute-start
  41.0 0.8 collective-permute-done.2.part3_ref
  41.9 3.3 %collective-permute-done.1.part2_ref = f32[1,24,128]{2,1,0:T(8,128)S(1)} collective-permute-done((f32[1,24,128]{2,1,0:T(8,128)S(1)}, f32[1,24,128]{2,1,0:T(8,128)S(1)}, u32[]{:S(2)}, u32[]{:S(2)}) %collective-permute-start.1) | collective-permute-done | bytes 12320 | tf_op jit(solution)/shard_map/ppermute | solution.py:788
  45.2 4.2 %shard_map.112 = (f32[16,1024]{1,0:T(8,128)S(1)}, f32[16,128]{1,0:T(8,128)S(1)}, f32[8,104,128]{2,1,0:T(8,128)S(1)}, f32[8,128]{1,0:T(8,128)S(1)}, f32[16,2048]{1,0:T(8,128)S(1)}) custom-call(s32[1]{0:T(128)} %bitcast.me_ref, s32[4]{0:T(128)S(1)} %copy-done.9, f32[1,24,128]{2,1,0:T(8,128)S(1)} %get-tuple-element.39.part0_ref, ...), custom_call_target="tpu_custom_call" | custom-call | flops 6000000000 | tf_op jit(solution)/shard_map/pallas_call | solution.py:746
  49.4 11.7 %all_to_all.32.recv_ref = f32[8,104,128]{2,1,0:T(8,128)S(1)} all-to-all(f32[8,104,128]{2,1,0:T(8,128)S(1)} %get-tuple-element.46), channel_id=1, replica_groups={{0,1,2,3,4,5,6,7},{8,9,10,11,12,13,14,15},{16,17,18,19,20,21,22,23},{24..., dimensions={0} | all-to-all | bytes 851968 | tf_op jit(solution)/shard_map/all_to_all | solution.py:792
  61.1 2.9 %shard_map.113 = (f32[8,40,128]{2,1,0:T(8,128)S(1)}, f32[9,16,128]{2,1,0:T(8,128)S(1)}, f32[8,128]{1,0:T(8,128)S(1)}, bf16[2,14,128,128]{3,2,1,0:T(8,128)(2,1)S(1)}, f32[72,128]{1,0:T(8,128)S(1)}) custom-call(s32[1]{0:T(128)} %bitcast.me_ref, f32[8,104,128]{2,1,0:T(8,128)S(1)} %all_to_all.32.recv_ref, f32[7,256,128]{2,1,0:T(8,128)S(1)} %copy-done.3, ...), custom_call_target="tpu_custom_call" | custom-call | flops 6000000000 | tf_op jit(solution)/shard_map/pallas_call | solution.py:746
  64.0 12.2 %all_to_all.33.recv_ref = f32[8,40,128]{2,1,0:T(8,128)S(1)} all-to-all(f32[8,40,128]{2,1,0:T(8,128)S(1)} %get-tuple-element.49), channel_id=1, replica_groups={{0,8,16,24,32,40,48,56},{1,9,17,25,33,41,49,57},{2,10,18,26,34,42,50,58..., dimensions={0} | all-to-all | bytes 327680 | tf_op jit(solution)/shard_map/all_to_all | solution.py:792
  76.2 1.3 %shard_map.114 = (f32[1,112,128]{2,1,0:T(8,128)S(1)}, f32[9,16,128]{2,1,0:T(8,128)S(1)}, f32[8,128]{1,0:T(8,128)S(1)}) custom-call(s32[1]{0:T(128)} %bitcast.me_ref, f32[8,40,128]{2,1,0:T(8,128)S(1)} %all_to_all.33.recv_ref, f32[7,256,128]{2,1,0:T(8,128)S(1)} %copy-done.3, f32[7,256,128]{2,1,0:T(8,128)S(1)} %copy-done.4, f32[8,2,128,128]{3,2,1,0:T(8,128)S(1)} %copy-done.2, ...), custom_call_target="tpu_custom_call" | custom-call | flops 6000000000 | tf_op jit(solution)/shard_map/pallas_call | solution.py:746
  77.5 1.4 %collective-permute-start.5 = (f32[1,112,128]{2,1,0:T(8,128)S(1)}, f32[1,112,128]{2,1,0:T(8,128)S(1)}, u32[]{:S(2)}, u32[]{:S(2)}) collective-permute-start(f32[1,112,128]{2,1,0:T(8,128)S(1)} %get-tuple-element.52.part0_ref), channel_id=1, source_target_pairs={{0,192},{1,193},{2,194},{3,195},{4,196},{5,197},{6,198},{7,199},{8... | collective-permute-start | bytes 172040 | tf_op jit(solution)/shard_map/ppermute | solution.py:788
  78.8 0.9 collective-permute-start.4
  79.7 1.9 %collective-permute-start.3 = (f32[1,112,128]{2,1,0:T(8,128)S(1)}, f32[1,112,128]{2,1,0:T(8,128)S(1)}, u32[]{:S(2)}, u32[]{:S(2)}) collective-permute-start(f32[1,112,128]{2,1,0:T(8,128)S(1)} %get-tuple-element.52.part0_ref), channel_id=1, source_target_pairs={{0,64},{1,65},{2,66},{3,67},{4,68},{5,69},{6,70},{7,71},{8,72},{9,... | collective-permute-start | bytes 172040 | tf_op jit(solution)/shard_map/ppermute | solution.py:788
  81.6 1.3 %collective-permute-done.5.part3_ref = f32[1,112,128]{2,1,0:T(8,128)S(1)} collective-permute-done((f32[1,112,128]{2,1,0:T(8,128)S(1)}, f32[1,112,128]{2,1,0:T(8,128)S(1)}, u32[]{:S(2)}, u32[]{:S(2)}) %collective-permute-start.5) | collective-permute-done | bytes 57376 | tf_op jit(solution)/shard_map/ppermute | solution.py:788
  82.9 1.6 %collective-permute-done.4.part2_ref = f32[1,112,128]{2,1,0:T(8,128)S(1)} collective-permute-done((f32[1,112,128]{2,1,0:T(8,128)S(1)}, f32[1,112,128]{2,1,0:T(8,128)S(1)}, u32[]{:S(2)}, u32[]{:S(2)}) %collective-permute-start.4) | collective-permute-done | bytes 57376 | tf_op jit(solution)/shard_map/ppermute | solution.py:788
  84.5 6.7 %shard_map.115 = (f32[16,1024]{1,0:T(8,128)S(1)}, f32[16,1024]{1,0:T(8,128)S(1)}, f32[16,128]{1,0:T(8,128)S(1)}, f32[16,128]{1,0:T(8,128)S(1)}, f32[8,40,128]{2,...) custom-call(s32[1]{0:T(128)} %bitcast.me_ref, s32[4]{0:T(128)S(1)} %copy-done.9, ...), custom_call_target="tpu_custom_call" | custom-call | flops 6000000000 | tf_op jit(solution)/shard_map/pallas_call | solution.py:746
  91.2 8.9 %all_to_all.34.recv_ref = f32[8,40,128]{2,1,0:T(8,128)S(1)} all-to-all(f32[8,40,128]{2,1,0:T(8,128)S(1)} %get-tuple-element.60), channel_id=1, replica_groups={{0,1,2,3,4,5,6,7},{8,9,10,11,12,13,14,15},{16,17,18,19,20,21,22,23},{24..., dimensions={0} | all-to-all | bytes 327680 | tf_op jit(solution)/shard_map/all_to_all | solution.py:792
  100.1 1.3 %shard_map.116 = f32[8,40,128]{2,1,0:T(8,128)S(1)} custom-call(s32[1]{0:T(128)} %bitcast.me_ref, f32[8,40,128]{2,1,0:T(8,128)S(1)} %all_to_all.34.recv_ref, f32[7,256,128]{2,1,0:T(8,128)S(1)} %copy-done.3, f32[7,256,128]{2,1,0:T(8,128)S(1)} %copy-done.4, f32[8,2,128,128]{3,2,1,0:T(8,128)S(1)} %copy-done.2, ...), custom_call_target="tpu_custom_call" | custom-call | flops 6000000000 | tf_op jit(solution)/shard_map/pallas_call | solution.py:746
  101.3 12.2 %all_to_all.35.recv_ref = f32[8,40,128]{2,1,0:T(8,128)S(1)} all-to-all(f32[8,40,128]{2,1,0:T(8,128)S(1)} %shard_map.116), channel_id=1, replica_groups={{0,8,16,24,32,40,48,56},{1,9,17,25,33,41,49,57},{2,10,18,26,34,42,50,58..., dimensions={0} | all-to-all | bytes 327680 | tf_op jit(solution)/shard_map/all_to_all | solution.py:792
  113.5 1.3 %shard_map.117.part0_ref = f32[1,40,128]{2,1,0:T(8,128)S(1)} custom-call(s32[1]{0:T(128)} %bitcast.me_ref, f32[8,40,128]{2,1,0:T(8,128)S(1)} %all_to_all.35.recv_ref, f32[7,256,128]{2,1,0:T(8,128)S(1)} %copy-done.3, f32[7,256,128]{2,1,0:T(8,128)S(1)} %copy-done.4, f32[8,2,128,128]{3,2,1,0:T(8,128)S(1)} %copy-done.2, ...), custom_call_target="tpu_custom_call" | custom-call | flops 6000000000 | tf_op jit(solution)/shard_map/pallas_call | solution.py:746
  114.8 2.0 %collective-permute-start.8 = (f32[1,40,128]{2,1,0:T(8,128)S(1)}, f32[1,40,128]{2,1,0:T(8,128)S(1)}, u32[]{:S(2)}, u32[]{:S(2)}) collective-permute-start(f32[1,40,128]{2,1,0:T(8,128)S(1)} %shard_map.117.part0_ref), channel_id=1, source_target_pairs={{0,192},{1,193},{2,194},{3,195},{4,196},{5,197},{6,198},{7,199},{8... | collective-permute-start | bytes 61448 | tf_op jit(solution)/shard_map/ppermute | solution.py:788
  116.8 1.4 %collective-permute-start.7 = (f32[1,40,128]{2,1,0:T(8,128)S(1)}, f32[1,40,128]{2,1,0:T(8,128)S(1)}, u32[]{:S(2)}, u32[]{:S(2)}) collective-permute-start(f32[1,40,128]{2,1,0:T(8,128)S(1)} %shard_map.117.part0_ref), channel_id=1, source_target_pairs={{0,128},{1,129},{2,130},{3,131},{4,132},{5,133},{6,134},{7,135},{8... | collective-permute-start | bytes 61448 | tf_op jit(solution)/shard_map/ppermute | solution.py:788
  118.2 0.7 collective-permute-start.6
  119.0 0.9 collective-permute-done.8.part3_ref
  119.9 2.2 %collective-permute-done.7.part2_ref = f32[1,40,128]{2,1,0:T(8,128)S(1)} collective-permute-done((f32[1,40,128]{2,1,0:T(8,128)S(1)}, f32[1,40,128]{2,1,0:T(8,128)S(1)}, u32[]{:S(2)}, u32[]{:S(2)}) %collective-permute-start.7) | collective-permute-done | bytes 20512 | tf_op jit(solution)/shard_map/ppermute | solution.py:788
  122.1 1.6 %shard_map.118 = f32[16,1024]{1,0:T(8,128)} custom-call(s32[1]{0:T(128)} %bitcast.me_ref, f32[1,40,128]{2,1,0:T(8,128)S(1)} %shard_map.117.part0_ref, f32[1,40,128]{2,1,0:T(8,128)S(1)} %collective-permute-done.6.part1_ref, f32[1,40,128]{2,1,0:T(8,128)S(1)} %collective-permute-done.7.part2_ref, f32[1,40,128]{2,1,0:T(8,128)S(1)} %collective-permute-done.8.part3_ref, ...), custom_call_target="tpu_custom_call" | custom-call | flops 6000000000 | tf_op jit(solution)/shard_map/pallas_call | solution.py:746
  (24 shorter events, 0.1 us)
Async XLA Ops:
  0.0 16.9 %copy-start.2 = (f32[8,2,128,128]{3,2,1,0:T(8,128)S(1)}, f32[8,2,128,128]{3,2,1,0:T(8,128)}, u32[]{:S(2)}) copy-start(f32[8,2,128,128]{3,2,1,0:T(8,128)} %up_couple_ref.15) | copy-start | bytes 3145732
  0.0 16.9 %copy-start.3 = (f32[7,256,128]{2,1,0:T(8,128)S(1)}, f32[7,256,128]{2,1,0:T(8,128)}, u32[]{:S(2)}) copy-start(f32[7,256,128]{2,1,0:T(8,128)} %up_row_ref.17) | copy-start | bytes 2752516
  0.0 16.9 %copy-start.4 = (f32[7,256,128]{2,1,0:T(8,128)S(1)}, f32[7,256,128]{2,1,0:T(8,128)}, u32[]{:S(2)}) copy-start(f32[7,256,128]{2,1,0:T(8,128)} %up_col_ref.15) | copy-start | bytes 2752516
  35.6 9.6 %copy-start = (f32[4,512,256]{2,1,0:T(8,128)S(1)}, f32[4,512,256]{2,1,0:T(8,128)}, u32[]{:S(2)}) copy-start(f32[4,512,256]{2,1,0:T(8,128)} %dense_ref.3) | copy-start | bytes 6291460
  35.6 9.6 %copy-start.1 = (f32[4,512,128]{2,1,0:T(8,128)S(1)}, f32[4,512,128]{2,1,0:T(8,128)}, u32[]{:S(2)}) copy-start(f32[4,512,128]{2,1,0:T(8,128)} %row_basis_ref.3) | copy-start | bytes 3145732
  35.6 9.6 %copy-start.5 = (f32[4,256,128]{2,1,0:T(8,128)S(1)}, f32[4,256,128]{2,1,0:T(8,128)}, u32[]{:S(2)}) copy-start(f32[4,256,128]{2,1,0:T(8,128)} %col_basis_ref.3) | copy-start | bytes 1572868
  35.6 9.6 %copy-start.6 = (f32[3,256,128]{2,1,0:T(8,128)S(1)}, f32[3,256,128]{2,1,0:T(8,128)}, u32[]{:S(2)}) copy-start(f32[3,256,128]{2,1,0:T(8,128)} %local_row_ref.3) | copy-start | bytes 1179652
  35.6 9.6 %copy-start.7 = (f32[3,256,128]{2,1,0:T(8,128)S(1)}, f32[3,256,128]{2,1,0:T(8,128)}, u32[]{:S(2)}) copy-start(f32[3,256,128]{2,1,0:T(8,128)} %local_col_ref.3) | copy-start | bytes 1179652
  35.6 9.6 %copy-start.8 = (f32[3,2,128,128]{3,2,1,0:T(8,128)S(1)}, f32[3,2,128,128]{3,2,1,0:T(8,128)}, u32[]{:S(2)}) copy-start(f32[3,2,128,128]{3,2,1,0:T(8,128)} %local_couple_ref.3) | copy-start | bytes 1179652
  35.7 9.6 %copy-start.9 = (s32[4]{0:T(128)S(1)}, s32[4]{0:T(128)}, u32[]{:S(2)}) copy-start(s32[4]{0:T(128)} %rows_ref.3) | copy-start | bytes 52
  35.7 9.6 %copy-start.10 = (f32[16,2816]{1,0:T(8,128)S(1)}, f32[16,2816]{1,0:T(8,128)}, u32[]{:S(2)}) copy-start(f32[16,2816]{1,0:T(8,128)} %get-tuple-element.45.z_ref) | copy-start | bytes 540676
  36.9 5.0 %collective-permute-start.2 = (f32[1,24,128]{2,1,0:T(8,128)S(1)}, f32[1,24,128]{2,1,0:T(8,128)S(1)}, u32[]{:S(2)}, u32[]{:S(2)}) collective-permute-start(f32[1,24,128]{2,1,0:T(8,128)S(1)} %get-tuple-element.39.part0_ref), channel_id=1, source_target_pairs={{0,192},{1,193},{2,194},{3,195},{4,196},{5,197},{6,198},{7,199},{8... | collective-permute-start | bytes 36872 | tf_op jit(solution)/shard_map/ppermute | solution.py:788
  40.0 5.2 %collective-permute-start.1 = (f32[1,24,128]{2,1,0:T(8,128)S(1)}, f32[1,24,128]{2,1,0:T(8,128)S(1)}, u32[]{:S(2)}, u32[]{:S(2)}) collective-permute-start(f32[1,24,128]{2,1,0:T(8,128)S(1)} %get-tuple-element.39.part0_ref), channel_id=1, source_target_pairs={{0,128},{1,129},{2,130},{3,131},{4,132},{5,133},{6,134},{7,135},{8... | collective-permute-start | bytes 36872 | tf_op jit(solution)/shard_map/ppermute | solution.py:788
  40.6 4.6 %collective-permute-start = (f32[1,24,128]{2,1,0:T(8,128)S(1)}, f32[1,24,128]{2,1,0:T(8,128)S(1)}, u32[]{:S(2)}, u32[]{:S(2)}) collective-permute-start(f32[1,24,128]{2,1,0:T(8,128)S(1)} %get-tuple-element.39.part0_ref), channel_id=1, source_target_pairs={{0,64},{1,65},{2,66},{3,67},{4,68},{5,69},{6,70},{7,71},{8,72},{9,... | collective-permute-start | bytes 36872 | tf_op jit(solution)/shard_map/ppermute | solution.py:788
  77.5 5.5 %collective-permute-start.5 = (f32[1,112,128]{2,1,0:T(8,128)S(1)}, f32[1,112,128]{2,1,0:T(8,128)S(1)}, u32[]{:S(2)}, u32[]{:S(2)}) collective-permute-start(f32[1,112,128]{2,1,0:T(8,128)S(1)} %get-tuple-element.52.part0_ref), channel_id=1, source_target_pairs={{0,192},{1,193},{2,194},{3,195},{4,196},{5,197},{6,198},{7,199},{8... | collective-permute-start | bytes 172040 | tf_op jit(solution)/shard_map/ppermute | solution.py:788
  78.8 5.7 %collective-permute-start.4 = (f32[1,112,128]{2,1,0:T(8,128)S(1)}, f32[1,112,128]{2,1,0:T(8,128)S(1)}, u32[]{:S(2)}, u32[]{:S(2)}) collective-permute-start(f32[1,112,128]{2,1,0:T(8,128)S(1)} %get-tuple-element.52.part0_ref), channel_id=1, source_target_pairs={{0,128},{1,129},{2,130},{3,131},{4,132},{5,133},{6,134},{7,135},{8... | collective-permute-start | bytes 172040 | tf_op jit(solution)/shard_map/ppermute | solution.py:788
  79.7 4.8 %collective-permute-start.3 = (f32[1,112,128]{2,1,0:T(8,128)S(1)}, f32[1,112,128]{2,1,0:T(8,128)S(1)}, u32[]{:S(2)}, u32[]{:S(2)}) collective-permute-start(f32[1,112,128]{2,1,0:T(8,128)S(1)} %get-tuple-element.52.part0_ref), channel_id=1, source_target_pairs={{0,64},{1,65},{2,66},{3,67},{4,68},{5,69},{6,70},{7,71},{8,72},{9,... | collective-permute-start | bytes 172040 | tf_op jit(solution)/shard_map/ppermute | solution.py:788
  114.8 5.1 %collective-permute-start.8 = (f32[1,40,128]{2,1,0:T(8,128)S(1)}, f32[1,40,128]{2,1,0:T(8,128)S(1)}, u32[]{:S(2)}, u32[]{:S(2)}) collective-permute-start(f32[1,40,128]{2,1,0:T(8,128)S(1)} %shard_map.117.part0_ref), channel_id=1, source_target_pairs={{0,192},{1,193},{2,194},{3,195},{4,196},{5,197},{6,198},{7,199},{8... | collective-permute-start | bytes 61448 | tf_op jit(solution)/shard_map/ppermute | solution.py:788
  116.8 5.3 %collective-permute-start.7 = (f32[1,40,128]{2,1,0:T(8,128)S(1)}, f32[1,40,128]{2,1,0:T(8,128)S(1)}, u32[]{:S(2)}, u32[]{:S(2)}) collective-permute-start(f32[1,40,128]{2,1,0:T(8,128)S(1)} %shard_map.117.part0_ref), channel_id=1, source_target_pairs={{0,128},{1,129},{2,130},{3,131},{4,132},{5,133},{6,134},{7,135},{8... | collective-permute-start | bytes 61448 | tf_op jit(solution)/shard_map/ppermute | solution.py:788
  118.2 3.9 %collective-permute-start.6 = (f32[1,40,128]{2,1,0:T(8,128)S(1)}, f32[1,40,128]{2,1,0:T(8,128)S(1)}, u32[]{:S(2)}, u32[]{:S(2)}) collective-permute-start(f32[1,40,128]{2,1,0:T(8,128)S(1)} %shard_map.117.part0_ref), channel_id=1, source_target_pairs={{0,64},{1,65},{2,66},{3,67},{4,68},{5,69},{6,70},{7,71},{8,72},{9,... | collective-permute-start | bytes 61448 | tf_op jit(solution)/shard_map/ppermute | solution.py:788

commit v5 on v4

--- a/solution.py
+++ b/solution.py
@@ -12,16 +12,13 @@
 LEAF_DEV = 4
 LEAF_ROWS = 512
 LEAF_COLS = 256
-PATH = 3
-LEVEL_BASE = (0, 8, 12)
 HALF = RANK // 2
 SLICE = 8
 COST_FLOPS = 6000000000
 KEEP = LEAF_DEV * LEAF_ROWS
 TINY = 1.2e-38
 NEAR = 8
-MID = 8
-FAR = 4
+STAGES = {"core": (0, 1), "row": (1, 2), "mid": (3, 3), "far": (6, 2)}
 VMEM_MIB = 24
 VMEM_LIMIT = VMEM_MIB * 1024 * 1024
 START_LIMIT = 60 * 1024 * 1024
@@ -249,17 +246,41 @@
     return part + jnp.transpose(part)
 
 
+def stage(name):
+    level, heights = STAGES[name]
+    return level, heights, 1 << heights
+
+
+def place_of(me, name):
+    level, _, count = stage(name)
+    return (me >> level) % count
+
+
+def bases(name):
+    _, heights, count = stage(name)
+    return [sum(count >> k for k in range(height)) for height in range(heights)]
+
+
+def node_count(name):
+    return 2 * stage(name)[2] - 2
+
+
+def gather_parts(me, name, parts, out_ref):
+    for k, part in enumerate(parts):
+        out_ref[place_of(me, name) ^ k] = part[0]
+
+
 def store_pair(ref, index, value):
     high, low = split(value)
     ref[0, index] = high
     ref[1, index] = low
 
 
-def group_grams(level, grams, up_row_ref, nodes_ref):
-    for height in range(PATH):
+def group_grams(name, grams, up_row_ref, nodes_ref):
+    for height, base in enumerate(bases(name)):
         for k, value in enumerate(grams):
-            store_pair(nodes_ref, LEVEL_BASE[height] + k, value)
-        grams = gram_climb(grams, pair_at(up_row_ref, level + height))
+            store_pair(nodes_ref, base + k, value)
+        grams = gram_climb(grams, pair_at(up_row_ref, stage(name)[0] + height))
     return grams[0]
 
 
@@ -322,11 +343,11 @@
     return stats
 
 
-def climb_group(level, me_ref, recv_ref, climb_ref, sib_ref, scratch_ref):
-    place = (me_ref[0] >> level) % NEAR
+def climb_group(name, me_ref, recv_ref, climb_ref, sib_ref, scratch_ref):
+    level = stage(name)[0]
+    place = place_of(me_ref[0], name)
     summaries = [recv_ref[d, :RHS] for d in range(recv_ref.shape[0])]
-    for height in range(PATH):
-        base = LEVEL_BASE[height]
+    for height, base in enumerate(bases(name)):
         for m, value in enumerate(summaries):
             scratch_ref[base + m] = value
         sib_ref[height] = scratch_ref[base + ((place >> height) ^ 1)]
@@ -334,6 +355,12 @@
     return summaries[0]
 
 
+def received_grams(recv_ref):
+    base = RHS + 8
+    count = recv_ref.shape[0]
+    return [unpack(recv_ref[d, base:], recv_ref[d, RHS + 2 : RHS + 3]) for d in range(count)]
+
+
 def path_product(me, level, path, up_col_ref):
     half = half_of(up_col_ref, level, (me >> level) & 1)
     return mm(path, half)
@@ -344,9 +371,30 @@
     return mm(path, pair_at(up_couple_ref, level, child))
 
 
-def near_kernel(
+def core_kernel(
     me_ref,
+    part0_ref,
+    part1_ref,
+    up_row_ref,
+    msg_ref,
+    sib_ref,
+    nodes_ref,
     recv_ref,
+    scratch_ref,
+):
+    gather_parts(me_ref[0], "core", (part0_ref, part1_ref), recv_ref)
+    summary = climb_group("core", me_ref, recv_ref, up_row_ref, sib_ref, scratch_ref)
+    top, diagonal = pack(group_grams("core", received_grams(recv_ref), up_row_ref, nodes_ref))
+    stats = sum_stats(recv_ref)
+    send(msg_ref, stack([summary, stat_block(stats[:1], stats[1:2], diagonal), top]))
+
+
+def row_kernel(
+    me_ref,
+    part0_ref,
+    part1_ref,
+    part2_ref,
+    part3_ref,
     up_row_ref,
     up_col_ref,
     up_couple_ref,
@@ -355,19 +403,18 @@
     nodes_ref,
     gain_ref,
     path_ref,
+    recv_ref,
     scratch_ref,
     slice_ref,
 ):
     me = me_ref[0]
-    summary = climb_group(0, me_ref, recv_ref, up_row_ref, sib_ref, scratch_ref)
-    base = RHS + 8
-    grams = [unpack(recv_ref[d, base:], recv_ref[d, RHS + 2 : RHS + 3]) for d in range(NEAR)]
-    gram = group_grams(0, grams, up_row_ref, nodes_ref)
+    gather_parts(me, "row", (part0_ref, part1_ref, part2_ref, part3_ref), recv_ref)
+    summary = climb_group("row", me_ref, recv_ref, up_row_ref, sib_ref, scratch_ref)
+    gram = group_grams("row", received_grams(recv_ref), up_row_ref, nodes_ref)
     child = 1 - (me & 1)
-    first = up_couple_ref[0, child]
-    store_pair(gain_ref, 0, first)
+    store_pair(gain_ref, 0, up_couple_ref[0, child])
     path = up_col_ref[0, pl.ds(pl.multiple_of((me & 1) * RANK, RANK), RANK), :]
-    for j in range(1, PATH):
+    for j in range(1, 3):
         store_pair(gain_ref, j, sibling_gain(me, j, path, up_couple_ref))
         path = path_product(me, j, path, up_col_ref)
     path_ref[...] = path
@@ -393,29 +440,24 @@
     scratch_ref,
 ):
     me = me_ref[0]
-    summary = climb_group(PATH, me_ref, recv_ref, up_row_ref, sib_ref, scratch_ref)
+    level, _, count = stage("mid")
+    summary = climb_group("mid", me_ref, recv_ref, up_row_ref, sib_ref, scratch_ref)
     path = path_ref[...]
-    for j in range(PATH, 8):
-        store_pair(gain_ref, j - PATH, sibling_gain(me, j, path, up_couple_ref))
+    for j in range(level, 8):
+        store_pair(gain_ref, j - level, sibling_gain(me, j, path, up_couple_ref))
         if j < 7:
             path = path_product(me, j, path, up_col_ref)
-    for d in range(MID):
+    for d in range(count):
         part_ref[d * SLICE : (d + 1) * SLICE] = recv_ref[d, RHS + 8 :]
         diagonal_ref[d : d + 1] = recv_ref[d, RHS + 2 : RHS + 3]
     send(msg_ref, stack([summary, sum_stats(recv_ref)]))
 
 
 def from_siblings(siblings, near_gain_ref, mid_gain_ref):
-    gains = [pair_at(near_gain_ref, j) for j in range(PATH)]
-    gains += [pair_at(mid_gain_ref, j) for j in range(8 - PATH)]
+    gains = [pair_at(near_gain_ref, j) for j in range(3)]
+    gains += [pair_at(mid_gain_ref, j) for j in range(5)]
     gains = tuple(jnp.concatenate([g[k] for g in gains], 1) for k in range(2))
     return mm(jnp.concatenate(siblings, 1), gains, transposed=True)
-
-
-def gather_far(me, parts, out_ref):
-    place = me >> (2 * PATH)
-    for k, part in enumerate(parts):
-        out_ref[place ^ k] = part[0]
 
 
 def readers(local):
@@ -429,8 +471,9 @@
     part1_ref,
     part2_ref,
     part3_ref,
-    near_ref,
-    mid_ref,
+    core_sib_ref,
+    row_sib_ref,
+    mid_sib_ref,
     near_gain_ref,
     mid_gain_ref,
     part_ref,
@@ -451,10 +494,10 @@
     recv_ref,
 ):
     me = me_ref[0]
-    gather_far(me, (part0_ref, part1_ref, part2_ref, part3_ref), recv_ref)
-    place = me >> (2 * PATH)
-    summaries = [recv_ref[d, :RHS] for d in range(FAR)]
-    siblings = [near_ref[j] for j in range(PATH)] + [mid_ref[j] for j in range(PATH)]
+    gather_parts(me, "far", (part0_ref, part1_ref, part2_ref, part3_ref), recv_ref)
+    place = place_of(me, "far")
+    summaries = [recv_ref[d, :RHS] for d in range(recv_ref.shape[0])]
+    siblings = [core_sib_ref[0]] + [row_sib_ref[j] for j in range(2)] + [mid_sib_ref[j] for j in range(3)]
     siblings.append(recv_ref[place ^ 1, :RHS])
     summaries = climb(summaries, pair_at(up_row_ref, 6))
     for m, value in enumerate(summaries):
@@ -496,13 +539,14 @@
     return first, second, factor, total, energy
 
 
-def pair_group(level, me_ref, recv_ref, up_row_ref, up_col_ref, up_couple_ref, nodes_ref, keep):
-    place = (me_ref[0] >> level) % NEAR
+def pair_group(name, me_ref, recv_ref, tables, nodes_ref, keep):
+    up_row_ref, up_col_ref, up_couple_ref = tables
+    level = stage(name)[0]
+    place = place_of(me_ref[0], name)
     first, second, _, total, energy = rescale(recv_ref)
     cross = jnp.zeros((RHS, RANK), f32)
-    for height in range(PATH):
+    for height, base in enumerate(bases(name)):
         j = level + height
-        base = LEVEL_BASE[height]
         gained = couple_all(first, (pair_at(up_couple_ref, j, 0), pair_at(up_couple_ref, j, 1)))
         summed = []
         for k in range(len(first)):
@@ -525,9 +569,36 @@
     return first[0], second[0], stat_block(total, energy)
 
 
-def near_pair_kernel(
+def core_pair_kernel(
     me_ref,
+    part0_ref,
+    part1_ref,
+    up_row_ref,
+    up_col_ref,
+    up_couple_ref,
+    nodes_ref,
+    msg_ref,
+    path_ref,
+    own_ref,
     recv_ref,
+    gain_ref,
+    below_ref,
+):
+    gather_parts(me_ref[0], "core", (part0_ref, part1_ref), recv_ref)
+    tables = (up_row_ref, up_col_ref, up_couple_ref)
+    keep = (path_ref, gain_ref, below_ref)
+    first, second, stats = pair_group("core", me_ref, recv_ref, tables, nodes_ref, keep)
+    own_ref[...] = stats
+    base = 2 * RHS + 8
+    send(msg_ref, stack([first, second, stats, recv_ref[0, base:], recv_ref[1, base:]]))
+
+
+def row_pair_kernel(
+    me_ref,
+    part0_ref,
+    part1_ref,
+    part2_ref,
+    part3_ref,
     up_row_ref,
     up_col_ref,
     up_couple_ref,
@@ -538,22 +609,25 @@
     own_ref,
     mid_nodes_ref,
     gram_ref,
+    recv_ref,
     gain_ref,
     below_ref,
 ):
+    gather_parts(me_ref[0], "row", (part0_ref, part1_ref, part2_ref, part3_ref), recv_ref)
+    tables = (up_row_ref, up_col_ref, up_couple_ref)
     keep = (path_ref, gain_ref, below_ref)
-    first, second, stats = pair_group(
-        0, me_ref, recv_ref, up_row_ref, up_col_ref, up_couple_ref, nodes_ref, keep
-    )
+    first, second, stats = pair_group("row", me_ref, recv_ref, tables, nodes_ref, keep)
     own_ref[...] = stats
     send(msg_ref, stack([first, second, stats]))
     base = 2 * RHS + 8
     grams = []
-    for d in range(MID):
-        low = base + d * SLICE
-        top = stack([recv_ref[p, low : low + SLICE] for p in range(NEAR)])
-        grams.append(unpack(top, diagonal_ref[d : d + 1]))
-    top, diagonal = pack(group_grams(PATH, grams, up_row_ref, mid_nodes_ref))
+    for d in range(stage("mid")[2]):
+        slices = []
+        for p in range(NEAR):
+            low = base + (p % 2) * HALF + d * SLICE
+            slices.append(recv_ref[p // 2, low : low + SLICE])
+        grams.append(unpack(stack(slices), diagonal_ref[d : d + 1]))
+    top, diagonal = pack(group_grams("mid", grams, up_row_ref, mid_nodes_ref))
     gram_ref[...] = stack([top, stat_block(diagonal)])
 
 
@@ -571,21 +645,22 @@
     gain_ref,
     below_ref,
 ):
+    tables = (up_row_ref, up_col_ref, up_couple_ref)
     keep = (path_ref, gain_ref, below_ref)
-    first, second, stats = pair_group(
-        PATH, me_ref, recv_ref, up_row_ref, up_col_ref, up_couple_ref, nodes_ref, keep
-    )
+    first, second, stats = pair_group("mid", me_ref, recv_ref, tables, nodes_ref, keep)
     own_ref[...] = stats
     send(msg_ref, stack([first, second, stats, gram_ref[...]]))
 
 
-def last_pair_kernel(
-    level, me_ref, recv_ref, up_row_ref, up_col_ref, up_couple_ref, nodes_ref, msg_ref
-):
-    parts = pair_group(
-        level, me_ref, recv_ref, up_row_ref, up_col_ref, up_couple_ref, nodes_ref, None
-    )
-    send(msg_ref, stack(parts))
+def last_pair_kernel(name, me_ref, *refs):
+    if name == "mid":
+        recv_ref, up_row_ref, up_col_ref, up_couple_ref, nodes_ref, msg_ref = refs
+    else:
+        count = stage(name)[2]
+        up_row_ref, up_col_ref, up_couple_ref, nodes_ref, msg_ref, recv_ref = refs[count:]
+        gather_parts(me_ref[0], name, refs[:count], recv_ref)
+    tables = (up_row_ref, up_col_ref, up_couple_ref)
+    send(msg_ref, stack(pair_group(name, me_ref, recv_ref, tables, nodes_ref, None)))
 
 
 def top_levels(recv_ref, up_row_ref, up_col_ref, up_couple_ref, gram_ref):
@@ -597,7 +672,7 @@
     potential = [a + b for a, b in zip(gained, below)]
     cross = jnp.zeros((RHS, RANK), f32)
     summed = []
-    for d in range(FAR):
+    for d in range(recv_ref.shape[0]):
         moved = mm(potential[d], pair_at(gram_ref, d))
         cross = cross + potential[d] * (2.0 * second[d] + moved)
         summed.append(second[d] + moved)
@@ -612,8 +687,10 @@
     part1_ref,
     part2_ref,
     part3_ref,
-    near_path_ref,
-    near_own_ref,
+    core_path_ref,
+    core_own_ref,
+    row_path_ref,
+    row_own_ref,
     mid_path_ref,
     mid_own_ref,
     near_gain_ref,
@@ -621,7 +698,8 @@
     up_row_ref,
     up_col_ref,
     up_couple_ref,
-    near_nodes_ref,
+    core_nodes_ref,
+    row_nodes_ref,
     mid_nodes_ref,
     dense_ref,
     row_basis_ref,
@@ -643,10 +721,10 @@
     recv_ref,
 ):
     me = me_ref[0]
-    gather_far(me, (part0_ref, part1_ref, part2_ref, part3_ref), recv_ref)
-    place = me >> (2 * PATH)
+    gather_parts(me, "far", (part0_ref, part1_ref, part2_ref, part3_ref), recv_ref)
+    place = place_of(me, "far")
     base = 2 * RHS + 8
-    for d in range(FAR):
+    for d in range(recv_ref.shape[0]):
         gram = unpack(recv_ref[d, base : base + HALF], recv_ref[d, base + HALF : base + HALF + 1])
         store_pair(top_gram_ref, d, gram)
     potential, summed, squares, energy = top_levels(
@@ -657,21 +735,23 @@
     alpha_ref[...] = jnp.broadcast_to(alpha, (RHS, RANK))
     rho_ref[...] = jnp.broadcast_to(rho, (RHS, RANK))
     scale = inverse_norm(squares)
-    for d in range(FAR):
+    for d in range(recv_ref.shape[0]):
         a_ref[d] = potential[d]
         b_ref[d] = summed[d]
     forward = a_ref[place]
     siblings = {6: b_ref[place ^ 1]}
     for k, value in enumerate(climb(summed, pair_at(up_row_ref, 6))):
-        a_ref[FAR + k] = value
-    siblings[7] = a_ref[FAR + ((place >> 1) ^ 1)]
-    for level, path_ref, part_ref, nodes_ref in (
-        (PATH, mid_path_ref, mid_own_ref, mid_nodes_ref),
-        (0, near_path_ref, near_own_ref, near_nodes_ref),
+        a_ref[4 + k] = value
+    siblings[7] = a_ref[4 + ((place >> 1) ^ 1)]
+    for name, path_ref, part_ref, nodes_ref in (
+        ("mid", mid_path_ref, mid_own_ref, mid_nodes_ref),
+        ("row", row_path_ref, row_own_ref, row_nodes_ref),
+        ("core", core_path_ref, core_own_ref, core_nodes_ref),
     ):
+        level, heights, _ = stage(name)
         factor = scale / inverse_norm(column_of(part_ref[:1]))
-        inside = (me >> level) % NEAR
-        for height in reversed(range(PATH)):
+        inside = place_of(me, name)
+        for height in reversed(range(heights)):
             j = level + height
             child = (me >> j) & 1
             spread = mm(forward, pair_at(up_row_ref, j), transposed=True)
@@ -679,7 +759,7 @@
             high = spread[:, RANK:]
             forward = path_ref[3 * height] * factor + jnp.where(child == 0, low, high)
             other = path_ref[3 * height + 1] * factor + jnp.where(child == 0, high, low)
-            gram = pair_at(nodes_ref, LEVEL_BASE[height] + ((inside >> height) ^ 1))
+            gram = pair_at(nodes_ref, bases(name)[height] + ((inside >> height) ^ 1))
             siblings[j] = path_ref[3 * height + 2] * factor + mm(other, gram)
     backward = from_siblings([siblings[j] for j in range(8)], near_gain_ref, mid_gain_ref)
     local = readers(
@@ -724,7 +804,7 @@
     out_ref,
     recv_ref,
 ):
-    gather_far(me_ref[0], (part0_ref, part1_ref, part2_ref, part3_ref), recv_ref)
+    gather_parts(me_ref[0], "far", (part0_ref, part1_ref, part2_ref, part3_ref), recv_ref)
     _, _, squares, energy = top_levels(
         recv_ref, up_row_ref, up_col_ref, up_couple_ref, top_gram_ref
     )
@@ -779,17 +859,19 @@
     up_couple,
 ):
     me = lax.axis_index("leaf").astype(jnp.int32).reshape(1)
-    near, mid = (1, NEAR), (NEAR, MID)
-
-    def swap_far(message):
+
+    def swap_parts(message, name):
+        level, _, count = stage(name)
         parts = [message]
-        for k in range(1, FAR):
-            pairs = [(i, i ^ (k * NEAR * MID)) for i in range(devices)]
+        for k in range(1, count):
+            pairs = [(i, i ^ (k << level)) for i in range(devices)]
             parts.append(lax.ppermute(message, "leaf", pairs))
         return parts
 
-    def swap(message, group):
-        return lax.all_to_all(message, "leaf", 0, 0, axis_index_groups=device_groups(devices, *group))
+    def swap_mid(message):
+        level, _, count = stage("mid")
+        groups = device_groups(devices, 1 << level, count)
+        return lax.all_to_all(message, "leaf", 0, 0, axis_index_groups=groups)
 
     tile = (RHS, RANK)
     row_shape = (RHS, LEAF_DEV * LEAF_ROWS)
@@ -807,19 +889,26 @@
     def nodes_shape(count):
         return jax.ShapeDtypeStruct((2, count) + gram_shape, bf16)
 
-    path_shape = (3 * PATH,) + tile
-    pair_scratch = [(14,) + tile, (14,) + tile]
-
-    def last_pair(level, message, peers, nodes):
-        return call(
-            functools.partial(last_pair_kernel, level),
-            [(peers,) + double],
-            [me, message] + tables + [nodes],
-        )[0]
+    def path_shape(name):
+        return (3 * stage(name)[1],) + tile
+
+    def sibling_shape(name):
+        return (stage(name)[1],) + tile
+
+    def nodes_of(name):
+        return nodes_shape(node_count(name))
+
+    def node_scratch(name, count=1):
+        return [(node_count(name),) + tile] * count
+
+    def received(name, shape):
+        return [(stage(name)[2],) + shape]
+
+    groups = stage("mid")[2]
 
     z, message = call(
         start_kernel,
-        [(RHS, KEEP + 6 * RANK), (NEAR,) + longer(single, HALF)],
+        [(RHS, KEEP + 6 * RANK), (1,) + longer(single, HALF)],
         [me, box_rows, rhs, row_basis, local_row],
         [pltpu.SMEM(box_rows.shape, jnp.int32)]
         + [k.shape for k in (rhs, row_basis, local_row)]
@@ -828,63 +917,85 @@
         START_LIMIT,
     )
     blocks = [dense, row_basis, col_basis, local_row, local_col, local_couple]
-    message, near_sib, near_nodes, near_gain, path = call(
-        near_kernel,
-        [(MID,) + longer(single, SLICE), (PATH,) + tile, nodes_shape(14), nodes_shape(PATH), gram_shape],
-        [me, swap(message, near)] + tables,
-        [(14,) + tile, (HALF, RANK)],
+    message, core_sib, core_nodes = call(
+        core_kernel,
+        [(1,) + longer(single, HALF), sibling_shape("core"), nodes_of("core")],
+        [me] + swap_parts(message, "core") + [up_row],
+        received("core", longer(single, HALF)) + node_scratch("core"),
+    )
+    message, row_sib, row_nodes, near_gain, path = call(
+        row_kernel,
+        [(groups,) + longer(single, SLICE), sibling_shape("row"), nodes_of("row"), nodes_shape(3), gram_shape],
+        [me] + swap_parts(message, "row") + tables,
+        received("row", longer(single, HALF)) + node_scratch("row") + [(HALF, RANK)],
     )
     message, mid_sib, mid_gain, part, diagonal = call(
         mid_kernel,
-        [(1,) + single, (PATH,) + tile, nodes_shape(8 - PATH), (HALF, RANK), stat],
-        [me, swap(message, mid)] + tables + [path],
-        [(14,) + tile],
+        [(1,) + single, sibling_shape("mid"), nodes_shape(5), (HALF, RANK), stat],
+        [me, swap_mid(message)] + tables + [path],
+        node_scratch("mid"),
     )
     gains = [near_gain, mid_gain]
     x, beta, message, own, inner = call(
         first_kernel,
-        [col_shape, tile, (NEAR,) + longer(double, HALF), stat, row_shape],
+        [col_shape, tile, (1,) + longer(double, HALF), stat, row_shape],
         [me, box_rows]
-        + swap_far(message)
-        + [near_sib, mid_sib]
+        + swap_parts(message, "far")
+        + [core_sib, row_sib, mid_sib]
         + gains
         + [part, up_row]
         + blocks
         + [z],
-        [(2,) + tile, (FAR,) + single],
-    )
-    message, near_path, near_own, mid_nodes, gram = call(
-        near_pair_kernel,
-        [(MID,) + double, path_shape, stat, nodes_shape(14), (HALF + 8, RANK)],
-        [me, swap(message, near)] + tables + [near_nodes, diagonal],
-        pair_scratch,
+        [(2,) + tile] + received("far", single),
+    )
+    message, core_path, core_own = call(
+        core_pair_kernel,
+        [(1,) + longer(double, 2 * HALF), path_shape("core"), stat],
+        [me] + swap_parts(message, "core") + tables + [core_nodes],
+        received("core", longer(double, HALF)) + node_scratch("core", 2),
+    )
+    message, row_path, row_own, mid_nodes, gram = call(
+        row_pair_kernel,
+        [(groups,) + double, path_shape("row"), stat, nodes_of("mid"), (HALF + 8, RANK)],
+        [me] + swap_parts(message, "row") + tables + [row_nodes, diagonal],
+        received("row", longer(double, 2 * HALF)) + node_scratch("row", 2),
     )
     message, mid_path, mid_own = call(
         mid_pair_kernel,
-        [(1,) + longer(double, HALF + 8), path_shape, stat],
-        [me, swap(message, mid)] + tables + [mid_nodes, gram],
-        pair_scratch,
+        [(1,) + longer(double, HALF + 8), path_shape("mid"), stat],
+        [me, swap_mid(message)] + tables + [mid_nodes, gram],
+        node_scratch("mid", 2),
     )
     v, x, alpha, rho, message, top_nodes = call(
         middle_kernel,
-        [col_shape, col_shape, tile, tile, (NEAR,) + double, nodes_shape(FAR)],
+        [col_shape, col_shape, tile, tile, (1,) + double, nodes_shape(4)],
         [me, box_rows]
-        + swap_far(message)
-        + [near_path, near_own, mid_path, mid_own]
+        + swap_parts(message, "far")
+        + [core_path, core_own, row_path, row_own, mid_path, mid_own]
         + gains
         + tables
-        + [near_nodes, mid_nodes]
+        + [core_nodes, row_nodes, mid_nodes]
         + blocks
         + [x, own, inner],
-        [(6,) + tile, (4,) + tile, (FAR,) + longer(double, HALF + 8)],
-    )
-    message = last_pair(0, swap(message, near), MID, near_nodes)
-    message = last_pair(PATH, swap(message, mid), 1, mid_nodes)
+        [(6,) + tile, (4,) + tile] + received("far", longer(double, HALF + 8)),
+    )
+    for name, nodes, peers in (
+        ("core", core_nodes, 1),
+        ("row", row_nodes, groups),
+        ("mid", mid_nodes, 1),
+    ):
+        parts = [swap_mid(message)] if name == "mid" else swap_parts(message, name)
+        (message,) = call(
+            functools.partial(last_pair_kernel, name),
+            [(peers,) + double],
+            [me] + parts + tables + [nodes],
+            [] if name == "mid" else received(name, double),
+        )
     (out,) = call(
         final_kernel,
         [col_shape],
-        [me] + swap_far(message) + tables + [top_nodes, beta, alpha, rho, v, x],
-        [(FAR,) + double],
+        [me] + swap_parts(message, "far") + tables + [top_nodes, beta, alpha, rho, v, x],
+        received("far", double),
     )
     return out
 

time: 124 us -> 118 us (0.952)
  blocking collectives: 74.3 us -> 40.1 us
  waiting for transfers between devices: 10.1 us -> 25.3 us
  starting transfers between devices: 12.5 us -> 25.3 us
    all_to_all x6 -> x3, blocking collectives: 74.3 us -> 40.1 us  [swap_mid(): return lax.all_to_all(message, 'leaf', 0, 0, axis_index_groups=groups)]
    ppermute x9 -> x21, waiting for transfers between devices: 10.1 us -> 25.3 us  [swap_parts(): parts.append(lax.ppermute(message, 'leaf', pairs))]
    ppermute x9 -> x21, starting transfers between devices: 12.5 us -> 25.3 us  [swap_parts(): parts.append(lax.ppermute(message, 'leaf', pairs))]
    pallas_call x10 -> x13, Pallas kernels: 26.6 us -> 26.3 us  [call(): pl.pallas_call(kernel, out_shape=outs, in_specs=[pl.BlockSpec(memory_spac...]
  transfers between devices with their start and end apart: 9 -> 21, of which waited for: 6 -> 16; matrix products, arithmetic and copies ran while one was open for 0% -> 0% of each run, Pallas kernels for 0% -> 0%
where the time goes in v5:
time: 118 us
  blocking collectives  40.1 us (34%)
  Pallas kernels  26.3 us (22%)
  starting transfers between devices  25.3 us (21%)
  waiting for transfers between devices  25.3 us (21%)
    all_to_all x3, blocking collectives, swap_mid(): return lax.all_to_all(message, 'leaf', 0, 0, axis_index_groups=groups)  40.1 us
    pallas_call x13, Pallas kernels, call(): pl.pallas_call(kernel, out_shape=outs, in_specs=[pl.BlockSpec(memory_spac...  26.3 us
    ppermute x21, starting transfers between devices, swap_parts(): parts.append(lax.ppermute(message, 'leaf', pairs))  25.3 us
    ppermute x21, waiting for transfers between devices, swap_parts(): parts.append(lax.ppermute(message, 'leaf', pairs))  25.3 us
  transfers between devices with their start and end apart: 21, of which 16 were waited for; matrix products, arithmetic and copies ran while one was open for 0% of the time, Pallas kernels for 0%

profile of v5, /device:TPU:2, one launch (start us, length us, event | category | flops | bytes accessed | tf_op | source)
XLA Modules:
  0.0 118.1 jit_solution(6326862938512855432)
XLA Ops:
  0.0 3.9 %shard_map.109 = (f32[16,2816]{1,0:T(8,128)}, f32[1,88,128]{2,1,0:T(8,128)}) custom-call(s32[1]{0:T(128)} %bitcast.me_ref, s32[4]{0:T(128)} %rows_ref.3, f32[16,2048]{1,0:T(8,128)} %rhs_hbm.1, f32[4,512,128]{2,1,0:T(8,128)} %row_basis_ref.3, f32[3,256,128]{2,1,0:T(8,128)} %local_row_ref.3), custom_call_target="tpu_custom_call" | custom-call | flops 6000000000 | tf_op jit(solution)/shard_map/pallas_call | solution.py:826
  4.0 1.4 %collective-permute-done.part1_ref = f32[1,88,128]{2,1,0:T(8,128)S(1)} collective-permute-done((f32[1,88,128]{2,1,0:T(8,128)}, f32[1,88,128]{2,1,0:T(8,128)S(1)}, u32[]{:S(2)}, u32[]{:S(2)}) %collective-permute-start) | collective-permute-done | bytes 45088 | tf_op jit(solution)/shard_map/ppermute | solution.py:868
  6.9 1.6 %collective-permute-start.3 = (f32[1,88,128]{2,1,0:T(8,128)S(1)}, f32[1,88,128]{2,1,0:T(8,128)S(1)}, u32[]{:S(2)}, u32[]{:S(2)}) collective-permute-start(f32[1,88,128]{2,1,0:T(8,128)S(1)} %get-tuple-element.43.part0_ref), channel_id=1, source_target_pairs={{0,6},{1,7},{2,4},{3,5},{4,2},{5,3},{6,0},{7,1},{8,14},{9,15},{10,... | collective-permute-start | bytes 135176 | tf_op jit(solution)/shard_map/ppermute | solution.py:868
  8.4 2.9 %collective-permute-start.2 = (f32[1,88,128]{2,1,0:T(8,128)S(1)}, f32[1,88,128]{2,1,0:T(8,128)S(1)}, u32[]{:S(2)}, u32[]{:S(2)}) collective-permute-start(f32[1,88,128]{2,1,0:T(8,128)S(1)} %get-tuple-element.43.part0_ref), channel_id=1, source_target_pairs={{0,4},{1,5},{2,6},{3,7},{4,0},{5,1},{6,2},{7,3},{8,12},{9,13},{10,... | collective-permute-start | bytes 135176 | tf_op jit(solution)/shard_map/ppermute | solution.py:868
  11.3 3.0 %collective-permute-done.2.part2_ref = f32[1,88,128]{2,1,0:T(8,128)S(1)} collective-permute-done((f32[1,88,128]{2,1,0:T(8,128)S(1)}, f32[1,88,128]{2,1,0:T(8,128)S(1)}, u32[]{:S(2)}, u32[]{:S(2)}) %collective-permute-start.2) | collective-permute-done | bytes 45088 | tf_op jit(solution)/shard_map/ppermute | solution.py:868
  15.3 1.3 %shard_map.111 = (f32[8,32,128]{2,1,0:T(8,128)S(1)}, f32[2,16,128]{2,1,0:T(8,128)S(1)}, bf16[2,6,128,128]{3,2,1,0:T(8,128)(2,1)S(1)}, bf16[2,3,128,128]{3,2,1,0:T(8,128)(2,1)S(1)}, f32[128,128]{1,0:T(8,128)S(1)}) custom-call(s32[1]{0:T(128)} %bitcast.me_ref, f32[1,88,128]{2,1,0:T(8,128)S(1)} %get-tuple-element.43.part0_ref, ...), custom_call_target="tpu_custom_call" | custom-call | flops 6000000000 | tf_op jit(solution)/shard_map/pallas_call | solution.py:826
  16.7 16.3 %all_to_all.15.recv_ref = f32[8,32,128]{2,1,0:T(8,128)S(1)} all-to-all(f32[8,32,128]{2,1,0:T(8,128)S(1)} %get-tuple-element.44), channel_id=1, replica_groups={{0,8,16,24,32,40,48,56},{1,9,17,25,33,41,49,57},{2,10,18,26,34,42,50,58..., dimensions={0} | all-to-all | bytes 262144 | tf_op jit(solution)/shard_map/all_to_all | solution.py:874
  34.2 3.1 %collective-permute-start.6 = (f32[1,24,128]{2,1,0:T(8,128)S(1)}, f32[1,24,128]{2,1,0:T(8,128)S(1)}, u32[]{:S(2)}, u32[]{:S(2)}) collective-permute-start(f32[1,24,128]{2,1,0:T(8,128)S(1)} %get-tuple-element.46.part0_ref), channel_id=1, source_target_pairs={{0,192},{1,193},{2,194},{3,195},{4,196},{5,197},{6,198},{7,199},{8... | collective-permute-start | bytes 36872 | tf_op jit(solution)/shard_map/ppermute | solution.py:868
  39.2 3.3 %collective-permute-done.5.part2_ref = f32[1,24,128]{2,1,0:T(8,128)S(1)} collective-permute-done((f32[1,24,128]{2,1,0:T(8,128)S(1)}, f32[1,24,128]{2,1,0:T(8,128)S(1)}, u32[]{:S(2)}, u32[]{:S(2)}) %collective-permute-start.5) | collective-permute-done | bytes 12320 | tf_op jit(solution)/shard_map/ppermute | solution.py:868
  42.6 4.2 %shard_map.113 = (f32[16,1024]{1,0:T(8,128)S(1)}, f32[16,128]{1,0:T(8,128)S(1)}, f32[1,104,128]{2,1,0:T(8,128)S(1)}, f32[8,128]{1,0:T(8,128)S(1)}, f32[16,2048]{1,0:T(8,128)S(1)}) custom-call(s32[1]{0:T(128)} %bitcast.me_ref, s32[4]{0:T(128)S(1)} %copy-done.10, f32[1,24,128]{2,1,0:T(8,128)S(1)} %get-tuple-element.46.part0_ref, ...), custom_call_target="tpu_custom_call" | custom-call | flops 6000000000 | tf_op jit(solution)/shard_map/pallas_call | solution.py:826
  46.8 1.2 %collective-permute-done.7.part1_ref = f32[1,104,128]{2,1,0:T(8,128)S(1)} collective-permute-done((f32[1,104,128]{2,1,0:T(8,128)S(1)}, f32[1,104,128]{2,1,0:T(8,128)S(1)}, u32[]{:S(2)}, u32[]{:S(2)}) %collective-permute-start.7) | collective-permute-done | bytes 53280 | tf_op jit(solution)/shard_map/ppermute | solution.py:868
  48.6 1.5 %collective-permute-start.10 = (f32[1,168,128]{2,1,0:T(8,128)S(1)}, f32[1,168,128]{2,1,0:T(8,128)S(1)}, u32[]{:S(2)}, u32[]{:S(2)}) collective-permute-start(f32[1,168,128]{2,1,0:T(8,128)S(1)} %get-tuple-element.56.part0_ref), channel_id=1, source_target_pairs={{0,6},{1,7},{2,4},{3,5},{4,2},{5,3},{6,0},{7,1},{8,14},{9,15},{10,... | collective-permute-start | bytes 258056 | tf_op jit(solution)/shard_map/ppermute | solution.py:868
  50.1 2.1 %collective-permute-start.9 = (f32[1,168,128]{2,1,0:T(8,128)S(1)}, f32[1,168,128]{2,1,0:T(8,128)S(1)}, u32[]{:S(2)}, u32[]{:S(2)}) collective-permute-start(f32[1,168,128]{2,1,0:T(8,128)S(1)} %get-tuple-element.56.part0_ref), channel_id=1, source_target_pairs={{0,4},{1,5},{2,6},{3,7},{4,0},{5,1},{6,2},{7,3},{8,12},{9,13},{10,... | collective-permute-start | bytes 258056 | tf_op jit(solution)/shard_map/ppermute | solution.py:868
  53.2 3.6 %collective-permute-done.9.part2_ref = f32[1,168,128]{2,1,0:T(8,128)S(1)} collective-permute-done((f32[1,168,128]{2,1,0:T(8,128)S(1)}, f32[1,168,128]{2,1,0:T(8,128)S(1)}, u32[]{:S(2)}, u32[]{:S(2)}) %collective-permute-start.9) | collective-permute-done | bytes 86048 | tf_op jit(solution)/shard_map/ppermute | solution.py:868
  57.0 2.4 %shard_map.115 = (f32[8,40,128]{2,1,0:T(8,128)S(1)}, f32[6,16,128]{2,1,0:T(8,128)S(1)}, f32[8,128]{1,0:T(8,128)S(1)}, bf16[2,14,128,128]{3,2,1,0:T(8,128)(2,1)S(1)}, f32[72,128]{1,0:T(8,128)S(1)}) custom-call(s32[1]{0:T(128)} %bitcast.me_ref, f32[1,168,128]{2,1,0:T(8,128)S(1)} %get-tuple-element.56.part0_ref, ...), custom_call_target="tpu_custom_call" | custom-call | flops 6000000000 | tf_op jit(solution)/shard_map/pallas_call | solution.py:826
  59.5 11.9 %all_to_all.16.recv_ref = f32[8,40,128]{2,1,0:T(8,128)S(1)} all-to-all(f32[8,40,128]{2,1,0:T(8,128)S(1)} %get-tuple-element.59), channel_id=1, replica_groups={{0,8,16,24,32,40,48,56},{1,9,17,25,33,41,49,57},{2,10,18,26,34,42,50,58..., dimensions={0} | all-to-all | bytes 327680 | tf_op jit(solution)/shard_map/all_to_all | solution.py:874
  71.4 1.3 %shard_map.116 = (f32[1,112,128]{2,1,0:T(8,128)S(1)}, f32[9,16,128]{2,1,0:T(8,128)S(1)}, f32[8,128]{1,0:T(8,128)S(1)}) custom-call(s32[1]{0:T(128)} %bitcast.me_ref, f32[8,40,128]{2,1,0:T(8,128)S(1)} %all_to_all.16.recv_ref, f32[7,256,128]{2,1,0:T(8,128)S(1)} %copy-done.3, f32[7,256,128]{2,1,0:T(8,128)S(1)} %copy-done.4, f32[8,2,128,128]{3,2,1,0:T(8,128)S(1)} %copy-done.2, ...), custom_call_target="tpu_custom_call" | custom-call | flops 6000000000 | tf_op jit(solution)/shard_map/pallas_call | solution.py:826
  72.7 1.4 %collective-permute-start.13 = (f32[1,112,128]{2,1,0:T(8,128)S(1)}, f32[1,112,128]{2,1,0:T(8,128)S(1)}, u32[]{:S(2)}, u32[]{:S(2)}) collective-permute-start(f32[1,112,128]{2,1,0:T(8,128)S(1)} %get-tuple-element.62.part0_ref), channel_id=1, source_target_pairs={{0,192},{1,193},{2,194},{3,195},{4,196},{5,197},{6,198},{7,199},{8... | collective-permute-start | bytes 172040 | tf_op jit(solution)/shard_map/ppermute | solution.py:868
  75.0 1.9 %collective-permute-start.11 = (f32[1,112,128]{2,1,0:T(8,128)S(1)}, f32[1,112,128]{2,1,0:T(8,128)S(1)}, u32[]{:S(2)}, u32[]{:S(2)}) collective-permute-start(f32[1,112,128]{2,1,0:T(8,128)S(1)} %get-tuple-element.62.part0_ref), channel_id=1, source_target_pairs={{0,64},{1,65},{2,66},{3,67},{4,68},{5,69},{6,70},{7,71},{8,72},{9,... | collective-permute-start | bytes 172040 | tf_op jit(solution)/shard_map/ppermute | solution.py:868
  76.8 1.3 %collective-permute-done.13.part3_ref = f32[1,112,128]{2,1,0:T(8,128)S(1)} collective-permute-done((f32[1,112,128]{2,1,0:T(8,128)S(1)}, f32[1,112,128]{2,1,0:T(8,128)S(1)}, u32[]{:S(2)}, u32[]{:S(2)}) %collective-permute-start.13) | collective-permute-done | bytes 57376 | tf_op jit(solution)/shard_map/ppermute | solution.py:868
  78.1 1.6 %collective-permute-done.12.part2_ref = f32[1,112,128]{2,1,0:T(8,128)S(1)} collective-permute-done((f32[1,112,128]{2,1,0:T(8,128)S(1)}, f32[1,112,128]{2,1,0:T(8,128)S(1)}, u32[]{:S(2)}, u32[]{:S(2)}) %collective-permute-start.12) | collective-permute-done | bytes 57376 | tf_op jit(solution)/shard_map/ppermute | solution.py:868
  79.7 6.7 %shard_map.117 = (f32[16,1024]{1,0:T(8,128)S(1)}, f32[16,1024]{1,0:T(8,128)S(1)}, f32[16,128]{1,0:T(8,128)S(1)}, f32[16,128]{1,0:T(8,128)S(1)}, f32[1,40,128]{2,...) custom-call(s32[1]{0:T(128)} %bitcast.me_ref, s32[4]{0:T(128)S(1)} %copy-done.10, ...), custom_call_target="tpu_custom_call" | custom-call | flops 6000000000 | tf_op jit(solution)/shard_map/pallas_call | solution.py:826
  86.4 1.2 %collective-permute-done.14.refs_1_ = f32[1,40,128]{2,1,0:T(8,128)S(1)} collective-permute-done((f32[1,40,128]{2,1,0:T(8,128)S(1)}, f32[1,40,128]{2,1,0:T(8,128)S(1)}, u32[]{:S(2)}, u32[]{:S(2)}) %collective-permute-start.14) | collective-permute-done | bytes 20512 | tf_op jit(solution)/shard_map/ppermute | solution.py:868
  88.1 1.2 %collective-permute-start.17 = (f32[1,40,128]{2,1,0:T(8,128)S(1)}, f32[1,40,128]{2,1,0:T(8,128)S(1)}, u32[]{:S(2)}, u32[]{:S(2)}) collective-permute-start(f32[1,40,128]{2,1,0:T(8,128)S(1)} %shard_map.118.refs_0_), channel_id=1, source_target_pairs={{0,6},{1,7},{2,4},{3,5},{4,2},{5,3},{6,0},{7,1},{8,14},{9,15},{10,... | collective-permute-start | bytes 61448 | tf_op jit(solution)/shard_map/ppermute | solution.py:868
  89.3 2.1 %collective-permute-start.16 = (f32[1,40,128]{2,1,0:T(8,128)S(1)}, f32[1,40,128]{2,1,0:T(8,128)S(1)}, u32[]{:S(2)}, u32[]{:S(2)}) collective-permute-start(f32[1,40,128]{2,1,0:T(8,128)S(1)} %shard_map.118.refs_0_), channel_id=1, source_target_pairs={{0,4},{1,5},{2,6},{3,7},{4,0},{5,1},{6,2},{7,3},{8,12},{9,13},{10,... | collective-permute-start | bytes 61448 | tf_op jit(solution)/shard_map/ppermute | solution.py:868
  92.3 2.4 %collective-permute-done.16.refs_2_ = f32[1,40,128]{2,1,0:T(8,128)S(1)} collective-permute-done((f32[1,40,128]{2,1,0:T(8,128)S(1)}, f32[1,40,128]{2,1,0:T(8,128)S(1)}, u32[]{:S(2)}, u32[]{:S(2)}) %collective-permute-start.16) | collective-permute-done | bytes 20512 | tf_op jit(solution)/shard_map/ppermute | solution.py:868
  96.1 11.8 %all_to_all.17.refs_0_ = f32[8,40,128]{2,1,0:T(8,128)S(1)} all-to-all(f32[8,40,128]{2,1,0:T(8,128)S(1)} %shard_map.119), channel_id=1, replica_groups={{0,8,16,24,32,40,48,56},{1,9,17,25,33,41,49,57},{2,10,18,26,34,42,50,58..., dimensions={0} | all-to-all | bytes 327680 | tf_op jit(solution)/shard_map/all_to_all | solution.py:874
  107.9 1.3 %shard_map.120.part0_ref = f32[1,40,128]{2,1,0:T(8,128)S(1)} custom-call(s32[1]{0:T(128)} %bitcast.me_ref, f32[8,40,128]{2,1,0:T(8,128)S(1)} %all_to_all.17.refs_0_, f32[7,256,128]{2,1,0:T(8,128)S(1)} %copy-done.3, f32[7,256,128]{2,1,0:T(8,128)S(1)} %copy-done.4, f32[8,2,128,128]{3,2,1,0:T(8,128)S(1)} %copy-done.2, ...), custom_call_target="tpu_custom_call" | custom-call | flops 6000000000 | tf_op jit(solution)/shard_map/pallas_call | solution.py:826
  109.2 2.0 %collective-permute-start.20 = (f32[1,40,128]{2,1,0:T(8,128)S(1)}, f32[1,40,128]{2,1,0:T(8,128)S(1)}, u32[]{:S(2)}, u32[]{:S(2)}) collective-permute-start(f32[1,40,128]{2,1,0:T(8,128)S(1)} %shard_map.120.part0_ref), channel_id=1, source_target_pairs={{0,192},{1,193},{2,194},{3,195},{4,196},{5,197},{6,198},{7,199},{8... | collective-permute-start | bytes 61448 | tf_op jit(solution)/shard_map/ppermute | solution.py:868
  111.2 1.4 %collective-permute-start.19 = (f32[1,40,128]{2,1,0:T(8,128)S(1)}, f32[1,40,128]{2,1,0:T(8,128)S(1)}, u32[]{:S(2)}, u32[]{:S(2)}) collective-permute-start(f32[1,40,128]{2,1,0:T(8,128)S(1)} %shard_map.120.part0_ref), channel_id=1, source_target_pairs={{0,128},{1,129},{2,130},{3,131},{4,132},{5,133},{6,134},{7,135},{8... | collective-permute-start | bytes 61448 | tf_op jit(solution)/shard_map/ppermute | solution.py:868
  114.2 2.2 %collective-permute-done.19.part2_ref = f32[1,40,128]{2,1,0:T(8,128)S(1)} collective-permute-done((f32[1,40,128]{2,1,0:T(8,128)S(1)}, f32[1,40,128]{2,1,0:T(8,128)S(1)}, u32[]{:S(2)}, u32[]{:S(2)}) %collective-permute-start.19) | collective-permute-done | bytes 20512 | tf_op jit(solution)/shard_map/ppermute | solution.py:868
  116.5 1.6 %shard_map.121 = f32[16,1024]{1,0:T(8,128)} custom-call(s32[1]{0:T(128)} %bitcast.me_ref, f32[1,40,128]{2,1,0:T(8,128)S(1)} %shard_map.120.part0_ref, f32[1,40,128]{2,1,0:T(8,128)S(1)} %collective-permute-done.18.part1_ref, f32[1,40,128]{2,1,0:T(8,128)S(1)} %collective-permute-done.19.part2_ref, f32[1,40,128]{2,1,0:T(8,128)S(1)} %collective-permute-done.20.part3_ref, ...), custom_call_target="tpu_custom_call" | custom-call | flops 6000000000 | tf_op jit(solution)/shard_map/pallas_call | solution.py:826
  (50 shorter events, 12.7 us)
Async XLA Ops:
  0.0 5.4 %copy-start.3 = (f32[7,256,128]{2,1,0:T(8,128)S(1)}, f32[7,256,128]{2,1,0:T(8,128)}, u32[]{:S(2)}) copy-start(f32[7,256,128]{2,1,0:T(8,128)} %up_row_ref.17) | copy-start | bytes 2752516
  3.9 11.4 %copy-start.2 = (f32[8,2,128,128]{3,2,1,0:T(8,128)S(1)}, f32[8,2,128,128]{3,2,1,0:T(8,128)}, u32[]{:S(2)}) copy-start(f32[8,2,128,128]{3,2,1,0:T(8,128)} %up_couple_ref.13) | copy-start | bytes 3145732
  3.9 11.4 %copy-start.4 = (f32[7,256,128]{2,1,0:T(8,128)S(1)}, f32[7,256,128]{2,1,0:T(8,128)}, u32[]{:S(2)}) copy-start(f32[7,256,128]{2,1,0:T(8,128)} %up_col_ref.13) | copy-start | bytes 2752516
  3.9 1.5 %collective-permute-start = (f32[1,88,128]{2,1,0:T(8,128)}, f32[1,88,128]{2,1,0:T(8,128)S(1)}, u32[]{:S(2)}, u32[]{:S(2)}) collective-permute-start(f32[1,88,128]{2,1,0:T(8,128)} %get-tuple-element.42.part0_ref), channel_id=1, source_target_pairs={{0,1},{1,0},{2,3},{3,2},{4,5},{5,4},{6,7},{7,6},{8,9},{9,8},{10,11... | collective-permute-start | bytes 135176 | tf_op jit(solution)/shard_map/ppermute | solution.py:868
  6.9 4.4 %collective-permute-start.3 = (f32[1,88,128]{2,1,0:T(8,128)S(1)}, f32[1,88,128]{2,1,0:T(8,128)S(1)}, u32[]{:S(2)}, u32[]{:S(2)}) collective-permute-start(f32[1,88,128]{2,1,0:T(8,128)S(1)} %get-tuple-element.43.part0_ref), channel_id=1, source_target_pairs={{0,6},{1,7},{2,4},{3,5},{4,2},{5,3},{6,0},{7,1},{8,14},{9,15},{10,... | collective-permute-start | bytes 135176 | tf_op jit(solution)/shard_map/ppermute | solution.py:868
  8.4 5.9 %collective-permute-start.2 = (f32[1,88,128]{2,1,0:T(8,128)S(1)}, f32[1,88,128]{2,1,0:T(8,128)S(1)}, u32[]{:S(2)}, u32[]{:S(2)}) collective-permute-start(f32[1,88,128]{2,1,0:T(8,128)S(1)} %get-tuple-element.43.part0_ref), channel_id=1, source_target_pairs={{0,4},{1,5},{2,6},{3,7},{4,0},{5,1},{6,2},{7,3},{8,12},{9,13},{10,... | collective-permute-start | bytes 135176 | tf_op jit(solution)/shard_map/ppermute | solution.py:868
  11.3 4.0 %collective-permute-start.1 = (f32[1,88,128]{2,1,0:T(8,128)S(1)}, f32[1,88,128]{2,1,0:T(8,128)S(1)}, u32[]{:S(2)}, u32[]{:S(2)}) collective-permute-start(f32[1,88,128]{2,1,0:T(8,128)S(1)} %get-tuple-element.43.part0_ref), channel_id=1, source_target_pairs={{0,2},{1,3},{2,0},{3,1},{4,6},{5,7},{6,4},{7,5},{8,10},{9,11},{10,... | collective-permute-start | bytes 135176 | tf_op jit(solution)/shard_map/ppermute | solution.py:868
  33.0 9.5 %copy-start = (f32[4,512,256]{2,1,0:T(8,128)S(1)}, f32[4,512,256]{2,1,0:T(8,128)}, u32[]{:S(2)}) copy-start(f32[4,512,256]{2,1,0:T(8,128)} %dense_ref.3) | copy-start | bytes 6291460
  33.0 9.5 %copy-start.1 = (f32[4,512,128]{2,1,0:T(8,128)S(1)}, f32[4,512,128]{2,1,0:T(8,128)}, u32[]{:S(2)}) copy-start(f32[4,512,128]{2,1,0:T(8,128)} %row_basis_ref.3) | copy-start | bytes 3145732
  33.0 9.5 %copy-start.5 = (f32[4,256,128]{2,1,0:T(8,128)S(1)}, f32[4,256,128]{2,1,0:T(8,128)}, u32[]{:S(2)}) copy-start(f32[4,256,128]{2,1,0:T(8,128)} %col_basis_ref.3) | copy-start | bytes 1572868
  33.0 9.6 %copy-start.6 = (f32[3,256,128]{2,1,0:T(8,128)S(1)}, f32[3,256,128]{2,1,0:T(8,128)}, u32[]{:S(2)}) copy-start(f32[3,256,128]{2,1,0:T(8,128)} %local_row_ref.3) | copy-start | bytes 1179652
  33.0 9.6 %copy-start.7 = (f32[3,256,128]{2,1,0:T(8,128)S(1)}, f32[3,256,128]{2,1,0:T(8,128)}, u32[]{:S(2)}) copy-start(f32[3,256,128]{2,1,0:T(8,128)} %local_col_ref.3) | copy-start | bytes 1179652
  33.0 9.6 %copy-start.8 = (f32[3,2,128,128]{3,2,1,0:T(8,128)S(1)}, f32[3,2,128,128]{3,2,1,0:T(8,128)}, u32[]{:S(2)}) copy-start(f32[3,2,128,128]{3,2,1,0:T(8,128)} %local_couple_ref.3) | copy-start | bytes 1179652
  33.0 9.6 %copy-start.10 = (s32[4]{0:T(128)S(1)}, s32[4]{0:T(128)}, u32[]{:S(2)}) copy-start(s32[4]{0:T(128)} %rows_ref.3) | copy-start | bytes 52
  33.0 9.6 %copy-start.11 = (f32[16,2816]{1,0:T(8,128)S(1)}, f32[16,2816]{1,0:T(8,128)}, u32[]{:S(2)}) copy-start(f32[16,2816]{1,0:T(8,128)} %get-tuple-element.53.z_ref) | copy-start | bytes 540676
  34.2 5.0 %collective-permute-start.6 = (f32[1,24,128]{2,1,0:T(8,128)S(1)}, f32[1,24,128]{2,1,0:T(8,128)S(1)}, u32[]{:S(2)}, u32[]{:S(2)}) collective-permute-start(f32[1,24,128]{2,1,0:T(8,128)S(1)} %get-tuple-element.46.part0_ref), channel_id=1, source_target_pairs={{0,192},{1,193},{2,194},{3,195},{4,196},{5,197},{6,198},{7,199},{8... | collective-permute-start | bytes 36872 | tf_op jit(solution)/shard_map/ppermute | solution.py:868
  37.3 5.2 %collective-permute-start.5 = (f32[1,24,128]{2,1,0:T(8,128)S(1)}, f32[1,24,128]{2,1,0:T(8,128)S(1)}, u32[]{:S(2)}, u32[]{:S(2)}) collective-permute-start(f32[1,24,128]{2,1,0:T(8,128)S(1)} %get-tuple-element.46.part0_ref), channel_id=1, source_target_pairs={{0,128},{1,129},{2,130},{3,131},{4,132},{5,133},{6,134},{7,135},{8... | collective-permute-start | bytes 36872 | tf_op jit(solution)/shard_map/ppermute | solution.py:868
  38.0 4.6 %collective-permute-start.4 = (f32[1,24,128]{2,1,0:T(8,128)S(1)}, f32[1,24,128]{2,1,0:T(8,128)S(1)}, u32[]{:S(2)}, u32[]{:S(2)}) collective-permute-start(f32[1,24,128]{2,1,0:T(8,128)S(1)} %get-tuple-element.46.part0_ref), channel_id=1, source_target_pairs={{0,64},{1,65},{2,66},{3,67},{4,68},{5,69},{6,70},{7,71},{8,72},{9,... | collective-permute-start | bytes 36872 | tf_op jit(solution)/shard_map/ppermute | solution.py:868
  46.8 1.2 %collective-permute-start.7 = (f32[1,104,128]{2,1,0:T(8,128)S(1)}, f32[1,104,128]{2,1,0:T(8,128)S(1)}, u32[]{:S(2)}, u32[]{:S(2)}) collective-permute-start(f32[1,104,128]{2,1,0:T(8,128)S(1)} %get-tuple-element.54.part0_ref), channel_id=1, source_target_pairs={{0,1},{1,0},{2,3},{3,2},{4,5},{5,4},{6,7},{7,6},{8,9},{9,8},{10,11... | collective-permute-start | bytes 159752 | tf_op jit(solution)/shard_map/ppermute | solution.py:868
  48.6 4.7 %collective-permute-start.10 = (f32[1,168,128]{2,1,0:T(8,128)S(1)}, f32[1,168,128]{2,1,0:T(8,128)S(1)}, u32[]{:S(2)}, u32[]{:S(2)}) collective-permute-start(f32[1,168,128]{2,1,0:T(8,128)S(1)} %get-tuple-element.56.part0_ref), channel_id=1, source_target_pairs={{0,6},{1,7},{2,4},{3,5},{4,2},{5,3},{6,0},{7,1},{8,14},{9,15},{10,... | collective-permute-start | bytes 258056 | tf_op jit(solution)/shard_map/ppermute | solution.py:868
  50.1 6.7 %collective-permute-start.9 = (f32[1,168,128]{2,1,0:T(8,128)S(1)}, f32[1,168,128]{2,1,0:T(8,128)S(1)}, u32[]{:S(2)}, u32[]{:S(2)}) collective-permute-start(f32[1,168,128]{2,1,0:T(8,128)S(1)} %get-tuple-element.56.part0_ref), channel_id=1, source_target_pairs={{0,4},{1,5},{2,6},{3,7},{4,0},{5,1},{6,2},{7,3},{8,12},{9,13},{10,... | collective-permute-start | bytes 258056 | tf_op jit(solution)/shard_map/ppermute | solution.py:868
  52.2 4.8 %collective-permute-start.8 = (f32[1,168,128]{2,1,0:T(8,128)S(1)}, f32[1,168,128]{2,1,0:T(8,128)S(1)}, u32[]{:S(2)}, u32[]{:S(2)}) collective-permute-start(f32[1,168,128]{2,1,0:T(8,128)S(1)} %get-tuple-element.56.part0_ref), channel_id=1, source_target_pairs={{0,2},{1,3},{2,0},{3,1},{4,6},{5,7},{6,4},{7,5},{8,10},{9,11},{10,... | collective-permute-start | bytes 258056 | tf_op jit(solution)/shard_map/ppermute | solution.py:868
  72.7 5.5 %collective-permute-start.13 = (f32[1,112,128]{2,1,0:T(8,128)S(1)}, f32[1,112,128]{2,1,0:T(8,128)S(1)}, u32[]{:S(2)}, u32[]{:S(2)}) collective-permute-start(f32[1,112,128]{2,1,0:T(8,128)S(1)} %get-tuple-element.62.part0_ref), channel_id=1, source_target_pairs={{0,192},{1,193},{2,194},{3,195},{4,196},{5,197},{6,198},{7,199},{8... | collective-permute-start | bytes 172040 | tf_op jit(solution)/shard_map/ppermute | solution.py:868
  74.0 5.7 %collective-permute-start.12 = (f32[1,112,128]{2,1,0:T(8,128)S(1)}, f32[1,112,128]{2,1,0:T(8,128)S(1)}, u32[]{:S(2)}, u32[]{:S(2)}) collective-permute-start(f32[1,112,128]{2,1,0:T(8,128)S(1)} %get-tuple-element.62.part0_ref), channel_id=1, source_target_pairs={{0,128},{1,129},{2,130},{3,131},{4,132},{5,133},{6,134},{7,135},{8... | collective-permute-start | bytes 172040 | tf_op jit(solution)/shard_map/ppermute | solution.py:868
  75.0 4.8 %collective-permute-start.11 = (f32[1,112,128]{2,1,0:T(8,128)S(1)}, f32[1,112,128]{2,1,0:T(8,128)S(1)}, u32[]{:S(2)}, u32[]{:S(2)}) collective-permute-start(f32[1,112,128]{2,1,0:T(8,128)S(1)} %get-tuple-element.62.part0_ref), channel_id=1, source_target_pairs={{0,64},{1,65},{2,66},{3,67},{4,68},{5,69},{6,70},{7,71},{8,72},{9,... | collective-permute-start | bytes 172040 | tf_op jit(solution)/shard_map/ppermute | solution.py:868
  86.4 1.2 %collective-permute-start.14 = (f32[1,40,128]{2,1,0:T(8,128)S(1)}, f32[1,40,128]{2,1,0:T(8,128)S(1)}, u32[]{:S(2)}, u32[]{:S(2)}) collective-permute-start(f32[1,40,128]{2,1,0:T(8,128)S(1)} %get-tuple-element.72.refs_0_), channel_id=1, source_target_pairs={{0,1},{1,0},{2,3},{3,2},{4,5},{5,4},{6,7},{7,6},{8,9},{9,8},{10,11... | collective-permute-start | bytes 61448 | tf_op jit(solution)/shard_map/ppermute | solution.py:868
  88.1 4.2 %collective-permute-start.17 = (f32[1,40,128]{2,1,0:T(8,128)S(1)}, f32[1,40,128]{2,1,0:T(8,128)S(1)}, u32[]{:S(2)}, u32[]{:S(2)}) collective-permute-start(f32[1,40,128]{2,1,0:T(8,128)S(1)} %shard_map.118.refs_0_), channel_id=1, source_target_pairs={{0,6},{1,7},{2,4},{3,5},{4,2},{5,3},{6,0},{7,1},{8,14},{9,15},{10,... | collective-permute-start | bytes 61448 | tf_op jit(solution)/shard_map/ppermute | solution.py:868
  89.3 5.3 %collective-permute-start.16 = (f32[1,40,128]{2,1,0:T(8,128)S(1)}, f32[1,40,128]{2,1,0:T(8,128)S(1)}, u32[]{:S(2)}, u32[]{:S(2)}) collective-permute-start(f32[1,40,128]{2,1,0:T(8,128)S(1)} %shard_map.118.refs_0_), channel_id=1, source_target_pairs={{0,4},{1,5},{2,6},{3,7},{4,0},{5,1},{6,2},{7,3},{8,12},{9,13},{10,... | collective-permute-start | bytes 61448 | tf_op jit(solution)/shard_map/ppermute | solution.py:868
  91.4 3.8 %collective-permute-start.15 = (f32[1,40,128]{2,1,0:T(8,128)S(1)}, f32[1,40,128]{2,1,0:T(8,128)S(1)}, u32[]{:S(2)}, u32[]{:S(2)}) collective-permute-start(f32[1,40,128]{2,1,0:T(8,128)S(1)} %shard_map.118.refs_0_), channel_id=1, source_target_pairs={{0,2},{1,3},{2,0},{3,1},{4,6},{5,7},{6,4},{7,5},{8,10},{9,11},{10,... | collective-permute-start | bytes 61448 | tf_op jit(solution)/shard_map/ppermute | solution.py:868
  109.2 5.1 %collective-permute-start.20 = (f32[1,40,128]{2,1,0:T(8,128)S(1)}, f32[1,40,128]{2,1,0:T(8,128)S(1)}, u32[]{:S(2)}, u32[]{:S(2)}) collective-permute-start(f32[1,40,128]{2,1,0:T(8,128)S(1)} %shard_map.120.part0_ref), channel_id=1, source_target_pairs={{0,192},{1,193},{2,194},{3,195},{4,196},{5,197},{6,198},{7,199},{8... | collective-permute-start | bytes 61448 | tf_op jit(solution)/shard_map/ppermute | solution.py:868
  111.2 5.3 %collective-permute-start.19 = (f32[1,40,128]{2,1,0:T(8,128)S(1)}, f32[1,40,128]{2,1,0:T(8,128)S(1)}, u32[]{:S(2)}, u32[]{:S(2)}) collective-permute-start(f32[1,40,128]{2,1,0:T(8,128)S(1)} %shard_map.120.part0_ref), channel_id=1, source_target_pairs={{0,128},{1,129},{2,130},{3,131},{4,132},{5,133},{6,134},{7,135},{8... | collective-permute-start | bytes 61448 | tf_op jit(solution)/shard_map/ppermute | solution.py:868
  112.6 3.9 %collective-permute-start.18 = (f32[1,40,128]{2,1,0:T(8,128)S(1)}, f32[1,40,128]{2,1,0:T(8,128)S(1)}, u32[]{:S(2)}, u32[]{:S(2)}) collective-permute-start(f32[1,40,128]{2,1,0:T(8,128)S(1)} %shard_map.120.part0_ref), channel_id=1, source_target_pairs={{0,64},{1,65},{2,66},{3,67},{4,68},{5,69},{6,70},{7,71},{8,72},{9,... | collective-permute-start | bytes 61448 | tf_op jit(solution)/shard_map/ppermute | solution.py:868
  (1 other events, 0.8 us)

commit v6 on v5

--- a/solution.py
+++ b/solution.py
@@ -15,8 +15,8 @@
 HALF = RANK // 2
 SLICE = 8
 COST_FLOPS = 6000000000
-KEEP = LEAF_DEV * LEAF_ROWS
 TINY = 1.2e-38
+ORDER = (0, 1, 3, 2)
 NEAR = 8
 STAGES = {"core": (0, 1), "row": (1, 2), "mid": (3, 3), "far": (6, 2)}
 VMEM_MIB = 24
@@ -52,14 +52,17 @@
     return both[:m] + (both[m:] + rest)
 
 
+def gram_of(a):
+    high, low = split(a)
+    dims = (((0,), (0,)), ((), ()))
+    rest = lax.dot_general(high, low, dims, preferred_element_type=f32)
+    return lax.dot_general(high, high, dims, preferred_element_type=f32) + (rest + jnp.transpose(rest))
+
+
 def pair_at(ref, *index):
     if ref.dtype == bf16:
         return ref[(0,) + index], ref[(1,) + index]
     return split(ref[index])
-
-
-def pairs_of(ref):
-    return functools.partial(pair_at, ref)
 
 
 def half_of(ref, j, child):
@@ -135,39 +138,8 @@
     return out
 
 
-def local_up(parts, basis, transfer):
-    leaf = [mm(parts[q], basis(q)) for q in range(LEAF_DEV)]
-    node = [
-        mm(jnp.concatenate([leaf[2 * m], leaf[2 * m + 1]], 1), transfer(m)) for m in range(2)
-    ]
-    return leaf, node
-
-
-def local_root(node, transfer):
-    return mm(jnp.concatenate(node, 1), transfer(2))
-
-
-def couple(sibling, coupling, node, child, adjoint):
-    if adjoint:
-        return mm(sibling, coupling(node, 1 - child), transposed=True)
-    return mm(sibling, coupling(node, child))
-
-
-def local_down(root, leaf, node, coupling, transfer, adjoint):
-    spread = None if root is None else mm(root, transfer(2), transposed=True)
-    out = []
-    for m in range(2):
-        here = None if spread is None else spread[:, m * RANK : (m + 1) * RANK]
-        if node is not None:
-            gained = couple(node[1 - m], coupling, 2, m, adjoint)
-            here = gained if here is None else here + gained
-        below = mm(here, transfer(m), transposed=True)
-        for i in range(2):
-            value = below[:, i * RANK : (i + 1) * RANK]
-            if leaf is not None:
-                value = value + couple(leaf[2 * m + 1 - i], coupling, m, i, adjoint)
-            out.append(value)
-    return out
+def lanes(value, k):
+    return value[:, k * RANK : (k + 1) * RANK]
 
 
 def live_mask(rows_ref, q):
@@ -184,31 +156,99 @@
 
 
 def pair_up(parts, local, rows_ref, msg_ref, own_ref, inner_ref, extra):
-    dense, row_basis, col_basis, local_row, local_col, coupling = local
+    dense_ref, row_basis_ref, col_basis_ref, cross_ref, columns_ref, paths_ref, images_ref = local
     squares = sum_squares(parts[0])
     for part in parts[1:]:
         squares = squares + sum_squares(part)
     scale = inverse_norm(squares)
-    parts = [part * scale for part in parts]
-    leaf, node = local_up(parts, col_basis, local_col)
-    root = local_root(node, local_col)
-    down = local_down(None, leaf, node, coupling, local_row, False)
-    result = []
+    whole = jnp.concatenate(parts, 1)
+    root = mm(whole, pair_at(columns_ref)) * scale
+    leaf = [mm(parts[q], pair_at(col_basis_ref, q)) for q in range(LEAF_DEV)]
+    down = mm(jnp.concatenate(leaf, 1), pair_at(cross_ref))
     energy = jnp.zeros((RHS, 1), f32)
+    rows = []
     for q in range(LEAF_DEV):
-        y = mm(parts[q], dense(q), transposed=True)
-        y = y + mm(down[q], row_basis(q), transposed=True)
-        y = y * live_mask(rows_ref, q)
+        y = mm(parts[q], pair_at(dense_ref, q), transposed=True)
+        y = y + mm(lanes(down, q), pair_at(row_basis_ref, q), transposed=True)
+        y = y * (live_mask(rows_ref, q) * scale)
         if inner_ref is not None:
             inner_ref[:, row_part(q)] = y
         energy = energy + sum_squares(y)
-        result.append(y)
-    _, row_node = local_up(result, row_basis, local_row)
-    row_root = local_root(row_node, local_row)
+        if images_ref is None:
+            rows.append(mm(y, pair_at(row_basis_ref, q)))
+    if images_ref is None:
+        row_root = mm(jnp.concatenate(rows, 1), pair_at(paths_ref))
+    else:
+        row_root = mm(whole * scale, pair_at(images_ref), transposed=True)
     stats = stat_block(row_of(squares), row_of(energy))
     if own_ref is not None:
         own_ref[...] = stats
     send(msg_ref, stack([root, row_root, stats] + extra))
+
+
+def paths_kernel(
+    order_ref,
+    col_basis_ref,
+    local_row_ref,
+    local_col_ref,
+    local_couple_ref,
+    cross_ref,
+    columns_ref,
+    paths_ref,
+):
+    del order_ref
+    halves = [slice(0, RANK), slice(RANK, 2 * RANK)]
+
+    def store(ref, index, value):
+        high, low = split(value)
+        ref[(0,) + index] = high
+        ref[(1,) + index] = low
+
+    def part(q, size=RANK):
+        return slice(q * size, (q + 1) * size)
+
+    for q in range(LEAF_DEV):
+        m, i = q // 2, q % 2
+        store(cross_ref, (part(q), part(q)), jnp.zeros((RANK, RANK), f32))
+        store(cross_ref, (part(q), part(q ^ 1)), local_couple_ref[m, 1 - i])
+        gained = mm(local_col_ref[m, halves[i]], pair_at(local_couple_ref, 2, 1 - m))
+        spread = mm(gained, pair_at(local_row_ref, 1 - m), transposed=True)
+        store(cross_ref, (part(q), slice(2 * (1 - m) * RANK, 2 * (2 - m) * RANK)), spread)
+        store(paths_ref, (part(q),), mm(local_row_ref[m, halves[i]], split(local_row_ref[2, halves[m]])))
+        path = mm(local_col_ref[m, halves[i]], split(local_col_ref[2, halves[m]]))
+        store(columns_ref, (part(q, LEAF_COLS),), mm(col_basis_ref[q], split(path)))
+
+
+def images_kernel(
+    order_ref, rows_ref, dense_ref, row_basis_ref, col_basis_ref, cross_ref, paths_ref, images_ref
+):
+    del order_ref
+    turned = []
+    images = []
+    moved = []
+    for q in range(LEAF_DEV):
+        path = pair_at(paths_ref, slice(q * RANK, (q + 1) * RANK))
+        turned.append(jnp.transpose(path[0].astype(f32) + path[1].astype(f32)))
+        slots = lax.broadcasted_iota(jnp.int32, (LEAF_ROWS, RANK), 0)
+        basis = jnp.where(slots < rows_ref[q], row_basis_ref[q], 0.0)
+        images.append(mm_inner(basis, dense_ref[q]))
+        moved.append(mm(turned[q], split(gram_of(basis))))
+    inner = mm(jnp.concatenate(moved, 1), pair_at(cross_ref), transposed=True)
+    for q in range(LEAF_DEV):
+        image = mm(turned[q], split(images[q]))
+        image = image + mm(lanes(inner, q), pair_at(col_basis_ref, q), transposed=True)
+        high, low = split(image)
+        images_ref[0, :, col_part(q)] = high
+        images_ref[1, :, col_part(q)] = low
+
+
+def inner_kernel(order_ref, y_ref, dense_ref, row_basis_ref, col_basis_ref, cross_ref, x_ref):
+    del order_ref
+    leaf = [mm(y_ref[:, row_part(q)], pair_at(row_basis_ref, q)) for q in range(LEAF_DEV)]
+    down = mm(jnp.concatenate(leaf, 1), pair_at(cross_ref), transposed=True)
+    for q in range(LEAF_DEV):
+        x = mm(y_ref[:, row_part(q)], pair_at(dense_ref, q))
+        x_ref[:, col_part(q)] = x + mm(lanes(down, q), pair_at(col_basis_ref, q), transposed=True)
 
 
 def both_sides(grams, half):
@@ -266,7 +306,7 @@
 
 
 def gather_parts(me, name, parts, out_ref):
-    for k, part in enumerate(parts):
+    for k, part in zip(ORDER, parts):
         out_ref[place_of(me, name) ^ k] = part[0]
 
 
@@ -313,7 +353,11 @@
     for copy in start_copies(pairs, sems):
         copy.wait()
     squares = jnp.zeros((RHS, 1), f32)
-    local_row = [split(local_row_ref[m]) for m in range(3)]
+    paths = []
+    for q in range(LEAF_DEV):
+        m, i = q // 2, q % 2
+        top = split(local_row_ref[2, m * RANK : (m + 1) * RANK])
+        paths.append(mm(local_row_ref[m, i * RANK : (i + 1) * RANK], top))
     leaf = []
     grams = []
     for q in range(LEAF_DEV):
@@ -324,14 +368,11 @@
     for q in range(LEAF_DEV):
         slots = lax.broadcasted_iota(jnp.int32, (LEAF_ROWS, RANK), 0)
         basis = jnp.where(slots < rows_ref[q], row_basis_ref[q], 0.0)
-        grams.append(mm_inner(basis, basis))
-    node = [climb(leaf[2 * m : 2 * m + 2], local_row[m])[0] for m in range(2)]
-    for k, value in enumerate(leaf + node):
-        z_ref[:, KEEP + k * RANK : KEEP + (k + 1) * RANK] = value
-    root = climb(node, local_row[2])[0]
+        grams.append(gram_of(basis))
+    root = mm(jnp.concatenate(leaf, 1), split(stack(paths)))
     row = row_of(squares)
-    nodes = [gram_climb(grams[2 * m : 2 * m + 2], local_row[m])[0] for m in range(2)]
-    gram = gram_climb(nodes, local_row[2])[0]
+    left = [mm(jnp.transpose(paths[q]), split(grams[q])) for q in range(LEAF_DEV)]
+    gram = mm(jnp.concatenate(left, 1), split(stack(paths)))
     top, diagonal = pack(gram)
     send(msg_ref, stack([root, stat_block(row, row, diagonal), top]))
 
@@ -391,6 +432,7 @@
 
 def row_kernel(
     me_ref,
+    order_ref,
     part0_ref,
     part1_ref,
     part2_ref,
@@ -407,6 +449,7 @@
     scratch_ref,
     slice_ref,
 ):
+    del order_ref
     me = me_ref[0]
     gather_parts(me, "row", (part0_ref, part1_ref, part2_ref, part3_ref), recv_ref)
     summary = climb_group("row", me_ref, recv_ref, up_row_ref, sib_ref, scratch_ref)
@@ -429,28 +472,28 @@
     me_ref,
     recv_ref,
     up_row_ref,
-    up_col_ref,
-    up_couple_ref,
-    path_ref,
     msg_ref,
     sib_ref,
-    gain_ref,
     part_ref,
     diagonal_ref,
     scratch_ref,
 ):
-    me = me_ref[0]
-    level, _, count = stage("mid")
+    count = stage("mid")[2]
     summary = climb_group("mid", me_ref, recv_ref, up_row_ref, sib_ref, scratch_ref)
-    path = path_ref[...]
-    for j in range(level, 8):
-        store_pair(gain_ref, j - level, sibling_gain(me, j, path, up_couple_ref))
-        if j < 7:
-            path = path_product(me, j, path, up_col_ref)
     for d in range(count):
         part_ref[d * SLICE : (d + 1) * SLICE] = recv_ref[d, RHS + 8 :]
         diagonal_ref[d : d + 1] = recv_ref[d, RHS + 2 : RHS + 3]
     send(msg_ref, stack([summary, sum_stats(recv_ref)]))
+
+
+def gains_kernel(me_ref, order_ref, up_col_ref, up_couple_ref, path_ref, gain_ref):
+    del order_ref
+    me = me_ref[0]
+    path = path_ref[...]
+    for k, j in enumerate(range(stage("mid")[0], 8)):
+        store_pair(gain_ref, k, sibling_gain(me, j, path, up_couple_ref))
+        if j < 7:
+            path = path_product(me, j, path, up_col_ref)
 
 
 def from_siblings(siblings, near_gain_ref, mid_gain_ref):
@@ -458,10 +501,6 @@
     gains += [pair_at(mid_gain_ref, j) for j in range(5)]
     gains = tuple(jnp.concatenate([g[k] for g in gains], 1) for k in range(2))
     return mm(jnp.concatenate(siblings, 1), gains, transposed=True)
-
-
-def readers(local):
-    return [pairs_of(ref) for ref in local]
 
 
 def first_kernel(
@@ -481,10 +520,10 @@
     dense_ref,
     row_basis_ref,
     col_basis_ref,
-    local_row_ref,
-    local_col_ref,
-    local_couple_ref,
-    z_ref,
+    cross_ref,
+    columns_ref,
+    paths_ref,
+    within_ref,
     x_ref,
     beta_ref,
     msg_ref,
@@ -507,19 +546,13 @@
     beta = jnp.sqrt(column_of(sum_stats(recv_ref)[:1]))
     inverse = 1.0 / beta
     beta_ref[...] = jnp.broadcast_to(beta, (RHS, RANK))
-    local = readers(
-        (dense_ref, row_basis_ref, col_basis_ref, local_row_ref, local_col_ref, local_couple_ref)
-    )
-    dense, _, col_basis, _, local_col, coupling = local
-    keep = [z_ref[:, KEEP + k * RANK : KEEP + (k + 1) * RANK] for k in range(LEAF_DEV + 2)]
-    leaf, node = keep[:LEAF_DEV], keep[LEAF_DEV:]
-    down = local_down(potential, leaf, node, coupling, local_col, True)
+    spread = mm(potential, pair_at(columns_ref), transposed=True)
     parts = []
     for q in range(LEAF_DEV):
-        x = mm(z_ref[:, row_part(q)], dense(q))
-        x = (x + mm(down[q], col_basis(q), transposed=True)) * inverse
+        x = (within_ref[:, col_part(q)] + spread[:, col_part(q)]) * inverse
         x_ref[:, col_part(q)] = x
         parts.append(x)
+    local = (dense_ref, row_basis_ref, col_basis_ref, cross_ref, columns_ref, paths_ref, None)
     pair_up(parts, local, rows_ref, msg_ref, own_ref, inner_ref, [part_ref[...]])
 
 
@@ -595,6 +628,7 @@
 
 def row_pair_kernel(
     me_ref,
+    order_ref,
     part0_ref,
     part1_ref,
     part2_ref,
@@ -613,6 +647,7 @@
     gain_ref,
     below_ref,
 ):
+    del order_ref
     gather_parts(me_ref[0], "row", (part0_ref, part1_ref, part2_ref, part3_ref), recv_ref)
     tables = (up_row_ref, up_col_ref, up_couple_ref)
     keep = (path_ref, gain_ref, below_ref)
@@ -704,12 +739,12 @@
     dense_ref,
     row_basis_ref,
     col_basis_ref,
-    local_row_ref,
-    local_col_ref,
-    local_couple_ref,
+    cross_ref,
+    columns_ref,
+    images_ref,
     x_ref,
     own_in_ref,
-    inner_ref,
+    within_ref,
     v_ref,
     next_ref,
     alpha_ref,
@@ -762,27 +797,19 @@
             gram = pair_at(nodes_ref, bases(name)[height] + ((inside >> height) ^ 1))
             siblings[j] = path_ref[3 * height + 2] * factor + mm(other, gram)
     backward = from_siblings([siblings[j] for j in range(8)], near_gain_ref, mid_gain_ref)
-    local = readers(
-        (dense_ref, row_basis_ref, col_basis_ref, local_row_ref, local_col_ref, local_couple_ref)
-    )
-    dense, row_basis, col_basis, local_row, local_col, coupling = local
     own_factor = scale / inverse_norm(column_of(own_in_ref[:1]))
-    outer = local_down(forward, None, None, coupling, local_row, False)
-    images = []
-    for q in range(LEAF_DEV):
-        y = mm(outer[q], row_basis(q), transposed=True) * live_mask(rows_ref, q)
-        images.append(y + inner_ref[:, row_part(q)] * own_factor)
-    leaf, node = local_up(images, row_basis, local_row)
-    down = local_down(backward, leaf, node, coupling, local_col, True)
     inverse = 1.0 / rho
+    spread = mm(backward, pair_at(columns_ref), transposed=True)
+    spread = spread + mm(forward, pair_at(images_ref))
     parts = []
     for q in range(LEAF_DEV):
         v = x_ref[:, col_part(q)] * scale
         v_ref[:, col_part(q)] = v
-        x = mm(images[q], dense(q)) + mm(down[q], col_basis(q), transposed=True)
+        x = spread[:, col_part(q)] + within_ref[:, col_part(q)] * own_factor
         x = x * inverse - rho * v
         next_ref[:, col_part(q)] = x
         parts.append(x)
+    local = (dense_ref, row_basis_ref, col_basis_ref, cross_ref, columns_ref, None, images_ref)
     pair_up(parts, local, rows_ref, msg_ref, None, None, [])
 
 
@@ -863,7 +890,7 @@
     def swap_parts(message, name):
         level, _, count = stage(name)
         parts = [message]
-        for k in range(1, count):
+        for k in ORDER[1:count]:
             pairs = [(i, i ^ (k << level)) for i in range(devices)]
             parts.append(lax.ppermute(message, "leaf", pairs))
         return parts
@@ -908,7 +935,7 @@
 
     z, message = call(
         start_kernel,
-        [(RHS, KEEP + 6 * RANK), (1,) + longer(single, HALF)],
+        [row_shape, (1,) + longer(single, HALF)],
         [me, box_rows, rhs, row_basis, local_row],
         [pltpu.SMEM(box_rows.shape, jnp.int32)]
         + [k.shape for k in (rhs, row_basis, local_row)]
@@ -916,24 +943,45 @@
         range(1, 5),
         START_LIMIT,
     )
-    blocks = [dense, row_basis, col_basis, local_row, local_col, local_couple]
+    def pair_shape(*shape):
+        return jax.ShapeDtypeStruct((2,) + shape, bf16)
+
+    def within(y, earlier):
+        operands = [earlier, y, dense, row_basis, col_basis, cross]
+        return call(inner_kernel, [col_shape], operands, (), (0,))[0]
+
     message, core_sib, core_nodes = call(
         core_kernel,
         [(1,) + longer(single, HALF), sibling_shape("core"), nodes_of("core")],
         [me] + swap_parts(message, "core") + [up_row],
         received("core", longer(single, HALF)) + node_scratch("core"),
     )
+    cross, columns, paths = call(
+        paths_kernel,
+        [
+            pair_shape(LEAF_DEV * RANK, LEAF_DEV * RANK),
+            pair_shape(LEAF_DEV * LEAF_COLS, RANK),
+            pair_shape(LEAF_DEV * RANK, RANK),
+        ],
+        [message, col_basis, local_row, local_col, local_couple],
+        (),
+        (0,),
+    )
     message, row_sib, row_nodes, near_gain, path = call(
         row_kernel,
         [(groups,) + longer(single, SLICE), sibling_shape("row"), nodes_of("row"), nodes_shape(3), gram_shape],
-        [me] + swap_parts(message, "row") + tables,
+        [me, paths] + swap_parts(message, "row") + tables,
         received("row", longer(single, HALF)) + node_scratch("row") + [(HALF, RANK)],
-    )
-    message, mid_sib, mid_gain, part, diagonal = call(
+        (1,),
+    )
+    message, mid_sib, part, diagonal = call(
         mid_kernel,
-        [(1,) + single, sibling_shape("mid"), nodes_shape(5), (HALF, RANK), stat],
-        [me, swap_mid(message)] + tables + [path],
+        [(1,) + single, sibling_shape("mid"), (HALF, RANK), stat],
+        [me, swap_mid(message), up_row],
         node_scratch("mid"),
+    )
+    (mid_gain,) = call(
+        gains_kernel, [nodes_shape(5)], [me, message, up_col, up_couple, path], (), (1,)
     )
     gains = [near_gain, mid_gain]
     x, beta, message, own, inner = call(
@@ -943,9 +991,7 @@
         + swap_parts(message, "far")
         + [core_sib, row_sib, mid_sib]
         + gains
-        + [part, up_row]
-        + blocks
-        + [z],
+        + [part, up_row, dense, row_basis, col_basis, cross, columns, paths, within(z, message)],
         [(2,) + tile] + received("far", single),
     )
     message, core_path, core_own = call(
@@ -954,11 +1000,19 @@
         [me] + swap_parts(message, "core") + tables + [core_nodes],
         received("core", longer(double, HALF)) + node_scratch("core", 2),
     )
+    (images,) = call(
+        images_kernel,
+        [pair_shape(RANK, LEAF_DEV * LEAF_COLS)],
+        [message, box_rows, dense, row_basis, col_basis, cross, paths],
+        (),
+        (0,),
+    )
     message, row_path, row_own, mid_nodes, gram = call(
         row_pair_kernel,
         [(groups,) + double, path_shape("row"), stat, nodes_of("mid"), (HALF + 8, RANK)],
-        [me] + swap_parts(message, "row") + tables + [row_nodes, diagonal],
+        [me, images] + swap_parts(message, "row") + tables + [row_nodes, diagonal],
         received("row", longer(double, 2 * HALF)) + node_scratch("row", 2),
+        (1,),
     )
     message, mid_path, mid_own = call(
         mid_pair_kernel,
@@ -975,8 +1029,7 @@
         + gains
         + tables
         + [core_nodes, row_nodes, mid_nodes]
-        + blocks
-        + [x, own, inner],
+        + [dense, row_basis, col_basis, cross, columns, images, x, own, within(inner, message)],
         [(6,) + tile, (4,) + tile] + received("far", longer(double, HALF + 8)),
     )
     for name, nodes, peers in (

time: 118 us -> 115 us (0.975)
  waiting for transfers between devices: 25.3 us -> 15.9 us
  Pallas kernels: 26.3 us -> 30.1 us
    ppermute x21, waiting for transfers between devices: 25.3 us -> 15.9 us  [swap_parts(): parts.append(lax.ppermute(message, 'leaf', pairs))]
    pallas_call x13 -> x18, Pallas kernels: 26.3 us -> 30.1 us  [call(): pl.pallas_call(kernel, out_shape=outs, in_specs=[pl.BlockSpec(memory_spac...]
  transfers between devices with their start and end apart: 21 -> 21, of which waited for: 16 -> 14; matrix products, arithmetic and copies ran while one was open for 0% -> 0% of each run, Pallas kernels for 0% -> 6%
where the time goes in v6:
time: 115 us
  blocking collectives  40.3 us (35%)
  Pallas kernels  30.1 us (26%)
  starting transfers between devices  26.4 us (23%)
  waiting for transfers between devices  15.9 us (14%)
  local copies, waits for them, and re-layouts  1.79 us (2%)
    all_to_all x3, blocking collectives, swap_mid(): return lax.all_to_all(message, 'leaf', 0, 0, axis_index_groups=groups)  40.3 us
    pallas_call x18, Pallas kernels, call(): pl.pallas_call(kernel, out_shape=outs, in_specs=[pl.BlockSpec(memory_spac...  30.1 us
    ppermute x21, starting transfers between devices, swap_parts(): parts.append(lax.ppermute(message, 'leaf', pairs))  26.4 us
    ppermute x21, waiting for transfers between devices, swap_parts(): parts.append(lax.ppermute(message, 'leaf', pairs))  15.9 us
  transfers between devices with their start and end apart: 21, of which 14 were waited for; matrix products, arithmetic and copies ran while one was open for 0% of the time, Pallas kernels for 6%

profile of v6, /device:TPU:2, one launch (start us, length us, event | category | flops | bytes accessed | tf_op | source)
XLA Modules:
  0.0 114.7 jit_solution(3287596684271366381)
XLA Ops:
  0.0 3.5 %shard_map.109 = (f32[16,2048]{1,0:T(8,128)}, f32[1,88,128]{2,1,0:T(8,128)}) custom-call(s32[1]{0:T(128)} %bitcast.me_ref, s32[4]{0:T(128)} %rows_ref.5, f32[16,2048]{1,0:T(8,128)} %rhs_hbm.1, f32[4,512,128]{2,1,0:T(8,128)} %row_basis_ref.9, f32[3,256,128]{2,1,0:T(8,128)} %local_row_ref.1), custom_call_target="tpu_custom_call" | custom-call | flops 6000000000 | tf_op jit(solution)/shard_map/pallas_call | solution.py:853
  3.7 1.4 %collective-permute-done.part1_ref = f32[1,88,128]{2,1,0:T(8,128)S(1)} collective-permute-done((f32[1,88,128]{2,1,0:T(8,128)}, f32[1,88,128]{2,1,0:T(8,128)S(1)}, u32[]{:S(2)}, u32[]{:S(2)}) %collective-permute-start) | collective-permute-done | bytes 45088 | tf_op jit(solution)/shard_map/ppermute | solution.py:895
  6.6 2.2 %collective-permute-start.3 = (f32[1,88,128]{2,1,0:T(8,128)S(1)}, f32[1,88,128]{2,1,0:T(8,128)S(1)}, u32[]{:S(2)}, u32[]{:S(2)}) collective-permute-start(f32[1,88,128]{2,1,0:T(8,128)S(1)} %get-tuple-element.45.order_ref.part0_ref), channel_id=1, source_target_pairs={{0,4},{1,5},{2,6},{3,7},{4,0},{5,1},{6,2},{7,3},{8,12},{9,13},{10,... | collective-permute-start | bytes 135176 | tf_op jit(solution)/shard_map/ppermute | solution.py:895
  8.8 1.6 %collective-permute-start.2 = (f32[1,88,128]{2,1,0:T(8,128)S(1)}, f32[1,88,128]{2,1,0:T(8,128)S(1)}, u32[]{:S(2)}, u32[]{:S(2)}) collective-permute-start(f32[1,88,128]{2,1,0:T(8,128)S(1)} %get-tuple-element.45.order_ref.part0_ref), channel_id=1, source_target_pairs={{0,6},{1,7},{2,4},{3,5},{4,2},{5,3},{6,0},{7,1},{8,14},{9,15},{10,... | collective-permute-start | bytes 135176 | tf_op jit(solution)/shard_map/ppermute | solution.py:895
  11.4 1.6 %shard_map.111 = (bf16[2,512,512]{2,1,0:T(8,128)(2,1)S(1)}, bf16[2,1024,128]{2,1,0:T(8,128)(2,1)S(1)}, bf16[2,512,128]{2,1,0:T(8,128)(2,1)S(1)}) custom-call(f32[1,88,128]{2,1,0:T(8,128)S(1)} %get-tuple-element.45.order_ref.part0_ref, f32[4,256,128]{2,1,0:T(8,128)S(1)} %copy-done.5, f32[3,256,128]{2,1,0:T(8,128)S(1)} %copy-done.6, ...), custom_call_target="tpu_custom_call" | custom-call | flops 6000000000 | tf_op jit(solution)/shard_map/pallas_call | solution.py:853
  12.9 1.5 %collective-permute-done.1.part1_ref = f32[1,88,128]{2,1,0:T(8,128)S(1)} collective-permute-done((f32[1,88,128]{2,1,0:T(8,128)S(1)}, f32[1,88,128]{2,1,0:T(8,128)S(1)}, u32[]{:S(2)}, u32[]{:S(2)}) %collective-permute-start.1) | collective-permute-done | bytes 45088 | tf_op jit(solution)/shard_map/ppermute | solution.py:895
  14.4 1.3 %shard_map.112 = (f32[8,32,128]{2,1,0:T(8,128)S(1)}, f32[2,16,128]{2,1,0:T(8,128)S(1)}, bf16[2,6,128,128]{3,2,1,0:T(8,128)(2,1)S(1)}, bf16[2,3,128,128]{3,2,1,0:T(8,128)(2,1)S(1)}, f32[128,128]{1,0:T(8,128)S(1)}) custom-call(s32[1]{0:T(128)} %bitcast.me_ref, bf16[2,512,128]{2,1,0:T(8,128)(2,1)S(1)} %get-tuple-element.46.order_ref.paths_ref, ...), custom_call_target="tpu_custom_call" | custom-call | flops 6000000000 | tf_op jit(solution)/shard_map/pallas_call | solution.py:853
  15.8 16.3 %all_to_all.15.recv_ref = f32[8,32,128]{2,1,0:T(8,128)S(1)} all-to-all(f32[8,32,128]{2,1,0:T(8,128)S(1)} %get-tuple-element.47), channel_id=1, replica_groups={{0,8,16,24,32,40,48,56},{1,9,17,25,33,41,49,57},{2,10,18,26,34,42,50,58..., dimensions={0} | all-to-all | bytes 262144 | tf_op jit(solution)/shard_map/all_to_all | solution.py:901
  32.5 3.2 %collective-permute-start.6 = (f32[1,24,128]{2,1,0:T(8,128)S(1)}, f32[1,24,128]{2,1,0:T(8,128)S(1)}, u32[]{:S(2)}, u32[]{:S(2)}) collective-permute-start(f32[1,24,128]{2,1,0:T(8,128)S(1)} %get-tuple-element.48.order_ref.part0_ref), channel_id=1, source_target_pairs={{0,128},{1,129},{2,130},{3,131},{4,132},{5,133},{6,134},{7,135},{8... | collective-permute-start | bytes 36872 | tf_op jit(solution)/shard_map/ppermute | solution.py:895
  38.6 1.1 shard_map.115.within_ref
  40.6 3.4 %shard_map.116 = (f32[16,1024]{1,0:T(8,128)S(1)}, f32[16,128]{1,0:T(8,128)S(1)}, f32[1,104,128]{2,1,0:T(8,128)S(1)}, f32[8,128]{1,0:T(8,128)S(1)}, f32[16,2048]{1,0:T(8,128)S(1)}) custom-call(s32[1]{0:T(128)} %bitcast.me_ref, s32[4]{0:T(128)S(1)} %copy-done.10, f32[1,24,128]{2,1,0:T(8,128)S(1)} %get-tuple-element.48.order_ref.part0_ref, ...), custom_call_target="tpu_custom_call" | custom-call | flops 6000000000 | tf_op jit(solution)/shard_map/pallas_call | solution.py:853
  44.1 1.2 %collective-permute-done.7.part1_ref = f32[1,104,128]{2,1,0:T(8,128)S(1)} collective-permute-done((f32[1,104,128]{2,1,0:T(8,128)S(1)}, f32[1,104,128]{2,1,0:T(8,128)S(1)}, u32[]{:S(2)}, u32[]{:S(2)}) %collective-permute-start.7) | collective-permute-done | bytes 53280 | tf_op jit(solution)/shard_map/ppermute | solution.py:895
  45.8 3.0 %collective-permute-start.10 = (f32[1,168,128]{2,1,0:T(8,128)S(1)}, f32[1,168,128]{2,1,0:T(8,128)S(1)}, u32[]{:S(2)}, u32[]{:S(2)}) collective-permute-start(f32[1,168,128]{2,1,0:T(8,128)S(1)} %get-tuple-element.60.order_ref.part0_ref), channel_id=1, source_target_pairs={{0,4},{1,5},{2,6},{3,7},{4,0},{5,1},{6,2},{7,3},{8,12},{9,13},{10,... | collective-permute-start | bytes 258056 | tf_op jit(solution)/shard_map/ppermute | solution.py:895
  49.4 1.1 collective-permute-start.8
  50.6 2.7 %shard_map.118.order_ref.images_ref = bf16[2,128,1024]{2,1,0:T(8,128)(2,1)S(1)} custom-call(f32[1,168,128]{2,1,0:T(8,128)S(1)} %get-tuple-element.60.order_ref.part0_ref, s32[4]{0:T(128)S(1)} %copy-done.10, f32[4,512,256]{2,1,0:T(8,128)S(1)} %copy-done, f32[4,512,128]{2,1,0:T(8,128)S(1)} %copy-done.1, f32[4,256,128]{2,1,0:T(8,128)S(1)} %copy-done.5, ...), custom_call_target="tpu_custom_call" | custom-call | flops 6000000000 | tf_op jit(solution)/shard_map/pallas_call | solution.py:853
  53.9 2.4 %shard_map.119 = (f32[8,40,128]{2,1,0:T(8,128)S(1)}, f32[6,16,128]{2,1,0:T(8,128)S(1)}, f32[8,128]{1,0:T(8,128)S(1)}, bf16[2,14,128,128]{3,2,1,0:T(8,128)(2,1)S(1)}, f32[72,128]{1,0:T(8,128)S(1)}) custom-call(s32[1]{0:T(128)} %bitcast.me_ref, bf16[2,128,1024]{2,1,0:T(8,128)(2,1)S(1)} %shard_map.118.order_ref.images_ref, ...), custom_call_target="tpu_custom_call" | custom-call | flops 6000000000 | tf_op jit(solution)/shard_map/pallas_call | solution.py:853
  56.4 12.2 %all_to_all.16.recv_ref = f32[8,40,128]{2,1,0:T(8,128)S(1)} all-to-all(f32[8,40,128]{2,1,0:T(8,128)S(1)} %get-tuple-element.63), channel_id=1, replica_groups={{0,8,16,24,32,40,48,56},{1,9,17,25,33,41,49,57},{2,10,18,26,34,42,50,58..., dimensions={0} | all-to-all | bytes 327680 | tf_op jit(solution)/shard_map/all_to_all | solution.py:901
  68.5 1.3 %shard_map.120 = (f32[1,112,128]{2,1,0:T(8,128)S(1)}, f32[9,16,128]{2,1,0:T(8,128)S(1)}, f32[8,128]{1,0:T(8,128)S(1)}) custom-call(s32[1]{0:T(128)} %bitcast.me_ref, f32[8,40,128]{2,1,0:T(8,128)S(1)} %all_to_all.16.recv_ref, f32[7,256,128]{2,1,0:T(8,128)S(1)} %copy-done.3, f32[7,256,128]{2,1,0:T(8,128)S(1)} %copy-done.4, f32[8,2,128,128]{3,2,1,0:T(8,128)S(1)} %copy-done.2, ...), custom_call_target="tpu_custom_call" | custom-call | flops 6000000000 | tf_op jit(solution)/shard_map/pallas_call | solution.py:853
  69.8 2.9 %collective-permute-start.13 = (f32[1,112,128]{2,1,0:T(8,128)S(1)}, f32[1,112,128]{2,1,0:T(8,128)S(1)}, u32[]{:S(2)}, u32[]{:S(2)}) collective-permute-start(f32[1,112,128]{2,1,0:T(8,128)S(1)} %get-tuple-element.66.order_ref.part0_ref), channel_id=1, source_target_pairs={{0,128},{1,129},{2,130},{3,131},{4,132},{5,133},{6,134},{7,135},{8... | collective-permute-start | bytes 172040 | tf_op jit(solution)/shard_map/ppermute | solution.py:895
  72.7 1.1 collective-permute-start.12
  73.8 1.1 shard_map.121.within_ref
  75.9 2.2 %collective-permute-done.12.part2_ref = f32[1,112,128]{2,1,0:T(8,128)S(1)} collective-permute-done((f32[1,112,128]{2,1,0:T(8,128)S(1)}, f32[1,112,128]{2,1,0:T(8,128)S(1)}, u32[]{:S(2)}, u32[]{:S(2)}) %collective-permute-start.12) | collective-permute-done | bytes 57376 | tf_op jit(solution)/shard_map/ppermute | solution.py:895
  78.1 5.0 %shard_map.122 = (f32[16,1024]{1,0:T(8,128)S(1)}, f32[16,1024]{1,0:T(8,128)S(1)}, f32[16,128]{1,0:T(8,128)S(1)}, f32[16,128]{1,0:T(8,128)S(1)}, f32[1,40,128]{2,...) custom-call(s32[1]{0:T(128)} %bitcast.me_ref, s32[4]{0:T(128)S(1)} %copy-done.10, ...), custom_call_target="tpu_custom_call" | custom-call | flops 6000000000 | tf_op jit(solution)/shard_map/pallas_call | solution.py:853
  83.2 1.2 %collective-permute-done.14.refs_1_ = f32[1,40,128]{2,1,0:T(8,128)S(1)} collective-permute-done((f32[1,40,128]{2,1,0:T(8,128)S(1)}, f32[1,40,128]{2,1,0:T(8,128)S(1)}, u32[]{:S(2)}, u32[]{:S(2)}) %collective-permute-start.14) | collective-permute-done | bytes 20512 | tf_op jit(solution)/shard_map/ppermute | solution.py:895
  84.9 3.4 %collective-permute-start.17 = (f32[1,40,128]{2,1,0:T(8,128)S(1)}, f32[1,40,128]{2,1,0:T(8,128)S(1)}, u32[]{:S(2)}, u32[]{:S(2)}) collective-permute-start(f32[1,40,128]{2,1,0:T(8,128)S(1)} %shard_map.123.refs_0_), channel_id=1, source_target_pairs={{0,4},{1,5},{2,6},{3,7},{4,0},{5,1},{6,2},{7,3},{8,12},{9,13},{10,... | collective-permute-start | bytes 61448 | tf_op jit(solution)/shard_map/ppermute | solution.py:895
  90.2 1.8 %collective-permute-done.16.refs_2_ = f32[1,40,128]{2,1,0:T(8,128)S(1)} collective-permute-done((f32[1,40,128]{2,1,0:T(8,128)S(1)}, f32[1,40,128]{2,1,0:T(8,128)S(1)}, u32[]{:S(2)}, u32[]{:S(2)}) %collective-permute-start.16) | collective-permute-done | bytes 20512 | tf_op jit(solution)/shard_map/ppermute | solution.py:895
  93.5 11.8 %all_to_all.17.refs_0_ = f32[8,40,128]{2,1,0:T(8,128)S(1)} all-to-all(f32[8,40,128]{2,1,0:T(8,128)S(1)} %shard_map.124), channel_id=1, replica_groups={{0,8,16,24,32,40,48,56},{1,9,17,25,33,41,49,57},{2,10,18,26,34,42,50,58..., dimensions={0} | all-to-all | bytes 327680 | tf_op jit(solution)/shard_map/all_to_all | solution.py:901
  105.3 1.3 %shard_map.125.part0_ref = f32[1,40,128]{2,1,0:T(8,128)S(1)} custom-call(s32[1]{0:T(128)} %bitcast.me_ref, f32[8,40,128]{2,1,0:T(8,128)S(1)} %all_to_all.17.refs_0_, f32[7,256,128]{2,1,0:T(8,128)S(1)} %copy-done.3, f32[7,256,128]{2,1,0:T(8,128)S(1)} %copy-done.4, f32[8,2,128,128]{3,2,1,0:T(8,128)S(1)} %copy-done.2, ...), custom_call_target="tpu_custom_call" | custom-call | flops 6000000000 | tf_op jit(solution)/shard_map/pallas_call | solution.py:853
  106.6 1.5 %collective-permute-start.20 = (f32[1,40,128]{2,1,0:T(8,128)S(1)}, f32[1,40,128]{2,1,0:T(8,128)S(1)}, u32[]{:S(2)}, u32[]{:S(2)}) collective-permute-start(f32[1,40,128]{2,1,0:T(8,128)S(1)} %shard_map.125.part0_ref), channel_id=1, source_target_pairs={{0,128},{1,129},{2,130},{3,131},{4,132},{5,133},{6,134},{7,135},{8... | collective-permute-start | bytes 61448 | tf_op jit(solution)/shard_map/ppermute | solution.py:895
  110.1 1.8 %collective-permute-done.20.part3_ref = f32[1,40,128]{2,1,0:T(8,128)S(1)} collective-permute-done((f32[1,40,128]{2,1,0:T(8,128)S(1)}, f32[1,40,128]{2,1,0:T(8,128)S(1)}, u32[]{:S(2)}, u32[]{:S(2)}) %collective-permute-start.20) | collective-permute-done | bytes 20512 | tf_op jit(solution)/shard_map/ppermute | solution.py:895
  111.9 1.2 %collective-permute-done.19.part2_ref = f32[1,40,128]{2,1,0:T(8,128)S(1)} collective-permute-done((f32[1,40,128]{2,1,0:T(8,128)S(1)}, f32[1,40,128]{2,1,0:T(8,128)S(1)}, u32[]{:S(2)}, u32[]{:S(2)}) %collective-permute-start.19) | collective-permute-done | bytes 20512 | tf_op jit(solution)/shard_map/ppermute | solution.py:895
  113.1 1.6 %shard_map.126 = f32[16,1024]{1,0:T(8,128)} custom-call(s32[1]{0:T(128)} %bitcast.me_ref, f32[1,40,128]{2,1,0:T(8,128)S(1)} %shard_map.125.part0_ref, f32[1,40,128]{2,1,0:T(8,128)S(1)} %collective-permute-done.18.part1_ref, f32[1,40,128]{2,1,0:T(8,128)S(1)} %collective-permute-done.19.part2_ref, f32[1,40,128]{2,1,0:T(8,128)S(1)} %collective-permute-done.20.part3_ref, ...), custom_call_target="tpu_custom_call" | custom-call | flops 6000000000 | tf_op jit(solution)/shard_map/pallas_call | solution.py:853
  (55 shorter events, 15.6 us)
Async XLA Ops:
  0.0 5.1 %copy-start.3 = (f32[7,256,128]{2,1,0:T(8,128)S(1)}, f32[7,256,128]{2,1,0:T(8,128)}, u32[]{:S(2)}) copy-start(f32[7,256,128]{2,1,0:T(8,128)} %up_row_ref.17) | copy-start | bytes 2752516
  3.5 7.8 %copy-start.5 = (f32[4,256,128]{2,1,0:T(8,128)S(1)}, f32[4,256,128]{2,1,0:T(8,128)}, u32[]{:S(2)}) copy-start(f32[4,256,128]{2,1,0:T(8,128)} %col_basis_ref.11) | copy-start | bytes 1572868
  3.6 7.8 %copy-start.6 = (f32[3,256,128]{2,1,0:T(8,128)S(1)}, f32[3,256,128]{2,1,0:T(8,128)}, u32[]{:S(2)}) copy-start(f32[3,256,128]{2,1,0:T(8,128)} %local_row_ref.1) | copy-start | bytes 1179652
  3.6 7.8 %copy-start.7 = (f32[3,256,128]{2,1,0:T(8,128)S(1)}, f32[3,256,128]{2,1,0:T(8,128)}, u32[]{:S(2)}) copy-start(f32[3,256,128]{2,1,0:T(8,128)} %local_col_ref.1) | copy-start | bytes 1179652
  3.6 7.8 %copy-start.8 = (f32[3,2,128,128]{3,2,1,0:T(8,128)S(1)}, f32[3,2,128,128]{3,2,1,0:T(8,128)}, u32[]{:S(2)}) copy-start(f32[3,2,128,128]{3,2,1,0:T(8,128)} %local_couple_ref.1) | copy-start | bytes 1179652
  3.6 1.5 %collective-permute-start = (f32[1,88,128]{2,1,0:T(8,128)}, f32[1,88,128]{2,1,0:T(8,128)S(1)}, u32[]{:S(2)}, u32[]{:S(2)}) collective-permute-start(f32[1,88,128]{2,1,0:T(8,128)} %get-tuple-element.44.part0_ref), channel_id=1, source_target_pairs={{0,1},{1,0},{2,3},{3,2},{4,5},{5,4},{6,7},{7,6},{8,9},{9,8},{10,11... | collective-permute-start | bytes 135176 | tf_op jit(solution)/shard_map/ppermute | solution.py:895
  6.5 7.9 %copy-start.2 = (f32[8,2,128,128]{3,2,1,0:T(8,128)S(1)}, f32[8,2,128,128]{3,2,1,0:T(8,128)}, u32[]{:S(2)}) copy-start(f32[8,2,128,128]{3,2,1,0:T(8,128)} %up_couple_ref.13) | copy-start | bytes 3145732
  6.5 7.9 %copy-start.4 = (f32[7,256,128]{2,1,0:T(8,128)S(1)}, f32[7,256,128]{2,1,0:T(8,128)}, u32[]{:S(2)}) copy-start(f32[7,256,128]{2,1,0:T(8,128)} %up_col_ref.13) | copy-start | bytes 2752516
  6.6 6.4 %collective-permute-start.3 = (f32[1,88,128]{2,1,0:T(8,128)S(1)}, f32[1,88,128]{2,1,0:T(8,128)S(1)}, u32[]{:S(2)}, u32[]{:S(2)}) collective-permute-start(f32[1,88,128]{2,1,0:T(8,128)S(1)} %get-tuple-element.45.order_ref.part0_ref), channel_id=1, source_target_pairs={{0,4},{1,5},{2,6},{3,7},{4,0},{5,1},{6,2},{7,3},{8,12},{9,13},{10,... | collective-permute-start | bytes 135176 | tf_op jit(solution)/shard_map/ppermute | solution.py:895
  8.8 4.2 %collective-permute-start.2 = (f32[1,88,128]{2,1,0:T(8,128)S(1)}, f32[1,88,128]{2,1,0:T(8,128)S(1)}, u32[]{:S(2)}, u32[]{:S(2)}) collective-permute-start(f32[1,88,128]{2,1,0:T(8,128)S(1)} %get-tuple-element.45.order_ref.part0_ref), channel_id=1, source_target_pairs={{0,6},{1,7},{2,4},{3,5},{4,2},{5,3},{6,0},{7,1},{8,14},{9,15},{10,... | collective-permute-start | bytes 135176 | tf_op jit(solution)/shard_map/ppermute | solution.py:895
  10.4 4.0 %collective-permute-start.1 = (f32[1,88,128]{2,1,0:T(8,128)S(1)}, f32[1,88,128]{2,1,0:T(8,128)S(1)}, u32[]{:S(2)}, u32[]{:S(2)}) collective-permute-start(f32[1,88,128]{2,1,0:T(8,128)S(1)} %get-tuple-element.45.order_ref.part0_ref), channel_id=1, source_target_pairs={{0,2},{1,3},{2,0},{3,1},{4,6},{5,7},{6,4},{7,5},{8,10},{9,11},{10,... | collective-permute-start | bytes 135176 | tf_op jit(solution)/shard_map/ppermute | solution.py:895
  32.5 7.2 %collective-permute-start.6 = (f32[1,24,128]{2,1,0:T(8,128)S(1)}, f32[1,24,128]{2,1,0:T(8,128)S(1)}, u32[]{:S(2)}, u32[]{:S(2)}) collective-permute-start(f32[1,24,128]{2,1,0:T(8,128)S(1)} %get-tuple-element.48.order_ref.part0_ref), channel_id=1, source_target_pairs={{0,128},{1,129},{2,130},{3,131},{4,132},{5,133},{6,134},{7,135},{8... | collective-permute-start | bytes 36872 | tf_op jit(solution)/shard_map/ppermute | solution.py:895
  35.7 4.9 %collective-permute-start.5 = (f32[1,24,128]{2,1,0:T(8,128)S(1)}, f32[1,24,128]{2,1,0:T(8,128)S(1)}, u32[]{:S(2)}, u32[]{:S(2)}) collective-permute-start(f32[1,24,128]{2,1,0:T(8,128)S(1)} %get-tuple-element.48.order_ref.part0_ref), channel_id=1, source_target_pairs={{0,192},{1,193},{2,194},{3,195},{4,196},{5,197},{6,198},{7,199},{8... | collective-permute-start | bytes 36872 | tf_op jit(solution)/shard_map/ppermute | solution.py:895
  36.7 3.8 %collective-permute-start.4 = (f32[1,24,128]{2,1,0:T(8,128)S(1)}, f32[1,24,128]{2,1,0:T(8,128)S(1)}, u32[]{:S(2)}, u32[]{:S(2)}) collective-permute-start(f32[1,24,128]{2,1,0:T(8,128)S(1)} %get-tuple-element.48.order_ref.part0_ref), channel_id=1, source_target_pairs={{0,64},{1,65},{2,66},{3,67},{4,68},{5,69},{6,70},{7,71},{8,72},{9,... | collective-permute-start | bytes 36872 | tf_op jit(solution)/shard_map/ppermute | solution.py:895
  36.7 1.6 %copy-start = (f32[4,512,256]{2,1,0:T(8,128)S(1)}, f32[4,512,256]{2,1,0:T(8,128)}, u32[]{:S(2)}) copy-start(f32[4,512,256]{2,1,0:T(8,128)} %dense_ref.9) | copy-start | bytes 6291460
  36.7 1.9 %copy-start.1 = (f32[4,512,128]{2,1,0:T(8,128)S(1)}, f32[4,512,128]{2,1,0:T(8,128)}, u32[]{:S(2)}) copy-start(f32[4,512,128]{2,1,0:T(8,128)} %row_basis_ref.9) | copy-start | bytes 3145732
  36.8 1.9 %copy-start.11 = (f32[16,2048]{1,0:T(8,128)S(1)}, f32[16,2048]{1,0:T(8,128)}, u32[]{:S(2)}) copy-start(f32[16,2048]{1,0:T(8,128)} %get-tuple-element.57.y_ref) | copy-start | bytes 393220
  38.6 2.0 %copy-start.10 = (s32[4]{0:T(128)S(1)}, s32[4]{0:T(128)}, u32[]{:S(2)}) copy-start(s32[4]{0:T(128)} %rows_ref.5) | copy-start | bytes 52
  44.0 1.3 %collective-permute-start.7 = (f32[1,104,128]{2,1,0:T(8,128)S(1)}, f32[1,104,128]{2,1,0:T(8,128)S(1)}, u32[]{:S(2)}, u32[]{:S(2)}) collective-permute-start(f32[1,104,128]{2,1,0:T(8,128)S(1)} %get-tuple-element.58.part0_ref), channel_id=1, source_target_pairs={{0,1},{1,0},{2,3},{3,2},{4,5},{5,4},{6,7},{7,6},{8,9},{9,8},{10,11... | collective-permute-start | bytes 159752 | tf_op jit(solution)/shard_map/ppermute | solution.py:895
  45.8 7.5 %collective-permute-start.10 = (f32[1,168,128]{2,1,0:T(8,128)S(1)}, f32[1,168,128]{2,1,0:T(8,128)S(1)}, u32[]{:S(2)}, u32[]{:S(2)}) collective-permute-start(f32[1,168,128]{2,1,0:T(8,128)S(1)} %get-tuple-element.60.order_ref.part0_ref), channel_id=1, source_target_pairs={{0,4},{1,5},{2,6},{3,7},{4,0},{5,1},{6,2},{7,3},{8,12},{9,13},{10,... | collective-permute-start | bytes 258056 | tf_op jit(solution)/shard_map/ppermute | solution.py:895
  48.8 5.0 %collective-permute-start.9 = (f32[1,168,128]{2,1,0:T(8,128)S(1)}, f32[1,168,128]{2,1,0:T(8,128)S(1)}, u32[]{:S(2)}, u32[]{:S(2)}) collective-permute-start(f32[1,168,128]{2,1,0:T(8,128)S(1)} %get-tuple-element.60.order_ref.part0_ref), channel_id=1, source_target_pairs={{0,6},{1,7},{2,4},{3,5},{4,2},{5,3},{6,0},{7,1},{8,14},{9,15},{10,... | collective-permute-start | bytes 258056 | tf_op jit(solution)/shard_map/ppermute | solution.py:895
  49.4 4.5 %collective-permute-start.8 = (f32[1,168,128]{2,1,0:T(8,128)S(1)}, f32[1,168,128]{2,1,0:T(8,128)S(1)}, u32[]{:S(2)}, u32[]{:S(2)}) collective-permute-start(f32[1,168,128]{2,1,0:T(8,128)S(1)} %get-tuple-element.60.order_ref.part0_ref), channel_id=1, source_target_pairs={{0,2},{1,3},{2,0},{3,1},{4,6},{5,7},{6,4},{7,5},{8,10},{9,11},{10,... | collective-permute-start | bytes 258056 | tf_op jit(solution)/shard_map/ppermute | solution.py:895
  69.8 6.1 %collective-permute-start.13 = (f32[1,112,128]{2,1,0:T(8,128)S(1)}, f32[1,112,128]{2,1,0:T(8,128)S(1)}, u32[]{:S(2)}, u32[]{:S(2)}) collective-permute-start(f32[1,112,128]{2,1,0:T(8,128)S(1)} %get-tuple-element.66.order_ref.part0_ref), channel_id=1, source_target_pairs={{0,128},{1,129},{2,130},{3,131},{4,132},{5,133},{6,134},{7,135},{8... | collective-permute-start | bytes 172040 | tf_op jit(solution)/shard_map/ppermute | solution.py:895
  72.7 5.4 %collective-permute-start.12 = (f32[1,112,128]{2,1,0:T(8,128)S(1)}, f32[1,112,128]{2,1,0:T(8,128)S(1)}, u32[]{:S(2)}, u32[]{:S(2)}) collective-permute-start(f32[1,112,128]{2,1,0:T(8,128)S(1)} %get-tuple-element.66.order_ref.part0_ref), channel_id=1, source_target_pairs={{0,192},{1,193},{2,194},{3,195},{4,196},{5,197},{6,198},{7,199},{8... | collective-permute-start | bytes 172040 | tf_op jit(solution)/shard_map/ppermute | solution.py:895
  73.8 4.3 %collective-permute-start.11 = (f32[1,112,128]{2,1,0:T(8,128)S(1)}, f32[1,112,128]{2,1,0:T(8,128)S(1)}, u32[]{:S(2)}, u32[]{:S(2)}) collective-permute-start(f32[1,112,128]{2,1,0:T(8,128)S(1)} %get-tuple-element.66.order_ref.part0_ref), channel_id=1, source_target_pairs={{0,64},{1,65},{2,66},{3,67},{4,68},{5,69},{6,70},{7,71},{8,72},{9,... | collective-permute-start | bytes 172040 | tf_op jit(solution)/shard_map/ppermute | solution.py:895
  83.1 1.3 %collective-permute-start.14 = (f32[1,40,128]{2,1,0:T(8,128)S(1)}, f32[1,40,128]{2,1,0:T(8,128)S(1)}, u32[]{:S(2)}, u32[]{:S(2)}) collective-permute-start(f32[1,40,128]{2,1,0:T(8,128)S(1)} %get-tuple-element.76.refs_0_), channel_id=1, source_target_pairs={{0,1},{1,0},{2,3},{3,2},{4,5},{5,4},{6,7},{7,6},{8,9},{9,8},{10,11... | collective-permute-start | bytes 61448 | tf_op jit(solution)/shard_map/ppermute | solution.py:895
  84.9 5.4 %collective-permute-start.17 = (f32[1,40,128]{2,1,0:T(8,128)S(1)}, f32[1,40,128]{2,1,0:T(8,128)S(1)}, u32[]{:S(2)}, u32[]{:S(2)}) collective-permute-start(f32[1,40,128]{2,1,0:T(8,128)S(1)} %shard_map.123.refs_0_), channel_id=1, source_target_pairs={{0,4},{1,5},{2,6},{3,7},{4,0},{5,1},{6,2},{7,3},{8,12},{9,13},{10,... | collective-permute-start | bytes 61448 | tf_op jit(solution)/shard_map/ppermute | solution.py:895
  88.2 3.8 %collective-permute-start.16 = (f32[1,40,128]{2,1,0:T(8,128)S(1)}, f32[1,40,128]{2,1,0:T(8,128)S(1)}, u32[]{:S(2)}, u32[]{:S(2)}) collective-permute-start(f32[1,40,128]{2,1,0:T(8,128)S(1)} %shard_map.123.refs_0_), channel_id=1, source_target_pairs={{0,6},{1,7},{2,4},{3,5},{4,2},{5,3},{6,0},{7,1},{8,14},{9,15},{10,... | collective-permute-start | bytes 61448 | tf_op jit(solution)/shard_map/ppermute | solution.py:895
  88.8 3.8 %collective-permute-start.15 = (f32[1,40,128]{2,1,0:T(8,128)S(1)}, f32[1,40,128]{2,1,0:T(8,128)S(1)}, u32[]{:S(2)}, u32[]{:S(2)}) collective-permute-start(f32[1,40,128]{2,1,0:T(8,128)S(1)} %shard_map.123.refs_0_), channel_id=1, source_target_pairs={{0,2},{1,3},{2,0},{3,1},{4,6},{5,7},{6,4},{7,5},{8,10},{9,11},{10,... | collective-permute-start | bytes 61448 | tf_op jit(solution)/shard_map/ppermute | solution.py:895
  106.6 5.4 %collective-permute-start.20 = (f32[1,40,128]{2,1,0:T(8,128)S(1)}, f32[1,40,128]{2,1,0:T(8,128)S(1)}, u32[]{:S(2)}, u32[]{:S(2)}) collective-permute-start(f32[1,40,128]{2,1,0:T(8,128)S(1)} %shard_map.125.part0_ref), channel_id=1, source_target_pairs={{0,128},{1,129},{2,130},{3,131},{4,132},{5,133},{6,134},{7,135},{8... | collective-permute-start | bytes 61448 | tf_op jit(solution)/shard_map/ppermute | solution.py:895
  108.1 5.0 %collective-permute-start.19 = (f32[1,40,128]{2,1,0:T(8,128)S(1)}, f32[1,40,128]{2,1,0:T(8,128)S(1)}, u32[]{:S(2)}, u32[]{:S(2)}) collective-permute-start(f32[1,40,128]{2,1,0:T(8,128)S(1)} %shard_map.125.part0_ref), channel_id=1, source_target_pairs={{0,192},{1,193},{2,194},{3,195},{4,196},{5,197},{6,198},{7,199},{8... | collective-permute-start | bytes 61448 | tf_op jit(solution)/shard_map/ppermute | solution.py:895
  109.2 3.9 %collective-permute-start.18 = (f32[1,40,128]{2,1,0:T(8,128)S(1)}, f32[1,40,128]{2,1,0:T(8,128)S(1)}, u32[]{:S(2)}, u32[]{:S(2)}) collective-permute-start(f32[1,40,128]{2,1,0:T(8,128)S(1)} %shard_map.125.part0_ref), channel_id=1, source_target_pairs={{0,64},{1,65},{2,66},{3,67},{4,68},{5,69},{6,70},{7,71},{8,72},{9,... | collective-permute-start | bytes 61448 | tf_op jit(solution)/shard_map/ppermute | solution.py:895
  (1 other events, 0.8 us)

commit v7 on v6

--- a/solution.py
+++ b/solution.py
@@ -192,11 +192,15 @@
     local_row_ref,
     local_col_ref,
     local_couple_ref,
+    up_row_ref,
     cross_ref,
     columns_ref,
     paths_ref,
+    products_ref,
+    turned_ref,
 ):
     del order_ref
+    store_products("row", up_row_ref, products_ref, turned_ref)
     halves = [slice(0, RANK), slice(RANK, 2 * RANK)]
 
     def store(ref, index, value):
@@ -219,10 +223,42 @@
         store(columns_ref, (part(q, LEAF_COLS),), mm(col_basis_ref[q], split(path)))
 
 
+def store_top(up_row_ref, up_col_ref, up_couple_ref, top_ref):
+    def store(source, target, value):
+        high, low = split(value)
+        rows = slice(source * RANK, (source + 1) * RANK)
+        cols = slice(target * RANK, target * RANK + value.shape[1])
+        top_ref[0, rows, cols] = high
+        top_ref[1, rows, cols] = low
+
+    for p in range(4):
+        m, i = p // 2, p % 2
+        store(p, p, jnp.zeros((RANK, RANK), f32))
+        store(p, p ^ 1, up_couple_ref[6, 1 - i])
+        half = up_col_ref[6, i * RANK : (i + 1) * RANK]
+        gained = mm(half, pair_at(up_couple_ref, 7, 1 - m))
+        store(p, 2 * (1 - m), mm(gained, pair_at(up_row_ref, 6), transposed=True))
+
+
 def images_kernel(
-    order_ref, rows_ref, dense_ref, row_basis_ref, col_basis_ref, cross_ref, paths_ref, images_ref
+    order_ref,
+    rows_ref,
+    dense_ref,
+    row_basis_ref,
+    col_basis_ref,
+    cross_ref,
+    paths_ref,
+    up_row_ref,
+    up_col_ref,
+    up_couple_ref,
+    images_ref,
+    top_ref,
+    products_ref,
+    turned_ref,
 ):
     del order_ref
+    store_products("mid", up_row_ref, products_ref, turned_ref)
+    store_top(up_row_ref, up_col_ref, up_couple_ref, top_ref)
     turned = []
     images = []
     moved = []
@@ -322,6 +358,46 @@
             store_pair(nodes_ref, base + k, value)
         grams = gram_climb(grams, pair_at(up_row_ref, stage(name)[0] + height))
     return grams[0]
+
+
+def product_base(height):
+    return (2 << height) - 2
+
+
+def store_products(name, up_row_ref, products_ref, turned_ref):
+    level, heights, _ = stage(name)
+    products = None
+    for height in range(heights):
+        halves = [half_of(up_row_ref, level + height, child) for child in range(2)]
+        if products is None:
+            products = [half[0].astype(f32) + half[1].astype(f32) for half in halves]
+        else:
+            products = [mm(product, half) for half in halves for product in products]
+        for k, product in enumerate(products):
+            store_pair(products_ref, product_base(height) + k, product)
+            turned_ref[product_base(height) + k] = jnp.transpose(product)
+
+
+def member_grams(name, grams, products_ref, turned_ref, nodes_ref):
+    _, heights, count = stage(name)
+    left = []
+    for d in range(count):
+        store_pair(nodes_ref, d, grams[d])
+        turned = [turned_ref[product_base(h) + d % (2 << h)] for h in range(heights)]
+        left.append(unstack(mm(stack(turned), split(grams[d])), heights))
+    for height in range(heights):
+        size = 2 << height
+        base = product_base(height)
+        terms = [pair_at(products_ref, base + t) for t in range(size)]
+        table = tuple(stack([term[k] for term in terms]) for k in range(2))
+        rows = []
+        for n in range(count // size):
+            rows.append(jnp.concatenate([left[n * size + t][height] for t in range(size)], 1))
+        nodes = unstack(mm(stack(rows), table), len(rows))
+        if height + 1 < heights:
+            for k, value in enumerate(nodes):
+                store_pair(nodes_ref, bases(name)[height + 1] + k, value)
+    return nodes[0]
 
 
 def start_copies(pairs, sems):
@@ -402,6 +478,10 @@
     return [unpack(recv_ref[d, base:], recv_ref[d, RHS + 2 : RHS + 3]) for d in range(count)]
 
 
+def own_kernel(message_ref, out_ref):
+    out_ref[...] = message_ref[...]
+
+
 def path_product(me, level, path, up_col_ref):
     half = half_of(up_col_ref, level, (me >> level) & 1)
     return mm(path, half)
@@ -432,7 +512,8 @@
 
 def row_kernel(
     me_ref,
-    order_ref,
+    products_ref,
+    turned_ref,
     part0_ref,
     part1_ref,
     part2_ref,
@@ -449,11 +530,10 @@
     scratch_ref,
     slice_ref,
 ):
-    del order_ref
     me = me_ref[0]
     gather_parts(me, "row", (part0_ref, part1_ref, part2_ref, part3_ref), recv_ref)
     summary = climb_group("row", me_ref, recv_ref, up_row_ref, sib_ref, scratch_ref)
-    gram = group_grams("row", received_grams(recv_ref), up_row_ref, nodes_ref)
+    gram = member_grams("row", received_grams(recv_ref), products_ref, turned_ref, nodes_ref)
     child = 1 - (me & 1)
     store_pair(gain_ref, 0, up_couple_ref[0, child])
     path = up_col_ref[0, pl.ds(pl.multiple_of((me & 1) * RANK, RANK), RANK), :]
@@ -628,7 +708,8 @@
 
 def row_pair_kernel(
     me_ref,
-    order_ref,
+    products_ref,
+    turned_ref,
     part0_ref,
     part1_ref,
     part2_ref,
@@ -647,7 +728,6 @@
     gain_ref,
     below_ref,
 ):
-    del order_ref
     gather_parts(me_ref[0], "row", (part0_ref, part1_ref, part2_ref, part3_ref), recv_ref)
     tables = (up_row_ref, up_col_ref, up_couple_ref)
     keep = (path_ref, gain_ref, below_ref)
@@ -662,7 +742,7 @@
             low = base + (p % 2) * HALF + d * SLICE
             slices.append(recv_ref[p // 2, low : low + SLICE])
         grams.append(unpack(stack(slices), diagonal_ref[d : d + 1]))
-    top, diagonal = pack(group_grams("mid", grams, up_row_ref, mid_nodes_ref))
+    top, diagonal = pack(member_grams("mid", grams, products_ref, turned_ref, mid_nodes_ref))
     gram_ref[...] = stack([top, stat_block(diagonal)])
 
 
@@ -698,13 +778,10 @@
     send(msg_ref, stack(pair_group(name, me_ref, recv_ref, tables, nodes_ref, None)))
 
 
-def top_levels(recv_ref, up_row_ref, up_col_ref, up_couple_ref, gram_ref):
+def top_levels(recv_ref, top_ref, gram_ref):
     first, second, _, total, energy = rescale(recv_ref)
-    gained = couple_all(first, (pair_at(up_couple_ref, 6, 0), pair_at(up_couple_ref, 6, 1)))
-    first = climb(first, pair_at(up_col_ref, 6))
-    potential = couple_all(first, (pair_at(up_couple_ref, 7, 0), pair_at(up_couple_ref, 7, 1)))
-    below = descend(potential, pair_at(up_row_ref, 6))
-    potential = [a + b for a, b in zip(gained, below)]
+    potential = mm(jnp.concatenate(first, 1), pair_at(top_ref))
+    potential = [lanes(potential, d) for d in range(recv_ref.shape[0])]
     cross = jnp.zeros((RHS, RANK), f32)
     summed = []
     for d in range(recv_ref.shape[0]):
@@ -731,8 +808,7 @@
     near_gain_ref,
     mid_gain_ref,
     up_row_ref,
-    up_col_ref,
-    up_couple_ref,
+    top_ref,
     core_nodes_ref,
     row_nodes_ref,
     mid_nodes_ref,
@@ -762,9 +838,7 @@
     for d in range(recv_ref.shape[0]):
         gram = unpack(recv_ref[d, base : base + HALF], recv_ref[d, base + HALF : base + HALF + 1])
         store_pair(top_gram_ref, d, gram)
-    potential, summed, squares, energy = top_levels(
-        recv_ref, up_row_ref, up_col_ref, up_couple_ref, top_gram_ref
-    )
+    potential, summed, squares, energy = top_levels(recv_ref, top_ref, top_gram_ref)
     alpha = jnp.sqrt(squares)
     rho = jnp.sqrt(energy)
     alpha_ref[...] = jnp.broadcast_to(alpha, (RHS, RANK))
@@ -819,9 +893,7 @@
     part1_ref,
     part2_ref,
     part3_ref,
-    up_row_ref,
-    up_col_ref,
-    up_couple_ref,
+    top_ref,
     top_gram_ref,
     beta_ref,
     alpha_ref,
@@ -832,9 +904,7 @@
     recv_ref,
 ):
     gather_parts(me_ref[0], "far", (part0_ref, part1_ref, part2_ref, part3_ref), recv_ref)
-    _, _, squares, energy = top_levels(
-        recv_ref, up_row_ref, up_col_ref, up_couple_ref, top_gram_ref
-    )
+    _, _, squares, energy = top_levels(recv_ref, top_ref, top_gram_ref)
     theta = jnp.sqrt(squares)
     rho2 = jnp.sqrt(energy - squares)
     rho = rho_ref[:, :1]
@@ -950,29 +1020,35 @@
         operands = [earlier, y, dense, row_basis, col_basis, cross]
         return call(inner_kernel, [col_shape], operands, (), (0,))[0]
 
+    parts = swap_parts(message, "core")
+    parts[0] = call(own_kernel, [message.shape], [message])[0]
     message, core_sib, core_nodes = call(
         core_kernel,
         [(1,) + longer(single, HALF), sibling_shape("core"), nodes_of("core")],
-        [me] + swap_parts(message, "core") + [up_row],
+        [me] + parts + [up_row],
         received("core", longer(single, HALF)) + node_scratch("core"),
     )
-    cross, columns, paths = call(
+    def products_of(name):
+        count = node_count(name)
+        return [pair_shape(count, RANK, RANK), (count, RANK, RANK)]
+
+    cross, columns, paths, *products = call(
         paths_kernel,
         [
             pair_shape(LEAF_DEV * RANK, LEAF_DEV * RANK),
             pair_shape(LEAF_DEV * LEAF_COLS, RANK),
             pair_shape(LEAF_DEV * RANK, RANK),
-        ],
-        [message, col_basis, local_row, local_col, local_couple],
+        ]
+        + products_of("row"),
+        [message, col_basis, local_row, local_col, local_couple, up_row],
         (),
         (0,),
     )
     message, row_sib, row_nodes, near_gain, path = call(
         row_kernel,
         [(groups,) + longer(single, SLICE), sibling_shape("row"), nodes_of("row"), nodes_shape(3), gram_shape],
-        [me, paths] + swap_parts(message, "row") + tables,
+        [me] + products + swap_parts(message, "row") + tables,
         received("row", longer(single, HALF)) + node_scratch("row") + [(HALF, RANK)],
-        (1,),
     )
     message, mid_sib, part, diagonal = call(
         mid_kernel,
@@ -1000,19 +1076,18 @@
         [me] + swap_parts(message, "core") + tables + [core_nodes],
         received("core", longer(double, HALF)) + node_scratch("core", 2),
     )
-    (images,) = call(
+    images, top, *products = call(
         images_kernel,
-        [pair_shape(RANK, LEAF_DEV * LEAF_COLS)],
-        [message, box_rows, dense, row_basis, col_basis, cross, paths],
+        [pair_shape(RANK, LEAF_DEV * LEAF_COLS), pair_shape(4 * RANK, 4 * RANK)] + products_of("mid"),
+        [message, box_rows, dense, row_basis, col_basis, cross, paths] + tables,
         (),
         (0,),
     )
     message, row_path, row_own, mid_nodes, gram = call(
         row_pair_kernel,
         [(groups,) + double, path_shape("row"), stat, nodes_of("mid"), (HALF + 8, RANK)],
-        [me, images] + swap_parts(message, "row") + tables + [row_nodes, diagonal],
+        [me] + products + swap_parts(message, "row") + tables + [row_nodes, diagonal],
         received("row", longer(double, 2 * HALF)) + node_scratch("row", 2),
-        (1,),
     )
     message, mid_path, mid_own = call(
         mid_pair_kernel,
@@ -1027,8 +1102,7 @@
         + swap_parts(message, "far")
         + [core_path, core_own, row_path, row_own, mid_path, mid_own]
         + gains
-        + tables
-        + [core_nodes, row_nodes, mid_nodes]
+        + [up_row, top, core_nodes, row_nodes, mid_nodes]
         + [dense, row_basis, col_basis, cross, columns, images, x, own, within(inner, message)],
         [(6,) + tile, (4,) + tile] + received("far", longer(double, HALF + 8)),
     )
@@ -1047,7 +1121,7 @@
     (out,) = call(
         final_kernel,
         [col_shape],
-        [me] + swap_parts(message, "far") + tables + [top_nodes, beta, alpha, rho, v, x],
+        [me] + swap_parts(message, "far") + [top, top_nodes, beta, alpha, rho, v, x],
         received("far", double),
     )
     return out

time: 115 us -> 113 us (0.983)
  waiting for transfers between devices: 15.9 us -> 14.2 us
    ppermute x21, waiting for transfers between devices: 15.9 us -> 14.2 us  [swap_parts(): parts.append(lax.ppermute(message, 'leaf', pairs))]
    pallas_call x18 -> x19, Pallas kernels: 30.1 us -> 30.2 us  [call(): pl.pallas_call(kernel, out_shape=outs, in_specs=[pl.BlockSpec(memory_spac...]
  transfers between devices with their start and end apart: 21 -> 21, of which waited for: 14 -> 12; matrix products, arithmetic and copies ran while one was open for 0% -> 0% of each run, Pallas kernels for 6% -> 8%
where the time goes in v7:
time: 113 us
  blocking collectives  40 us (35%)
  Pallas kernels  30.2 us (27%)
  starting transfers between devices  26.3 us (23%)
  waiting for transfers between devices  14.2 us (13%)
  local copies, waits for them, and re-layouts  1.83 us (2%)
    all_to_all x3, blocking collectives, swap_mid(): return lax.all_to_all(message, 'leaf', 0, 0, axis_index_groups=groups)  40 us
    pallas_call x19, Pallas kernels, call(): pl.pallas_call(kernel, out_shape=outs, in_specs=[pl.BlockSpec(memory_spac...  30.2 us
    ppermute x21, starting transfers between devices, swap_parts(): parts.append(lax.ppermute(message, 'leaf', pairs))  26.3 us
    ppermute x21, waiting for transfers between devices, swap_parts(): parts.append(lax.ppermute(message, 'leaf', pairs))  14.2 us
  transfers between devices with their start and end apart: 21, of which 12 were waited for; matrix products, arithmetic and copies ran while one was open for 0% of the time, Pallas kernels for 8%

profile of v7, /device:TPU:2, one launch (start us, length us, event | category | flops | bytes accessed | tf_op | source)
XLA Modules:
  0.0 112.8 jit_solution(16689941961474200039)
XLA Ops:
  0.0 3.5 %shard_map.109 = (f32[16,2048]{1,0:T(8,128)}, f32[1,88,128]{2,1,0:T(8,128)}) custom-call(s32[1]{0:T(128)} %bitcast.me_ref, s32[4]{0:T(128)} %rows_ref.5, f32[16,2048]{1,0:T(8,128)} %rhs_hbm.1, f32[4,512,128]{2,1,0:T(8,128)} %row_basis_ref.9, f32[3,256,128]{2,1,0:T(8,128)} %local_row_ref.1), custom_call_target="tpu_custom_call" | custom-call | flops 6000000000 | tf_op jit(solution)/shard_map/pallas_call | solution.py:923
  5.7 2.2 %collective-permute-start.3 = (f32[1,88,128]{2,1,0:T(8,128)S(1)}, f32[1,88,128]{2,1,0:T(8,128)S(1)}, u32[]{:S(2)}, u32[]{:S(2)}) collective-permute-start(f32[1,88,128]{2,1,0:T(8,128)S(1)} %get-tuple-element.51.order_ref.part0_ref), channel_id=1, source_target_pairs={{0,4},{1,5},{2,6},{3,7},{4,0},{5,1},{6,2},{7,3},{8,12},{9,13},{10,... | collective-permute-start | bytes 135176 | tf_op jit(solution)/shard_map/ppermute | solution.py:965
  7.9 1.6 %collective-permute-start.2 = (f32[1,88,128]{2,1,0:T(8,128)S(1)}, f32[1,88,128]{2,1,0:T(8,128)S(1)}, u32[]{:S(2)}, u32[]{:S(2)}) collective-permute-start(f32[1,88,128]{2,1,0:T(8,128)S(1)} %get-tuple-element.51.order_ref.part0_ref), channel_id=1, source_target_pairs={{0,6},{1,7},{2,4},{3,5},{4,2},{5,3},{6,0},{7,1},{8,14},{9,15},{10,... | collective-permute-start | bytes 135176 | tf_op jit(solution)/shard_map/ppermute | solution.py:965
  10.5 1.7 %shard_map.112 = (bf16[2,512,512]{2,1,0:T(8,128)(2,1)S(1)}, bf16[2,1024,128]{2,1,0:T(8,128)(2,1)S(1)}, bf16[2,512,128]{2,1,0:T(8,128)(2,1)S(1)}, bf16[2,6,128,128]{3,2,1,0:T(8,128)(2,1)S(1)}, f32[6,128,128]{2,1,0:T(8,128)S(1)}) custom-call(f32[1,88,128]{2,1,0:T(8,128)S(1)} %get-tuple-element.51.order_ref.part0_ref, f32[4,256,128]{2,1,0:T(8,128)S(1)} %copy-done.5, ...), custom_call_target="tpu_custom_call" | custom-call | flops 6000000000 | tf_op jit(solution)/shard_map/pallas_call | solution.py:923
  12.2 1.4 %collective-permute-done.1.part1_ref = f32[1,88,128]{2,1,0:T(8,128)S(1)} collective-permute-done((f32[1,88,128]{2,1,0:T(8,128)S(1)}, f32[1,88,128]{2,1,0:T(8,128)S(1)}, u32[]{:S(2)}, u32[]{:S(2)}) %collective-permute-start.1) | collective-permute-done | bytes 45088 | tf_op jit(solution)/shard_map/ppermute | solution.py:965
  14.6 16.3 %all_to_all.15.recv_ref = f32[8,32,128]{2,1,0:T(8,128)S(1)} all-to-all(f32[8,32,128]{2,1,0:T(8,128)S(1)} %get-tuple-element.54), channel_id=1, replica_groups={{0,8,16,24,32,40,48,56},{1,9,17,25,33,41,49,57},{2,10,18,26,34,42,50,58..., dimensions={0} | all-to-all | bytes 262144 | tf_op jit(solution)/shard_map/all_to_all | solution.py:971
  31.3 3.2 %collective-permute-start.6 = (f32[1,24,128]{2,1,0:T(8,128)S(1)}, f32[1,24,128]{2,1,0:T(8,128)S(1)}, u32[]{:S(2)}, u32[]{:S(2)}) collective-permute-start(f32[1,24,128]{2,1,0:T(8,128)S(1)} %get-tuple-element.55.order_ref.part0_ref), channel_id=1, source_target_pairs={{0,128},{1,129},{2,130},{3,131},{4,132},{5,133},{6,134},{7,135},{8... | collective-permute-start | bytes 36872 | tf_op jit(solution)/shard_map/ppermute | solution.py:965
  34.5 1.1 collective-permute-start.5
  37.4 1.1 shard_map.116.within_ref
  39.4 3.4 %shard_map.117 = (f32[16,1024]{1,0:T(8,128)S(1)}, f32[16,128]{1,0:T(8,128)S(1)}, f32[1,104,128]{2,1,0:T(8,128)S(1)}, f32[8,128]{1,0:T(8,128)S(1)}, f32[16,2048]{1,0:T(8,128)S(1)}) custom-call(s32[1]{0:T(128)} %bitcast.me_ref, s32[4]{0:T(128)S(1)} %copy-done.10, f32[1,24,128]{2,1,0:T(8,128)S(1)} %get-tuple-element.55.order_ref.part0_ref, ...), custom_call_target="tpu_custom_call" | custom-call | flops 6000000000 | tf_op jit(solution)/shard_map/pallas_call | solution.py:923
  42.9 1.2 %collective-permute-done.7.part1_ref = f32[1,104,128]{2,1,0:T(8,128)S(1)} collective-permute-done((f32[1,104,128]{2,1,0:T(8,128)S(1)}, f32[1,104,128]{2,1,0:T(8,128)S(1)}, u32[]{:S(2)}, u32[]{:S(2)}) %collective-permute-start.7) | collective-permute-done | bytes 53280 | tf_op jit(solution)/shard_map/ppermute | solution.py:965
  44.6 3.0 %collective-permute-start.10 = (f32[1,168,128]{2,1,0:T(8,128)S(1)}, f32[1,168,128]{2,1,0:T(8,128)S(1)}, u32[]{:S(2)}, u32[]{:S(2)}) collective-permute-start(f32[1,168,128]{2,1,0:T(8,128)S(1)} %get-tuple-element.68.order_ref.part0_ref), channel_id=1, source_target_pairs={{0,4},{1,5},{2,6},{3,7},{4,0},{5,1},{6,2},{7,3},{8,12},{9,13},{10,... | collective-permute-start | bytes 258056 | tf_op jit(solution)/shard_map/ppermute | solution.py:965
  48.2 1.1 %collective-permute-start.8 = (f32[1,168,128]{2,1,0:T(8,128)S(1)}, f32[1,168,128]{2,1,0:T(8,128)S(1)}, u32[]{:S(2)}, u32[]{:S(2)}) collective-permute-start(f32[1,168,128]{2,1,0:T(8,128)S(1)} %get-tuple-element.68.order_ref.part0_ref), channel_id=1, source_target_pairs={{0,2},{1,3},{2,0},{3,1},{4,6},{5,7},{6,4},{7,5},{8,10},{9,11},{10,... | collective-permute-start | bytes 258056 | tf_op jit(solution)/shard_map/ppermute | solution.py:965
  49.4 3.8 %shard_map.119 = (bf16[2,128,1024]{2,1,0:T(8,128)(2,1)S(1)}, bf16[2,512,512]{2,1,0:T(8,128)(2,1)S(1)}, bf16[2,14,128,128]{3,2,1,0:T(8,128)(2,1)S(1)}, f32[14,128,128]{2,1,0:T(8,128)S(1)}) custom-call(f32[1,168,128]{2,1,0:T(8,128)S(1)} %get-tuple-element.68.order_ref.part0_ref, s32[4]{0:T(128)S(1)} %copy-done.10, f32[4,512,256]{2,1,0:T(8,128)S(1)} %copy-done, ...), custom_call_target="tpu_custom_call" | custom-call | flops 6000000000 | tf_op jit(solution)/shard_map/pallas_call | solution.py:923
  53.2 2.2 %shard_map.120 = (f32[8,40,128]{2,1,0:T(8,128)S(1)}, f32[6,16,128]{2,1,0:T(8,128)S(1)}, f32[8,128]{1,0:T(8,128)S(1)}, bf16[2,14,128,128]{3,2,1,0:T(8,128)(2,1)S(1)}, f32[72,128]{1,0:T(8,128)S(1)}) custom-call(s32[1]{0:T(128)} %bitcast.me_ref, bf16[2,14,128,128]{3,2,1,0:T(8,128)(2,1)S(1)} %get-tuple-element.69.products_ref, ...), custom_call_target="tpu_custom_call" | custom-call | flops 6000000000 | tf_op jit(solution)/shard_map/pallas_call | solution.py:923
  55.4 11.9 %all_to_all.16.recv_ref = f32[8,40,128]{2,1,0:T(8,128)S(1)} all-to-all(f32[8,40,128]{2,1,0:T(8,128)S(1)} %get-tuple-element.73), channel_id=1, replica_groups={{0,8,16,24,32,40,48,56},{1,9,17,25,33,41,49,57},{2,10,18,26,34,42,50,58..., dimensions={0} | all-to-all | bytes 327680 | tf_op jit(solution)/shard_map/all_to_all | solution.py:971
  67.3 1.3 %shard_map.121 = (f32[1,112,128]{2,1,0:T(8,128)S(1)}, f32[9,16,128]{2,1,0:T(8,128)S(1)}, f32[8,128]{1,0:T(8,128)S(1)}) custom-call(s32[1]{0:T(128)} %bitcast.me_ref, f32[8,40,128]{2,1,0:T(8,128)S(1)} %all_to_all.16.recv_ref, f32[7,256,128]{2,1,0:T(8,128)S(1)} %copy-done.3, f32[7,256,128]{2,1,0:T(8,128)S(1)} %copy-done.4, f32[8,2,128,128]{3,2,1,0:T(8,128)S(1)} %copy-done.2, ...), custom_call_target="tpu_custom_call" | custom-call | flops 6000000000 | tf_op jit(solution)/shard_map/pallas_call | solution.py:923
  68.6 2.9 %collective-permute-start.13 = (f32[1,112,128]{2,1,0:T(8,128)S(1)}, f32[1,112,128]{2,1,0:T(8,128)S(1)}, u32[]{:S(2)}, u32[]{:S(2)}) collective-permute-start(f32[1,112,128]{2,1,0:T(8,128)S(1)} %get-tuple-element.76.order_ref.part0_ref), channel_id=1, source_target_pairs={{0,128},{1,129},{2,130},{3,131},{4,132},{5,133},{6,134},{7,135},{8... | collective-permute-start | bytes 172040 | tf_op jit(solution)/shard_map/ppermute | solution.py:965
  71.5 1.1 collective-permute-start.12
  72.5 1.1 shard_map.122.within_ref
  73.6 1.1 collective-permute-done.13.part3_ref
  74.7 2.2 %collective-permute-done.12.part2_ref = f32[1,112,128]{2,1,0:T(8,128)S(1)} collective-permute-done((f32[1,112,128]{2,1,0:T(8,128)S(1)}, f32[1,112,128]{2,1,0:T(8,128)S(1)}, u32[]{:S(2)}, u32[]{:S(2)}) %collective-permute-start.12) | collective-permute-done | bytes 57376 | tf_op jit(solution)/shard_map/ppermute | solution.py:965
  76.9 4.8 %shard_map.123 = (f32[16,1024]{1,0:T(8,128)S(1)}, f32[16,1024]{1,0:T(8,128)S(1)}, f32[16,128]{1,0:T(8,128)S(1)}, f32[16,128]{1,0:T(8,128)S(1)}, f32[1,40,128]{2,...) custom-call(s32[1]{0:T(128)} %bitcast.me_ref, s32[4]{0:T(128)S(1)} %copy-done.10, ...), custom_call_target="tpu_custom_call" | custom-call | flops 6000000000 | tf_op jit(solution)/shard_map/pallas_call | solution.py:923
  81.8 1.2 %collective-permute-done.14.refs_1_ = f32[1,40,128]{2,1,0:T(8,128)S(1)} collective-permute-done((f32[1,40,128]{2,1,0:T(8,128)S(1)}, f32[1,40,128]{2,1,0:T(8,128)S(1)}, u32[]{:S(2)}, u32[]{:S(2)}) %collective-permute-start.14) | collective-permute-done | bytes 20512 | tf_op jit(solution)/shard_map/ppermute | solution.py:965
  83.4 3.1 %collective-permute-start.17 = (f32[1,40,128]{2,1,0:T(8,128)S(1)}, f32[1,40,128]{2,1,0:T(8,128)S(1)}, u32[]{:S(2)}, u32[]{:S(2)}) collective-permute-start(f32[1,40,128]{2,1,0:T(8,128)S(1)} %shard_map.124.refs_0_), channel_id=1, source_target_pairs={{0,4},{1,5},{2,6},{3,7},{4,0},{5,1},{6,2},{7,3},{8,12},{9,13},{10,... | collective-permute-start | bytes 61448 | tf_op jit(solution)/shard_map/ppermute | solution.py:965
  88.8 1.6 %collective-permute-done.16.refs_2_ = f32[1,40,128]{2,1,0:T(8,128)S(1)} collective-permute-done((f32[1,40,128]{2,1,0:T(8,128)S(1)}, f32[1,40,128]{2,1,0:T(8,128)S(1)}, u32[]{:S(2)}, u32[]{:S(2)}) %collective-permute-start.16) | collective-permute-done | bytes 20512 | tf_op jit(solution)/shard_map/ppermute | solution.py:965
  91.8 11.8 %all_to_all.17.refs_0_ = f32[8,40,128]{2,1,0:T(8,128)S(1)} all-to-all(f32[8,40,128]{2,1,0:T(8,128)S(1)} %shard_map.125), channel_id=1, replica_groups={{0,8,16,24,32,40,48,56},{1,9,17,25,33,41,49,57},{2,10,18,26,34,42,50,58..., dimensions={0} | all-to-all | bytes 327680 | tf_op jit(solution)/shard_map/all_to_all | solution.py:971
  103.7 1.3 %shard_map.126.part0_ref = f32[1,40,128]{2,1,0:T(8,128)S(1)} custom-call(s32[1]{0:T(128)} %bitcast.me_ref, f32[8,40,128]{2,1,0:T(8,128)S(1)} %all_to_all.17.refs_0_, f32[7,256,128]{2,1,0:T(8,128)S(1)} %copy-done.3, f32[7,256,128]{2,1,0:T(8,128)S(1)} %copy-done.4, f32[8,2,128,128]{3,2,1,0:T(8,128)S(1)} %copy-done.2, ...), custom_call_target="tpu_custom_call" | custom-call | flops 6000000000 | tf_op jit(solution)/shard_map/pallas_call | solution.py:923
  104.9 1.5 %collective-permute-start.20 = (f32[1,40,128]{2,1,0:T(8,128)S(1)}, f32[1,40,128]{2,1,0:T(8,128)S(1)}, u32[]{:S(2)}, u32[]{:S(2)}) collective-permute-start(f32[1,40,128]{2,1,0:T(8,128)S(1)} %shard_map.126.part0_ref), channel_id=1, source_target_pairs={{0,128},{1,129},{2,130},{3,131},{4,132},{5,133},{6,134},{7,135},{8... | collective-permute-start | bytes 61448 | tf_op jit(solution)/shard_map/ppermute | solution.py:965
  108.5 1.8 %collective-permute-done.20.part3_ref = f32[1,40,128]{2,1,0:T(8,128)S(1)} collective-permute-done((f32[1,40,128]{2,1,0:T(8,128)S(1)}, f32[1,40,128]{2,1,0:T(8,128)S(1)}, u32[]{:S(2)}, u32[]{:S(2)}) %collective-permute-start.20) | collective-permute-done | bytes 20512 | tf_op jit(solution)/shard_map/ppermute | solution.py:965
  110.3 1.2 %collective-permute-done.19.part2_ref = f32[1,40,128]{2,1,0:T(8,128)S(1)} collective-permute-done((f32[1,40,128]{2,1,0:T(8,128)S(1)}, f32[1,40,128]{2,1,0:T(8,128)S(1)}, u32[]{:S(2)}, u32[]{:S(2)}) %collective-permute-start.19) | collective-permute-done | bytes 20512 | tf_op jit(solution)/shard_map/ppermute | solution.py:965
  111.5 1.3 %shard_map.127 = f32[16,1024]{1,0:T(8,128)} custom-call(s32[1]{0:T(128)} %bitcast.me_ref, f32[1,40,128]{2,1,0:T(8,128)S(1)} %shard_map.126.part0_ref, f32[1,40,128]{2,1,0:T(8,128)S(1)} %collective-permute-done.18.part1_ref, f32[1,40,128]{2,1,0:T(8,128)S(1)} %collective-permute-done.19.part2_ref, f32[1,40,128]{2,1,0:T(8,128)S(1)} %collective-permute-done.20.part3_ref, ...), custom_call_target="tpu_custom_call" | custom-call | flops 6000000000 | tf_op jit(solution)/shard_map/pallas_call | solution.py:923
  (56 shorter events, 14.8 us)
Async XLA Ops:
  3.5 1.5 %copy-start.3 = (f32[7,256,128]{2,1,0:T(8,128)S(1)}, f32[7,256,128]{2,1,0:T(8,128)}, u32[]{:S(2)}) copy-start(f32[7,256,128]{2,1,0:T(8,128)} %refs_1_.1) | copy-start | bytes 2752516
  3.5 1.5 %collective-permute-start = (f32[1,88,128]{2,1,0:T(8,128)}, f32[1,88,128]{2,1,0:T(8,128)S(1)}, u32[]{:S(2)}, u32[]{:S(2)}) collective-permute-start(f32[1,88,128]{2,1,0:T(8,128)} %get-tuple-element.50.message_ref), channel_id=1, source_target_pairs={{0,1},{1,0},{2,3},{3,2},{4,5},{5,4},{6,7},{7,6},{8,9},{9,8},{10,11... | collective-permute-start | bytes 135176 | tf_op jit(solution)/shard_map/ppermute | solution.py:965
  4.4 6.0 %copy-start.5 = (f32[4,256,128]{2,1,0:T(8,128)S(1)}, f32[4,256,128]{2,1,0:T(8,128)}, u32[]{:S(2)}) copy-start(f32[4,256,128]{2,1,0:T(8,128)} %col_basis_ref.11) | copy-start | bytes 1572868
  4.4 6.0 %copy-start.6 = (f32[3,256,128]{2,1,0:T(8,128)S(1)}, f32[3,256,128]{2,1,0:T(8,128)}, u32[]{:S(2)}) copy-start(f32[3,256,128]{2,1,0:T(8,128)} %local_row_ref.1) | copy-start | bytes 1179652
  4.5 6.0 %copy-start.7 = (f32[3,256,128]{2,1,0:T(8,128)S(1)}, f32[3,256,128]{2,1,0:T(8,128)}, u32[]{:S(2)}) copy-start(f32[3,256,128]{2,1,0:T(8,128)} %local_col_ref.1) | copy-start | bytes 1179652
  4.5 6.0 %copy-start.8 = (f32[3,2,128,128]{3,2,1,0:T(8,128)S(1)}, f32[3,2,128,128]{3,2,1,0:T(8,128)}, u32[]{:S(2)}) copy-start(f32[3,2,128,128]{3,2,1,0:T(8,128)} %local_couple_ref.1) | copy-start | bytes 1179652
  5.6 7.9 %copy-start.2 = (f32[8,2,128,128]{3,2,1,0:T(8,128)S(1)}, f32[8,2,128,128]{3,2,1,0:T(8,128)}, u32[]{:S(2)}) copy-start(f32[8,2,128,128]{3,2,1,0:T(8,128)} %refs_3_.3) | copy-start | bytes 3145732
  5.6 7.9 %copy-start.4 = (f32[7,256,128]{2,1,0:T(8,128)S(1)}, f32[7,256,128]{2,1,0:T(8,128)}, u32[]{:S(2)}) copy-start(f32[7,256,128]{2,1,0:T(8,128)} %refs_2_.3) | copy-start | bytes 2752516
  5.7 6.5 %collective-permute-start.3 = (f32[1,88,128]{2,1,0:T(8,128)S(1)}, f32[1,88,128]{2,1,0:T(8,128)S(1)}, u32[]{:S(2)}, u32[]{:S(2)}) collective-permute-start(f32[1,88,128]{2,1,0:T(8,128)S(1)} %get-tuple-element.51.order_ref.part0_ref), channel_id=1, source_target_pairs={{0,4},{1,5},{2,6},{3,7},{4,0},{5,1},{6,2},{7,3},{8,12},{9,13},{10,... | collective-permute-start | bytes 135176 | tf_op jit(solution)/shard_map/ppermute | solution.py:965
  7.9 4.3 %collective-permute-start.2 = (f32[1,88,128]{2,1,0:T(8,128)S(1)}, f32[1,88,128]{2,1,0:T(8,128)S(1)}, u32[]{:S(2)}, u32[]{:S(2)}) collective-permute-start(f32[1,88,128]{2,1,0:T(8,128)S(1)} %get-tuple-element.51.order_ref.part0_ref), channel_id=1, source_target_pairs={{0,6},{1,7},{2,4},{3,5},{4,2},{5,3},{6,0},{7,1},{8,14},{9,15},{10,... | collective-permute-start | bytes 135176 | tf_op jit(solution)/shard_map/ppermute | solution.py:965
  9.5 4.0 %collective-permute-start.1 = (f32[1,88,128]{2,1,0:T(8,128)S(1)}, f32[1,88,128]{2,1,0:T(8,128)S(1)}, u32[]{:S(2)}, u32[]{:S(2)}) collective-permute-start(f32[1,88,128]{2,1,0:T(8,128)S(1)} %get-tuple-element.51.order_ref.part0_ref), channel_id=1, source_target_pairs={{0,2},{1,3},{2,0},{3,1},{4,6},{5,7},{6,4},{7,5},{8,10},{9,11},{10,... | collective-permute-start | bytes 135176 | tf_op jit(solution)/shard_map/ppermute | solution.py:965
  31.3 7.2 %collective-permute-start.6 = (f32[1,24,128]{2,1,0:T(8,128)S(1)}, f32[1,24,128]{2,1,0:T(8,128)S(1)}, u32[]{:S(2)}, u32[]{:S(2)}) collective-permute-start(f32[1,24,128]{2,1,0:T(8,128)S(1)} %get-tuple-element.55.order_ref.part0_ref), channel_id=1, source_target_pairs={{0,128},{1,129},{2,130},{3,131},{4,132},{5,133},{6,134},{7,135},{8... | collective-permute-start | bytes 36872 | tf_op jit(solution)/shard_map/ppermute | solution.py:965
  34.5 4.9 %collective-permute-start.5 = (f32[1,24,128]{2,1,0:T(8,128)S(1)}, f32[1,24,128]{2,1,0:T(8,128)S(1)}, u32[]{:S(2)}, u32[]{:S(2)}) collective-permute-start(f32[1,24,128]{2,1,0:T(8,128)S(1)} %get-tuple-element.55.order_ref.part0_ref), channel_id=1, source_target_pairs={{0,192},{1,193},{2,194},{3,195},{4,196},{5,197},{6,198},{7,199},{8... | collective-permute-start | bytes 36872 | tf_op jit(solution)/shard_map/ppermute | solution.py:965
  35.6 3.9 %collective-permute-start.4 = (f32[1,24,128]{2,1,0:T(8,128)S(1)}, f32[1,24,128]{2,1,0:T(8,128)S(1)}, u32[]{:S(2)}, u32[]{:S(2)}) collective-permute-start(f32[1,24,128]{2,1,0:T(8,128)S(1)} %get-tuple-element.55.order_ref.part0_ref), channel_id=1, source_target_pairs={{0,64},{1,65},{2,66},{3,67},{4,68},{5,69},{6,70},{7,71},{8,72},{9,... | collective-permute-start | bytes 36872 | tf_op jit(solution)/shard_map/ppermute | solution.py:965
  35.6 1.6 %copy-start = (f32[4,512,256]{2,1,0:T(8,128)S(1)}, f32[4,512,256]{2,1,0:T(8,128)}, u32[]{:S(2)}) copy-start(f32[4,512,256]{2,1,0:T(8,128)} %dense_ref.9) | copy-start | bytes 6291460
  35.6 1.9 %copy-start.1 = (f32[4,512,128]{2,1,0:T(8,128)S(1)}, f32[4,512,128]{2,1,0:T(8,128)}, u32[]{:S(2)}) copy-start(f32[4,512,128]{2,1,0:T(8,128)} %row_basis_ref.9) | copy-start | bytes 3145732
  35.6 1.9 %copy-start.11 = (f32[16,2048]{1,0:T(8,128)S(1)}, f32[16,2048]{1,0:T(8,128)}, u32[]{:S(2)}) copy-start(f32[16,2048]{1,0:T(8,128)} %get-tuple-element.65.y_ref) | copy-start | bytes 393220
  37.4 2.0 %copy-start.10 = (s32[4]{0:T(128)S(1)}, s32[4]{0:T(128)}, u32[]{:S(2)}) copy-start(s32[4]{0:T(128)} %rows_ref.5) | copy-start | bytes 52
  42.8 1.3 %collective-permute-start.7 = (f32[1,104,128]{2,1,0:T(8,128)S(1)}, f32[1,104,128]{2,1,0:T(8,128)S(1)}, u32[]{:S(2)}, u32[]{:S(2)}) collective-permute-start(f32[1,104,128]{2,1,0:T(8,128)S(1)} %get-tuple-element.66.part0_ref), channel_id=1, source_target_pairs={{0,1},{1,0},{2,3},{3,2},{4,5},{5,4},{6,7},{7,6},{8,9},{9,8},{10,11... | collective-permute-start | bytes 159752 | tf_op jit(solution)/shard_map/ppermute | solution.py:965
  44.6 8.5 %collective-permute-start.10 = (f32[1,168,128]{2,1,0:T(8,128)S(1)}, f32[1,168,128]{2,1,0:T(8,128)S(1)}, u32[]{:S(2)}, u32[]{:S(2)}) collective-permute-start(f32[1,168,128]{2,1,0:T(8,128)S(1)} %get-tuple-element.68.order_ref.part0_ref), channel_id=1, source_target_pairs={{0,4},{1,5},{2,6},{3,7},{4,0},{5,1},{6,2},{7,3},{8,12},{9,13},{10,... | collective-permute-start | bytes 258056 | tf_op jit(solution)/shard_map/ppermute | solution.py:965
  47.6 5.5 %collective-permute-start.9 = (f32[1,168,128]{2,1,0:T(8,128)S(1)}, f32[1,168,128]{2,1,0:T(8,128)S(1)}, u32[]{:S(2)}, u32[]{:S(2)}) collective-permute-start(f32[1,168,128]{2,1,0:T(8,128)S(1)} %get-tuple-element.68.order_ref.part0_ref), channel_id=1, source_target_pairs={{0,6},{1,7},{2,4},{3,5},{4,2},{5,3},{6,0},{7,1},{8,14},{9,15},{10,... | collective-permute-start | bytes 258056 | tf_op jit(solution)/shard_map/ppermute | solution.py:965
  48.2 4.9 %collective-permute-start.8 = (f32[1,168,128]{2,1,0:T(8,128)S(1)}, f32[1,168,128]{2,1,0:T(8,128)S(1)}, u32[]{:S(2)}, u32[]{:S(2)}) collective-permute-start(f32[1,168,128]{2,1,0:T(8,128)S(1)} %get-tuple-element.68.order_ref.part0_ref), channel_id=1, source_target_pairs={{0,2},{1,3},{2,0},{3,1},{4,6},{5,7},{6,4},{7,5},{8,10},{9,11},{10,... | collective-permute-start | bytes 258056 | tf_op jit(solution)/shard_map/ppermute | solution.py:965
  68.6 6.1 %collective-permute-start.13 = (f32[1,112,128]{2,1,0:T(8,128)S(1)}, f32[1,112,128]{2,1,0:T(8,128)S(1)}, u32[]{:S(2)}, u32[]{:S(2)}) collective-permute-start(f32[1,112,128]{2,1,0:T(8,128)S(1)} %get-tuple-element.76.order_ref.part0_ref), channel_id=1, source_target_pairs={{0,128},{1,129},{2,130},{3,131},{4,132},{5,133},{6,134},{7,135},{8... | collective-permute-start | bytes 172040 | tf_op jit(solution)/shard_map/ppermute | solution.py:965
  71.5 5.4 %collective-permute-start.12 = (f32[1,112,128]{2,1,0:T(8,128)S(1)}, f32[1,112,128]{2,1,0:T(8,128)S(1)}, u32[]{:S(2)}, u32[]{:S(2)}) collective-permute-start(f32[1,112,128]{2,1,0:T(8,128)S(1)} %get-tuple-element.76.order_ref.part0_ref), channel_id=1, source_target_pairs={{0,192},{1,193},{2,194},{3,195},{4,196},{5,197},{6,198},{7,199},{8... | collective-permute-start | bytes 172040 | tf_op jit(solution)/shard_map/ppermute | solution.py:965
  72.5 4.3 %collective-permute-start.11 = (f32[1,112,128]{2,1,0:T(8,128)S(1)}, f32[1,112,128]{2,1,0:T(8,128)S(1)}, u32[]{:S(2)}, u32[]{:S(2)}) collective-permute-start(f32[1,112,128]{2,1,0:T(8,128)S(1)} %get-tuple-element.76.order_ref.part0_ref), channel_id=1, source_target_pairs={{0,64},{1,65},{2,66},{3,67},{4,68},{5,69},{6,70},{7,71},{8,72},{9,... | collective-permute-start | bytes 172040 | tf_op jit(solution)/shard_map/ppermute | solution.py:965
  81.7 1.3 %collective-permute-start.14 = (f32[1,40,128]{2,1,0:T(8,128)S(1)}, f32[1,40,128]{2,1,0:T(8,128)S(1)}, u32[]{:S(2)}, u32[]{:S(2)}) collective-permute-start(f32[1,40,128]{2,1,0:T(8,128)S(1)} %get-tuple-element.88.refs_0_), channel_id=1, source_target_pairs={{0,1},{1,0},{2,3},{3,2},{4,5},{5,4},{6,7},{7,6},{8,9},{9,8},{10,11... | collective-permute-start | bytes 61448 | tf_op jit(solution)/shard_map/ppermute | solution.py:965
  83.4 5.4 %collective-permute-start.17 = (f32[1,40,128]{2,1,0:T(8,128)S(1)}, f32[1,40,128]{2,1,0:T(8,128)S(1)}, u32[]{:S(2)}, u32[]{:S(2)}) collective-permute-start(f32[1,40,128]{2,1,0:T(8,128)S(1)} %shard_map.124.refs_0_), channel_id=1, source_target_pairs={{0,4},{1,5},{2,6},{3,7},{4,0},{5,1},{6,2},{7,3},{8,12},{9,13},{10,... | collective-permute-start | bytes 61448 | tf_op jit(solution)/shard_map/ppermute | solution.py:965
  86.6 3.8 %collective-permute-start.16 = (f32[1,40,128]{2,1,0:T(8,128)S(1)}, f32[1,40,128]{2,1,0:T(8,128)S(1)}, u32[]{:S(2)}, u32[]{:S(2)}) collective-permute-start(f32[1,40,128]{2,1,0:T(8,128)S(1)} %shard_map.124.refs_0_), channel_id=1, source_target_pairs={{0,6},{1,7},{2,4},{3,5},{4,2},{5,3},{6,0},{7,1},{8,14},{9,15},{10,... | collective-permute-start | bytes 61448 | tf_op jit(solution)/shard_map/ppermute | solution.py:965
  87.2 3.8 %collective-permute-start.15 = (f32[1,40,128]{2,1,0:T(8,128)S(1)}, f32[1,40,128]{2,1,0:T(8,128)S(1)}, u32[]{:S(2)}, u32[]{:S(2)}) collective-permute-start(f32[1,40,128]{2,1,0:T(8,128)S(1)} %shard_map.124.refs_0_), channel_id=1, source_target_pairs={{0,2},{1,3},{2,0},{3,1},{4,6},{5,7},{6,4},{7,5},{8,10},{9,11},{10,... | collective-permute-start | bytes 61448 | tf_op jit(solution)/shard_map/ppermute | solution.py:965
  104.9 5.4 %collective-permute-start.20 = (f32[1,40,128]{2,1,0:T(8,128)S(1)}, f32[1,40,128]{2,1,0:T(8,128)S(1)}, u32[]{:S(2)}, u32[]{:S(2)}) collective-permute-start(f32[1,40,128]{2,1,0:T(8,128)S(1)} %shard_map.126.part0_ref), channel_id=1, source_target_pairs={{0,128},{1,129},{2,130},{3,131},{4,132},{5,133},{6,134},{7,135},{8... | collective-permute-start | bytes 61448 | tf_op jit(solution)/shard_map/ppermute | solution.py:965
  106.5 5.0 %collective-permute-start.19 = (f32[1,40,128]{2,1,0:T(8,128)S(1)}, f32[1,40,128]{2,1,0:T(8,128)S(1)}, u32[]{:S(2)}, u32[]{:S(2)}) collective-permute-start(f32[1,40,128]{2,1,0:T(8,128)S(1)} %shard_map.126.part0_ref), channel_id=1, source_target_pairs={{0,192},{1,193},{2,194},{3,195},{4,196},{5,197},{6,198},{7,199},{8... | collective-permute-start | bytes 61448 | tf_op jit(solution)/shard_map/ppermute | solution.py:965
  107.5 3.9 %collective-permute-start.18 = (f32[1,40,128]{2,1,0:T(8,128)S(1)}, f32[1,40,128]{2,1,0:T(8,128)S(1)}, u32[]{:S(2)}, u32[]{:S(2)}) collective-permute-start(f32[1,40,128]{2,1,0:T(8,128)S(1)} %shard_map.126.part0_ref), channel_id=1, source_target_pairs={{0,64},{1,65},{2,66},{3,67},{4,68},{5,69},{6,70},{7,71},{8,72},{9,... | collective-permute-start | bytes 61448 | tf_op jit(solution)/shard_map/ppermute | solution.py:965
  (1 other events, 0.8 us)

commit v8 on v7

--- a/solution.py
+++ b/solution.py
@@ -33,13 +33,32 @@
 
 
 def mm(x, pair, transposed=False):
-    xh, xl = split(x)
+    xh, xl = x if isinstance(x, tuple) else split(x)
     wh, wl = pair
     dims = (((1,), (1 if transposed else 0,)), ((), ()))
-    n = x.shape[0]
+    n = xh.shape[0]
     both = lax.dot_general(jnp.concatenate([xh, xl], 0), wh, dims, preferred_element_type=f32)
     rest = lax.dot_general(xh, wl, dims, preferred_element_type=f32)
     return both[:n] + (both[n:] + rest)
+
+
+def mm_square(x, pair):
+    xh, xl = x
+    wh, wl = pair
+    upper = jnp.concatenate([wh, wl], 1)
+    lower = jnp.concatenate([wh, jnp.zeros_like(wl)], 1)
+    out = jnp.dot(
+        jnp.concatenate([xh, xl], 1), jnp.concatenate([upper, lower], 0), preferred_element_type=f32
+    )
+    return out[:, :RANK] + out[:, RANK:]
+
+
+def mm_narrow(x, pair):
+    xh, xl = split(x)
+    wh, wl = pair
+    out = jnp.dot(xh, jnp.concatenate([wh, wl], 1), preferred_element_type=f32)
+    rest = jnp.dot(xl, wh, preferred_element_type=f32)
+    return out[:, :RANK] + (out[:, RANK:] + rest)
 
 
 def mm_inner(a, b):
@@ -375,7 +394,7 @@
             products = [mm(product, half) for half in halves for product in products]
         for k, product in enumerate(products):
             store_pair(products_ref, product_base(height) + k, product)
-            turned_ref[product_base(height) + k] = jnp.transpose(product)
+            store_pair(turned_ref, product_base(height) + k, jnp.transpose(product))
 
 
 def member_grams(name, grams, products_ref, turned_ref, nodes_ref):
@@ -383,8 +402,9 @@
     left = []
     for d in range(count):
         store_pair(nodes_ref, d, grams[d])
-        turned = [turned_ref[product_base(h) + d % (2 << h)] for h in range(heights)]
-        left.append(unstack(mm(stack(turned), split(grams[d])), heights))
+        turned = [pair_at(turned_ref, product_base(h) + d % (2 << h)) for h in range(heights)]
+        turned = tuple(stack([term[k] for term in turned]) for k in range(2))
+        left.append(unstack(mm_square(turned, split(grams[d])), heights))
     for height in range(heights):
         size = 2 << height
         base = product_base(height)
@@ -393,7 +413,7 @@
         rows = []
         for n in range(count // size):
             rows.append(jnp.concatenate([left[n * size + t][height] for t in range(size)], 1))
-        nodes = unstack(mm(stack(rows), table), len(rows))
+        nodes = unstack(mm_narrow(stack(rows), table), len(rows))
         if height + 1 < heights:
             for k, value in enumerate(nodes):
                 store_pair(nodes_ref, bases(name)[height + 1] + k, value)
@@ -447,8 +467,8 @@
         grams.append(gram_of(basis))
     root = mm(jnp.concatenate(leaf, 1), split(stack(paths)))
     row = row_of(squares)
-    left = [mm(jnp.transpose(paths[q]), split(grams[q])) for q in range(LEAF_DEV)]
-    gram = mm(jnp.concatenate(left, 1), split(stack(paths)))
+    left = [mm_square(split(jnp.transpose(paths[q])), split(grams[q])) for q in range(LEAF_DEV)]
+    gram = mm_narrow(jnp.concatenate(left, 1), split(stack(paths)))
     top, diagonal = pack(gram)
     send(msg_ref, stack([root, stat_block(row, row, diagonal), top]))
 
@@ -519,28 +539,19 @@
     part2_ref,
     part3_ref,
     up_row_ref,
-    up_col_ref,
-    up_couple_ref,
+    order_ref,
     msg_ref,
     sib_ref,
     nodes_ref,
-    gain_ref,
-    path_ref,
     recv_ref,
     scratch_ref,
     slice_ref,
 ):
+    del order_ref
     me = me_ref[0]
     gather_parts(me, "row", (part0_ref, part1_ref, part2_ref, part3_ref), recv_ref)
     summary = climb_group("row", me_ref, recv_ref, up_row_ref, sib_ref, scratch_ref)
     gram = member_grams("row", received_grams(recv_ref), products_ref, turned_ref, nodes_ref)
-    child = 1 - (me & 1)
-    store_pair(gain_ref, 0, up_couple_ref[0, child])
-    path = up_col_ref[0, pl.ds(pl.multiple_of((me & 1) * RANK, RANK), RANK), :]
-    for j in range(1, 3):
-        store_pair(gain_ref, j, sibling_gain(me, j, path, up_couple_ref))
-        path = path_product(me, j, path, up_col_ref)
-    path_ref[...] = path
     top, diagonal = pack(gram)
     slice_ref[...] = top
     part = slice_ref[pl.ds(pl.multiple_of((me % NEAR) * SLICE, SLICE), SLICE), :]
@@ -566,19 +577,19 @@
     send(msg_ref, stack([summary, sum_stats(recv_ref)]))
 
 
-def gains_kernel(me_ref, order_ref, up_col_ref, up_couple_ref, path_ref, gain_ref):
+def gains_kernel(me_ref, order_ref, up_col_ref, up_couple_ref, gain_ref):
     del order_ref
     me = me_ref[0]
-    path = path_ref[...]
-    for k, j in enumerate(range(stage("mid")[0], 8)):
-        store_pair(gain_ref, k, sibling_gain(me, j, path, up_couple_ref))
+    store_pair(gain_ref, 0, up_couple_ref[0, 1 - (me & 1)])
+    path = up_col_ref[0, pl.ds(pl.multiple_of((me & 1) * RANK, RANK), RANK), :]
+    for j in range(1, 8):
+        store_pair(gain_ref, j, sibling_gain(me, j, path, up_couple_ref))
         if j < 7:
             path = path_product(me, j, path, up_col_ref)
 
 
-def from_siblings(siblings, near_gain_ref, mid_gain_ref):
-    gains = [pair_at(near_gain_ref, j) for j in range(3)]
-    gains += [pair_at(mid_gain_ref, j) for j in range(5)]
+def from_siblings(siblings, gain_ref):
+    gains = [pair_at(gain_ref, j) for j in range(8)]
     gains = tuple(jnp.concatenate([g[k] for g in gains], 1) for k in range(2))
     return mm(jnp.concatenate(siblings, 1), gains, transposed=True)
 
@@ -593,8 +604,7 @@
     core_sib_ref,
     row_sib_ref,
     mid_sib_ref,
-    near_gain_ref,
-    mid_gain_ref,
+    gain_ref,
     part_ref,
     up_row_ref,
     dense_ref,
@@ -622,7 +632,7 @@
     for m, value in enumerate(summaries):
         scratch_ref[m] = value
     siblings.append(scratch_ref[(place >> 1) ^ 1])
-    potential = from_siblings(siblings, near_gain_ref, mid_gain_ref)
+    potential = from_siblings(siblings, gain_ref)
     beta = jnp.sqrt(column_of(sum_stats(recv_ref)[:1]))
     inverse = 1.0 / beta
     beta_ref[...] = jnp.broadcast_to(beta, (RHS, RANK))
@@ -805,8 +815,7 @@
     row_own_ref,
     mid_path_ref,
     mid_own_ref,
-    near_gain_ref,
-    mid_gain_ref,
+    gain_ref,
     up_row_ref,
     top_ref,
     core_nodes_ref,
@@ -870,7 +879,7 @@
             other = path_ref[3 * height + 1] * factor + jnp.where(child == 0, high, low)
             gram = pair_at(nodes_ref, bases(name)[height] + ((inside >> height) ^ 1))
             siblings[j] = path_ref[3 * height + 2] * factor + mm(other, gram)
-    backward = from_siblings([siblings[j] for j in range(8)], near_gain_ref, mid_gain_ref)
+    backward = from_siblings([siblings[j] for j in range(8)], gain_ref)
     own_factor = scale / inverse_norm(column_of(own_in_ref[:1]))
     inverse = 1.0 / rho
     spread = mm(backward, pair_at(columns_ref), transposed=True)
@@ -1030,7 +1039,7 @@
     )
     def products_of(name):
         count = node_count(name)
-        return [pair_shape(count, RANK, RANK), (count, RANK, RANK)]
+        return [pair_shape(count, RANK, RANK)] * 2
 
     cross, columns, paths, *products = call(
         paths_kernel,
@@ -1044,11 +1053,13 @@
         (),
         (0,),
     )
-    message, row_sib, row_nodes, near_gain, path = call(
+    (gain,) = call(gains_kernel, [nodes_shape(8)], [me, paths, up_col, up_couple], (), (1,))
+    message, row_sib, row_nodes = call(
         row_kernel,
-        [(groups,) + longer(single, SLICE), sibling_shape("row"), nodes_of("row"), nodes_shape(3), gram_shape],
-        [me] + products + swap_parts(message, "row") + tables,
+        [(groups,) + longer(single, SLICE), sibling_shape("row"), nodes_of("row")],
+        [me] + products + swap_parts(message, "row") + [up_row, gain],
         received("row", longer(single, HALF)) + node_scratch("row") + [(HALF, RANK)],
+        (8,),
     )
     message, mid_sib, part, diagonal = call(
         mid_kernel,
@@ -1056,17 +1067,13 @@
         [me, swap_mid(message), up_row],
         node_scratch("mid"),
     )
-    (mid_gain,) = call(
-        gains_kernel, [nodes_shape(5)], [me, message, up_col, up_couple, path], (), (1,)
-    )
-    gains = [near_gain, mid_gain]
     x, beta, message, own, inner = call(
         first_kernel,
         [col_shape, tile, (1,) + longer(double, HALF), stat, row_shape],
         [me, box_rows]
         + swap_parts(message, "far")
         + [core_sib, row_sib, mid_sib]
-        + gains
+        + [gain]
         + [part, up_row, dense, row_basis, col_basis, cross, columns, paths, within(z, message)],
         [(2,) + tile] + received("far", single),
     )
@@ -1101,7 +1108,7 @@
         [me, box_rows]
         + swap_parts(message, "far")
         + [core_path, core_own, row_path, row_own, mid_path, mid_own]
-        + gains
+        + [gain]
         + [up_row, top, core_nodes, row_nodes, mid_nodes]
         + [dense, row_basis, col_basis, cross, columns, images, x, own, within(inner, message)],
         [(6,) + tile, (4,) + tile] + received("far", longer(double, HALF + 8)),

time: 113 us -> 113 us (level); the launches traced: 113 us -> 112 us
  no operation moved by 1% of the time
where the time goes in v8:
time: 113 us; the launch traced here: 112 us
  blocking collectives  41.1 us (36%)
  Pallas kernels  29.7 us (26%)
  starting transfers between devices  26 us (23%)
  waiting for transfers between devices  13.6 us (12%)
    all_to_all x3, blocking collectives, swap_mid(): return lax.all_to_all(message, 'leaf', 0, 0, axis_index_groups=groups)  41.1 us
    pallas_call x19, Pallas kernels, call(): pl.pallas_call(kernel, out_shape=outs, in_specs=[pl.BlockSpec(memory_spac...  29.7 us
    ppermute x21, starting transfers between devices, swap_parts(): parts.append(lax.ppermute(message, 'leaf', pairs))  26 us
    ppermute x21, waiting for transfers between devices, swap_parts(): parts.append(lax.ppermute(message, 'leaf', pairs))  13.6 us
  transfers between devices with their start and end apart: 21, of which 12 were waited for; matrix products, arithmetic and copies ran while one was open for 0% of the time, Pallas kernels for 8%

profile of v8, /device:TPU:2, one launch (start us, length us, event | category | flops | bytes accessed | tf_op | source)
XLA Modules:
  0.0 111.6 jit_solution(4397271676480313479)
XLA Ops:
  0.0 3.4 %shard_map.109 = (f32[16,2048]{1,0:T(8,128)}, f32[1,88,128]{2,1,0:T(8,128)}) custom-call(s32[1]{0:T(128)} %bitcast.me_ref, s32[4]{0:T(128)} %rows_ref.5, f32[16,2048]{1,0:T(8,128)} %rhs_hbm.1, f32[4,512,128]{2,1,0:T(8,128)} %row_basis_ref.9, f32[3,256,128]{2,1,0:T(8,128)} %local_row_ref.1), custom_call_target="tpu_custom_call" | custom-call | flops 6000000000 | tf_op jit(solution)/shard_map/pallas_call | solution.py:932
  5.6 2.2 %collective-permute-start.3 = (f32[1,88,128]{2,1,0:T(8,128)S(1)}, f32[1,88,128]{2,1,0:T(8,128)S(1)}, u32[]{:S(2)}, u32[]{:S(2)}) collective-permute-start(f32[1,88,128]{2,1,0:T(8,128)S(1)} %get-tuple-element.49.order_ref.part0_ref), channel_id=1, source_target_pairs={{0,4},{1,5},{2,6},{3,7},{4,0},{5,1},{6,2},{7,3},{8,12},{9,13},{10,... | collective-permute-start | bytes 135176 | tf_op jit(solution)/shard_map/ppermute | solution.py:974
  7.8 1.6 %collective-permute-start.2 = (f32[1,88,128]{2,1,0:T(8,128)S(1)}, f32[1,88,128]{2,1,0:T(8,128)S(1)}, u32[]{:S(2)}, u32[]{:S(2)}) collective-permute-start(f32[1,88,128]{2,1,0:T(8,128)S(1)} %get-tuple-element.49.order_ref.part0_ref), channel_id=1, source_target_pairs={{0,6},{1,7},{2,4},{3,5},{4,2},{5,3},{6,0},{7,1},{8,14},{9,15},{10,... | collective-permute-start | bytes 135176 | tf_op jit(solution)/shard_map/ppermute | solution.py:974
  10.4 1.7 %shard_map.112 = (bf16[2,512,512]{2,1,0:T(8,128)(2,1)S(1)}, bf16[2,1024,128]{2,1,0:T(8,128)(2,1)S(1)}, bf16[2,512,128]{2,1,0:T(8,128)(2,1)S(1)}, bf16[2,6,128,12...) custom-call(f32[1,88,128]{2,1,0:T(8,128)S(1)} %get-tuple-element.49.order_ref.part0_ref, f32[4,256,128]{2,1,0:T(8,128)S(1)} %copy-done.5, ...), custom_call_target="tpu_custom_call" | custom-call | flops 6000000000 | tf_op jit(solution)/shard_map/pallas_call | solution.py:932
  12.1 1.2 %shard_map.113.order_ref.gain_ref = bf16[2,8,128,128]{3,2,1,0:T(8,128)(2,1)S(1)} custom-call(s32[1]{0:T(128)} %bitcast.me_ref, bf16[2,512,128]{2,1,0:T(8,128)(2,1)S(1)} %get-tuple-element.52.order_ref.paths_ref, f32[7,256,128]{2,1,0:T(8,128)S(1)} %copy-done.4, f32[8,2,128,128]{3,2,1,0:T(8,128)S(1)} %copy-done.2), custom_call_target="tpu_custom_call" | custom-call | flops 6000000000 | tf_op jit(solution)/shard_map/pallas_call | solution.py:932
  14.2 17.3 %all_to_all.15.recv_ref = f32[8,32,128]{2,1,0:T(8,128)S(1)} all-to-all(f32[8,32,128]{2,1,0:T(8,128)S(1)} %get-tuple-element.53), channel_id=1, replica_groups={{0,8,16,24,32,40,48,56},{1,9,17,25,33,41,49,57},{2,10,18,26,34,42,50,58..., dimensions={0} | all-to-all | bytes 262144 | tf_op jit(solution)/shard_map/all_to_all | solution.py:980
  31.9 3.2 %collective-permute-start.6 = (f32[1,24,128]{2,1,0:T(8,128)S(1)}, f32[1,24,128]{2,1,0:T(8,128)S(1)}, u32[]{:S(2)}, u32[]{:S(2)}) collective-permute-start(f32[1,24,128]{2,1,0:T(8,128)S(1)} %get-tuple-element.54.order_ref.part0_ref), channel_id=1, source_target_pairs={{0,128},{1,129},{2,130},{3,131},{4,132},{5,133},{6,134},{7,135},{8... | collective-permute-start | bytes 36872 | tf_op jit(solution)/shard_map/ppermute | solution.py:974
  36.2 1.1 shard_map.116.within_ref
  37.3 2.7 %collective-permute-done.5.part2_ref = f32[1,24,128]{2,1,0:T(8,128)S(1)} collective-permute-done((f32[1,24,128]{2,1,0:T(8,128)S(1)}, f32[1,24,128]{2,1,0:T(8,128)S(1)}, u32[]{:S(2)}, u32[]{:S(2)}) %collective-permute-start.5) | collective-permute-done | bytes 12320 | tf_op jit(solution)/shard_map/ppermute | solution.py:974
  40.0 3.4 %shard_map.117 = (f32[16,1024]{1,0:T(8,128)S(1)}, f32[16,128]{1,0:T(8,128)S(1)}, f32[1,104,128]{2,1,0:T(8,128)S(1)}, f32[8,128]{1,0:T(8,128)S(1)}, f32[16,2048]{1,0:T(8,128)S(1)}) custom-call(s32[1]{0:T(128)} %bitcast.me_ref, s32[4]{0:T(128)S(1)} %copy-done.10, f32[1,24,128]{2,1,0:T(8,128)S(1)} %get-tuple-element.54.order_ref.part0_ref, ...), custom_call_target="tpu_custom_call" | custom-call | flops 6000000000 | tf_op jit(solution)/shard_map/pallas_call | solution.py:932
  43.5 1.2 %collective-permute-done.7.part1_ref = f32[1,104,128]{2,1,0:T(8,128)S(1)} collective-permute-done((f32[1,104,128]{2,1,0:T(8,128)S(1)}, f32[1,104,128]{2,1,0:T(8,128)S(1)}, u32[]{:S(2)}, u32[]{:S(2)}) %collective-permute-start.7) | collective-permute-done | bytes 53280 | tf_op jit(solution)/shard_map/ppermute | solution.py:974
  45.2 2.1 %collective-permute-start.10 = (f32[1,168,128]{2,1,0:T(8,128)S(1)}, f32[1,168,128]{2,1,0:T(8,128)S(1)}, u32[]{:S(2)}, u32[]{:S(2)}) collective-permute-start(f32[1,168,128]{2,1,0:T(8,128)S(1)} %get-tuple-element.64.order_ref.part0_ref), channel_id=1, source_target_pairs={{0,4},{1,5},{2,6},{3,7},{4,0},{5,1},{6,2},{7,3},{8,12},{9,13},{10,... | collective-permute-start | bytes 258056 | tf_op jit(solution)/shard_map/ppermute | solution.py:974
  47.9 2.1 %collective-permute-start.8 = (f32[1,168,128]{2,1,0:T(8,128)S(1)}, f32[1,168,128]{2,1,0:T(8,128)S(1)}, u32[]{:S(2)}, u32[]{:S(2)}) collective-permute-start(f32[1,168,128]{2,1,0:T(8,128)S(1)} %get-tuple-element.64.order_ref.part0_ref), channel_id=1, source_target_pairs={{0,2},{1,3},{2,0},{3,1},{4,6},{5,7},{6,4},{7,5},{8,10},{9,11},{10,... | collective-permute-start | bytes 258056 | tf_op jit(solution)/shard_map/ppermute | solution.py:974
  50.0 3.8 %shard_map.119 = (bf16[2,128,1024]{2,1,0:T(8,128)(2,1)S(1)}, bf16[2,512,512]{2,1,0:T(8,128)(2,1)S(1)}, bf16[2,14,128,128]{3,2,1,0:T(8,128)(2,1)S(1)}, bf16[2,14,128,128]{3,2,1,0:T(8,128)(2,1)S(1)}) custom-call(f32[1,168,128]{2,1,0:T(8,128)S(1)} %get-tuple-element.64.order_ref.part0_ref, s32[4]{0:T(128)S(1)} %copy-done.10, f32[4,512,256]{2,1,0:T(8,128)S(1)} %copy-done, ...), custom_call_target="tpu_custom_call" | custom-call | flops 6000000000 | tf_op jit(solution)/shard_map/pallas_call | solution.py:932
  53.8 1.8 %shard_map.120 = (f32[8,40,128]{2,1,0:T(8,128)S(1)}, f32[6,16,128]{2,1,0:T(8,128)S(1)}, f32[8,128]{1,0:T(8,128)S(1)}, bf16[2,14,128,128]{3,2,1,0:T(8,128)(2,1)S(1)}, f32[72,128]{1,0:T(8,128)S(1)}) custom-call(s32[1]{0:T(128)} %bitcast.me_ref, bf16[2,14,128,128]{3,2,1,0:T(8,128)(2,1)S(1)} %get-tuple-element.65.products_ref, ...), custom_call_target="tpu_custom_call" | custom-call | flops 6000000000 | tf_op jit(solution)/shard_map/pallas_call | solution.py:932
  55.6 12.1 %all_to_all.16.recv_ref = f32[8,40,128]{2,1,0:T(8,128)S(1)} all-to-all(f32[8,40,128]{2,1,0:T(8,128)S(1)} %get-tuple-element.69), channel_id=1, replica_groups={{0,8,16,24,32,40,48,56},{1,9,17,25,33,41,49,57},{2,10,18,26,34,42,50,58..., dimensions={0} | all-to-all | bytes 327680 | tf_op jit(solution)/shard_map/all_to_all | solution.py:980
  67.7 1.3 %shard_map.121 = (f32[1,112,128]{2,1,0:T(8,128)S(1)}, f32[9,16,128]{2,1,0:T(8,128)S(1)}, f32[8,128]{1,0:T(8,128)S(1)}) custom-call(s32[1]{0:T(128)} %bitcast.me_ref, f32[8,40,128]{2,1,0:T(8,128)S(1)} %all_to_all.16.recv_ref, f32[7,256,128]{2,1,0:T(8,128)S(1)} %copy-done.3, f32[7,256,128]{2,1,0:T(8,128)S(1)} %copy-done.4, f32[8,2,128,128]{3,2,1,0:T(8,128)S(1)} %copy-done.2, ...), custom_call_target="tpu_custom_call" | custom-call | flops 6000000000 | tf_op jit(solution)/shard_map/pallas_call | solution.py:932
  69.0 1.6 %collective-permute-start.13 = (f32[1,112,128]{2,1,0:T(8,128)S(1)}, f32[1,112,128]{2,1,0:T(8,128)S(1)}, u32[]{:S(2)}, u32[]{:S(2)}) collective-permute-start(f32[1,112,128]{2,1,0:T(8,128)S(1)} %get-tuple-element.72.order_ref.part0_ref), channel_id=1, source_target_pairs={{0,128},{1,129},{2,130},{3,131},{4,132},{5,133},{6,134},{7,135},{8... | collective-permute-start | bytes 172040 | tf_op jit(solution)/shard_map/ppermute | solution.py:974
  72.5 1.1 shard_map.122.within_ref
  73.6 1.1 collective-permute-done.13.part3_ref
  74.7 1.2 %collective-permute-done.12.part2_ref = f32[1,112,128]{2,1,0:T(8,128)S(1)} collective-permute-done((f32[1,112,128]{2,1,0:T(8,128)S(1)}, f32[1,112,128]{2,1,0:T(8,128)S(1)}, u32[]{:S(2)}, u32[]{:S(2)}) %collective-permute-start.12) | collective-permute-done | bytes 57376 | tf_op jit(solution)/shard_map/ppermute | solution.py:974
  75.9 4.8 %shard_map.123 = (f32[16,1024]{1,0:T(8,128)S(1)}, f32[16,1024]{1,0:T(8,128)S(1)}, f32[16,128]{1,0:T(8,128)S(1)}, f32[16,128]{1,0:T(8,128)S(1)}, f32[1,40,128]{2,...) custom-call(s32[1]{0:T(128)} %bitcast.me_ref, s32[4]{0:T(128)S(1)} %copy-done.10, ...), custom_call_target="tpu_custom_call" | custom-call | flops 6000000000 | tf_op jit(solution)/shard_map/pallas_call | solution.py:932
  80.8 1.2 %collective-permute-done.14.refs_1_ = f32[1,40,128]{2,1,0:T(8,128)S(1)} collective-permute-done((f32[1,40,128]{2,1,0:T(8,128)S(1)}, f32[1,40,128]{2,1,0:T(8,128)S(1)}, u32[]{:S(2)}, u32[]{:S(2)}) %collective-permute-start.14) | collective-permute-done | bytes 20512 | tf_op jit(solution)/shard_map/ppermute | solution.py:974
  82.5 1.9 %collective-permute-start.17 = (f32[1,40,128]{2,1,0:T(8,128)S(1)}, f32[1,40,128]{2,1,0:T(8,128)S(1)}, u32[]{:S(2)}, u32[]{:S(2)}) collective-permute-start(f32[1,40,128]{2,1,0:T(8,128)S(1)} %shard_map.124.refs_0_), channel_id=1, source_target_pairs={{0,4},{1,5},{2,6},{3,7},{4,0},{5,1},{6,2},{7,3},{8,12},{9,13},{10,... | collective-permute-start | bytes 61448 | tf_op jit(solution)/shard_map/ppermute | solution.py:974
  84.5 2.7 %collective-permute-start.15 = (f32[1,40,128]{2,1,0:T(8,128)S(1)}, f32[1,40,128]{2,1,0:T(8,128)S(1)}, u32[]{:S(2)}, u32[]{:S(2)}) collective-permute-start(f32[1,40,128]{2,1,0:T(8,128)S(1)} %shard_map.124.refs_0_), channel_id=1, source_target_pairs={{0,2},{1,3},{2,0},{3,1},{4,6},{5,7},{6,4},{7,5},{8,10},{9,11},{10,... | collective-permute-start | bytes 61448 | tf_op jit(solution)/shard_map/ppermute | solution.py:974
  89.9 11.8 %all_to_all.17.refs_0_ = f32[8,40,128]{2,1,0:T(8,128)S(1)} all-to-all(f32[8,40,128]{2,1,0:T(8,128)S(1)} %shard_map.125), channel_id=1, replica_groups={{0,8,16,24,32,40,48,56},{1,9,17,25,33,41,49,57},{2,10,18,26,34,42,50,58..., dimensions={0} | all-to-all | bytes 327680 | tf_op jit(solution)/shard_map/all_to_all | solution.py:980
  101.7 1.3 %shard_map.126.part0_ref = f32[1,40,128]{2,1,0:T(8,128)S(1)} custom-call(s32[1]{0:T(128)} %bitcast.me_ref, f32[8,40,128]{2,1,0:T(8,128)S(1)} %all_to_all.17.refs_0_, f32[7,256,128]{2,1,0:T(8,128)S(1)} %copy-done.3, f32[7,256,128]{2,1,0:T(8,128)S(1)} %copy-done.4, f32[8,2,128,128]{3,2,1,0:T(8,128)S(1)} %copy-done.2, ...), custom_call_target="tpu_custom_call" | custom-call | flops 6000000000 | tf_op jit(solution)/shard_map/pallas_call | solution.py:932
  103.0 2.3 %collective-permute-start.20 = (f32[1,40,128]{2,1,0:T(8,128)S(1)}, f32[1,40,128]{2,1,0:T(8,128)S(1)}, u32[]{:S(2)}, u32[]{:S(2)}) collective-permute-start(f32[1,40,128]{2,1,0:T(8,128)S(1)} %shard_map.126.part0_ref), channel_id=1, source_target_pairs={{0,128},{1,129},{2,130},{3,131},{4,132},{5,133},{6,134},{7,135},{8... | collective-permute-start | bytes 61448 | tf_op jit(solution)/shard_map/ppermute | solution.py:974
  105.3 1.2 %collective-permute-start.19 = (f32[1,40,128]{2,1,0:T(8,128)S(1)}, f32[1,40,128]{2,1,0:T(8,128)S(1)}, u32[]{:S(2)}, u32[]{:S(2)}) collective-permute-start(f32[1,40,128]{2,1,0:T(8,128)S(1)} %shard_map.126.part0_ref), channel_id=1, source_target_pairs={{0,192},{1,193},{2,194},{3,195},{4,196},{5,197},{6,198},{7,199},{8... | collective-permute-start | bytes 61448 | tf_op jit(solution)/shard_map/ppermute | solution.py:974
  106.5 1.8 %collective-permute-done.20.part3_ref = f32[1,40,128]{2,1,0:T(8,128)S(1)} collective-permute-done((f32[1,40,128]{2,1,0:T(8,128)S(1)}, f32[1,40,128]{2,1,0:T(8,128)S(1)}, u32[]{:S(2)}, u32[]{:S(2)}) %collective-permute-start.20) | collective-permute-done | bytes 20512 | tf_op jit(solution)/shard_map/ppermute | solution.py:974
  108.3 1.9 %collective-permute-done.19.part2_ref = f32[1,40,128]{2,1,0:T(8,128)S(1)} collective-permute-done((f32[1,40,128]{2,1,0:T(8,128)S(1)}, f32[1,40,128]{2,1,0:T(8,128)S(1)}, u32[]{:S(2)}, u32[]{:S(2)}) %collective-permute-start.19) | collective-permute-done | bytes 20512 | tf_op jit(solution)/shard_map/ppermute | solution.py:974
  110.3 1.3 %shard_map.127 = f32[16,1024]{1,0:T(8,128)} custom-call(s32[1]{0:T(128)} %bitcast.me_ref, f32[1,40,128]{2,1,0:T(8,128)S(1)} %shard_map.126.part0_ref, f32[1,40,128]{2,1,0:T(8,128)S(1)} %collective-permute-done.18.part1_ref, f32[1,40,128]{2,1,0:T(8,128)S(1)} %collective-permute-done.19.part2_ref, f32[1,40,128]{2,1,0:T(8,128)S(1)} %collective-permute-done.20.part3_ref, ...), custom_call_target="tpu_custom_call" | custom-call | flops 6000000000 | tf_op jit(solution)/shard_map/pallas_call | solution.py:932
  (56 shorter events, 12.1 us)
Async XLA Ops:
  3.4 1.5 %copy-start.3 = (f32[7,256,128]{2,1,0:T(8,128)S(1)}, f32[7,256,128]{2,1,0:T(8,128)}, u32[]{:S(2)}) copy-start(f32[7,256,128]{2,1,0:T(8,128)} %refs_1_.1) | copy-start | bytes 2752516
  3.4 1.5 %collective-permute-start = (f32[1,88,128]{2,1,0:T(8,128)}, f32[1,88,128]{2,1,0:T(8,128)S(1)}, u32[]{:S(2)}, u32[]{:S(2)}) collective-permute-start(f32[1,88,128]{2,1,0:T(8,128)} %get-tuple-element.48.message_ref), channel_id=1, source_target_pairs={{0,1},{1,0},{2,3},{3,2},{4,5},{5,4},{6,7},{7,6},{8,9},{9,8},{10,11... | collective-permute-start | bytes 135176 | tf_op jit(solution)/shard_map/ppermute | solution.py:974
  4.4 6.0 %copy-start.5 = (f32[4,256,128]{2,1,0:T(8,128)S(1)}, f32[4,256,128]{2,1,0:T(8,128)}, u32[]{:S(2)}) copy-start(f32[4,256,128]{2,1,0:T(8,128)} %col_basis_ref.11) | copy-start | bytes 1572868
  4.4 6.0 %copy-start.6 = (f32[3,256,128]{2,1,0:T(8,128)S(1)}, f32[3,256,128]{2,1,0:T(8,128)}, u32[]{:S(2)}) copy-start(f32[3,256,128]{2,1,0:T(8,128)} %local_row_ref.1) | copy-start | bytes 1179652
  4.4 6.0 %copy-start.7 = (f32[3,256,128]{2,1,0:T(8,128)S(1)}, f32[3,256,128]{2,1,0:T(8,128)}, u32[]{:S(2)}) copy-start(f32[3,256,128]{2,1,0:T(8,128)} %local_col_ref.1) | copy-start | bytes 1179652
  4.4 6.0 %copy-start.8 = (f32[3,2,128,128]{3,2,1,0:T(8,128)S(1)}, f32[3,2,128,128]{3,2,1,0:T(8,128)}, u32[]{:S(2)}) copy-start(f32[3,2,128,128]{3,2,1,0:T(8,128)} %local_couple_ref.1) | copy-start | bytes 1179652
  5.5 6.5 %copy-start.2 = (f32[8,2,128,128]{3,2,1,0:T(8,128)S(1)}, f32[8,2,128,128]{3,2,1,0:T(8,128)}, u32[]{:S(2)}) copy-start(f32[8,2,128,128]{3,2,1,0:T(8,128)} %refs_3_.3) | copy-start | bytes 3145732
  5.6 6.5 %copy-start.4 = (f32[7,256,128]{2,1,0:T(8,128)S(1)}, f32[7,256,128]{2,1,0:T(8,128)}, u32[]{:S(2)}) copy-start(f32[7,256,128]{2,1,0:T(8,128)} %refs_2_.3) | copy-start | bytes 2752516
  5.6 7.7 %collective-permute-start.3 = (f32[1,88,128]{2,1,0:T(8,128)S(1)}, f32[1,88,128]{2,1,0:T(8,128)S(1)}, u32[]{:S(2)}, u32[]{:S(2)}) collective-permute-start(f32[1,88,128]{2,1,0:T(8,128)S(1)} %get-tuple-element.49.order_ref.part0_ref), channel_id=1, source_target_pairs={{0,4},{1,5},{2,6},{3,7},{4,0},{5,1},{6,2},{7,3},{8,12},{9,13},{10,... | collective-permute-start | bytes 135176 | tf_op jit(solution)/shard_map/ppermute | solution.py:974
  7.8 5.5 %collective-permute-start.2 = (f32[1,88,128]{2,1,0:T(8,128)S(1)}, f32[1,88,128]{2,1,0:T(8,128)S(1)}, u32[]{:S(2)}, u32[]{:S(2)}) collective-permute-start(f32[1,88,128]{2,1,0:T(8,128)S(1)} %get-tuple-element.49.order_ref.part0_ref), channel_id=1, source_target_pairs={{0,6},{1,7},{2,4},{3,5},{4,2},{5,3},{6,0},{7,1},{8,14},{9,15},{10,... | collective-permute-start | bytes 135176 | tf_op jit(solution)/shard_map/ppermute | solution.py:974
  9.4 4.0 %collective-permute-start.1 = (f32[1,88,128]{2,1,0:T(8,128)S(1)}, f32[1,88,128]{2,1,0:T(8,128)S(1)}, u32[]{:S(2)}, u32[]{:S(2)}) collective-permute-start(f32[1,88,128]{2,1,0:T(8,128)S(1)} %get-tuple-element.49.order_ref.part0_ref), channel_id=1, source_target_pairs={{0,2},{1,3},{2,0},{3,1},{4,6},{5,7},{6,4},{7,5},{8,10},{9,11},{10,... | collective-permute-start | bytes 135176 | tf_op jit(solution)/shard_map/ppermute | solution.py:974
  31.5 4.7 %copy-start = (f32[4,512,256]{2,1,0:T(8,128)S(1)}, f32[4,512,256]{2,1,0:T(8,128)}, u32[]{:S(2)}) copy-start(f32[4,512,256]{2,1,0:T(8,128)} %dense_ref.9) | copy-start | bytes 6291460
  31.5 4.7 %copy-start.1 = (f32[4,512,128]{2,1,0:T(8,128)S(1)}, f32[4,512,128]{2,1,0:T(8,128)}, u32[]{:S(2)}) copy-start(f32[4,512,128]{2,1,0:T(8,128)} %row_basis_ref.9) | copy-start | bytes 3145732
  31.5 4.7 %copy-start.11 = (f32[16,2048]{1,0:T(8,128)S(1)}, f32[16,2048]{1,0:T(8,128)}, u32[]{:S(2)}) copy-start(f32[16,2048]{1,0:T(8,128)} %get-tuple-element.61.y_ref) | copy-start | bytes 393220
  31.9 5.4 %collective-permute-start.6 = (f32[1,24,128]{2,1,0:T(8,128)S(1)}, f32[1,24,128]{2,1,0:T(8,128)S(1)}, u32[]{:S(2)}, u32[]{:S(2)}) collective-permute-start(f32[1,24,128]{2,1,0:T(8,128)S(1)} %get-tuple-element.54.order_ref.part0_ref), channel_id=1, source_target_pairs={{0,128},{1,129},{2,130},{3,131},{4,132},{5,133},{6,134},{7,135},{8... | collective-permute-start | bytes 36872 | tf_op jit(solution)/shard_map/ppermute | solution.py:974
  35.1 4.9 %collective-permute-start.5 = (f32[1,24,128]{2,1,0:T(8,128)S(1)}, f32[1,24,128]{2,1,0:T(8,128)S(1)}, u32[]{:S(2)}, u32[]{:S(2)}) collective-permute-start(f32[1,24,128]{2,1,0:T(8,128)S(1)} %get-tuple-element.54.order_ref.part0_ref), channel_id=1, source_target_pairs={{0,192},{1,193},{2,194},{3,195},{4,196},{5,197},{6,198},{7,199},{8... | collective-permute-start | bytes 36872 | tf_op jit(solution)/shard_map/ppermute | solution.py:974
  36.2 3.8 %collective-permute-start.4 = (f32[1,24,128]{2,1,0:T(8,128)S(1)}, f32[1,24,128]{2,1,0:T(8,128)S(1)}, u32[]{:S(2)}, u32[]{:S(2)}) collective-permute-start(f32[1,24,128]{2,1,0:T(8,128)S(1)} %get-tuple-element.54.order_ref.part0_ref), channel_id=1, source_target_pairs={{0,64},{1,65},{2,66},{3,67},{4,68},{5,69},{6,70},{7,71},{8,72},{9,... | collective-permute-start | bytes 36872 | tf_op jit(solution)/shard_map/ppermute | solution.py:974
  36.2 3.8 %copy-start.10 = (s32[4]{0:T(128)S(1)}, s32[4]{0:T(128)}, u32[]{:S(2)}) copy-start(s32[4]{0:T(128)} %rows_ref.5) | copy-start | bytes 52
  43.4 1.3 %collective-permute-start.7 = (f32[1,104,128]{2,1,0:T(8,128)S(1)}, f32[1,104,128]{2,1,0:T(8,128)S(1)}, u32[]{:S(2)}, u32[]{:S(2)}) collective-permute-start(f32[1,104,128]{2,1,0:T(8,128)S(1)} %get-tuple-element.62.part0_ref), channel_id=1, source_target_pairs={{0,1},{1,0},{2,3},{3,2},{4,5},{5,4},{6,7},{7,6},{8,9},{9,8},{10,11... | collective-permute-start | bytes 159752 | tf_op jit(solution)/shard_map/ppermute | solution.py:974
  45.2 8.5 %collective-permute-start.10 = (f32[1,168,128]{2,1,0:T(8,128)S(1)}, f32[1,168,128]{2,1,0:T(8,128)S(1)}, u32[]{:S(2)}, u32[]{:S(2)}) collective-permute-start(f32[1,168,128]{2,1,0:T(8,128)S(1)} %get-tuple-element.64.order_ref.part0_ref), channel_id=1, source_target_pairs={{0,4},{1,5},{2,6},{3,7},{4,0},{5,1},{6,2},{7,3},{8,12},{9,13},{10,... | collective-permute-start | bytes 258056 | tf_op jit(solution)/shard_map/ppermute | solution.py:974
  47.2 6.5 %collective-permute-start.9 = (f32[1,168,128]{2,1,0:T(8,128)S(1)}, f32[1,168,128]{2,1,0:T(8,128)S(1)}, u32[]{:S(2)}, u32[]{:S(2)}) collective-permute-start(f32[1,168,128]{2,1,0:T(8,128)S(1)} %get-tuple-element.64.order_ref.part0_ref), channel_id=1, source_target_pairs={{0,6},{1,7},{2,4},{3,5},{4,2},{5,3},{6,0},{7,1},{8,14},{9,15},{10,... | collective-permute-start | bytes 258056 | tf_op jit(solution)/shard_map/ppermute | solution.py:974
  47.9 5.9 %collective-permute-start.8 = (f32[1,168,128]{2,1,0:T(8,128)S(1)}, f32[1,168,128]{2,1,0:T(8,128)S(1)}, u32[]{:S(2)}, u32[]{:S(2)}) collective-permute-start(f32[1,168,128]{2,1,0:T(8,128)S(1)} %get-tuple-element.64.order_ref.part0_ref), channel_id=1, source_target_pairs={{0,2},{1,3},{2,0},{3,1},{4,6},{5,7},{6,4},{7,5},{8,10},{9,11},{10,... | collective-permute-start | bytes 258056 | tf_op jit(solution)/shard_map/ppermute | solution.py:974
  69.0 5.7 %collective-permute-start.13 = (f32[1,112,128]{2,1,0:T(8,128)S(1)}, f32[1,112,128]{2,1,0:T(8,128)S(1)}, u32[]{:S(2)}, u32[]{:S(2)}) collective-permute-start(f32[1,112,128]{2,1,0:T(8,128)S(1)} %get-tuple-element.72.order_ref.part0_ref), channel_id=1, source_target_pairs={{0,128},{1,129},{2,130},{3,131},{4,132},{5,133},{6,134},{7,135},{8... | collective-permute-start | bytes 172040 | tf_op jit(solution)/shard_map/ppermute | solution.py:974
  70.5 5.4 %collective-permute-start.12 = (f32[1,112,128]{2,1,0:T(8,128)S(1)}, f32[1,112,128]{2,1,0:T(8,128)S(1)}, u32[]{:S(2)}, u32[]{:S(2)}) collective-permute-start(f32[1,112,128]{2,1,0:T(8,128)S(1)} %get-tuple-element.72.order_ref.part0_ref), channel_id=1, source_target_pairs={{0,192},{1,193},{2,194},{3,195},{4,196},{5,197},{6,198},{7,199},{8... | collective-permute-start | bytes 172040 | tf_op jit(solution)/shard_map/ppermute | solution.py:974
  71.5 4.4 %collective-permute-start.11 = (f32[1,112,128]{2,1,0:T(8,128)S(1)}, f32[1,112,128]{2,1,0:T(8,128)S(1)}, u32[]{:S(2)}, u32[]{:S(2)}) collective-permute-start(f32[1,112,128]{2,1,0:T(8,128)S(1)} %get-tuple-element.72.order_ref.part0_ref), channel_id=1, source_target_pairs={{0,64},{1,65},{2,66},{3,67},{4,68},{5,69},{6,70},{7,71},{8,72},{9,... | collective-permute-start | bytes 172040 | tf_op jit(solution)/shard_map/ppermute | solution.py:974
  80.7 1.3 %collective-permute-start.14 = (f32[1,40,128]{2,1,0:T(8,128)S(1)}, f32[1,40,128]{2,1,0:T(8,128)S(1)}, u32[]{:S(2)}, u32[]{:S(2)}) collective-permute-start(f32[1,40,128]{2,1,0:T(8,128)S(1)} %get-tuple-element.84.refs_0_), channel_id=1, source_target_pairs={{0,1},{1,0},{2,3},{3,2},{4,5},{5,4},{6,7},{7,6},{8,9},{9,8},{10,11... | collective-permute-start | bytes 61448 | tf_op jit(solution)/shard_map/ppermute | solution.py:974
  82.5 5.4 %collective-permute-start.17 = (f32[1,40,128]{2,1,0:T(8,128)S(1)}, f32[1,40,128]{2,1,0:T(8,128)S(1)}, u32[]{:S(2)}, u32[]{:S(2)}) collective-permute-start(f32[1,40,128]{2,1,0:T(8,128)S(1)} %shard_map.124.refs_0_), channel_id=1, source_target_pairs={{0,4},{1,5},{2,6},{3,7},{4,0},{5,1},{6,2},{7,3},{8,12},{9,13},{10,... | collective-permute-start | bytes 61448 | tf_op jit(solution)/shard_map/ppermute | solution.py:974
  84.4 3.8 %collective-permute-start.16 = (f32[1,40,128]{2,1,0:T(8,128)S(1)}, f32[1,40,128]{2,1,0:T(8,128)S(1)}, u32[]{:S(2)}, u32[]{:S(2)}) collective-permute-start(f32[1,40,128]{2,1,0:T(8,128)S(1)} %shard_map.124.refs_0_), channel_id=1, source_target_pairs={{0,6},{1,7},{2,4},{3,5},{4,2},{5,3},{6,0},{7,1},{8,14},{9,15},{10,... | collective-permute-start | bytes 61448 | tf_op jit(solution)/shard_map/ppermute | solution.py:974
  84.5 4.5 %collective-permute-start.15 = (f32[1,40,128]{2,1,0:T(8,128)S(1)}, f32[1,40,128]{2,1,0:T(8,128)S(1)}, u32[]{:S(2)}, u32[]{:S(2)}) collective-permute-start(f32[1,40,128]{2,1,0:T(8,128)S(1)} %shard_map.124.refs_0_), channel_id=1, source_target_pairs={{0,2},{1,3},{2,0},{3,1},{4,6},{5,7},{6,4},{7,5},{8,10},{9,11},{10,... | collective-permute-start | bytes 61448 | tf_op jit(solution)/shard_map/ppermute | solution.py:974
  103.0 5.4 %collective-permute-start.20 = (f32[1,40,128]{2,1,0:T(8,128)S(1)}, f32[1,40,128]{2,1,0:T(8,128)S(1)}, u32[]{:S(2)}, u32[]{:S(2)}) collective-permute-start(f32[1,40,128]{2,1,0:T(8,128)S(1)} %shard_map.126.part0_ref), channel_id=1, source_target_pairs={{0,128},{1,129},{2,130},{3,131},{4,132},{5,133},{6,134},{7,135},{8... | collective-permute-start | bytes 61448 | tf_op jit(solution)/shard_map/ppermute | solution.py:974
  105.3 5.0 %collective-permute-start.19 = (f32[1,40,128]{2,1,0:T(8,128)S(1)}, f32[1,40,128]{2,1,0:T(8,128)S(1)}, u32[]{:S(2)}, u32[]{:S(2)}) collective-permute-start(f32[1,40,128]{2,1,0:T(8,128)S(1)} %shard_map.126.part0_ref), channel_id=1, source_target_pairs={{0,192},{1,193},{2,194},{3,195},{4,196},{5,197},{6,198},{7,199},{8... | collective-permute-start | bytes 61448 | tf_op jit(solution)/shard_map/ppermute | solution.py:974
  106.5 3.8 %collective-permute-start.18 = (f32[1,40,128]{2,1,0:T(8,128)S(1)}, f32[1,40,128]{2,1,0:T(8,128)S(1)}, u32[]{:S(2)}, u32[]{:S(2)}) collective-permute-start(f32[1,40,128]{2,1,0:T(8,128)S(1)} %shard_map.126.part0_ref), channel_id=1, source_target_pairs={{0,64},{1,65},{2,66},{3,67},{4,68},{5,69},{6,70},{7,71},{8,72},{9,... | collective-permute-start | bytes 61448 | tf_op jit(solution)/shard_map/ppermute | solution.py:974
  (1 other events, 0.8 us)

commit v9 on v8

--- a/solution.py
+++ b/solution.py
@@ -234,12 +234,13 @@
         m, i = q // 2, q % 2
         store(cross_ref, (part(q), part(q)), jnp.zeros((RANK, RANK), f32))
         store(cross_ref, (part(q), part(q ^ 1)), local_couple_ref[m, 1 - i])
-        gained = mm(local_col_ref[m, halves[i]], pair_at(local_couple_ref, 2, 1 - m))
+        gained = mm_square(pair_at(local_col_ref, m, halves[i]), pair_at(local_couple_ref, 2, 1 - m))
         spread = mm(gained, pair_at(local_row_ref, 1 - m), transposed=True)
         store(cross_ref, (part(q), slice(2 * (1 - m) * RANK, 2 * (2 - m) * RANK)), spread)
-        store(paths_ref, (part(q),), mm(local_row_ref[m, halves[i]], split(local_row_ref[2, halves[m]])))
-        path = mm(local_col_ref[m, halves[i]], split(local_col_ref[2, halves[m]]))
-        store(columns_ref, (part(q, LEAF_COLS),), mm(col_basis_ref[q], split(path)))
+        row_path = mm_square(pair_at(local_row_ref, m, halves[i]), pair_at(local_row_ref, 2, halves[m]))
+        store(paths_ref, (part(q),), row_path)
+        path = mm_square(pair_at(local_col_ref, m, halves[i]), pair_at(local_col_ref, 2, halves[m]))
+        store(columns_ref, (part(q, LEAF_COLS),), mm_square(pair_at(col_basis_ref, q), split(path)))
 
 
 def store_top(up_row_ref, up_col_ref, up_couple_ref, top_ref):
@@ -287,7 +288,7 @@
         slots = lax.broadcasted_iota(jnp.int32, (LEAF_ROWS, RANK), 0)
         basis = jnp.where(slots < rows_ref[q], row_basis_ref[q], 0.0)
         images.append(mm_inner(basis, dense_ref[q]))
-        moved.append(mm(turned[q], split(gram_of(basis))))
+        moved.append(mm_square(split(turned[q]), split(gram_of(basis))))
     inner = mm(jnp.concatenate(moved, 1), pair_at(cross_ref), transposed=True)
     for q in range(LEAF_DEV):
         image = mm(turned[q], split(images[q]))
@@ -391,7 +392,7 @@
         if products is None:
             products = [half[0].astype(f32) + half[1].astype(f32) for half in halves]
         else:
-            products = [mm(product, half) for half in halves for product in products]
+            products = [mm_square(split(product), half) for half in halves for product in products]
         for k, product in enumerate(products):
             store_pair(products_ref, product_base(height) + k, product)
             store_pair(turned_ref, product_base(height) + k, jnp.transpose(product))
@@ -504,12 +505,12 @@
 
 def path_product(me, level, path, up_col_ref):
     half = half_of(up_col_ref, level, (me >> level) & 1)
-    return mm(path, half)
+    return mm_square(split(path), half)
 
 
 def sibling_gain(me, level, path, up_couple_ref):
     child = 1 - ((me >> level) & 1)
-    return mm(path, pair_at(up_couple_ref, level, child))
+    return mm_square(split(path), pair_at(up_couple_ref, level, child))
 
 
 def core_kernel(

time: 113 us -> 112 us (level)
  transfers between devices with their start and end apart: 21 -> 21, of which waited for: 12 -> 12; matrix products, arithmetic and copies ran while one was open for 0% -> 0% of each run, Pallas kernels for 8% -> 7%
where the time goes in v9:
time: 112 us; the launch traced here: 111 us
  blocking collectives  40.7 us (36%)
  Pallas kernels  29.1 us (26%)
  starting transfers between devices  26 us (23%)
  waiting for transfers between devices  14.1 us (13%)
    all_to_all x3, blocking collectives, swap_mid(): return lax.all_to_all(message, 'leaf', 0, 0, axis_index_groups=groups)  40.7 us
    pallas_call x19, Pallas kernels, call(): pl.pallas_call(kernel, out_shape=outs, in_specs=[pl.BlockSpec(memory_spac...  29.1 us
    ppermute x21, starting transfers between devices, swap_parts(): parts.append(lax.ppermute(message, 'leaf', pairs))  26 us
    ppermute x21, waiting for transfers between devices, swap_parts(): parts.append(lax.ppermute(message, 'leaf', pairs))  14.1 us
  transfers between devices with their start and end apart: 21, of which 12 were waited for; matrix products, arithmetic and copies ran while one was open for 0% of the time, Pallas kernels for 7%

profile of v9, /device:TPU:2, one launch (start us, length us, event | category | flops | bytes accessed | tf_op | source)
XLA Modules:
  0.0 111.0 jit_solution(349978339637189974)
XLA Ops:
  0.0 3.4 %shard_map.109 = (f32[16,2048]{1,0:T(8,128)}, f32[1,88,128]{2,1,0:T(8,128)}) custom-call(s32[1]{0:T(128)} %bitcast.me_ref, s32[4]{0:T(128)} %rows_ref.5, f32[16,2048]{1,0:T(8,128)} %rhs_hbm.1, f32[4,512,128]{2,1,0:T(8,128)} %row_basis_ref.9, f32[3,256,128]{2,1,0:T(8,128)} %local_row_ref.1), custom_call_target="tpu_custom_call" | custom-call | flops 6000000000 | tf_op jit(solution)/shard_map/pallas_call | solution.py:933
  5.6 2.2 %collective-permute-start.3 = (f32[1,88,128]{2,1,0:T(8,128)S(1)}, f32[1,88,128]{2,1,0:T(8,128)S(1)}, u32[]{:S(2)}, u32[]{:S(2)}) collective-permute-start(f32[1,88,128]{2,1,0:T(8,128)S(1)} %get-tuple-element.49.order_ref.part0_ref), channel_id=1, source_target_pairs={{0,4},{1,5},{2,6},{3,7},{4,0},{5,1},{6,2},{7,3},{8,12},{9,13},{10,... | collective-permute-start | bytes 135176 | tf_op jit(solution)/shard_map/ppermute | solution.py:975
  7.8 1.6 %collective-permute-start.2 = (f32[1,88,128]{2,1,0:T(8,128)S(1)}, f32[1,88,128]{2,1,0:T(8,128)S(1)}, u32[]{:S(2)}, u32[]{:S(2)}) collective-permute-start(f32[1,88,128]{2,1,0:T(8,128)S(1)} %get-tuple-element.49.order_ref.part0_ref), channel_id=1, source_target_pairs={{0,6},{1,7},{2,4},{3,5},{4,2},{5,3},{6,0},{7,1},{8,14},{9,15},{10,... | collective-permute-start | bytes 135176 | tf_op jit(solution)/shard_map/ppermute | solution.py:975
  10.4 1.4 %shard_map.112 = (bf16[2,512,512]{2,1,0:T(8,128)(2,1)S(1)}, bf16[2,1024,128]{2,1,0:T(8,128)(2,1)S(1)}, bf16[2,512,128]{2,1,0:T(8,128)(2,1)S(1)}, bf16[2,6,128,12...) custom-call(f32[1,88,128]{2,1,0:T(8,128)S(1)} %get-tuple-element.49.order_ref.part0_ref, f32[4,256,128]{2,1,0:T(8,128)S(1)} %copy-done.5, ...), custom_call_target="tpu_custom_call" | custom-call | flops 6000000000 | tf_op jit(solution)/shard_map/pallas_call | solution.py:933
  14.2 16.7 %all_to_all.15.recv_ref = f32[8,32,128]{2,1,0:T(8,128)S(1)} all-to-all(f32[8,32,128]{2,1,0:T(8,128)S(1)} %get-tuple-element.53), channel_id=1, replica_groups={{0,8,16,24,32,40,48,56},{1,9,17,25,33,41,49,57},{2,10,18,26,34,42,50,58..., dimensions={0} | all-to-all | bytes 262144 | tf_op jit(solution)/shard_map/all_to_all | solution.py:981
  31.3 3.2 %collective-permute-start.6 = (f32[1,24,128]{2,1,0:T(8,128)S(1)}, f32[1,24,128]{2,1,0:T(8,128)S(1)}, u32[]{:S(2)}, u32[]{:S(2)}) collective-permute-start(f32[1,24,128]{2,1,0:T(8,128)S(1)} %get-tuple-element.54.order_ref.part0_ref), channel_id=1, source_target_pairs={{0,128},{1,129},{2,130},{3,131},{4,132},{5,133},{6,134},{7,135},{8... | collective-permute-start | bytes 36872 | tf_op jit(solution)/shard_map/ppermute | solution.py:975
  34.5 1.1 collective-permute-start.5
  35.6 1.1 shard_map.116.within_ref
  36.7 2.7 %collective-permute-done.5.part2_ref = f32[1,24,128]{2,1,0:T(8,128)S(1)} collective-permute-done((f32[1,24,128]{2,1,0:T(8,128)S(1)}, f32[1,24,128]{2,1,0:T(8,128)S(1)}, u32[]{:S(2)}, u32[]{:S(2)}) %collective-permute-start.5) | collective-permute-done | bytes 12320 | tf_op jit(solution)/shard_map/ppermute | solution.py:975
  39.5 3.4 %shard_map.117 = (f32[16,1024]{1,0:T(8,128)S(1)}, f32[16,128]{1,0:T(8,128)S(1)}, f32[1,104,128]{2,1,0:T(8,128)S(1)}, f32[8,128]{1,0:T(8,128)S(1)}, f32[16,2048]{1,0:T(8,128)S(1)}) custom-call(s32[1]{0:T(128)} %bitcast.me_ref, s32[4]{0:T(128)S(1)} %copy-done.10, f32[1,24,128]{2,1,0:T(8,128)S(1)} %get-tuple-element.54.order_ref.part0_ref, ...), custom_call_target="tpu_custom_call" | custom-call | flops 6000000000 | tf_op jit(solution)/shard_map/pallas_call | solution.py:933
  42.9 1.2 %collective-permute-done.7.part1_ref = f32[1,104,128]{2,1,0:T(8,128)S(1)} collective-permute-done((f32[1,104,128]{2,1,0:T(8,128)S(1)}, f32[1,104,128]{2,1,0:T(8,128)S(1)}, u32[]{:S(2)}, u32[]{:S(2)}) %collective-permute-start.7) | collective-permute-done | bytes 53280 | tf_op jit(solution)/shard_map/ppermute | solution.py:975
  44.6 2.6 %collective-permute-start.10 = (f32[1,168,128]{2,1,0:T(8,128)S(1)}, f32[1,168,128]{2,1,0:T(8,128)S(1)}, u32[]{:S(2)}, u32[]{:S(2)}) collective-permute-start(f32[1,168,128]{2,1,0:T(8,128)S(1)} %get-tuple-element.64.order_ref.part0_ref), channel_id=1, source_target_pairs={{0,4},{1,5},{2,6},{3,7},{4,0},{5,1},{6,2},{7,3},{8,12},{9,13},{10,... | collective-permute-start | bytes 258056 | tf_op jit(solution)/shard_map/ppermute | solution.py:975
  47.9 1.5 %collective-permute-start.8 = (f32[1,168,128]{2,1,0:T(8,128)S(1)}, f32[1,168,128]{2,1,0:T(8,128)S(1)}, u32[]{:S(2)}, u32[]{:S(2)}) collective-permute-start(f32[1,168,128]{2,1,0:T(8,128)S(1)} %get-tuple-element.64.order_ref.part0_ref), channel_id=1, source_target_pairs={{0,2},{1,3},{2,0},{3,1},{4,6},{5,7},{6,4},{7,5},{8,10},{9,11},{10,... | collective-permute-start | bytes 258056 | tf_op jit(solution)/shard_map/ppermute | solution.py:975
  49.4 3.7 %shard_map.119 = (bf16[2,128,1024]{2,1,0:T(8,128)(2,1)S(1)}, bf16[2,512,512]{2,1,0:T(8,128)(2,1)S(1)}, bf16[2,14,128,128]{3,2,1,0:T(8,128)(2,1)S(1)}, bf16[2,14,128,128]{3,2,1,0:T(8,128)(2,1)S(1)}) custom-call(f32[1,168,128]{2,1,0:T(8,128)S(1)} %get-tuple-element.64.order_ref.part0_ref, s32[4]{0:T(128)S(1)} %copy-done.10, f32[4,512,256]{2,1,0:T(8,128)S(1)} %copy-done, ...), custom_call_target="tpu_custom_call" | custom-call | flops 6000000000 | tf_op jit(solution)/shard_map/pallas_call | solution.py:933
  53.1 1.8 %shard_map.120 = (f32[8,40,128]{2,1,0:T(8,128)S(1)}, f32[6,16,128]{2,1,0:T(8,128)S(1)}, f32[8,128]{1,0:T(8,128)S(1)}, bf16[2,14,128,128]{3,2,1,0:T(8,128)(2,1)S(1)}, f32[72,128]{1,0:T(8,128)S(1)}) custom-call(s32[1]{0:T(128)} %bitcast.me_ref, bf16[2,14,128,128]{3,2,1,0:T(8,128)(2,1)S(1)} %get-tuple-element.65.products_ref, ...), custom_call_target="tpu_custom_call" | custom-call | flops 6000000000 | tf_op jit(solution)/shard_map/pallas_call | solution.py:933
  55.0 12.1 %all_to_all.16.recv_ref = f32[8,40,128]{2,1,0:T(8,128)S(1)} all-to-all(f32[8,40,128]{2,1,0:T(8,128)S(1)} %get-tuple-element.69), channel_id=1, replica_groups={{0,8,16,24,32,40,48,56},{1,9,17,25,33,41,49,57},{2,10,18,26,34,42,50,58..., dimensions={0} | all-to-all | bytes 327680 | tf_op jit(solution)/shard_map/all_to_all | solution.py:981
  67.1 1.3 %shard_map.121 = (f32[1,112,128]{2,1,0:T(8,128)S(1)}, f32[9,16,128]{2,1,0:T(8,128)S(1)}, f32[8,128]{1,0:T(8,128)S(1)}) custom-call(s32[1]{0:T(128)} %bitcast.me_ref, f32[8,40,128]{2,1,0:T(8,128)S(1)} %all_to_all.16.recv_ref, f32[7,256,128]{2,1,0:T(8,128)S(1)} %copy-done.3, f32[7,256,128]{2,1,0:T(8,128)S(1)} %copy-done.4, f32[8,2,128,128]{3,2,1,0:T(8,128)S(1)} %copy-done.2, ...), custom_call_target="tpu_custom_call" | custom-call | flops 6000000000 | tf_op jit(solution)/shard_map/pallas_call | solution.py:933
  68.4 1.6 %collective-permute-start.13 = (f32[1,112,128]{2,1,0:T(8,128)S(1)}, f32[1,112,128]{2,1,0:T(8,128)S(1)}, u32[]{:S(2)}, u32[]{:S(2)}) collective-permute-start(f32[1,112,128]{2,1,0:T(8,128)S(1)} %get-tuple-element.72.order_ref.part0_ref), channel_id=1, source_target_pairs={{0,128},{1,129},{2,130},{3,131},{4,132},{5,133},{6,134},{7,135},{8... | collective-permute-start | bytes 172040 | tf_op jit(solution)/shard_map/ppermute | solution.py:975
  72.0 1.1 shard_map.122.within_ref
  73.1 1.1 collective-permute-done.13.part3_ref
  74.1 1.2 %collective-permute-done.12.part2_ref = f32[1,112,128]{2,1,0:T(8,128)S(1)} collective-permute-done((f32[1,112,128]{2,1,0:T(8,128)S(1)}, f32[1,112,128]{2,1,0:T(8,128)S(1)}, u32[]{:S(2)}, u32[]{:S(2)}) %collective-permute-start.12) | collective-permute-done | bytes 57376 | tf_op jit(solution)/shard_map/ppermute | solution.py:975
  75.4 4.8 %shard_map.123 = (f32[16,1024]{1,0:T(8,128)S(1)}, f32[16,1024]{1,0:T(8,128)S(1)}, f32[16,128]{1,0:T(8,128)S(1)}, f32[16,128]{1,0:T(8,128)S(1)}, f32[1,40,128]{2,...) custom-call(s32[1]{0:T(128)} %bitcast.me_ref, s32[4]{0:T(128)S(1)} %copy-done.10, ...), custom_call_target="tpu_custom_call" | custom-call | flops 6000000000 | tf_op jit(solution)/shard_map/pallas_call | solution.py:933
  80.3 1.2 %collective-permute-done.14.refs_1_ = f32[1,40,128]{2,1,0:T(8,128)S(1)} collective-permute-done((f32[1,40,128]{2,1,0:T(8,128)S(1)}, f32[1,40,128]{2,1,0:T(8,128)S(1)}, u32[]{:S(2)}, u32[]{:S(2)}) %collective-permute-start.14) | collective-permute-done | bytes 20512 | tf_op jit(solution)/shard_map/ppermute | solution.py:975
  82.0 2.6 %collective-permute-start.17 = (f32[1,40,128]{2,1,0:T(8,128)S(1)}, f32[1,40,128]{2,1,0:T(8,128)S(1)}, u32[]{:S(2)}, u32[]{:S(2)}) collective-permute-start(f32[1,40,128]{2,1,0:T(8,128)S(1)} %shard_map.124.refs_0_), channel_id=1, source_target_pairs={{0,4},{1,5},{2,6},{3,7},{4,0},{5,1},{6,2},{7,3},{8,12},{9,13},{10,... | collective-permute-start | bytes 61448 | tf_op jit(solution)/shard_map/ppermute | solution.py:975
  84.7 2.0 %collective-permute-start.15 = (f32[1,40,128]{2,1,0:T(8,128)S(1)}, f32[1,40,128]{2,1,0:T(8,128)S(1)}, u32[]{:S(2)}, u32[]{:S(2)}) collective-permute-start(f32[1,40,128]{2,1,0:T(8,128)S(1)} %shard_map.124.refs_0_), channel_id=1, source_target_pairs={{0,2},{1,3},{2,0},{3,1},{4,6},{5,7},{6,4},{7,5},{8,10},{9,11},{10,... | collective-permute-start | bytes 61448 | tf_op jit(solution)/shard_map/ppermute | solution.py:975
  89.4 11.8 %all_to_all.17.refs_0_ = f32[8,40,128]{2,1,0:T(8,128)S(1)} all-to-all(f32[8,40,128]{2,1,0:T(8,128)S(1)} %shard_map.125), channel_id=1, replica_groups={{0,8,16,24,32,40,48,56},{1,9,17,25,33,41,49,57},{2,10,18,26,34,42,50,58..., dimensions={0} | all-to-all | bytes 327680 | tf_op jit(solution)/shard_map/all_to_all | solution.py:981
  101.2 1.3 %shard_map.126.part0_ref = f32[1,40,128]{2,1,0:T(8,128)S(1)} custom-call(s32[1]{0:T(128)} %bitcast.me_ref, f32[8,40,128]{2,1,0:T(8,128)S(1)} %all_to_all.17.refs_0_, f32[7,256,128]{2,1,0:T(8,128)S(1)} %copy-done.3, f32[7,256,128]{2,1,0:T(8,128)S(1)} %copy-done.4, f32[8,2,128,128]{3,2,1,0:T(8,128)S(1)} %copy-done.2, ...), custom_call_target="tpu_custom_call" | custom-call | flops 6000000000 | tf_op jit(solution)/shard_map/pallas_call | solution.py:933
  102.5 2.3 %collective-permute-start.20 = (f32[1,40,128]{2,1,0:T(8,128)S(1)}, f32[1,40,128]{2,1,0:T(8,128)S(1)}, u32[]{:S(2)}, u32[]{:S(2)}) collective-permute-start(f32[1,40,128]{2,1,0:T(8,128)S(1)} %shard_map.126.part0_ref), channel_id=1, source_target_pairs={{0,128},{1,129},{2,130},{3,131},{4,132},{5,133},{6,134},{7,135},{8... | collective-permute-start | bytes 61448 | tf_op jit(solution)/shard_map/ppermute | solution.py:975
  104.7 1.2 %collective-permute-start.19 = (f32[1,40,128]{2,1,0:T(8,128)S(1)}, f32[1,40,128]{2,1,0:T(8,128)S(1)}, u32[]{:S(2)}, u32[]{:S(2)}) collective-permute-start(f32[1,40,128]{2,1,0:T(8,128)S(1)} %shard_map.126.part0_ref), channel_id=1, source_target_pairs={{0,192},{1,193},{2,194},{3,195},{4,196},{5,197},{6,198},{7,199},{8... | collective-permute-start | bytes 61448 | tf_op jit(solution)/shard_map/ppermute | solution.py:975
  106.0 1.8 %collective-permute-done.20.part3_ref = f32[1,40,128]{2,1,0:T(8,128)S(1)} collective-permute-done((f32[1,40,128]{2,1,0:T(8,128)S(1)}, f32[1,40,128]{2,1,0:T(8,128)S(1)}, u32[]{:S(2)}, u32[]{:S(2)}) %collective-permute-start.20) | collective-permute-done | bytes 20512 | tf_op jit(solution)/shard_map/ppermute | solution.py:975
  107.8 1.9 %collective-permute-done.19.part2_ref = f32[1,40,128]{2,1,0:T(8,128)S(1)} collective-permute-done((f32[1,40,128]{2,1,0:T(8,128)S(1)}, f32[1,40,128]{2,1,0:T(8,128)S(1)}, u32[]{:S(2)}, u32[]{:S(2)}) %collective-permute-start.19) | collective-permute-done | bytes 20512 | tf_op jit(solution)/shard_map/ppermute | solution.py:975
  109.7 1.3 %shard_map.127 = f32[16,1024]{1,0:T(8,128)} custom-call(s32[1]{0:T(128)} %bitcast.me_ref, f32[1,40,128]{2,1,0:T(8,128)S(1)} %shard_map.126.part0_ref, f32[1,40,128]{2,1,0:T(8,128)S(1)} %collective-permute-done.18.part1_ref, f32[1,40,128]{2,1,0:T(8,128)S(1)} %collective-permute-done.19.part2_ref, f32[1,40,128]{2,1,0:T(8,128)S(1)} %collective-permute-done.20.part3_ref, ...), custom_call_target="tpu_custom_call" | custom-call | flops 6000000000 | tf_op jit(solution)/shard_map/pallas_call | solution.py:933
  (56 shorter events, 12.6 us)
Async XLA Ops:
  3.4 1.5 %copy-start.3 = (f32[7,256,128]{2,1,0:T(8,128)S(1)}, f32[7,256,128]{2,1,0:T(8,128)}, u32[]{:S(2)}) copy-start(f32[7,256,128]{2,1,0:T(8,128)} %refs_1_.1) | copy-start | bytes 2752516
  3.4 1.5 %collective-permute-start = (f32[1,88,128]{2,1,0:T(8,128)}, f32[1,88,128]{2,1,0:T(8,128)S(1)}, u32[]{:S(2)}, u32[]{:S(2)}) collective-permute-start(f32[1,88,128]{2,1,0:T(8,128)} %get-tuple-element.48.message_ref), channel_id=1, source_target_pairs={{0,1},{1,0},{2,3},{3,2},{4,5},{5,4},{6,7},{7,6},{8,9},{9,8},{10,11... | collective-permute-start | bytes 135176 | tf_op jit(solution)/shard_map/ppermute | solution.py:975
  4.4 6.0 %copy-start.5 = (f32[4,256,128]{2,1,0:T(8,128)S(1)}, f32[4,256,128]{2,1,0:T(8,128)}, u32[]{:S(2)}) copy-start(f32[4,256,128]{2,1,0:T(8,128)} %col_basis_ref.11) | copy-start | bytes 1572868
  4.4 6.0 %copy-start.6 = (f32[3,256,128]{2,1,0:T(8,128)S(1)}, f32[3,256,128]{2,1,0:T(8,128)}, u32[]{:S(2)}) copy-start(f32[3,256,128]{2,1,0:T(8,128)} %local_row_ref.1) | copy-start | bytes 1179652
  4.4 6.0 %copy-start.7 = (f32[3,256,128]{2,1,0:T(8,128)S(1)}, f32[3,256,128]{2,1,0:T(8,128)}, u32[]{:S(2)}) copy-start(f32[3,256,128]{2,1,0:T(8,128)} %local_col_ref.1) | copy-start | bytes 1179652
  4.4 6.0 %copy-start.8 = (f32[3,2,128,128]{3,2,1,0:T(8,128)S(1)}, f32[3,2,128,128]{3,2,1,0:T(8,128)}, u32[]{:S(2)}) copy-start(f32[3,2,128,128]{3,2,1,0:T(8,128)} %local_couple_ref.1) | copy-start | bytes 1179652
  5.5 6.2 %copy-start.2 = (f32[8,2,128,128]{3,2,1,0:T(8,128)S(1)}, f32[8,2,128,128]{3,2,1,0:T(8,128)}, u32[]{:S(2)}) copy-start(f32[8,2,128,128]{3,2,1,0:T(8,128)} %refs_3_.3) | copy-start | bytes 3145732
  5.6 6.2 %copy-start.4 = (f32[7,256,128]{2,1,0:T(8,128)S(1)}, f32[7,256,128]{2,1,0:T(8,128)}, u32[]{:S(2)}) copy-start(f32[7,256,128]{2,1,0:T(8,128)} %refs_2_.3) | copy-start | bytes 2752516
  5.6 7.2 %collective-permute-start.3 = (f32[1,88,128]{2,1,0:T(8,128)S(1)}, f32[1,88,128]{2,1,0:T(8,128)S(1)}, u32[]{:S(2)}, u32[]{:S(2)}) collective-permute-start(f32[1,88,128]{2,1,0:T(8,128)S(1)} %get-tuple-element.49.order_ref.part0_ref), channel_id=1, source_target_pairs={{0,4},{1,5},{2,6},{3,7},{4,0},{5,1},{6,2},{7,3},{8,12},{9,13},{10,... | collective-permute-start | bytes 135176 | tf_op jit(solution)/shard_map/ppermute | solution.py:975
  7.8 5.0 %collective-permute-start.2 = (f32[1,88,128]{2,1,0:T(8,128)S(1)}, f32[1,88,128]{2,1,0:T(8,128)S(1)}, u32[]{:S(2)}, u32[]{:S(2)}) collective-permute-start(f32[1,88,128]{2,1,0:T(8,128)S(1)} %get-tuple-element.49.order_ref.part0_ref), channel_id=1, source_target_pairs={{0,6},{1,7},{2,4},{3,5},{4,2},{5,3},{6,0},{7,1},{8,14},{9,15},{10,... | collective-permute-start | bytes 135176 | tf_op jit(solution)/shard_map/ppermute | solution.py:975
  9.4 4.0 %collective-permute-start.1 = (f32[1,88,128]{2,1,0:T(8,128)S(1)}, f32[1,88,128]{2,1,0:T(8,128)S(1)}, u32[]{:S(2)}, u32[]{:S(2)}) collective-permute-start(f32[1,88,128]{2,1,0:T(8,128)S(1)} %get-tuple-element.49.order_ref.part0_ref), channel_id=1, source_target_pairs={{0,2},{1,3},{2,0},{3,1},{4,6},{5,7},{6,4},{7,5},{8,10},{9,11},{10,... | collective-permute-start | bytes 135176 | tf_op jit(solution)/shard_map/ppermute | solution.py:975
  30.9 4.7 %copy-start = (f32[4,512,256]{2,1,0:T(8,128)S(1)}, f32[4,512,256]{2,1,0:T(8,128)}, u32[]{:S(2)}) copy-start(f32[4,512,256]{2,1,0:T(8,128)} %dense_ref.9) | copy-start | bytes 6291460
  30.9 4.7 %copy-start.1 = (f32[4,512,128]{2,1,0:T(8,128)S(1)}, f32[4,512,128]{2,1,0:T(8,128)}, u32[]{:S(2)}) copy-start(f32[4,512,128]{2,1,0:T(8,128)} %row_basis_ref.9) | copy-start | bytes 3145732
  30.9 4.7 %copy-start.11 = (f32[16,2048]{1,0:T(8,128)S(1)}, f32[16,2048]{1,0:T(8,128)}, u32[]{:S(2)}) copy-start(f32[16,2048]{1,0:T(8,128)} %get-tuple-element.61.y_ref) | copy-start | bytes 393220
  31.3 5.4 %collective-permute-start.6 = (f32[1,24,128]{2,1,0:T(8,128)S(1)}, f32[1,24,128]{2,1,0:T(8,128)S(1)}, u32[]{:S(2)}, u32[]{:S(2)}) collective-permute-start(f32[1,24,128]{2,1,0:T(8,128)S(1)} %get-tuple-element.54.order_ref.part0_ref), channel_id=1, source_target_pairs={{0,128},{1,129},{2,130},{3,131},{4,132},{5,133},{6,134},{7,135},{8... | collective-permute-start | bytes 36872 | tf_op jit(solution)/shard_map/ppermute | solution.py:975
  34.5 4.9 %collective-permute-start.5 = (f32[1,24,128]{2,1,0:T(8,128)S(1)}, f32[1,24,128]{2,1,0:T(8,128)S(1)}, u32[]{:S(2)}, u32[]{:S(2)}) collective-permute-start(f32[1,24,128]{2,1,0:T(8,128)S(1)} %get-tuple-element.54.order_ref.part0_ref), channel_id=1, source_target_pairs={{0,192},{1,193},{2,194},{3,195},{4,196},{5,197},{6,198},{7,199},{8... | collective-permute-start | bytes 36872 | tf_op jit(solution)/shard_map/ppermute | solution.py:975
  35.6 3.8 %collective-permute-start.4 = (f32[1,24,128]{2,1,0:T(8,128)S(1)}, f32[1,24,128]{2,1,0:T(8,128)S(1)}, u32[]{:S(2)}, u32[]{:S(2)}) collective-permute-start(f32[1,24,128]{2,1,0:T(8,128)S(1)} %get-tuple-element.54.order_ref.part0_ref), channel_id=1, source_target_pairs={{0,64},{1,65},{2,66},{3,67},{4,68},{5,69},{6,70},{7,71},{8,72},{9,... | collective-permute-start | bytes 36872 | tf_op jit(solution)/shard_map/ppermute | solution.py:975
  35.6 3.8 %copy-start.10 = (s32[4]{0:T(128)S(1)}, s32[4]{0:T(128)}, u32[]{:S(2)}) copy-start(s32[4]{0:T(128)} %rows_ref.5) | copy-start | bytes 52
  42.8 1.3 %collective-permute-start.7 = (f32[1,104,128]{2,1,0:T(8,128)S(1)}, f32[1,104,128]{2,1,0:T(8,128)S(1)}, u32[]{:S(2)}, u32[]{:S(2)}) collective-permute-start(f32[1,104,128]{2,1,0:T(8,128)S(1)} %get-tuple-element.62.part0_ref), channel_id=1, source_target_pairs={{0,1},{1,0},{2,3},{3,2},{4,5},{5,4},{6,7},{7,6},{8,9},{9,8},{10,11... | collective-permute-start | bytes 159752 | tf_op jit(solution)/shard_map/ppermute | solution.py:975
  44.6 8.5 %collective-permute-start.10 = (f32[1,168,128]{2,1,0:T(8,128)S(1)}, f32[1,168,128]{2,1,0:T(8,128)S(1)}, u32[]{:S(2)}, u32[]{:S(2)}) collective-permute-start(f32[1,168,128]{2,1,0:T(8,128)S(1)} %get-tuple-element.64.order_ref.part0_ref), channel_id=1, source_target_pairs={{0,4},{1,5},{2,6},{3,7},{4,0},{5,1},{6,2},{7,3},{8,12},{9,13},{10,... | collective-permute-start | bytes 258056 | tf_op jit(solution)/shard_map/ppermute | solution.py:975
  47.2 5.9 %collective-permute-start.9 = (f32[1,168,128]{2,1,0:T(8,128)S(1)}, f32[1,168,128]{2,1,0:T(8,128)S(1)}, u32[]{:S(2)}, u32[]{:S(2)}) collective-permute-start(f32[1,168,128]{2,1,0:T(8,128)S(1)} %get-tuple-element.64.order_ref.part0_ref), channel_id=1, source_target_pairs={{0,6},{1,7},{2,4},{3,5},{4,2},{5,3},{6,0},{7,1},{8,14},{9,15},{10,... | collective-permute-start | bytes 258056 | tf_op jit(solution)/shard_map/ppermute | solution.py:975
  47.9 5.3 %collective-permute-start.8 = (f32[1,168,128]{2,1,0:T(8,128)S(1)}, f32[1,168,128]{2,1,0:T(8,128)S(1)}, u32[]{:S(2)}, u32[]{:S(2)}) collective-permute-start(f32[1,168,128]{2,1,0:T(8,128)S(1)} %get-tuple-element.64.order_ref.part0_ref), channel_id=1, source_target_pairs={{0,2},{1,3},{2,0},{3,1},{4,6},{5,7},{6,4},{7,5},{8,10},{9,11},{10,... | collective-permute-start | bytes 258056 | tf_op jit(solution)/shard_map/ppermute | solution.py:975
  68.4 5.7 %collective-permute-start.13 = (f32[1,112,128]{2,1,0:T(8,128)S(1)}, f32[1,112,128]{2,1,0:T(8,128)S(1)}, u32[]{:S(2)}, u32[]{:S(2)}) collective-permute-start(f32[1,112,128]{2,1,0:T(8,128)S(1)} %get-tuple-element.72.order_ref.part0_ref), channel_id=1, source_target_pairs={{0,128},{1,129},{2,130},{3,131},{4,132},{5,133},{6,134},{7,135},{8... | collective-permute-start | bytes 172040 | tf_op jit(solution)/shard_map/ppermute | solution.py:975
  70.0 5.4 %collective-permute-start.12 = (f32[1,112,128]{2,1,0:T(8,128)S(1)}, f32[1,112,128]{2,1,0:T(8,128)S(1)}, u32[]{:S(2)}, u32[]{:S(2)}) collective-permute-start(f32[1,112,128]{2,1,0:T(8,128)S(1)} %get-tuple-element.72.order_ref.part0_ref), channel_id=1, source_target_pairs={{0,192},{1,193},{2,194},{3,195},{4,196},{5,197},{6,198},{7,199},{8... | collective-permute-start | bytes 172040 | tf_op jit(solution)/shard_map/ppermute | solution.py:975
  71.0 4.4 %collective-permute-start.11 = (f32[1,112,128]{2,1,0:T(8,128)S(1)}, f32[1,112,128]{2,1,0:T(8,128)S(1)}, u32[]{:S(2)}, u32[]{:S(2)}) collective-permute-start(f32[1,112,128]{2,1,0:T(8,128)S(1)} %get-tuple-element.72.order_ref.part0_ref), channel_id=1, source_target_pairs={{0,64},{1,65},{2,66},{3,67},{4,68},{5,69},{6,70},{7,71},{8,72},{9,... | collective-permute-start | bytes 172040 | tf_op jit(solution)/shard_map/ppermute | solution.py:975
  80.2 1.3 %collective-permute-start.14 = (f32[1,40,128]{2,1,0:T(8,128)S(1)}, f32[1,40,128]{2,1,0:T(8,128)S(1)}, u32[]{:S(2)}, u32[]{:S(2)}) collective-permute-start(f32[1,40,128]{2,1,0:T(8,128)S(1)} %get-tuple-element.84.refs_0_), channel_id=1, source_target_pairs={{0,1},{1,0},{2,3},{3,2},{4,5},{5,4},{6,7},{7,6},{8,9},{9,8},{10,11... | collective-permute-start | bytes 61448 | tf_op jit(solution)/shard_map/ppermute | solution.py:975
  82.0 5.5 %collective-permute-start.17 = (f32[1,40,128]{2,1,0:T(8,128)S(1)}, f32[1,40,128]{2,1,0:T(8,128)S(1)}, u32[]{:S(2)}, u32[]{:S(2)}) collective-permute-start(f32[1,40,128]{2,1,0:T(8,128)S(1)} %shard_map.124.refs_0_), channel_id=1, source_target_pairs={{0,4},{1,5},{2,6},{3,7},{4,0},{5,1},{6,2},{7,3},{8,12},{9,13},{10,... | collective-permute-start | bytes 61448 | tf_op jit(solution)/shard_map/ppermute | solution.py:975
  84.6 3.8 %collective-permute-start.16 = (f32[1,40,128]{2,1,0:T(8,128)S(1)}, f32[1,40,128]{2,1,0:T(8,128)S(1)}, u32[]{:S(2)}, u32[]{:S(2)}) collective-permute-start(f32[1,40,128]{2,1,0:T(8,128)S(1)} %shard_map.124.refs_0_), channel_id=1, source_target_pairs={{0,6},{1,7},{2,4},{3,5},{4,2},{5,3},{6,0},{7,1},{8,14},{9,15},{10,... | collective-permute-start | bytes 61448 | tf_op jit(solution)/shard_map/ppermute | solution.py:975
  84.7 3.8 %collective-permute-start.15 = (f32[1,40,128]{2,1,0:T(8,128)S(1)}, f32[1,40,128]{2,1,0:T(8,128)S(1)}, u32[]{:S(2)}, u32[]{:S(2)}) collective-permute-start(f32[1,40,128]{2,1,0:T(8,128)S(1)} %shard_map.124.refs_0_), channel_id=1, source_target_pairs={{0,2},{1,3},{2,0},{3,1},{4,6},{5,7},{6,4},{7,5},{8,10},{9,11},{10,... | collective-permute-start | bytes 61448 | tf_op jit(solution)/shard_map/ppermute | solution.py:975
  102.5 5.4 %collective-permute-start.20 = (f32[1,40,128]{2,1,0:T(8,128)S(1)}, f32[1,40,128]{2,1,0:T(8,128)S(1)}, u32[]{:S(2)}, u32[]{:S(2)}) collective-permute-start(f32[1,40,128]{2,1,0:T(8,128)S(1)} %shard_map.126.part0_ref), channel_id=1, source_target_pairs={{0,128},{1,129},{2,130},{3,131},{4,132},{5,133},{6,134},{7,135},{8... | collective-permute-start | bytes 61448 | tf_op jit(solution)/shard_map/ppermute | solution.py:975
  104.7 5.0 %collective-permute-start.19 = (f32[1,40,128]{2,1,0:T(8,128)S(1)}, f32[1,40,128]{2,1,0:T(8,128)S(1)}, u32[]{:S(2)}, u32[]{:S(2)}) collective-permute-start(f32[1,40,128]{2,1,0:T(8,128)S(1)} %shard_map.126.part0_ref), channel_id=1, source_target_pairs={{0,192},{1,193},{2,194},{3,195},{4,196},{5,197},{6,198},{7,199},{8... | collective-permute-start | bytes 61448 | tf_op jit(solution)/shard_map/ppermute | solution.py:975
  105.9 3.8 %collective-permute-start.18 = (f32[1,40,128]{2,1,0:T(8,128)S(1)}, f32[1,40,128]{2,1,0:T(8,128)S(1)}, u32[]{:S(2)}, u32[]{:S(2)}) collective-permute-start(f32[1,40,128]{2,1,0:T(8,128)S(1)} %shard_map.126.part0_ref), channel_id=1, source_target_pairs={{0,64},{1,65},{2,66},{3,67},{4,68},{5,69},{6,70},{7,71},{8,72},{9,... | collective-permute-start | bytes 61448 | tf_op jit(solution)/shard_map/ppermute | solution.py:975
  (1 other events, 0.8 us)

commit v10 on v9

--- a/solution.py
+++ b/solution.py
@@ -308,10 +308,8 @@
 
 
 def both_sides(grams, half):
-    full = half[0].astype(f32) + half[1].astype(f32)
-    left = mm(jnp.transpose(full), split(jnp.concatenate(grams, 1)))
-    columns = [left[:, k * RANK : (k + 1) * RANK] for k in range(len(grams))]
-    return unstack(mm(stack(columns), half), len(grams))
+    turned = split(jnp.transpose(half[0].astype(f32) + half[1].astype(f32)))
+    return [mm_square(split(mm_square(turned, split(gram))), half) for gram in grams]
 
 
 def gram_climb(grams, transfer):
@@ -454,7 +452,7 @@
     for q in range(LEAF_DEV):
         m, i = q // 2, q % 2
         top = split(local_row_ref[2, m * RANK : (m + 1) * RANK])
-        paths.append(mm(local_row_ref[m, i * RANK : (i + 1) * RANK], top))
+        paths.append(mm_square(pair_at(local_row_ref, m, slice(i * RANK, (i + 1) * RANK)), top))
     leaf = []
     grams = []
     for q in range(LEAF_DEV):

time: 112 us -> 112 us (level)
  no operation moved by 1% of the time
where the time goes in v10:
time: 112 us; the launch traced here: 111 us
  blocking collectives  40.6 us (36%)
  Pallas kernels  29 us (26%)
  starting transfers between devices  26 us (23%)
  waiting for transfers between devices  14.1 us (13%)
    all_to_all x3, blocking collectives, swap_mid(): return lax.all_to_all(message, 'leaf', 0, 0, axis_index_groups=groups)  40.6 us
    pallas_call x19, Pallas kernels, call(): pl.pallas_call(kernel, out_shape=outs, in_specs=[pl.BlockSpec(memory_spac...  29 us
    ppermute x21, starting transfers between devices, swap_parts(): parts.append(lax.ppermute(message, 'leaf', pairs))  26 us
    ppermute x21, waiting for transfers between devices, swap_parts(): parts.append(lax.ppermute(message, 'leaf', pairs))  14.1 us
  transfers between devices with their start and end apart: 21, of which 12 were waited for; matrix products, arithmetic and copies ran while one was open for 0% of the time, Pallas kernels for 7%

profile of v10, /device:TPU:2, one launch (start us, length us, event | category | flops | bytes accessed | tf_op | source)
XLA Modules:
  0.0 110.9 jit_solution(13098774025025650598)
XLA Ops:
  0.0 3.3 %shard_map.109 = (f32[16,2048]{1,0:T(8,128)}, f32[1,88,128]{2,1,0:T(8,128)}) custom-call(s32[1]{0:T(128)} %bitcast.me_ref, s32[4]{0:T(128)} %rows_ref.5, f32[16,2048]{1,0:T(8,128)} %rhs_hbm.1, f32[4,512,128]{2,1,0:T(8,128)} %row_basis_ref.9, f32[3,256,128]{2,1,0:T(8,128)} %local_row_ref.1), custom_call_target="tpu_custom_call" | custom-call | flops 6000000000 | tf_op jit(solution)/shard_map/pallas_call | solution.py:931
  5.5 2.2 %collective-permute-start.3 = (f32[1,88,128]{2,1,0:T(8,128)S(1)}, f32[1,88,128]{2,1,0:T(8,128)S(1)}, u32[]{:S(2)}, u32[]{:S(2)}) collective-permute-start(f32[1,88,128]{2,1,0:T(8,128)S(1)} %get-tuple-element.49.order_ref.part0_ref), channel_id=1, source_target_pairs={{0,4},{1,5},{2,6},{3,7},{4,0},{5,1},{6,2},{7,3},{8,12},{9,13},{10,... | collective-permute-start | bytes 135176 | tf_op jit(solution)/shard_map/ppermute | solution.py:973
  7.7 1.6 %collective-permute-start.2 = (f32[1,88,128]{2,1,0:T(8,128)S(1)}, f32[1,88,128]{2,1,0:T(8,128)S(1)}, u32[]{:S(2)}, u32[]{:S(2)}) collective-permute-start(f32[1,88,128]{2,1,0:T(8,128)S(1)} %get-tuple-element.49.order_ref.part0_ref), channel_id=1, source_target_pairs={{0,6},{1,7},{2,4},{3,5},{4,2},{5,3},{6,0},{7,1},{8,14},{9,15},{10,... | collective-permute-start | bytes 135176 | tf_op jit(solution)/shard_map/ppermute | solution.py:973
  10.3 1.4 %shard_map.112 = (bf16[2,512,512]{2,1,0:T(8,128)(2,1)S(1)}, bf16[2,1024,128]{2,1,0:T(8,128)(2,1)S(1)}, bf16[2,512,128]{2,1,0:T(8,128)(2,1)S(1)}, bf16[2,6,128,12...) custom-call(f32[1,88,128]{2,1,0:T(8,128)S(1)} %get-tuple-element.49.order_ref.part0_ref, f32[4,256,128]{2,1,0:T(8,128)S(1)} %copy-done.5, ...), custom_call_target="tpu_custom_call" | custom-call | flops 6000000000 | tf_op jit(solution)/shard_map/pallas_call | solution.py:931
  14.1 16.7 %all_to_all.15.recv_ref = f32[8,32,128]{2,1,0:T(8,128)S(1)} all-to-all(f32[8,32,128]{2,1,0:T(8,128)S(1)} %get-tuple-element.53), channel_id=1, replica_groups={{0,8,16,24,32,40,48,56},{1,9,17,25,33,41,49,57},{2,10,18,26,34,42,50,58..., dimensions={0} | all-to-all | bytes 262144 | tf_op jit(solution)/shard_map/all_to_all | solution.py:979
  31.2 3.2 %collective-permute-start.6 = (f32[1,24,128]{2,1,0:T(8,128)S(1)}, f32[1,24,128]{2,1,0:T(8,128)S(1)}, u32[]{:S(2)}, u32[]{:S(2)}) collective-permute-start(f32[1,24,128]{2,1,0:T(8,128)S(1)} %get-tuple-element.54.order_ref.part0_ref), channel_id=1, source_target_pairs={{0,128},{1,129},{2,130},{3,131},{4,132},{5,133},{6,134},{7,135},{8... | collective-permute-start | bytes 36872 | tf_op jit(solution)/shard_map/ppermute | solution.py:973
  34.4 1.1 collective-permute-start.5
  35.5 1.1 shard_map.116.within_ref
  36.6 2.7 %collective-permute-done.5.part2_ref = f32[1,24,128]{2,1,0:T(8,128)S(1)} collective-permute-done((f32[1,24,128]{2,1,0:T(8,128)S(1)}, f32[1,24,128]{2,1,0:T(8,128)S(1)}, u32[]{:S(2)}, u32[]{:S(2)}) %collective-permute-start.5) | collective-permute-done | bytes 12320 | tf_op jit(solution)/shard_map/ppermute | solution.py:973
  39.3 3.4 %shard_map.117 = (f32[16,1024]{1,0:T(8,128)S(1)}, f32[16,128]{1,0:T(8,128)S(1)}, f32[1,104,128]{2,1,0:T(8,128)S(1)}, f32[8,128]{1,0:T(8,128)S(1)}, f32[16,2048]{1,0:T(8,128)S(1)}) custom-call(s32[1]{0:T(128)} %bitcast.me_ref, s32[4]{0:T(128)S(1)} %copy-done.10, f32[1,24,128]{2,1,0:T(8,128)S(1)} %get-tuple-element.54.order_ref.part0_ref, ...), custom_call_target="tpu_custom_call" | custom-call | flops 6000000000 | tf_op jit(solution)/shard_map/pallas_call | solution.py:931
  42.8 1.2 %collective-permute-done.7.part1_ref = f32[1,104,128]{2,1,0:T(8,128)S(1)} collective-permute-done((f32[1,104,128]{2,1,0:T(8,128)S(1)}, f32[1,104,128]{2,1,0:T(8,128)S(1)}, u32[]{:S(2)}, u32[]{:S(2)}) %collective-permute-start.7) | collective-permute-done | bytes 53280 | tf_op jit(solution)/shard_map/ppermute | solution.py:973
  44.5 2.6 %collective-permute-start.10 = (f32[1,168,128]{2,1,0:T(8,128)S(1)}, f32[1,168,128]{2,1,0:T(8,128)S(1)}, u32[]{:S(2)}, u32[]{:S(2)}) collective-permute-start(f32[1,168,128]{2,1,0:T(8,128)S(1)} %get-tuple-element.64.order_ref.part0_ref), channel_id=1, source_target_pairs={{0,4},{1,5},{2,6},{3,7},{4,0},{5,1},{6,2},{7,3},{8,12},{9,13},{10,... | collective-permute-start | bytes 258056 | tf_op jit(solution)/shard_map/ppermute | solution.py:973
  47.8 1.5 %collective-permute-start.8 = (f32[1,168,128]{2,1,0:T(8,128)S(1)}, f32[1,168,128]{2,1,0:T(8,128)S(1)}, u32[]{:S(2)}, u32[]{:S(2)}) collective-permute-start(f32[1,168,128]{2,1,0:T(8,128)S(1)} %get-tuple-element.64.order_ref.part0_ref), channel_id=1, source_target_pairs={{0,2},{1,3},{2,0},{3,1},{4,6},{5,7},{6,4},{7,5},{8,10},{9,11},{10,... | collective-permute-start | bytes 258056 | tf_op jit(solution)/shard_map/ppermute | solution.py:973
  49.3 3.7 %shard_map.119 = (bf16[2,128,1024]{2,1,0:T(8,128)(2,1)S(1)}, bf16[2,512,512]{2,1,0:T(8,128)(2,1)S(1)}, bf16[2,14,128,128]{3,2,1,0:T(8,128)(2,1)S(1)}, bf16[2,14,128,128]{3,2,1,0:T(8,128)(2,1)S(1)}) custom-call(f32[1,168,128]{2,1,0:T(8,128)S(1)} %get-tuple-element.64.order_ref.part0_ref, s32[4]{0:T(128)S(1)} %copy-done.10, f32[4,512,256]{2,1,0:T(8,128)S(1)} %copy-done, ...), custom_call_target="tpu_custom_call" | custom-call | flops 6000000000 | tf_op jit(solution)/shard_map/pallas_call | solution.py:931
  53.0 1.8 %shard_map.120 = (f32[8,40,128]{2,1,0:T(8,128)S(1)}, f32[6,16,128]{2,1,0:T(8,128)S(1)}, f32[8,128]{1,0:T(8,128)S(1)}, bf16[2,14,128,128]{3,2,1,0:T(8,128)(2,1)S(1)}, f32[72,128]{1,0:T(8,128)S(1)}) custom-call(s32[1]{0:T(128)} %bitcast.me_ref, bf16[2,14,128,128]{3,2,1,0:T(8,128)(2,1)S(1)} %get-tuple-element.65.products_ref, ...), custom_call_target="tpu_custom_call" | custom-call | flops 6000000000 | tf_op jit(solution)/shard_map/pallas_call | solution.py:931
  54.9 12.1 %all_to_all.16.recv_ref = f32[8,40,128]{2,1,0:T(8,128)S(1)} all-to-all(f32[8,40,128]{2,1,0:T(8,128)S(1)} %get-tuple-element.69), channel_id=1, replica_groups={{0,8,16,24,32,40,48,56},{1,9,17,25,33,41,49,57},{2,10,18,26,34,42,50,58..., dimensions={0} | all-to-all | bytes 327680 | tf_op jit(solution)/shard_map/all_to_all | solution.py:979
  67.0 1.3 %shard_map.121 = (f32[1,112,128]{2,1,0:T(8,128)S(1)}, f32[9,16,128]{2,1,0:T(8,128)S(1)}, f32[8,128]{1,0:T(8,128)S(1)}) custom-call(s32[1]{0:T(128)} %bitcast.me_ref, f32[8,40,128]{2,1,0:T(8,128)S(1)} %all_to_all.16.recv_ref, f32[7,256,128]{2,1,0:T(8,128)S(1)} %copy-done.3, f32[7,256,128]{2,1,0:T(8,128)S(1)} %copy-done.4, f32[8,2,128,128]{3,2,1,0:T(8,128)S(1)} %copy-done.2, ...), custom_call_target="tpu_custom_call" | custom-call | flops 6000000000 | tf_op jit(solution)/shard_map/pallas_call | solution.py:931
  68.3 1.6 %collective-permute-start.13 = (f32[1,112,128]{2,1,0:T(8,128)S(1)}, f32[1,112,128]{2,1,0:T(8,128)S(1)}, u32[]{:S(2)}, u32[]{:S(2)}) collective-permute-start(f32[1,112,128]{2,1,0:T(8,128)S(1)} %get-tuple-element.72.order_ref.part0_ref), channel_id=1, source_target_pairs={{0,128},{1,129},{2,130},{3,131},{4,132},{5,133},{6,134},{7,135},{8... | collective-permute-start | bytes 172040 | tf_op jit(solution)/shard_map/ppermute | solution.py:973
  71.8 1.1 shard_map.122.within_ref
  72.9 1.1 collective-permute-done.13.part3_ref
  74.0 1.2 %collective-permute-done.12.part2_ref = f32[1,112,128]{2,1,0:T(8,128)S(1)} collective-permute-done((f32[1,112,128]{2,1,0:T(8,128)S(1)}, f32[1,112,128]{2,1,0:T(8,128)S(1)}, u32[]{:S(2)}, u32[]{:S(2)}) %collective-permute-start.12) | collective-permute-done | bytes 57376 | tf_op jit(solution)/shard_map/ppermute | solution.py:973
  75.3 4.8 %shard_map.123 = (f32[16,1024]{1,0:T(8,128)S(1)}, f32[16,1024]{1,0:T(8,128)S(1)}, f32[16,128]{1,0:T(8,128)S(1)}, f32[16,128]{1,0:T(8,128)S(1)}, f32[1,40,128]{2,...) custom-call(s32[1]{0:T(128)} %bitcast.me_ref, s32[4]{0:T(128)S(1)} %copy-done.10, ...), custom_call_target="tpu_custom_call" | custom-call | flops 6000000000 | tf_op jit(solution)/shard_map/pallas_call | solution.py:931
  80.2 1.2 %collective-permute-done.14.refs_1_ = f32[1,40,128]{2,1,0:T(8,128)S(1)} collective-permute-done((f32[1,40,128]{2,1,0:T(8,128)S(1)}, f32[1,40,128]{2,1,0:T(8,128)S(1)}, u32[]{:S(2)}, u32[]{:S(2)}) %collective-permute-start.14) | collective-permute-done | bytes 20512 | tf_op jit(solution)/shard_map/ppermute | solution.py:973
  81.8 2.6 %collective-permute-start.17 = (f32[1,40,128]{2,1,0:T(8,128)S(1)}, f32[1,40,128]{2,1,0:T(8,128)S(1)}, u32[]{:S(2)}, u32[]{:S(2)}) collective-permute-start(f32[1,40,128]{2,1,0:T(8,128)S(1)} %shard_map.124.refs_0_), channel_id=1, source_target_pairs={{0,4},{1,5},{2,6},{3,7},{4,0},{5,1},{6,2},{7,3},{8,12},{9,13},{10,... | collective-permute-start | bytes 61448 | tf_op jit(solution)/shard_map/ppermute | solution.py:973
  84.6 2.0 %collective-permute-start.15 = (f32[1,40,128]{2,1,0:T(8,128)S(1)}, f32[1,40,128]{2,1,0:T(8,128)S(1)}, u32[]{:S(2)}, u32[]{:S(2)}) collective-permute-start(f32[1,40,128]{2,1,0:T(8,128)S(1)} %shard_map.124.refs_0_), channel_id=1, source_target_pairs={{0,2},{1,3},{2,0},{3,1},{4,6},{5,7},{6,4},{7,5},{8,10},{9,11},{10,... | collective-permute-start | bytes 61448 | tf_op jit(solution)/shard_map/ppermute | solution.py:973
  89.2 11.8 %all_to_all.17.refs_0_ = f32[8,40,128]{2,1,0:T(8,128)S(1)} all-to-all(f32[8,40,128]{2,1,0:T(8,128)S(1)} %shard_map.125), channel_id=1, replica_groups={{0,8,16,24,32,40,48,56},{1,9,17,25,33,41,49,57},{2,10,18,26,34,42,50,58..., dimensions={0} | all-to-all | bytes 327680 | tf_op jit(solution)/shard_map/all_to_all | solution.py:979
  101.1 1.3 %shard_map.126.part0_ref = f32[1,40,128]{2,1,0:T(8,128)S(1)} custom-call(s32[1]{0:T(128)} %bitcast.me_ref, f32[8,40,128]{2,1,0:T(8,128)S(1)} %all_to_all.17.refs_0_, f32[7,256,128]{2,1,0:T(8,128)S(1)} %copy-done.3, f32[7,256,128]{2,1,0:T(8,128)S(1)} %copy-done.4, f32[8,2,128,128]{3,2,1,0:T(8,128)S(1)} %copy-done.2, ...), custom_call_target="tpu_custom_call" | custom-call | flops 6000000000 | tf_op jit(solution)/shard_map/pallas_call | solution.py:931
  102.3 2.3 %collective-permute-start.20 = (f32[1,40,128]{2,1,0:T(8,128)S(1)}, f32[1,40,128]{2,1,0:T(8,128)S(1)}, u32[]{:S(2)}, u32[]{:S(2)}) collective-permute-start(f32[1,40,128]{2,1,0:T(8,128)S(1)} %shard_map.126.part0_ref), channel_id=1, source_target_pairs={{0,128},{1,129},{2,130},{3,131},{4,132},{5,133},{6,134},{7,135},{8... | collective-permute-start | bytes 61448 | tf_op jit(solution)/shard_map/ppermute | solution.py:973
  104.6 1.2 %collective-permute-start.19 = (f32[1,40,128]{2,1,0:T(8,128)S(1)}, f32[1,40,128]{2,1,0:T(8,128)S(1)}, u32[]{:S(2)}, u32[]{:S(2)}) collective-permute-start(f32[1,40,128]{2,1,0:T(8,128)S(1)} %shard_map.126.part0_ref), channel_id=1, source_target_pairs={{0,192},{1,193},{2,194},{3,195},{4,196},{5,197},{6,198},{7,199},{8... | collective-permute-start | bytes 61448 | tf_op jit(solution)/shard_map/ppermute | solution.py:973
  105.9 1.8 %collective-permute-done.20.part3_ref = f32[1,40,128]{2,1,0:T(8,128)S(1)} collective-permute-done((f32[1,40,128]{2,1,0:T(8,128)S(1)}, f32[1,40,128]{2,1,0:T(8,128)S(1)}, u32[]{:S(2)}, u32[]{:S(2)}) %collective-permute-start.20) | collective-permute-done | bytes 20512 | tf_op jit(solution)/shard_map/ppermute | solution.py:973
  107.7 1.9 %collective-permute-done.19.part2_ref = f32[1,40,128]{2,1,0:T(8,128)S(1)} collective-permute-done((f32[1,40,128]{2,1,0:T(8,128)S(1)}, f32[1,40,128]{2,1,0:T(8,128)S(1)}, u32[]{:S(2)}, u32[]{:S(2)}) %collective-permute-start.19) | collective-permute-done | bytes 20512 | tf_op jit(solution)/shard_map/ppermute | solution.py:973
  109.6 1.3 %shard_map.127 = f32[16,1024]{1,0:T(8,128)} custom-call(s32[1]{0:T(128)} %bitcast.me_ref, f32[1,40,128]{2,1,0:T(8,128)S(1)} %shard_map.126.part0_ref, f32[1,40,128]{2,1,0:T(8,128)S(1)} %collective-permute-done.18.part1_ref, f32[1,40,128]{2,1,0:T(8,128)S(1)} %collective-permute-done.19.part2_ref, f32[1,40,128]{2,1,0:T(8,128)S(1)} %collective-permute-done.20.part3_ref, ...), custom_call_target="tpu_custom_call" | custom-call | flops 6000000000 | tf_op jit(solution)/shard_map/pallas_call | solution.py:931
  (56 shorter events, 12.5 us)
Async XLA Ops:
  3.3 1.5 %copy-start.3 = (f32[7,256,128]{2,1,0:T(8,128)S(1)}, f32[7,256,128]{2,1,0:T(8,128)}, u32[]{:S(2)}) copy-start(f32[7,256,128]{2,1,0:T(8,128)} %refs_1_.1) | copy-start | bytes 2752516
  3.3 1.5 %collective-permute-start = (f32[1,88,128]{2,1,0:T(8,128)}, f32[1,88,128]{2,1,0:T(8,128)S(1)}, u32[]{:S(2)}, u32[]{:S(2)}) collective-permute-start(f32[1,88,128]{2,1,0:T(8,128)} %get-tuple-element.48.message_ref), channel_id=1, source_target_pairs={{0,1},{1,0},{2,3},{3,2},{4,5},{5,4},{6,7},{7,6},{8,9},{9,8},{10,11... | collective-permute-start | bytes 135176 | tf_op jit(solution)/shard_map/ppermute | solution.py:973
  4.3 6.0 %copy-start.5 = (f32[4,256,128]{2,1,0:T(8,128)S(1)}, f32[4,256,128]{2,1,0:T(8,128)}, u32[]{:S(2)}) copy-start(f32[4,256,128]{2,1,0:T(8,128)} %col_basis_ref.11) | copy-start | bytes 1572868
  4.3 6.0 %copy-start.6 = (f32[3,256,128]{2,1,0:T(8,128)S(1)}, f32[3,256,128]{2,1,0:T(8,128)}, u32[]{:S(2)}) copy-start(f32[3,256,128]{2,1,0:T(8,128)} %local_row_ref.1) | copy-start | bytes 1179652
  4.3 6.0 %copy-start.7 = (f32[3,256,128]{2,1,0:T(8,128)S(1)}, f32[3,256,128]{2,1,0:T(8,128)}, u32[]{:S(2)}) copy-start(f32[3,256,128]{2,1,0:T(8,128)} %local_col_ref.1) | copy-start | bytes 1179652
  4.3 5.9 %copy-start.8 = (f32[3,2,128,128]{3,2,1,0:T(8,128)S(1)}, f32[3,2,128,128]{3,2,1,0:T(8,128)}, u32[]{:S(2)}) copy-start(f32[3,2,128,128]{3,2,1,0:T(8,128)} %local_couple_ref.1) | copy-start | bytes 1179652
  5.4 6.2 %copy-start.2 = (f32[8,2,128,128]{3,2,1,0:T(8,128)S(1)}, f32[8,2,128,128]{3,2,1,0:T(8,128)}, u32[]{:S(2)}) copy-start(f32[8,2,128,128]{3,2,1,0:T(8,128)} %refs_3_.3) | copy-start | bytes 3145732
  5.4 6.2 %copy-start.4 = (f32[7,256,128]{2,1,0:T(8,128)S(1)}, f32[7,256,128]{2,1,0:T(8,128)}, u32[]{:S(2)}) copy-start(f32[7,256,128]{2,1,0:T(8,128)} %refs_2_.3) | copy-start | bytes 2752516
  5.5 7.2 %collective-permute-start.3 = (f32[1,88,128]{2,1,0:T(8,128)S(1)}, f32[1,88,128]{2,1,0:T(8,128)S(1)}, u32[]{:S(2)}, u32[]{:S(2)}) collective-permute-start(f32[1,88,128]{2,1,0:T(8,128)S(1)} %get-tuple-element.49.order_ref.part0_ref), channel_id=1, source_target_pairs={{0,4},{1,5},{2,6},{3,7},{4,0},{5,1},{6,2},{7,3},{8,12},{9,13},{10,... | collective-permute-start | bytes 135176 | tf_op jit(solution)/shard_map/ppermute | solution.py:973
  7.7 5.0 %collective-permute-start.2 = (f32[1,88,128]{2,1,0:T(8,128)S(1)}, f32[1,88,128]{2,1,0:T(8,128)S(1)}, u32[]{:S(2)}, u32[]{:S(2)}) collective-permute-start(f32[1,88,128]{2,1,0:T(8,128)S(1)} %get-tuple-element.49.order_ref.part0_ref), channel_id=1, source_target_pairs={{0,6},{1,7},{2,4},{3,5},{4,2},{5,3},{6,0},{7,1},{8,14},{9,15},{10,... | collective-permute-start | bytes 135176 | tf_op jit(solution)/shard_map/ppermute | solution.py:973
  9.3 4.0 %collective-permute-start.1 = (f32[1,88,128]{2,1,0:T(8,128)S(1)}, f32[1,88,128]{2,1,0:T(8,128)S(1)}, u32[]{:S(2)}, u32[]{:S(2)}) collective-permute-start(f32[1,88,128]{2,1,0:T(8,128)S(1)} %get-tuple-element.49.order_ref.part0_ref), channel_id=1, source_target_pairs={{0,2},{1,3},{2,0},{3,1},{4,6},{5,7},{6,4},{7,5},{8,10},{9,11},{10,... | collective-permute-start | bytes 135176 | tf_op jit(solution)/shard_map/ppermute | solution.py:973
  30.8 4.7 %copy-start = (f32[4,512,256]{2,1,0:T(8,128)S(1)}, f32[4,512,256]{2,1,0:T(8,128)}, u32[]{:S(2)}) copy-start(f32[4,512,256]{2,1,0:T(8,128)} %dense_ref.9) | copy-start | bytes 6291460
  30.8 4.7 %copy-start.1 = (f32[4,512,128]{2,1,0:T(8,128)S(1)}, f32[4,512,128]{2,1,0:T(8,128)}, u32[]{:S(2)}) copy-start(f32[4,512,128]{2,1,0:T(8,128)} %row_basis_ref.9) | copy-start | bytes 3145732
  30.8 4.7 %copy-start.11 = (f32[16,2048]{1,0:T(8,128)S(1)}, f32[16,2048]{1,0:T(8,128)}, u32[]{:S(2)}) copy-start(f32[16,2048]{1,0:T(8,128)} %get-tuple-element.61.y_ref) | copy-start | bytes 393220
  31.2 5.4 %collective-permute-start.6 = (f32[1,24,128]{2,1,0:T(8,128)S(1)}, f32[1,24,128]{2,1,0:T(8,128)S(1)}, u32[]{:S(2)}, u32[]{:S(2)}) collective-permute-start(f32[1,24,128]{2,1,0:T(8,128)S(1)} %get-tuple-element.54.order_ref.part0_ref), channel_id=1, source_target_pairs={{0,128},{1,129},{2,130},{3,131},{4,132},{5,133},{6,134},{7,135},{8... | collective-permute-start | bytes 36872 | tf_op jit(solution)/shard_map/ppermute | solution.py:973
  34.4 4.9 %collective-permute-start.5 = (f32[1,24,128]{2,1,0:T(8,128)S(1)}, f32[1,24,128]{2,1,0:T(8,128)S(1)}, u32[]{:S(2)}, u32[]{:S(2)}) collective-permute-start(f32[1,24,128]{2,1,0:T(8,128)S(1)} %get-tuple-element.54.order_ref.part0_ref), channel_id=1, source_target_pairs={{0,192},{1,193},{2,194},{3,195},{4,196},{5,197},{6,198},{7,199},{8... | collective-permute-start | bytes 36872 | tf_op jit(solution)/shard_map/ppermute | solution.py:973
  35.5 3.8 %collective-permute-start.4 = (f32[1,24,128]{2,1,0:T(8,128)S(1)}, f32[1,24,128]{2,1,0:T(8,128)S(1)}, u32[]{:S(2)}, u32[]{:S(2)}) collective-permute-start(f32[1,24,128]{2,1,0:T(8,128)S(1)} %get-tuple-element.54.order_ref.part0_ref), channel_id=1, source_target_pairs={{0,64},{1,65},{2,66},{3,67},{4,68},{5,69},{6,70},{7,71},{8,72},{9,... | collective-permute-start | bytes 36872 | tf_op jit(solution)/shard_map/ppermute | solution.py:973
  35.5 3.8 %copy-start.10 = (s32[4]{0:T(128)S(1)}, s32[4]{0:T(128)}, u32[]{:S(2)}) copy-start(s32[4]{0:T(128)} %rows_ref.5) | copy-start | bytes 52
  42.7 1.3 %collective-permute-start.7 = (f32[1,104,128]{2,1,0:T(8,128)S(1)}, f32[1,104,128]{2,1,0:T(8,128)S(1)}, u32[]{:S(2)}, u32[]{:S(2)}) collective-permute-start(f32[1,104,128]{2,1,0:T(8,128)S(1)} %get-tuple-element.62.part0_ref), channel_id=1, source_target_pairs={{0,1},{1,0},{2,3},{3,2},{4,5},{5,4},{6,7},{7,6},{8,9},{9,8},{10,11... | collective-permute-start | bytes 159752 | tf_op jit(solution)/shard_map/ppermute | solution.py:973
  44.5 8.5 %collective-permute-start.10 = (f32[1,168,128]{2,1,0:T(8,128)S(1)}, f32[1,168,128]{2,1,0:T(8,128)S(1)}, u32[]{:S(2)}, u32[]{:S(2)}) collective-permute-start(f32[1,168,128]{2,1,0:T(8,128)S(1)} %get-tuple-element.64.order_ref.part0_ref), channel_id=1, source_target_pairs={{0,4},{1,5},{2,6},{3,7},{4,0},{5,1},{6,2},{7,3},{8,12},{9,13},{10,... | collective-permute-start | bytes 258056 | tf_op jit(solution)/shard_map/ppermute | solution.py:973
  47.1 5.9 %collective-permute-start.9 = (f32[1,168,128]{2,1,0:T(8,128)S(1)}, f32[1,168,128]{2,1,0:T(8,128)S(1)}, u32[]{:S(2)}, u32[]{:S(2)}) collective-permute-start(f32[1,168,128]{2,1,0:T(8,128)S(1)} %get-tuple-element.64.order_ref.part0_ref), channel_id=1, source_target_pairs={{0,6},{1,7},{2,4},{3,5},{4,2},{5,3},{6,0},{7,1},{8,14},{9,15},{10,... | collective-permute-start | bytes 258056 | tf_op jit(solution)/shard_map/ppermute | solution.py:973
  47.8 5.3 %collective-permute-start.8 = (f32[1,168,128]{2,1,0:T(8,128)S(1)}, f32[1,168,128]{2,1,0:T(8,128)S(1)}, u32[]{:S(2)}, u32[]{:S(2)}) collective-permute-start(f32[1,168,128]{2,1,0:T(8,128)S(1)} %get-tuple-element.64.order_ref.part0_ref), channel_id=1, source_target_pairs={{0,2},{1,3},{2,0},{3,1},{4,6},{5,7},{6,4},{7,5},{8,10},{9,11},{10,... | collective-permute-start | bytes 258056 | tf_op jit(solution)/shard_map/ppermute | solution.py:973
  68.3 5.7 %collective-permute-start.13 = (f32[1,112,128]{2,1,0:T(8,128)S(1)}, f32[1,112,128]{2,1,0:T(8,128)S(1)}, u32[]{:S(2)}, u32[]{:S(2)}) collective-permute-start(f32[1,112,128]{2,1,0:T(8,128)S(1)} %get-tuple-element.72.order_ref.part0_ref), channel_id=1, source_target_pairs={{0,128},{1,129},{2,130},{3,131},{4,132},{5,133},{6,134},{7,135},{8... | collective-permute-start | bytes 172040 | tf_op jit(solution)/shard_map/ppermute | solution.py:973
  69.9 5.4 %collective-permute-start.12 = (f32[1,112,128]{2,1,0:T(8,128)S(1)}, f32[1,112,128]{2,1,0:T(8,128)S(1)}, u32[]{:S(2)}, u32[]{:S(2)}) collective-permute-start(f32[1,112,128]{2,1,0:T(8,128)S(1)} %get-tuple-element.72.order_ref.part0_ref), channel_id=1, source_target_pairs={{0,192},{1,193},{2,194},{3,195},{4,196},{5,197},{6,198},{7,199},{8... | collective-permute-start | bytes 172040 | tf_op jit(solution)/shard_map/ppermute | solution.py:973
  70.9 4.4 %collective-permute-start.11 = (f32[1,112,128]{2,1,0:T(8,128)S(1)}, f32[1,112,128]{2,1,0:T(8,128)S(1)}, u32[]{:S(2)}, u32[]{:S(2)}) collective-permute-start(f32[1,112,128]{2,1,0:T(8,128)S(1)} %get-tuple-element.72.order_ref.part0_ref), channel_id=1, source_target_pairs={{0,64},{1,65},{2,66},{3,67},{4,68},{5,69},{6,70},{7,71},{8,72},{9,... | collective-permute-start | bytes 172040 | tf_op jit(solution)/shard_map/ppermute | solution.py:973
  80.1 1.3 %collective-permute-start.14 = (f32[1,40,128]{2,1,0:T(8,128)S(1)}, f32[1,40,128]{2,1,0:T(8,128)S(1)}, u32[]{:S(2)}, u32[]{:S(2)}) collective-permute-start(f32[1,40,128]{2,1,0:T(8,128)S(1)} %get-tuple-element.84.refs_0_), channel_id=1, source_target_pairs={{0,1},{1,0},{2,3},{3,2},{4,5},{5,4},{6,7},{7,6},{8,9},{9,8},{10,11... | collective-permute-start | bytes 61448 | tf_op jit(solution)/shard_map/ppermute | solution.py:973
  81.8 5.5 %collective-permute-start.17 = (f32[1,40,128]{2,1,0:T(8,128)S(1)}, f32[1,40,128]{2,1,0:T(8,128)S(1)}, u32[]{:S(2)}, u32[]{:S(2)}) collective-permute-start(f32[1,40,128]{2,1,0:T(8,128)S(1)} %shard_map.124.refs_0_), channel_id=1, source_target_pairs={{0,4},{1,5},{2,6},{3,7},{4,0},{5,1},{6,2},{7,3},{8,12},{9,13},{10,... | collective-permute-start | bytes 61448 | tf_op jit(solution)/shard_map/ppermute | solution.py:973
  84.4 3.8 %collective-permute-start.16 = (f32[1,40,128]{2,1,0:T(8,128)S(1)}, f32[1,40,128]{2,1,0:T(8,128)S(1)}, u32[]{:S(2)}, u32[]{:S(2)}) collective-permute-start(f32[1,40,128]{2,1,0:T(8,128)S(1)} %shard_map.124.refs_0_), channel_id=1, source_target_pairs={{0,6},{1,7},{2,4},{3,5},{4,2},{5,3},{6,0},{7,1},{8,14},{9,15},{10,... | collective-permute-start | bytes 61448 | tf_op jit(solution)/shard_map/ppermute | solution.py:973
  84.6 3.8 %collective-permute-start.15 = (f32[1,40,128]{2,1,0:T(8,128)S(1)}, f32[1,40,128]{2,1,0:T(8,128)S(1)}, u32[]{:S(2)}, u32[]{:S(2)}) collective-permute-start(f32[1,40,128]{2,1,0:T(8,128)S(1)} %shard_map.124.refs_0_), channel_id=1, source_target_pairs={{0,2},{1,3},{2,0},{3,1},{4,6},{5,7},{6,4},{7,5},{8,10},{9,11},{10,... | collective-permute-start | bytes 61448 | tf_op jit(solution)/shard_map/ppermute | solution.py:973
  102.3 5.4 %collective-permute-start.20 = (f32[1,40,128]{2,1,0:T(8,128)S(1)}, f32[1,40,128]{2,1,0:T(8,128)S(1)}, u32[]{:S(2)}, u32[]{:S(2)}) collective-permute-start(f32[1,40,128]{2,1,0:T(8,128)S(1)} %shard_map.126.part0_ref), channel_id=1, source_target_pairs={{0,128},{1,129},{2,130},{3,131},{4,132},{5,133},{6,134},{7,135},{8... | collective-permute-start | bytes 61448 | tf_op jit(solution)/shard_map/ppermute | solution.py:973
  104.6 5.0 %collective-permute-start.19 = (f32[1,40,128]{2,1,0:T(8,128)S(1)}, f32[1,40,128]{2,1,0:T(8,128)S(1)}, u32[]{:S(2)}, u32[]{:S(2)}) collective-permute-start(f32[1,40,128]{2,1,0:T(8,128)S(1)} %shard_map.126.part0_ref), channel_id=1, source_target_pairs={{0,192},{1,193},{2,194},{3,195},{4,196},{5,197},{6,198},{7,199},{8... | collective-permute-start | bytes 61448 | tf_op jit(solution)/shard_map/ppermute | solution.py:973
  105.8 3.8 %collective-permute-start.18 = (f32[1,40,128]{2,1,0:T(8,128)S(1)}, f32[1,40,128]{2,1,0:T(8,128)S(1)}, u32[]{:S(2)}, u32[]{:S(2)}) collective-permute-start(f32[1,40,128]{2,1,0:T(8,128)S(1)} %shard_map.126.part0_ref), channel_id=1, source_target_pairs={{0,64},{1,65},{2,66},{3,67},{4,68},{5,69},{6,70},{7,71},{8,72},{9,... | collective-permute-start | bytes 61448 | tf_op jit(solution)/shard_map/ppermute | solution.py:973
  (1 other events, 0.8 us)
